TPU v7x, 32 devices: a whole 2x2x4 slice. The times are simulated.
32 devices in a mesh: grp: 2 (over y), tp: 4 (over z), kv: 4 (over x, core).
Axes of the slice: x: 2, y: 2, z: 4, core: 2. Of those that a mesh axis runs over, the one named last changes fastest.
Arguments:
- states: bfloat16 [8, 8192], P('grp', 'tp'), parts along dimension 0, may hold values from -3000 to 3000
- norm_gains: float32 [2, 8192], P(None, 'tp'), may hold values from 0.1 to 1.9
- w_query: bfloat16 [8192, 32, 128], P('tp', 'kv'), may hold values from -0.0625 to 0.0625
- w_keyval: bfloat16 [8192, 4, 256], P('tp', 'kv'), may hold values from -0.0625 to 0.0625
- w_out: bfloat16 [4096, 8192], P('kv', 'tp'), may hold values from -0.5 to 0.5
- w_gate_up: bfloat16 [8192, 2, 14336], P('tp', None, 'kv'), may hold values from -0.0625 to 0.0625
- w_down: bfloat16 [14336, 8192], P('kv', 'tp'), may hold values from -0.046875 to 0.046875
- kv_cache: bfloat16 [8, 8192, 4, 256], P(('grp', 'tp'), None, 'kv'), parts along dimension 0, may hold values from -2000 to 2000
- lengths: int32 [8], P('grp'), parts along dimension 0, may hold values from 2048 to 8192, as said below
- owner_rows: int32 [8], P('grp'), parts along dimension 0, may hold values from 0 to 3, each once
Outputs:
- attn_out: bfloat16 [8, 8192], P('grp', 'tp'), parts along dimension 0
- ffn_out: bfloat16 [8, 8192], P('grp', 'tp'), parts along dimension 0
- new_kv: bfloat16 [8, 4, 256], P(('grp', 'tp'), 'kv'), parts along dimension 0
There are 2 independent parts, one for each index of `grp`. A program takes and returns all parts, laid end to end along the dimension named above; an argument that names none is the same for every part. Nothing has to cross between parts.
Inputs may be any that keep to these rules, and one draw needn't show every extreme that they name: `lengths`: some document has exactly 8192 cached tokens. `owner_rows`: A permutation of the documents.
All inputs are finite; a program needn't handle non-finite values.
Results may differ from a plain program's by a relative error of at most 0.0165.
The roundings to bfloat16 on the way count: a program that leaves them out, or rounds other values in their place, can miss the bound.
Values may be sent and summed in bfloat16 or wider, within the bound.
No kernel may reach another device: no remote copies, remote signals or barrier semaphores. Data moves between devices by JAX's collectives and lax.ppermute only.
A program may use at most 256 MiB of HBM per device.

v0:
```python
import jax
import jax.numpy as jnp
from jax import lax
from jax.sharding import PartitionSpec as P

D = 8192


eps_norm = 1e-05
rope_base = 500000.0


def rotate(values, places):
    extent = values.shape[-1]
    midway = extent // 2
    frequency = jnp.power(
        jnp.float32(rope_base), -(jnp.arange(midway, dtype=jnp.float32) * 2.0 / extent)
    )
    angles = places.astype(jnp.float32)[:, None] * frequency[None, :]
    cosine = jnp.cos(angles)[:, None, :]
    sines = jnp.sin(angles)[:, None, :]
    leading = values[..., :midway]
    trailing = values[..., midway:]
    return jnp.concatenate(
        [leading * cosine - trailing * sines, trailing * cosine + leading * sines], axis=-1
    )


def per_device(
    states, norm_gains, w_query, w_keyval, w_out, w_gate_up, w_down, kv_cache, lengths, owner_rows
):
    doc_count, local_width = states.shape
    owned_rows = kv_cache.shape[0]
    cache_len = kv_cache.shape[1]
    local_heads = w_query.shape[1]
    head_dim = w_query.shape[2]
    local_groups = w_keyval.shape[1]
    per_group = local_heads // local_groups
    score_scale = head_dim ** (-0.5)
    my_docs = lax.dynamic_slice_in_dim(owner_rows, lax.axis_index("tp") * owned_rows, owned_rows)
    places = jnp.take(lengths, my_docs, axis=0)
    inputs = states.astype(jnp.float32)
    squares = lax.psum(jnp.sum(inputs * inputs, axis=1), "tp")
    normed = (inputs * lax.rsqrt(squares[:, None] / D + eps_norm) * norm_gains[0][None, :]).astype(
        jnp.bfloat16
    )
    query_mat = w_query.reshape(local_width, local_heads * head_dim)
    keyval_mat = w_keyval.reshape(local_width, local_groups * 2 * head_dim)
    query_part = jnp.dot(normed, query_mat, preferred_element_type=jnp.float32)
    keyval_part = jnp.dot(normed, keyval_mat, preferred_element_type=jnp.float32)
    query_all, keyval_all = lax.psum((query_part, keyval_part), "tp")
    queries = jnp.take(query_all, my_docs, axis=0)
    keyvals = jnp.take(keyval_all, my_docs, axis=0)
    queries = queries.reshape(owned_rows, local_heads, head_dim)
    keyvals = keyvals.reshape(owned_rows, local_groups, 2 * head_dim)
    rotated = (
        rotate(queries, places)
        .astype(jnp.bfloat16)
        .reshape(owned_rows, local_groups, per_group, head_dim)
    )
    new_kv = jnp.concatenate(
        [rotate(keyvals[..., :head_dim], places), keyvals[..., head_dim:]], axis=-1
    ).astype(jnp.bfloat16)
    own_score = (
        jnp.einsum(
            "rhgd,rhd->rhg", rotated, new_kv[..., :head_dim], preferred_element_type=jnp.float32
        )
        * score_scale
    )
    scores = (
        jnp.einsum(
            "rhgd,rlhd->rhgl", rotated, kv_cache[..., :head_dim], preferred_element_type=jnp.float32
        )
        * score_scale
    )
    attended_mask = jnp.arange(cache_len, dtype=jnp.int32)[None, :] < places[:, None]
    scores = jnp.where(attended_mask[:, None, None, :], scores, -jnp.inf)
    highest = jnp.maximum(jnp.max(scores, axis=-1), own_score)
    weights = jnp.exp(scores - highest[..., None])
    cache_totals = jnp.sum(weights, axis=-1)
    weighted = jnp.einsum(
        "rhgl,rlhd->rhgd",
        weights.astype(jnp.bfloat16),
        kv_cache[..., head_dim:],
        preferred_element_type=jnp.float32,
    )
    own_weight = jnp.exp(own_score - highest)
    totals = cache_totals + own_weight
    own_rounded = lax.optimization_barrier(own_weight.astype(jnp.bfloat16))
    weighted = (
        weighted
        + own_rounded.astype(jnp.float32)[..., None]
        * new_kv[..., head_dim:].astype(jnp.float32)[:, :, None, :]
    )
    attended = (
        (weighted / totals[..., None])
        .astype(jnp.bfloat16)
        .reshape(owned_rows, local_heads * head_dim)
    )
    slot_terms = jnp.dot(
        lax.all_gather(attended, "tp", axis=0, tiled=True),
        w_out,
        preferred_element_type=jnp.float32,
    )
    slot_sums = lax.psum(slot_terms, "kv")
    placing = (owner_rows[:, None] == jnp.arange(doc_count, dtype=jnp.int32)[None, :]).astype(
        jnp.float32
    )
    attn_doc = jnp.dot(
        placing.T, slot_sums, precision=lax.Precision.HIGHEST, preferred_element_type=jnp.float32
    )
    attn_out = attn_doc.astype(jnp.bfloat16)
    resid = (inputs + attn_out.astype(jnp.float32)).astype(jnp.bfloat16)
    resid_float = resid.astype(jnp.float32)
    squares_two = lax.psum(jnp.sum(resid_float * resid_float, axis=1), "tp")
    normed_two = (
        resid_float * lax.rsqrt(squares_two[:, None] / D + eps_norm) * norm_gains[1][None, :]
    ).astype(jnp.bfloat16)
    hidden_local = w_gate_up.shape[2]
    partial_value = jnp.dot(
        normed_two,
        w_gate_up.reshape(local_width, 2 * hidden_local),
        preferred_element_type=jnp.float32,
    ).reshape(doc_count, 2, hidden_local)
    summed = lax.psum(partial_value, "tp")
    active = (jax.nn.silu(summed[:, 0]) * summed[:, 1]).astype(jnp.bfloat16)
    ffn_terms = jnp.dot(active, w_down, preferred_element_type=jnp.float32)
    ffn_out = lax.psum(ffn_terms, "kv").astype(jnp.bfloat16)
    return (attn_out, ffn_out, new_kv)


def solution(mesh):
    return jax.shard_map(
        per_device,
        mesh=mesh,
        in_specs=(
            P("grp", "tp"),
            P(None, "tp"),
            P("tp", "kv", None),
            P("tp", "kv", None),
            P("kv", "tp"),
            P("tp", None, "kv"),
            P("kv", "tp"),
            P(("grp", "tp"), None, "kv", None),
            P("grp"),
            P("grp"),
        ),
        out_specs=(P("grp", "tp"), P("grp", "tp"), P(("grp", "tp"), "kv", None)),
        check_vma=False,
    )
```

profile of v0, /device:TPU:0, one launch (start us, length us, event | category | flops | bytes accessed | tf_op | source)
XLA Modules:
  0.0 220.2 jit_solution(15797256473129606491)
XLA Ops:
  7.2 0.0 copy-start
  7.2 0.0 all-reduce.3.cloned.1.call-start
  7.2 1.3 dynamic_slice.3
  10.5 0.8 fusion.30
  11.3 1.2 dynamic-slice.8
  13.2 13.5 %psum.49 = f32[4]{0:T(128)S(1)} all-reduce(f32[4]{0:T(128)S(1)} %fusion.30), channel_id=1, replica_groups=mesh['grp'=2,'tp'=4,'kv'=4] {'tp'}, use_global_device_ids=true, to_apply=%region_1.2 | all-reduce | flops 4 | bytes 32 | tf_op jit(solution)/shard_map/psum | solution.py:43
  26.7 0.1 fusion.54
  26.8 0.8 fusion.62
  27.6 1.0 fusion.19
  28.6 2.9 %fusion.1 = f32[4,1024]{1,0:T(4,128)S(1)} fusion(bf16[256,8,8,128]{3,2,1,0:T(8,128)(2,1)} %bitcast.83, bf16[4,2048]{1,0:T(4,128)(2,1)} %param.10, f32[2048]{0:T(1024)S(1)} %bitcast.86, f32[4]{0:T(128)S(1)} %add_rsqrt_fusion.1), kind=kOutput, calls=%fused_computation.2 | convolution fusion | flops 16809984 | bytes 4235280 | tf_op jit(solution)/shard_map/dot_general | solution.py:49
  31.5 15.7 %all-reduce = (f32[4,1024]{1,0:T(4,128)S(1)}, f32[4,256]{1,0:T(4,128)S(1)}) all-reduce(f32[4,1024]{1,0:T(4,128)S(1)} %fusion.1, f32[4,256]{1,0:T(4,128)S(1)} %fusion.19), channel_id=1, replica_groups=mesh['grp'=2,'tp'=4,'kv'=4] {'tp'}, use_global_device_ids=true, to_apply=%region_2.3 | all-reduce | flops 5120 | bytes 40960 | tf_op jit(solution)/shard_map/psum | solution.py:51
  47.3 0.1 subtract_convert_fusion.1
  47.4 0.1 fusion.46
  47.4 0.2 fusion.18
  47.6 2.4 %fusion.64 = (f32[8]{0:T(128)S(1)}, f32[8,8192]{1,0:T(8,128)S(1)}) fusion(bf16[1,8192,1,256]{3,1,2,0:T(8,128)(2,1)} %param.17, bf16[8,64]{1,0:T(8,128)(2,1)S(1)} %get-tuple-element.43, bf16[8,64]{1,0:T(8,128)(2,1)S(1)} %get-tuple-element.42, pred[8192]{0:T(1024)(128)(4,1)S(1)} %iota_compare_fusion), kind=kOutput, calls=%fused_computation.84 | convolution fusion | flops 16977912 | bytes 2369568 | tf_op jit(solution)/shard_map/rhgd,rlhd->rhgl/dot_general | solution.py:71
  50.1 0.3 fusion.21
  50.4 2.0 fusion.15
  52.4 13.1 %all-gather = bf16[4,1,1024]{2,1,0:T(2,128)(2,1)S(1)} all-gather(bf16[1,1,1024]{2,1,0:T(2,128)(2,1)S(1)} %reshape.305), channel_id=1, replica_groups=mesh['grp'=2,'tp'=4,'kv'=4] {'tp'}, dimensions={0}, use_global_device_ids=true | all-gather | bytes 10240 | tf_op jit(solution)/shard_map/all_gather | solution.py:101
  65.5 2.8 %fusion.42 = f32[4,2048]{1,0:T(4,128)S(1)} fusion(bf16[1024,2048]{1,0:T(8,128)(2,1)} %param.14, bf16[4,1,1024]{2,1,0:T(2,128)(2,1)S(1)} %all-gather), kind=kOutput, calls=%fused_computation.46 | convolution fusion | flops 16777216 | bytes 4235264 | tf_op jit(solution)/shard_map/dot_general | solution.py:100
  68.4 10.3 %psum.52 = f32[4,2048]{1,0:T(4,128)S(1)} all-reduce(f32[4,2048]{1,0:T(4,128)S(1)} %fusion.42), channel_id=1, replica_groups=mesh['grp'=2,'tp'=4,'kv'=4] {'kv'}, use_global_device_ids=true, to_apply=%region_6.7 | all-reduce | flops 8192 | bytes 65536 | tf_op jit(solution)/shard_map/psum | solution.py:105
  78.6 0.0 copy-done.2
  78.7 0.0 copy-done.4
  78.7 0.4 fusion.27
  79.1 10.2 %psum.53 = f32[4]{0:T(128)S(1)} all-reduce(f32[4]{0:T(128)S(1)} %get-tuple-element.50), channel_id=1, replica_groups=mesh['grp'=2,'tp'=4,'kv'=4] {'tp'}, use_global_device_ids=true, to_apply=%region_8.9 | all-reduce | flops 4 | bytes 32 | tf_op jit(solution)/shard_map/psum | solution.py:115
  89.3 20.8 %copy.19 = bf16[256,8,2,3584]{3,1,2,0:T(8,128)(2,1)} copy(bf16[256,8,2,3584]{3,2,1,0:T(2,128)(2,1)} %bitcast.82) | data formatting | bytes 58720256
  110.0 38.6 %copy.16 = bf16[7168,2048]{1,0:T(8,128)(2,1)} copy(bf16[7168,2048]{0,1:T(8,128)(2,1)} %bitcast.81) | data formatting | bytes 58720256 | tf_op jit(solution)/shard_map/dot_general | solution.py:120
  148.6 13.9 %fusion.38 = f32[4,2,3584]{2,0,1:T(4,128)} fusion(bf16[2,3584,2048]{2,1,0:T(8,128)(2,1)} %bitcast.80, f32[2048]{0:T(1024)S(1)} %bitcast.84, f32[4]{0:T(128)S(1)} %add_rsqrt_fusion, bf16[4,2048]{1,0:T(4,128)(2,1)S(1)} %copy-done.2, bf16[4,2048]{1,0:T(4,128)(2,1)S(1)} %get-tuple-element.51), kind=kOutput, calls=%fused_computation.43 | convolution fusion | flops 117506048 | bytes 29515792 | tf_op jit(solution)/shard_map/dot_general | solution.py:120
  162.5 0.0 all-reduce.3.cloned.1.call-update
  162.6 0.6 pad_maximum_fusion.1
  163.2 32.0 %all-reduce.3.cloned.1.call-done = f32[4,2,3584]{2,0,1:T(4,128)} async-done(((f32[4,2,3584]{2,0,1:T(4,128)}), f32[4,2,3584]{2,0,1:T(4,128)}) %all-reduce.3.cloned.1.call-update) | async-done | bytes 114704 | tf_op jit(solution)/shard_map/psum | solution.py:125
  195.2 7.3 %fusion.34 = f32[4,2048]{1,0:T(4,128)S(1)} fusion(bf16[3584,2048]{1,0:T(8,128)(2,1)} %param.16, f32[4,2,3584]{2,0,1:T(4,128)} %all-reduce.3.cloned.1.call-done), kind=kOutput, calls=%fused_computation.40 | convolution fusion | flops 58806272 | bytes 14827520 | tf_op jit(solution)/shard_map/dot_general | solution.py:127
  202.5 10.8 %psum.55 = bf16[4,2048]{1,0:T(4,128)(2,1)} all-reduce(f32[4,2048]{1,0:T(4,128)S(1)} %fusion.34), channel_id=1, replica_groups=mesh['grp'=2,'tp'=4,'kv'=4] {'kv'}, use_global_device_ids=true, to_apply=%region_10.11 | all-reduce | flops 8192 | bytes 49152 | tf_op jit(solution)/shard_map/psum | solution.py:128
  (17 shorter events, 0.1 us)
Async XLA Ops:
  7.2 20.4 %copy-start = (bf16[2048,1,256]{2,0,1:T(8,128)(2,1)S(1)}, bf16[2048,1,256]{2,0,1:T(8,128)(2,1)}, u32[]{:S(2)}) copy-start(bf16[2048,1,256]{2,0,1:T(8,128)(2,1)} %param.13) | copy-start | bytes 3145732
  7.2 188.0 %all-reduce.3.cloned.1.call-start = ((), (), s32[]{:S(2)}) async-start(), calls=%async_computation | async-start | bytes 229376 | tf_op jit(solution)/shard_map/psum | solution.py:125
  47.6 31.0 %copy-start.2 = (bf16[4,2048]{1,0:T(4,128)(2,1)S(1)}, bf16[4,2048]{1,0:T(4,128)(2,1)}, u32[]{:S(2)}) copy-start(bf16[4,2048]{1,0:T(4,128)(2,1)} %param.10) | copy-start | bytes 49156
  47.6 31.0 %copy-start.4 = (s32[4]{0:T(128)S(1)}, s32[4]{0:T(128)}, u32[]{:S(2)}) copy-start(s32[4]{0:T(128)} %param.19) | copy-start | bytes 52
  79.1 69.6 %copy-start.3 = (bf16[4,2048]{1,0:T(4,128)(2,1)}, bf16[4,2048]{1,0:T(4,128)(2,1)S(1)}, u32[]{:S(2)}) copy-start(bf16[4,2048]{1,0:T(4,128)(2,1)S(1)} %get-tuple-element.51) | copy-start | bytes 49156
  195.2 18.2 %copy-start.1 = (bf16[2048,1,256]{2,0,1:T(8,128)(2,1)S(1)}, bf16[2048,1,256]{2,0,1:T(8,128)(2,1)}, u32[]{:S(2)}) copy-start(bf16[2048,1,256]{2,0,1:T(8,128)(2,1)} %param.13) | copy-start | bytes 3145732
Sparse Core Ops, SparseCore 0:
  162.7 32.4 all-reduce.2
where the time goes:
time: 222 us; the launch traced here: 220 us
  blocking collectives  73.6 us (33%)
  local copies, waits for them, and re-layouts  62.8 us (28%)
  matrix products  33 us (15%)
  waiting for transfers between devices  32 us (14%)
  between operations  16.7 us (8%)
    dot_general x1, local copies, waits for them, and re-layouts, per_device(): jnp.dot(normed_two, w_gate_up.reshape(local_width, 2 * hidden_local), pre...  38.6 us
    psum x1, waiting for transfers between devices, per_device(): summed = lax.psum(partial_value, 'tp')  32 us
    unnamed x12, local copies, waits for them, and re-layouts  20.8 us
    psum x1, blocking collectives, per_device(): query_all, keyval_all = lax.psum((query_part, keyval_part), 'tp')  15.7 us
    dot_general x1, matrix products, per_device(): jnp.dot(normed_two, w_gate_up.reshape(local_width, 2 * hidden_local), pre...  13.9 us
    psum x1, blocking collectives, per_device(): squares = lax.psum(jnp.sum(inputs * inputs, axis=1), 'tp')  13.5 us
    all_gather x1, blocking collectives, per_device(): lax.all_gather(attended, 'tp', axis=0, tiled=True)  13.1 us
    psum x1, blocking collectives, per_device(): ffn_out = lax.psum(ffn_terms, 'kv').astype(jnp.bfloat16)  10.8 us
  transfers between devices with their start and end apart: 1, of which 1 were waited for; matrix products, arithmetic and copies ran while one was open for 0% of the time, Pallas kernels for 0%

commit v1 on v0

v1 whole, which is shorter than its diff:
```python
import functools
import math

import jax
import jax.numpy as jnp
import numpy as np
from jax import lax
from jax.experimental import pallas as pl
from jax.experimental.pallas import tpu as pltpu
from jax.sharding import PartitionSpec as P

D = 8192
EPS = 1e-05
ROPE_BASE = 500000.0
LANES = 128
MIB = 1 << 20
GU_BLOCK = 256
F32 = jnp.float32
BF16 = jnp.bfloat16
TURN_A = 6.28125
TURN_B = 0.0019340515136718750
TURN_C = 2.0 * math.pi - TURN_A - TURN_B


def vmem():
    return pl.BlockSpec(memory_space=pltpu.VMEM)


def smem():
    return pl.BlockSpec(memory_space=pltpu.SMEM)


def hbm():
    return pl.BlockSpec(memory_space=pl.ANY)


def exchange(arrays, axis, size):
    return [arrays[0]] + [
        lax.ppermute(arrays[s], axis, [(i, i ^ s) for i in range(size)])
        for s in range(1, size)
    ]


def tree_sum(parts):
    while len(parts) > 1:
        parts = [a + b for a, b in zip(parts[::2], parts[1::2])]
    return parts[0]


def two_parts(scaled):
    high = scaled.astype(BF16).astype(F32)
    low = scaled - high
    return jnp.concatenate([high, high, low, low], axis=0).astype(BF16)


def spread(rows16, out_ref, docs):
    width = rows16.shape[1]
    source = lax.broadcasted_iota(jnp.int32, (LANES, 2 * LANES), 0)
    target = lax.broadcasted_iota(jnp.int32, (LANES, 2 * LANES), 1)
    pick = (lax.shift_right_logical(target, 1) == source).astype(F32).astype(BF16)
    row = lax.broadcasted_iota(jnp.int32, (4 * docs, 2 * LANES), 0)
    lane = lax.broadcasted_iota(jnp.int32, (4 * docs, 2 * LANES), 1)
    keep = lax.rem(lax.div(row, docs), 2) == lax.rem(lane, 2)
    for c in range(width // LANES):
        doubled = jnp.dot(
            rows16[:, c * LANES : (c + 1) * LANES], pick, preferred_element_type=F32
        )
        out_ref[:, 2 * c * LANES : 2 * (c + 1) * LANES] = jnp.where(keep, doubled, 0.0).astype(BF16)


def pick_row(ref, index):
    row = lax.broadcasted_iota(jnp.int32, ref.shape, 0)
    return jnp.sum(jnp.where(row == index, ref[...], 0.0), axis=0, keepdims=True)


def qkv_kernel(tp, owner, states, gains, wq, wkv, *rest):
    outs = rest[:tp]
    wq_buf, wkv_buf, spread_buf, res, kv_res, sq_res, sems = rest[tp:]
    docs, width = states.shape
    pairs = wq.shape[1]
    halves = wq_buf.shape[0]
    rows = 2 * width // halves
    copies = []
    for c in range(halves):
        for p in range(pairs):
            copies.append(
                pltpu.make_async_copy(
                    wq.at[pl.ds(c * rows // 2, rows // 2), p],
                    wq_buf.at[c, p],
                    sems.at[c * pairs + p],
                )
            )
    kv_copy = pltpu.make_async_copy(wkv, wkv_buf, sems.at[halves * pairs])
    for copy in copies:
        copy.start()
    kv_copy.start()
    me = lax.axis_index("tp")
    x = states[...].astype(F32)
    sq_res[...] = jnp.broadcast_to(jnp.sum(x * x, axis=1, keepdims=True), sq_res.shape)
    rows16 = two_parts(x * gains[0:1, :])
    spread(rows16, spread_buf, docs)
    total = jnp.zeros((4 * docs, pairs * LANES), F32)
    for c in range(halves):
        for p in range(pairs):
            copies[c * pairs + p].wait()
        block = jnp.concatenate(
            [wq_buf.at[c, p].reshape(rows, LANES)[...] for p in range(pairs)], axis=1
        )
        total = total + jnp.dot(
            spread_buf[:, c * rows : (c + 1) * rows], block, preferred_element_type=F32
        )
    res[...] = total[: 2 * docs] + total[2 * docs :]
    kv_copy.wait()
    kv_total = jnp.dot(rows16, wkv_buf[...], preferred_element_type=F32)
    kv_res[...] = kv_total[: 2 * docs] + kv_total[2 * docs :]
    for s in range(tp):
        doc = owner[me ^ s]
        for parity in range(2):
            chosen = pick_row(res, parity * docs + doc)
            for p in range(pairs):
                outs[s][2 * p + parity : 2 * p + parity + 1, :] = chosen[
                    :, p * LANES : (p + 1) * LANES
                ]
        chosen = pick_row(kv_res, doc)
        h = 2 * pairs
        outs[s][h : h + 1, :] = chosen[:, :LANES]
        outs[s][h + 1 : h + 2, :] = chosen[:, LANES:]
        outs[s][h + 2 : h + 3, :] = pick_row(sq_res, doc)
        outs[s][h + 3 :, :] = jnp.zeros((outs[s].shape[0] - h - 3, LANES), F32)


def attend_kernel(tp, heads, owner, lengths, frequency, cache, *rest):
    parts = rest[:tp]
    heads_out, new_kv_out, cache_buf, scores, sems = rest[tp:]
    blocks, rows = cache_buf.shape[:2]
    copies = [
        pltpu.make_async_copy(cache.at[pl.ds(b * rows, rows)], cache_buf.at[b], sems.at[b])
        for b in range(blocks)
    ]
    for copy in copies:
        copy.start()
    length = lengths[owner[lax.axis_index("tp")]]
    sums = tree_sum([part[...] for part in parts])
    sums = sums * lax.rsqrt(sums[heads + 2 : heads + 3, :] / D + EPS)
    angle = length.astype(F32) * frequency[...]
    turns = jnp.floor(angle * (0.5 / math.pi) + 0.5)
    angle = ((angle - turns * TURN_A) - turns * TURN_B) - turns * TURN_C
    cosine = jnp.cos(angle)
    sine = jnp.sin(angle)
    lane = lax.broadcasted_iota(jnp.int32, (1, LANES), 1)
    sine = jnp.where(lane < LANES // 2, -sine, sine)
    rotated = sums * cosine + pltpu.roll(sums, LANES // 2, 1) * sine
    query = rotated[:heads].astype(BF16)
    key = rotated[heads : heads + 1].astype(BF16)
    value = sums[heads + 1 : heads + 2].astype(BF16)
    new_kv_out[:, :LANES] = key
    new_kv_out[:, LANES:] = value
    key = key.astype(F32)
    value = value.astype(F32)
    scale = LANES ** (-0.5)
    own = jnp.sum(query.astype(F32) * key, axis=1, keepdims=True) * scale
    column = lax.broadcasted_iota(jnp.int32, (heads, rows), 1)
    top = own
    for b in range(blocks):
        copies[b].wait()
        block = lax.dot_general(
            query,
            cache_buf[b, :, :LANES],
            (((1,), (1,)), ((), ())),
            preferred_element_type=F32,
        )
        block = jnp.where(column < length - b * rows, block * scale, -jnp.inf)
        top = jnp.maximum(top, jnp.max(block, axis=1, keepdims=True))
        scores[:, b * rows : (b + 1) * rows] = block
    own = jnp.exp(own - top)
    total = own
    acc = own.astype(BF16).astype(F32) * value
    for b in range(blocks):
        weights = jnp.exp(scores[:, b * rows : (b + 1) * rows] - top)
        total = total + jnp.sum(weights, axis=1, keepdims=True)
        acc = acc + jnp.dot(
            weights.astype(BF16), cache_buf[b, :, LANES:], preferred_element_type=F32
        )
    heads_out[...] = (acc / total).astype(BF16)


def out_kernel(tp, owner, w_out, *rest):
    parts = rest[:tp]
    out, left = rest[tp:]
    docs = out.shape[0]
    me = lax.axis_index("tp")
    row = lax.broadcasted_iota(jnp.int32, (left.shape[0], LANES), 0)
    own = [parts[s][...].astype(F32) for s in range(tp)]
    for h in range(own[0].shape[0]):
        piece = jnp.zeros((left.shape[0], LANES), F32)
        for s in range(tp):
            piece = jnp.where(row == owner[me ^ s], own[s][h : h + 1, :], piece)
        left[:, h * LANES : (h + 1) * LANES] = piece
    out[...] = jnp.dot(left[...].astype(BF16), w_out[...], preferred_element_type=F32)[:docs]


def gate_up_kernel(kv, states, gains, w, *rest):
    parts = rest[:kv]
    attn_out, partial_out, w_buf, spread_buf, acc, sems = rest[kv:]
    docs, width = states.shape
    hidden = w.shape[2]
    blocks, rows = w_buf.shape[:2]
    w_rows = w.reshape(2 * width, hidden)

    def block_copy(b):
        return pltpu.make_async_copy(
            w_rows.at[pl.ds(b * rows, rows)], w_buf.at[b], sems.at[b]
        )

    for b in range(blocks):
        block_copy(b).start()
    attn = tree_sum([part[...] for part in parts]).astype(BF16)
    attn_out[...] = attn
    resid = (states[...].astype(F32) + attn.astype(F32)).astype(BF16).astype(F32)
    squares = jnp.sum(resid * resid, axis=1, keepdims=True)
    spread(two_parts(resid * gains[1:2, :]), spread_buf, docs)
    acc[...] = jnp.zeros_like(acc)

    def step(b, carry):
        block_copy(b).wait()
        left = spread_buf[:, pl.ds(pl.multiple_of(b * rows, rows), rows)]
        acc[...] += jnp.dot(left, w_buf[b], preferred_element_type=F32)
        return carry

    lax.fori_loop(0, blocks, step, 0)
    partial_out[:, :hidden] = (acc[: 2 * docs] + acc[2 * docs :]).astype(BF16)
    lane = lax.broadcasted_iota(jnp.int32, (docs, LANES), 1)
    first = squares.astype(BF16).astype(F32)
    second = (squares - first).astype(BF16).astype(F32)
    third = squares - first - second
    terms = jnp.where(lane == 0, first, jnp.where(lane == 1, second, jnp.where(lane == 2, third, 0.0)))
    partial_out[:, hidden:] = jnp.concatenate([terms, terms], axis=0).astype(BF16)


def down_kernel(tp, w_down, *rest):
    parts = rest[:tp]
    out, act_buf = rest[tp:]
    docs = out.shape[0]
    hidden = w_down.shape[0]
    summed = tree_sum([part[...].astype(F32) for part in parts])
    squares = jnp.sum(summed[:docs, hidden:], axis=1, keepdims=True)
    inverse = lax.rsqrt(squares / D + EPS)
    gate = summed[:docs, :hidden] * inverse
    up = summed[docs:, :hidden] * inverse
    act_buf[...] = (gate / (1.0 + jnp.exp(-gate)) * up).astype(BF16)
    step_rows = 512
    out[...] = jnp.zeros_like(out)

    def step(b, carry):
        start = pl.multiple_of(b * step_rows, step_rows)
        out[...] += jnp.dot(
            act_buf[:, pl.ds(start, step_rows)],
            w_down[pl.ds(start, step_rows), :],
            preferred_element_type=F32,
        )
        return carry

    lax.fori_loop(0, hidden // step_rows, step, 0)


def cost(flops, nbytes):
    return pl.CostEstimate(flops=flops, bytes_accessed=nbytes, transcendentals=0)


def params(mib):
    return pltpu.CompilerParams(vmem_limit_bytes=mib * MIB)


def per_device(
    tp, kv,
    states, norm_gains, w_query, w_keyval, w_out, w_gate_up, w_down, kv_cache, lengths, owner_rows
):
    docs, width = states.shape
    heads = w_query.shape[1]
    cache_len = kv_cache.shape[1]
    hidden = w_gate_up.shape[2]
    wq = w_query.reshape(width, heads // 2, 2, LANES)
    wkv = w_keyval.reshape(width, 2 * LANES)
    cache = kv_cache.reshape(cache_len, 2 * LANES)
    packed = 2 * heads
    pairs = heads // 2
    halves = 2

    qkv_parts = pl.pallas_call(
        functools.partial(qkv_kernel, tp),
        out_shape=[jax.ShapeDtypeStruct((packed, LANES), F32)] * tp,
        in_specs=[smem(), vmem(), vmem(), hbm(), hbm()],
        out_specs=[vmem()] * tp,
        scratch_shapes=[
            pltpu.VMEM((halves, pairs, width // halves, 2, LANES), BF16),
            pltpu.VMEM((width, 2 * LANES), BF16),
            pltpu.VMEM((4 * docs, 2 * width), BF16),
            pltpu.VMEM((2 * docs, pairs * LANES), F32),
            pltpu.VMEM((2 * docs, 2 * LANES), F32),
            pltpu.VMEM((docs, LANES), F32),
            pltpu.SemaphoreType.DMA((halves * pairs + 1,)),
        ],
        compiler_params=params(12),
        cost_estimate=cost(32 * docs * width * LANES, width * heads * 320),
        name="qkv",
    )(owner_rows, states, norm_gains, wq, wkv)
    qkv_parts = exchange(qkv_parts, "tp", tp)

    half = LANES // 2
    freq = ROPE_BASE ** (-(np.arange(half, dtype=np.float64) * 2.0 / LANES))
    freq = np.concatenate([freq, freq]).astype(np.float32)[None, :]
    rows = 512
    head_out, new_kv = pl.pallas_call(
        functools.partial(attend_kernel, tp, heads),
        out_shape=[
            jax.ShapeDtypeStruct((heads, LANES), BF16),
            jax.ShapeDtypeStruct((1, 2 * LANES), BF16),
        ],
        in_specs=[smem(), smem(), vmem(), hbm()] + [vmem()] * tp,
        out_specs=[vmem(), vmem()],
        scratch_shapes=[
            pltpu.VMEM((cache_len // rows, rows, 2 * LANES), BF16),
            pltpu.VMEM((heads, cache_len), F32),
            pltpu.SemaphoreType.DMA((cache_len // rows,)),
        ],
        compiler_params=params(10),
        cost_estimate=cost(32 * cache_len * LANES, cache_len * 512),
        name="attend",
    )(owner_rows, lengths, jnp.asarray(freq), cache, *qkv_parts)

    head_parts = exchange([head_out] * tp, "tp", tp)
    out_part = pl.pallas_call(
        functools.partial(out_kernel, tp),
        out_shape=jax.ShapeDtypeStruct((docs, width), F32),
        in_specs=[smem(), vmem()] + [vmem()] * tp,
        out_specs=vmem(),
        scratch_shapes=[pltpu.VMEM((max(docs, 8), heads * LANES), F32)],
        compiler_params=params(8),
        cost_estimate=cost(2 * docs * heads * LANES * width, heads * LANES * width * 2),
        name="attn_project",
    )(owner_rows, w_out, *head_parts)

    out_parts = exchange([out_part] * kv, "kv", kv)
    gu_rows = GU_BLOCK
    gu_blocks = 2 * width // gu_rows
    attn_out, gu_part = pl.pallas_call(
        functools.partial(gate_up_kernel, kv),
        out_shape=[
            jax.ShapeDtypeStruct((docs, width), BF16),
            jax.ShapeDtypeStruct((2 * docs, hidden + LANES), BF16),
        ],
        in_specs=[vmem(), vmem(), hbm()] + [vmem()] * kv,
        out_specs=[vmem(), vmem()],
        scratch_shapes=[
            pltpu.VMEM((gu_blocks, gu_rows, hidden), BF16),
            pltpu.VMEM((4 * docs, 2 * width), BF16),
            pltpu.VMEM((4 * docs, hidden), F32),
            pltpu.SemaphoreType.DMA((gu_blocks,)),
        ],
        compiler_params=params(34),
        cost_estimate=cost(8 * docs * width * hidden, width * hidden * 4),
        name="gate_up",
    )(states, norm_gains, w_gate_up, *out_parts)

    gu_parts = exchange([gu_part] * tp, "tp", tp)
    ffn_part = pl.pallas_call(
        functools.partial(down_kernel, tp),
        out_shape=jax.ShapeDtypeStruct((docs, width), F32),
        in_specs=[vmem()] + [vmem()] * tp,
        out_specs=vmem(),
        scratch_shapes=[pltpu.VMEM((docs, hidden), BF16)],
        compiler_params=params(20),
        cost_estimate=cost(2 * docs * hidden * width, hidden * width * 2),
        name="down",
    )(w_down, *gu_parts)
    ffn_out = tree_sum(exchange([ffn_part] * kv, "kv", kv)).astype(BF16)
    return attn_out, ffn_out, new_kv.reshape(1, 1, 2 * LANES)


def solution(mesh):
    return jax.shard_map(
        functools.partial(per_device, mesh.shape["tp"], mesh.shape["kv"]),
        mesh=mesh,
        in_specs=(
            P("grp", "tp"),
            P(None, "tp"),
            P("tp", "kv", None),
            P("tp", "kv", None),
            P("kv", "tp"),
            P("tp", None, "kv"),
            P("kv", "tp"),
            P(("grp", "tp"), None, "kv", None),
            P("grp"),
            P("grp"),
        ),
        out_specs=(P("grp", "tp"), P("grp", "tp"), P(("grp", "tp"), "kv", None)),
        check_vma=False,
    )
```

time: 222 us -> 70.1 us (0.32)
  blocking collectives: 73.6 us -> 0 us
  local copies, waits for them, and re-layouts: 62.8 us -> 7.16 us
  matrix products: 33 us -> 0 us
  Pallas kernels: 0 us -> 25.9 us
  starting transfers between devices: 0.04 us -> 18.4 us
  between operations: 16.7 us -> 0.75 us
  waiting for transfers between devices: 32 us -> 16.8 us
    psum x5 -> x0, blocking collectives: 60.5 us -> none  [the longest x1 15.7 us: per_device(): query_all, keyval_all = lax.psum((query_part, keyval_part), 'tp')]
    dot_general x1 -> x0, local copies, waits for them, and re-layouts: 38.6 us -> none  [per_device(): jnp.dot(normed_two, w_gate_up.reshape(local_width, 2 * hidden_local), pre...]
    dot_general x9 -> x0, matrix products: 33 us -> none  [the longest x1 13.9 us: per_device(): jnp.dot(normed_two, w_gate_up.reshape(local_width, 2 * hidden_local), pre...]
    psum x1 -> x0, waiting for transfers between devices: 32 us -> none  [per_device(): summed = lax.psum(partial_value, 'tp')]
    pallas_call x0 -> x5, Pallas kernels: none -> 25.9 us  [the longest x1 10.2 us: per_device(): pl.pallas_call(functools.partial(gate_up_kernel, kv), out_shape=[jax.Shap...]
    ppermute x0 -> x15, starting transfers between devices: none -> 18.4 us  [exchange(): lax.ppermute(arrays[s], axis, [(i, i ^ s) for i in range(size)])]
    ppermute x0 -> x15, waiting for transfers between devices: none -> 16.8 us  [exchange(): lax.ppermute(arrays[s], axis, [(i, i ^ s) for i in range(size)])]
    unnamed x12 -> x30, local copies, waits for them, and re-layouts: 20.8 us -> 7.16 us
  transfers between devices with their start and end apart: 1 -> 15, of which waited for: 1 -> 10; matrix products, arithmetic and copies ran while one was open for 0% -> 0% of each run, Pallas kernels for 0% -> 0%
where the time goes in v1:
time: 70.1 us; the launch traced here: 69.7 us
  Pallas kernels  25.9 us (37%)
  starting transfers between devices  18.4 us (26%)
  waiting for transfers between devices  16.8 us (24%)
  local copies, waits for them, and re-layouts  7.16 us (10%)
  between operations  0.75 us (1%)
    ppermute x15, starting transfers between devices, exchange(): lax.ppermute(arrays[s], axis, [(i, i ^ s) for i in range(size)])  18.4 us
    ppermute x15, waiting for transfers between devices, exchange(): lax.ppermute(arrays[s], axis, [(i, i ^ s) for i in range(size)])  16.8 us
    pallas_call x1, Pallas kernels, per_device(): pl.pallas_call(functools.partial(gate_up_kernel, kv), out_shape=[jax.Shap...  10.2 us
    unnamed x30, local copies, waits for them, and re-layouts  7.16 us
    pallas_call x1, Pallas kernels, per_device(): pl.pallas_call(functools.partial(qkv_kernel, tp), out_shape=[jax.ShapeDty...  6.47 us
    pallas_call x1, Pallas kernels, per_device(): pl.pallas_call(functools.partial(attend_kernel, tp, heads), out_shape=[ja...  5.2 us
    pallas_call x1, Pallas kernels, per_device(): pl.pallas_call(functools.partial(down_kernel, tp), out_shape=jax.ShapeDty...  2.89 us
  transfers between devices with their start and end apart: 15, of which 10 were waited for; matrix products, arithmetic and copies ran while one was open for 0% of the time, Pallas kernels for 0%

profile of v1, /device:TPU:0, one launch (start us, length us, event | category | flops | bytes accessed | tf_op | source)
XLA Modules:
  0.0 69.7 jit_solution(9353101444622573713)
XLA Ops:
  0.7 2.3 %copy-done.1 = bf16[2048,8,128]{2,1,0:T(8,128)(2,1)S(1)} copy-done((bf16[2048,8,128]{2,1,0:T(8,128)(2,1)S(1)}, bf16[2048,8,128]{2,1,0:T(8,128)(2,1)}, u32[]{:S(2)}) %copy-start.1) | copy-done | bytes 4194328
  3.0 1.4 %copy-done.3 = bf16[2048,1,256]{2,0,1:T(8,128)(2,1)S(1)} copy-done((bf16[2048,1,256]{2,0,1:T(8,128)(2,1)S(1)}, bf16[2048,1,256]{2,0,1:T(8,128)(2,1)}, u32[]{:S(2)}) %copy-start.3) | copy-done | bytes 1048600
  4.4 0.7 %copy-done.4 = bf16[4,2048]{1,0:T(4,128)(2,1)S(1)} copy-done((bf16[4,2048]{1,0:T(4,128)(2,1)S(1)}, bf16[4,2048]{1,0:T(4,128)(2,1)}, u32[]{:S(2)}) %copy-start.4) | copy-done | bytes 16408
  5.1 0.7 %copy-done.6 = f32[2,2048]{1,0:T(2,128)S(1)} copy-done((f32[2,2048]{1,0:T(2,128)S(1)}, f32[2,2048]{1,0:T(2,128)}, u32[]{:S(2)}) %copy-start.6) | copy-done | bytes 16408
  5.8 0.7 copy-done.8
  6.5 6.5 %qkv.1 = (f32[16,128]{1,0:T(8,128)S(1)}, f32[16,128]{1,0:T(8,128)S(1)}, f32[16,128]{1,0:T(8,128)S(1)}, f32[16,128]{1,0:T(8,128)S(1)}) custom-call(s32[4]{0:T(128)S(1)} %copy-done.8, bf16[4,2048]{1,0:T(4,128)(2,1)S(1)} %copy-done.4, f32[2,2048]{1,0:T(2,128)S(1)} %copy-done.6, bf16[2048,4,2,128]{3,2,1,0:T(2,128)(2,1)S(1)} %bitcast.7, bf16[2048,256]{1,0:T(8,128)(2,1)S(1)} %bitcast.8), custom_call_target="tpu_custom_call" | custom-call | flops 33554432 | bytes 5242880 | tf_op jit(solution)/shard_map/qkv/pallas_call | solution.py:289
  13.0 3.1 %collective-permute-start = (f32[16,128]{1,0:T(8,128)S(1)}, f32[16,128]{1,0:T(8,128)S(1)}, u32[]{:S(2)}, u32[]{:S(2)}) collective-permute-start(f32[16,128]{1,0:T(8,128)S(1)} %get-tuple-element.12), channel_id=1, source_target_pairs={{0,4},{4,0},{8,12},{12,8},{1,5},{5,1},{9,13},{13,9},{2,6},{6,2},{1... | collective-permute-start | bytes 24584 | tf_op jit(solution)/shard_map/ppermute | solution.py:39
  16.0 2.6 %collective-permute-start.1 = (f32[16,128]{1,0:T(8,128)S(1)}, f32[16,128]{1,0:T(8,128)S(1)}, u32[]{:S(2)}, u32[]{:S(2)}) collective-permute-start(f32[16,128]{1,0:T(8,128)S(1)} %get-tuple-element.13), channel_id=1, source_target_pairs={{0,8},{4,12},{8,0},{12,4},{1,9},{5,13},{9,1},{13,5},{2,10},{6,14},... | collective-permute-start | bytes 24584 | tf_op jit(solution)/shard_map/ppermute | solution.py:39
  18.6 2.0 %collective-permute-done.1.rest_2_ = f32[16,128]{1,0:T(8,128)S(1)} collective-permute-done((f32[16,128]{1,0:T(8,128)S(1)}, f32[16,128]{1,0:T(8,128)S(1)}, u32[]{:S(2)}, u32[]{:S(2)}) %collective-permute-start.1) | collective-permute-done | bytes 8224 | tf_op jit(solution)/shard_map/ppermute | solution.py:39
  20.6 3.5 %collective-permute-done.2.rest_3_ = f32[16,128]{1,0:T(8,128)S(1)} collective-permute-done((f32[16,128]{1,0:T(8,128)S(1)}, f32[16,128]{1,0:T(8,128)S(1)}, u32[]{:S(2)}, u32[]{:S(2)}) %collective-permute-start.2) | collective-permute-done | bytes 8224 | tf_op jit(solution)/shard_map/ppermute | solution.py:39
  24.1 0.7 copy-done.9
  24.7 0.7 copy-done.10
  25.4 5.2 %attend.1 = (bf16[8,128]{1,0:T(8,128)(2,1)S(1)}, bf16[1,256]{1,0:T(2,128)(2,1)}) custom-call(s32[4]{0:T(128)S(1)} %copy-done.8, s32[4]{0:T(128)S(1)} %copy-done.9, f32[1,128]{1,0:T(1,128)S(1)} %copy-done.10, bf16[8192,256]{1,0:T(8,128)(2,1)S(1)} %bitcast.6, f32[16,128]{1,0:T(8,128)S(1)} %get-tuple-element.11.rest_0_, ...), custom_call_target="tpu_custom_call" | custom-call | flops 33554432 | bytes 4194304 | tf_op jit(solution)/shard_map/attend/pallas_call | solution.py:313
  30.8 4.3 %collective-permute-start.3 = (bf16[8,128]{1,0:T(8,128)(2,1)S(1)}, bf16[8,128]{1,0:T(8,128)(2,1)S(1)}, u32[]{:S(2)}, u32[]{:S(2)}) collective-permute-start(bf16[8,128]{1,0:T(8,128)(2,1)S(1)} %get-tuple-element.15.rest_0_), channel_id=1, source_target_pairs={{0,4},{4,0},{8,12},{12,8},{1,5},{5,1},{9,13},{13,9},{2,6},{6,2},{1... | collective-permute-start | bytes 6152 | tf_op jit(solution)/shard_map/ppermute | solution.py:39
  35.1 1.0 %collective-permute-done.5.rest_3_ = bf16[8,128]{1,0:T(8,128)(2,1)S(1)} collective-permute-done((bf16[8,128]{1,0:T(8,128)(2,1)S(1)}, bf16[8,128]{1,0:T(8,128)(2,1)S(1)}, u32[]{:S(2)}, u32[]{:S(2)}) %collective-permute-start.5) | collective-permute-done | bytes 2080 | tf_op jit(solution)/shard_map/ppermute | solution.py:39
  36.1 0.6 collective-permute-done.3.rest_1_
  36.6 1.2 %attn_project.1.rest_0_ = f32[4,2048]{1,0:T(4,128)S(1)} custom-call(s32[4]{0:T(128)S(1)} %copy-done.8, bf16[1024,2048]{1,0:T(8,128)(2,1)S(1)} %copy-done.2, bf16[8,128]{1,0:T(8,128)(2,1)S(1)} %get-tuple-element.15.rest_0_, bf16[8,128]{1,0:T(8,128)(2,1)S(1)} %collective-permute-done.3.rest_1_, bf16[8,128]{1,0:T(8,128)(2,1)S(1)} %collective-permute-done.4.rest_2_, ...), custom_call_target="tpu_custom_call" | custom-call | flops 16777216 | bytes 4194304 | tf_op jit(solution)/shard_map/attn_project/pallas_call | solution.py:332
  37.9 1.6 %collective-permute-start.7 = (f32[4,2048]{1,0:T(4,128)S(1)}, f32[4,2048]{1,0:T(4,128)S(1)}, u32[]{:S(2)}, u32[]{:S(2)}) collective-permute-start(f32[4,2048]{1,0:T(4,128)S(1)} %attn_project.1.rest_0_), channel_id=1, source_target_pairs={{0,2},{1,3},{2,0},{3,1},{4,6},{5,7},{6,4},{7,5},{8,10},{9,11},{10,... | collective-permute-start | bytes 98312 | tf_op jit(solution)/shard_map/ppermute | solution.py:39
  39.8 1.8 %collective-permute-done.8.rest_3_ = f32[4,2048]{1,0:T(4,128)S(1)} collective-permute-done((f32[4,2048]{1,0:T(4,128)S(1)}, f32[4,2048]{1,0:T(4,128)S(1)}, u32[]{:S(2)}, u32[]{:S(2)}) %collective-permute-start.8) | collective-permute-done | bytes 32800 | tf_op jit(solution)/shard_map/ppermute | solution.py:39
  41.5 0.4 collective-permute-done.7.rest_2_
  41.9 10.2 %gate_up.1 = (bf16[4,2048]{1,0:T(4,128)(2,1)}, bf16[8,3712]{1,0:T(8,128)(2,1)S(1)}) custom-call(bf16[4,2048]{1,0:T(4,128)(2,1)S(1)} %copy-done.5, f32[2,2048]{1,0:T(2,128)S(1)} %copy-done.7, bf16[2048,2,3584]{2,1,0:T(2,128)(2,1)} %w.1, f32[4,2048]{1,0:T(4,128)S(1)} %attn_project.1.rest_0_, f32[4,2048]{1,0:T(4,128)S(1)} %collective-permute-done.6.rest_1_, ...), custom_call_target="tpu_custom_call" | custom-call | flops 234881024 | bytes 29360128 | tf_op jit(solution)/shard_map/gate_up/pallas_call | solution.py:346
  52.2 2.4 %collective-permute-start.11 = (bf16[8,3712]{1,0:T(8,128)(2,1)S(1)}, bf16[8,3712]{1,0:T(8,128)(2,1)S(1)}, u32[]{:S(2)}, u32[]{:S(2)}) collective-permute-start(bf16[8,3712]{1,0:T(8,128)(2,1)S(1)} %get-tuple-element.17.rest_0_), channel_id=1, source_target_pairs={{0,12},{4,8},{8,4},{12,0},{1,13},{5,9},{9,5},{13,1},{2,14},{6,10},... | collective-permute-start | bytes 178184 | tf_op jit(solution)/shard_map/ppermute | solution.py:39
  54.6 1.1 %collective-permute-start.10 = (bf16[8,3712]{1,0:T(8,128)(2,1)S(1)}, bf16[8,3712]{1,0:T(8,128)(2,1)S(1)}, u32[]{:S(2)}, u32[]{:S(2)}) collective-permute-start(bf16[8,3712]{1,0:T(8,128)(2,1)S(1)} %get-tuple-element.17.rest_0_), channel_id=1, source_target_pairs={{0,8},{4,12},{8,0},{12,4},{1,9},{5,13},{9,1},{13,5},{2,10},{6,14},... | collective-permute-start | bytes 178184 | tf_op jit(solution)/shard_map/ppermute | solution.py:39
  55.7 0.9 %collective-permute-start.9 = (bf16[8,3712]{1,0:T(8,128)(2,1)S(1)}, bf16[8,3712]{1,0:T(8,128)(2,1)S(1)}, u32[]{:S(2)}, u32[]{:S(2)}) collective-permute-start(bf16[8,3712]{1,0:T(8,128)(2,1)S(1)} %get-tuple-element.17.rest_0_), channel_id=1, source_target_pairs={{0,4},{4,0},{8,12},{12,8},{1,5},{5,1},{9,13},{13,9},{2,6},{6,2},{1... | collective-permute-start | bytes 178184 | tf_op jit(solution)/shard_map/ppermute | solution.py:39
  56.6 2.3 %collective-permute-done.11.rest_3_ = bf16[8,3712]{1,0:T(8,128)(2,1)S(1)} collective-permute-done((bf16[8,3712]{1,0:T(8,128)(2,1)S(1)}, bf16[8,3712]{1,0:T(8,128)(2,1)S(1)}, u32[]{:S(2)}, u32[]{:S(2)}) %collective-permute-start.11) | collective-permute-done | bytes 59424 | tf_op jit(solution)/shard_map/ppermute | solution.py:39
  59.0 2.7 %collective-permute-done.10.rest_2_ = bf16[8,3712]{1,0:T(8,128)(2,1)S(1)} collective-permute-done((bf16[8,3712]{1,0:T(8,128)(2,1)S(1)}, bf16[8,3712]{1,0:T(8,128)(2,1)S(1)}, u32[]{:S(2)}, u32[]{:S(2)}) %collective-permute-start.10) | collective-permute-done | bytes 59424 | tf_op jit(solution)/shard_map/ppermute | solution.py:39
  61.7 2.9 %down.1 = f32[4,2048]{1,0:T(4,128)S(1)} custom-call(bf16[3584,2048]{1,0:T(8,128)(2,1)S(1)} %bitcast.5, bf16[8,3712]{1,0:T(8,128)(2,1)S(1)} %get-tuple-element.17.rest_0_, bf16[8,3712]{1,0:T(8,128)(2,1)S(1)} %collective-permute-done.9.rest_1_, bf16[8,3712]{1,0:T(8,128)(2,1)S(1)} %collective-permute-done.10.rest_2_, ...), custom_call_target="tpu_custom_call" | custom-call | flops 58720256 | bytes 14680064 | tf_op jit(solution)/shard_map/down/pallas_call | solution.py:366
  64.9 1.1 %collective-permute-start.13 = (f32[4,2048]{1,0:T(4,128)S(1)}, f32[4,2048]{1,0:T(4,128)S(1)}, u32[]{:S(2)}, u32[]{:S(2)}) collective-permute-start(f32[4,2048]{1,0:T(4,128)S(1)} %down.1), channel_id=1, source_target_pairs={{0,2},{1,3},{2,0},{3,1},{4,6},{5,7},{6,4},{7,5},{8,10},{9,11},{10,... | collective-permute-start | bytes 98312 | tf_op jit(solution)/shard_map/ppermute | solution.py:39
  66.0 0.5 collective-permute-start.12
  66.5 1.7 %collective-permute-done.14 = f32[4,2048]{1,0:T(4,128)S(1)} collective-permute-done((f32[4,2048]{1,0:T(4,128)S(1)}, f32[4,2048]{1,0:T(4,128)S(1)}, u32[]{:S(2)}, u32[]{:S(2)}) %collective-permute-start.14) | collective-permute-done | bytes 32800 | tf_op jit(solution)/shard_map/ppermute | solution.py:39
  68.3 0.8 %collective-permute-done.13 = f32[4,2048]{1,0:T(4,128)S(1)} collective-permute-done((f32[4,2048]{1,0:T(4,128)S(1)}, f32[4,2048]{1,0:T(4,128)S(1)}, u32[]{:S(2)}, u32[]{:S(2)}) %collective-permute-start.13) | collective-permute-done | bytes 32800 | tf_op jit(solution)/shard_map/ppermute | solution.py:39
  69.1 0.6 add_convert_fusion
  (35 shorter events, 0.9 us)
Async XLA Ops:
  0.6 23.5 %copy-start = (bf16[1,8192,1,256]{3,1,2,0:T(8,128)(2,1)S(1)}, bf16[1,8192,1,256]{3,1,2,0:T(8,128)(2,1)}, u32[]{:S(2)}) copy-start(bf16[1,8192,1,256]{3,1,2,0:T(8,128)(2,1)} %param.18) | copy-start | bytes 12582916
  0.6 2.3 %copy-start.1 = (bf16[2048,8,128]{2,1,0:T(8,128)(2,1)S(1)}, bf16[2048,8,128]{2,1,0:T(8,128)(2,1)}, u32[]{:S(2)}) copy-start(bf16[2048,8,128]{2,1,0:T(8,128)(2,1)} %param.13) | copy-start | bytes 12582916
  3.0 1.4 %copy-start.3 = (bf16[2048,1,256]{2,0,1:T(8,128)(2,1)S(1)}, bf16[2048,1,256]{2,0,1:T(8,128)(2,1)}, u32[]{:S(2)}) copy-start(bf16[2048,1,256]{2,0,1:T(8,128)(2,1)} %param.14) | copy-start | bytes 3145732
  4.4 0.7 %copy-start.4 = (bf16[4,2048]{1,0:T(4,128)(2,1)S(1)}, bf16[4,2048]{1,0:T(4,128)(2,1)}, u32[]{:S(2)}) copy-start(bf16[4,2048]{1,0:T(4,128)(2,1)} %states.3) | copy-start | bytes 49156
  5.1 0.7 %copy-start.6 = (f32[2,2048]{1,0:T(2,128)S(1)}, f32[2,2048]{1,0:T(2,128)}, u32[]{:S(2)}) copy-start(f32[2,2048]{1,0:T(2,128)} %gains.3) | copy-start | bytes 49156
  5.8 0.7 copy-start.8
  6.5 30.2 %copy-start.2 = (bf16[1024,2048]{1,0:T(8,128)(2,1)S(1)}, bf16[1024,2048]{1,0:T(8,128)(2,1)}, u32[]{:S(2)}) copy-start(bf16[1024,2048]{1,0:T(8,128)(2,1)} %w_out.1) | copy-start | bytes 12582916
  13.0 5.7 %collective-permute-start = (f32[16,128]{1,0:T(8,128)S(1)}, f32[16,128]{1,0:T(8,128)S(1)}, u32[]{:S(2)}, u32[]{:S(2)}) collective-permute-start(f32[16,128]{1,0:T(8,128)S(1)} %get-tuple-element.12), channel_id=1, source_target_pairs={{0,4},{4,0},{8,12},{12,8},{1,5},{5,1},{9,13},{13,9},{2,6},{6,2},{1... | collective-permute-start | bytes 24584 | tf_op jit(solution)/shard_map/ppermute | solution.py:39
  16.0 4.5 %collective-permute-start.1 = (f32[16,128]{1,0:T(8,128)S(1)}, f32[16,128]{1,0:T(8,128)S(1)}, u32[]{:S(2)}, u32[]{:S(2)}) collective-permute-start(f32[16,128]{1,0:T(8,128)S(1)} %get-tuple-element.13), channel_id=1, source_target_pairs={{0,8},{4,12},{8,0},{12,4},{1,9},{5,13},{9,1},{13,5},{2,10},{6,14},... | collective-permute-start | bytes 24584 | tf_op jit(solution)/shard_map/ppermute | solution.py:39
  18.6 5.4 %collective-permute-start.2 = (f32[16,128]{1,0:T(8,128)S(1)}, f32[16,128]{1,0:T(8,128)S(1)}, u32[]{:S(2)}, u32[]{:S(2)}) collective-permute-start(f32[16,128]{1,0:T(8,128)S(1)} %get-tuple-element.14), channel_id=1, source_target_pairs={{0,12},{4,8},{8,4},{12,0},{1,13},{5,9},{9,5},{13,1},{2,14},{6,10},... | collective-permute-start | bytes 24584 | tf_op jit(solution)/shard_map/ppermute | solution.py:39
  24.1 0.7 copy-start.9
  24.7 0.7 copy-start.10
  25.4 16.5 %copy-start.5 = (bf16[4,2048]{1,0:T(4,128)(2,1)S(1)}, bf16[4,2048]{1,0:T(4,128)(2,1)}, u32[]{:S(2)}) copy-start(bf16[4,2048]{1,0:T(4,128)(2,1)} %states.3) | copy-start | bytes 49156
  25.4 16.5 %copy-start.7 = (f32[2,2048]{1,0:T(2,128)S(1)}, f32[2,2048]{1,0:T(2,128)}, u32[]{:S(2)}) copy-start(f32[2,2048]{1,0:T(2,128)} %gains.3) | copy-start | bytes 49156
  30.6 5.4 %collective-permute-start.5 = (bf16[8,128]{1,0:T(8,128)(2,1)S(1)}, bf16[8,128]{1,0:T(8,128)(2,1)S(1)}, u32[]{:S(2)}, u32[]{:S(2)}) collective-permute-start(bf16[8,128]{1,0:T(8,128)(2,1)S(1)} %get-tuple-element.15.rest_0_), channel_id=1, source_target_pairs={{0,12},{4,8},{8,4},{12,0},{1,13},{5,9},{9,5},{13,1},{2,14},{6,10},... | collective-permute-start | bytes 6152 | tf_op jit(solution)/shard_map/ppermute | solution.py:39
  30.8 5.3 %collective-permute-start.4 = (bf16[8,128]{1,0:T(8,128)(2,1)S(1)}, bf16[8,128]{1,0:T(8,128)(2,1)S(1)}, u32[]{:S(2)}, u32[]{:S(2)}) collective-permute-start(bf16[8,128]{1,0:T(8,128)(2,1)S(1)} %get-tuple-element.15.rest_0_), channel_id=1, source_target_pairs={{0,8},{4,12},{8,0},{12,4},{1,9},{5,13},{9,1},{13,5},{2,10},{6,14},... | collective-permute-start | bytes 6152 | tf_op jit(solution)/shard_map/ppermute | solution.py:39
  30.8 5.8 %collective-permute-start.3 = (bf16[8,128]{1,0:T(8,128)(2,1)S(1)}, bf16[8,128]{1,0:T(8,128)(2,1)S(1)}, u32[]{:S(2)}, u32[]{:S(2)}) collective-permute-start(bf16[8,128]{1,0:T(8,128)(2,1)S(1)} %get-tuple-element.15.rest_0_), channel_id=1, source_target_pairs={{0,4},{4,0},{8,12},{12,8},{1,5},{5,1},{9,13},{13,9},{2,6},{6,2},{1... | collective-permute-start | bytes 6152 | tf_op jit(solution)/shard_map/ppermute | solution.py:39
  36.6 25.1 %slice-start = ((s8[14680064]{0:T(1024)(128)(4,1)}), s8[4194304]{0:T(1024)(128)(4,1)S(1)}, s32[]{:S(2)}) async-start(s8[14680064]{0:T(1024)(128)(4,1)} %bitcast.4), calls=%async_computation | async-start | bytes 8388608
  37.8 23.9 %slice-start.1 = ((s8[14680064]{0:T(1024)(128)(4,1)}), s8[4194304]{0:T(1024)(128)(4,1)S(1)}, s32[]{:S(2)}) async-start(s8[14680064]{0:T(1024)(128)(4,1)} %bitcast.4), calls=%async_computation.1 | async-start | bytes 8388608
  37.8 23.9 %slice-start.2 = ((s8[14680064]{0:T(1024)(128)(4,1)}), s8[4194304]{0:T(1024)(128)(4,1)S(1)}, s32[]{:S(2)}) async-start(s8[14680064]{0:T(1024)(128)(4,1)} %bitcast.4), calls=%async_computation.2 | async-start | bytes 8388608
  37.8 23.9 %slice-start.3 = ((s8[14680064]{0:T(1024)(128)(4,1)}), s8[2097152]{0:T(1024)(128)(4,1)S(1)}, s32[]{:S(2)}) async-start(s8[14680064]{0:T(1024)(128)(4,1)} %bitcast.4), calls=%async_computation.3 | async-start | bytes 4194304
  37.8 3.7 %collective-permute-start.8 = (f32[4,2048]{1,0:T(4,128)S(1)}, f32[4,2048]{1,0:T(4,128)S(1)}, u32[]{:S(2)}, u32[]{:S(2)}) collective-permute-start(f32[4,2048]{1,0:T(4,128)S(1)} %attn_project.1.rest_0_), channel_id=1, source_target_pairs={{0,3},{1,2},{2,1},{3,0},{4,7},{5,6},{6,5},{7,4},{8,11},{9,10},{10,... | collective-permute-start | bytes 98312 | tf_op jit(solution)/shard_map/ppermute | solution.py:39
  37.9 4.0 %collective-permute-start.7 = (f32[4,2048]{1,0:T(4,128)S(1)}, f32[4,2048]{1,0:T(4,128)S(1)}, u32[]{:S(2)}, u32[]{:S(2)}) collective-permute-start(f32[4,2048]{1,0:T(4,128)S(1)} %attn_project.1.rest_0_), channel_id=1, source_target_pairs={{0,2},{1,3},{2,0},{3,1},{4,6},{5,7},{6,4},{7,5},{8,10},{9,11},{10,... | collective-permute-start | bytes 98312 | tf_op jit(solution)/shard_map/ppermute | solution.py:39
  39.5 2.5 %collective-permute-start.6 = (f32[4,2048]{1,0:T(4,128)S(1)}, f32[4,2048]{1,0:T(4,128)S(1)}, u32[]{:S(2)}, u32[]{:S(2)}) collective-permute-start(f32[4,2048]{1,0:T(4,128)S(1)} %attn_project.1.rest_0_), channel_id=1, source_target_pairs={{0,1},{1,0},{2,3},{3,2},{4,5},{5,4},{6,7},{7,6},{8,9},{9,8},{10,11... | collective-permute-start | bytes 98312 | tf_op jit(solution)/shard_map/ppermute | solution.py:39
  52.2 6.8 %collective-permute-start.11 = (bf16[8,3712]{1,0:T(8,128)(2,1)S(1)}, bf16[8,3712]{1,0:T(8,128)(2,1)S(1)}, u32[]{:S(2)}, u32[]{:S(2)}) collective-permute-start(bf16[8,3712]{1,0:T(8,128)(2,1)S(1)} %get-tuple-element.17.rest_0_), channel_id=1, source_target_pairs={{0,12},{4,8},{8,4},{12,0},{1,13},{5,9},{9,5},{13,1},{2,14},{6,10},... | collective-permute-start | bytes 178184 | tf_op jit(solution)/shard_map/ppermute | solution.py:39
  54.6 7.1 %collective-permute-start.10 = (bf16[8,3712]{1,0:T(8,128)(2,1)S(1)}, bf16[8,3712]{1,0:T(8,128)(2,1)S(1)}, u32[]{:S(2)}, u32[]{:S(2)}) collective-permute-start(bf16[8,3712]{1,0:T(8,128)(2,1)S(1)} %get-tuple-element.17.rest_0_), channel_id=1, source_target_pairs={{0,8},{4,12},{8,0},{12,4},{1,9},{5,13},{9,1},{13,5},{2,10},{6,14},... | collective-permute-start | bytes 178184 | tf_op jit(solution)/shard_map/ppermute | solution.py:39
  55.7 6.0 %collective-permute-start.9 = (bf16[8,3712]{1,0:T(8,128)(2,1)S(1)}, bf16[8,3712]{1,0:T(8,128)(2,1)S(1)}, u32[]{:S(2)}, u32[]{:S(2)}) collective-permute-start(bf16[8,3712]{1,0:T(8,128)(2,1)S(1)} %get-tuple-element.17.rest_0_), channel_id=1, source_target_pairs={{0,4},{4,0},{8,12},{12,8},{1,5},{5,1},{9,13},{13,9},{2,6},{6,2},{1... | collective-permute-start | bytes 178184 | tf_op jit(solution)/shard_map/ppermute | solution.py:39
  64.6 3.6 %collective-permute-start.14 = (f32[4,2048]{1,0:T(4,128)S(1)}, f32[4,2048]{1,0:T(4,128)S(1)}, u32[]{:S(2)}, u32[]{:S(2)}) collective-permute-start(f32[4,2048]{1,0:T(4,128)S(1)} %down.1), channel_id=1, source_target_pairs={{0,3},{1,2},{2,1},{3,0},{4,7},{5,6},{6,5},{7,4},{8,11},{9,10},{10,... | collective-permute-start | bytes 98312 | tf_op jit(solution)/shard_map/ppermute | solution.py:39
  64.9 4.1 %collective-permute-start.13 = (f32[4,2048]{1,0:T(4,128)S(1)}, f32[4,2048]{1,0:T(4,128)S(1)}, u32[]{:S(2)}, u32[]{:S(2)}) collective-permute-start(f32[4,2048]{1,0:T(4,128)S(1)} %down.1), channel_id=1, source_target_pairs={{0,2},{1,3},{2,0},{3,1},{4,6},{5,7},{6,4},{7,5},{8,10},{9,11},{10,... | collective-permute-start | bytes 98312 | tf_op jit(solution)/shard_map/ppermute | solution.py:39
  66.0 3.1 %collective-permute-start.12 = (f32[4,2048]{1,0:T(4,128)S(1)}, f32[4,2048]{1,0:T(4,128)S(1)}, u32[]{:S(2)}, u32[]{:S(2)}) collective-permute-start(f32[4,2048]{1,0:T(4,128)S(1)} %down.1), channel_id=1, source_target_pairs={{0,1},{1,0},{2,3},{3,2},{4,5},{5,4},{6,7},{7,6},{8,9},{9,8},{10,11... | collective-permute-start | bytes 98312 | tf_op jit(solution)/shard_map/ppermute | solution.py:39

commit v2 on v1

--- a/solution.py
+++ b/solution.py
@@ -26,12 +26,12 @@
     return pl.BlockSpec(memory_space=pltpu.VMEM)
 
 
-def smem():
-    return pl.BlockSpec(memory_space=pltpu.SMEM)
-
-
 def hbm():
-    return pl.BlockSpec(memory_space=pl.ANY)
+    return pl.BlockSpec(memory_space=pltpu.HBM)
+
+
+def in_hbm(array):
+    return pltpu.with_memory_space_constraint(array, pltpu.HBM)
 
 
 def exchange(arrays, axis, size):
@@ -68,18 +68,56 @@
         out_ref[:, 2 * c * LANES : 2 * (c + 1) * LANES] = jnp.where(keep, doubled, 0.0).astype(BF16)
 
 
+def weight_copy(w_rows, block, buf, slot, sems):
+    rows = buf.shape[1]
+    return pltpu.make_async_copy(
+        w_rows.at[pl.ds(block * rows, rows)], buf.at[slot], sems.at[slot]
+    )
+
+
+def weight_copies(w_rows, first, buf, sems):
+    return [weight_copy(w_rows, first + b, buf, b, sems) for b in range(buf.shape[0])]
+
+
 def pick_row(ref, index):
     row = lax.broadcasted_iota(jnp.int32, ref.shape, 0)
     return jnp.sum(jnp.where(row == index, ref[...], 0.0), axis=0, keepdims=True)
 
 
-def qkv_kernel(tp, owner, states, gains, wq, wkv, *rest):
+def rope_rows(length, frequency):
+    angle = length * frequency
+    turns = jnp.floor(angle * (0.5 / math.pi) + 0.5)
+    angle = ((angle - turns * TURN_A) - turns * TURN_B) - turns * TURN_C
+    lane = lax.broadcasted_iota(jnp.int32, (1, LANES), 1)
+    sine = jnp.sin(angle)
+    return jnp.cos(angle), jnp.where(lane < LANES // 2, -sine, sine)
+
+
+def qkv_kernel(tp, owner_hbm, lengths_hbm, frequency_hbm, states_hbm, gains_hbm, wq, wkv, *rest):
     outs = rest[:tp]
-    wq_buf, wkv_buf, spread_buf, res, kv_res, sq_res, sems = rest[tp:]
+    table, places = rest[tp : tp + 2]
+    owner, lengths, frequency, states, gains = rest[tp + 2 : tp + 7]
+    wq_buf, wkv_buf, spread_buf, res, kv_res, sq_res, sems, small_sems = rest[tp + 7 :]
     docs, width = states.shape
     pairs = wq.shape[1]
     halves = wq_buf.shape[0]
     rows = 2 * width // halves
+    small = [
+        pltpu.make_async_copy(source, target, small_sems.at[i])
+        for i, (source, target) in enumerate(
+            [
+                (states_hbm, states),
+                (gains_hbm, gains),
+                (owner_hbm, owner),
+                (lengths_hbm, lengths),
+                (frequency_hbm, frequency),
+            ]
+        )
+    ]
+    for copy in small:
+        copy.start()
+    kv_copy = pltpu.make_async_copy(wkv, wkv_buf, sems.at[halves * pairs])
+    kv_copy.start()
     copies = []
     for c in range(halves):
         for p in range(pairs):
@@ -90,15 +128,26 @@
                     sems.at[c * pairs + p],
                 )
             )
-    kv_copy = pltpu.make_async_copy(wkv, wkv_buf, sems.at[halves * pairs])
     for copy in copies:
         copy.start()
-    kv_copy.start()
+    for copy in small:
+        copy.wait()
     me = lax.axis_index("tp")
     x = states[...].astype(F32)
     sq_res[...] = jnp.broadcast_to(jnp.sum(x * x, axis=1, keepdims=True), sq_res.shape)
     rows16 = two_parts(x * gains[0:1, :])
     spread(rows16, spread_buf, docs)
+    length = lengths[owner[me]].astype(F32)
+    cosine, sine = rope_rows(length, frequency[...])
+    table[0:1, :] = cosine
+    table[1:2, :] = sine
+    table[2:3, :] = jnp.full((1, LANES), length, F32)
+    table[3:, :] = jnp.zeros((table.shape[0] - 3, LANES), F32)
+    for s in range(tp):
+        places[s : s + 1, :] = jnp.full((1, LANES), owner[me ^ s], jnp.int32)
+    kv_copy.wait()
+    kv_total = jnp.dot(rows16, wkv_buf[...], preferred_element_type=F32)
+    kv_res[...] = kv_total[: 2 * docs] + kv_total[2 * docs :]
     total = jnp.zeros((4 * docs, pairs * LANES), F32)
     for c in range(halves):
         for p in range(pairs):
@@ -110,9 +159,6 @@
             spread_buf[:, c * rows : (c + 1) * rows], block, preferred_element_type=F32
         )
     res[...] = total[: 2 * docs] + total[2 * docs :]
-    kv_copy.wait()
-    kv_total = jnp.dot(rows16, wkv_buf[...], preferred_element_type=F32)
-    kv_res[...] = kv_total[: 2 * docs] + kv_total[2 * docs :]
     for s in range(tp):
         doc = owner[me ^ s]
         for parity in range(2):
@@ -129,27 +175,17 @@
         outs[s][h + 3 :, :] = jnp.zeros((outs[s].shape[0] - h - 3, LANES), F32)
 
 
-def attend_kernel(tp, heads, owner, lengths, frequency, cache, *rest):
+def attend_kernel(tp, heads, rows, table, cache, w, *rest):
     parts = rest[:tp]
-    heads_out, new_kv_out, cache_buf, scores, sems = rest[tp:]
-    blocks, rows = cache_buf.shape[:2]
-    copies = [
-        pltpu.make_async_copy(cache.at[pl.ds(b * rows, rows)], cache_buf.at[b], sems.at[b])
-        for b in range(blocks)
-    ]
-    for copy in copies:
+    heads_out, new_kv_out, w_ready, scores, w_sems = rest[tp:]
+    width, _, hidden = w.shape
+    w_copies = weight_copies(w.reshape(2 * width, hidden), 0, w_ready, w_sems)
+    for copy in w_copies:
         copy.start()
-    length = lengths[owner[lax.axis_index("tp")]]
+    blocks = cache.shape[0] // rows
     sums = tree_sum([part[...] for part in parts])
     sums = sums * lax.rsqrt(sums[heads + 2 : heads + 3, :] / D + EPS)
-    angle = length.astype(F32) * frequency[...]
-    turns = jnp.floor(angle * (0.5 / math.pi) + 0.5)
-    angle = ((angle - turns * TURN_A) - turns * TURN_B) - turns * TURN_C
-    cosine = jnp.cos(angle)
-    sine = jnp.sin(angle)
-    lane = lax.broadcasted_iota(jnp.int32, (1, LANES), 1)
-    sine = jnp.where(lane < LANES // 2, -sine, sine)
-    rotated = sums * cosine + pltpu.roll(sums, LANES // 2, 1) * sine
+    rotated = sums * table[0:1, :] + pltpu.roll(sums, LANES // 2, 1) * table[1:2, :]
     query = rotated[:heads].astype(BF16)
     key = rotated[heads : heads + 1].astype(BF16)
     value = sums[heads + 1 : heads + 2].astype(BF16)
@@ -159,13 +195,13 @@
     value = value.astype(F32)
     scale = LANES ** (-0.5)
     own = jnp.sum(query.astype(F32) * key, axis=1, keepdims=True) * scale
-    column = lax.broadcasted_iota(jnp.int32, (heads, rows), 1)
+    column = lax.broadcasted_iota(jnp.int32, (heads, rows), 1).astype(F32)
+    length = table[2:3, 0:1]
     top = own
     for b in range(blocks):
-        copies[b].wait()
         block = lax.dot_general(
             query,
-            cache_buf[b, :, :LANES],
+            cache[b * rows : (b + 1) * rows, :LANES],
             (((1,), (1,)), ((), ())),
             preferred_element_type=F32,
         )
@@ -179,41 +215,45 @@
         weights = jnp.exp(scores[:, b * rows : (b + 1) * rows] - top)
         total = total + jnp.sum(weights, axis=1, keepdims=True)
         acc = acc + jnp.dot(
-            weights.astype(BF16), cache_buf[b, :, LANES:], preferred_element_type=F32
+            weights.astype(BF16),
+            cache[b * rows : (b + 1) * rows, LANES:],
+            preferred_element_type=F32,
         )
     heads_out[...] = (acc / total).astype(BF16)
-
-
-def out_kernel(tp, owner, w_out, *rest):
+    for copy in w_copies:
+        copy.wait()
+
+
+def out_kernel(tp, first, places, w_out, w, *rest):
     parts = rest[:tp]
-    out, left = rest[tp:]
+    out, w_ready, left, w_sems = rest[tp:]
+    width, _, hidden = w.shape
+    w_copies = weight_copies(w.reshape(2 * width, hidden), first, w_ready, w_sems)
+    for copy in w_copies:
+        copy.start()
     docs = out.shape[0]
-    me = lax.axis_index("tp")
     row = lax.broadcasted_iota(jnp.int32, (left.shape[0], LANES), 0)
     own = [parts[s][...].astype(F32) for s in range(tp)]
     for h in range(own[0].shape[0]):
         piece = jnp.zeros((left.shape[0], LANES), F32)
         for s in range(tp):
-            piece = jnp.where(row == owner[me ^ s], own[s][h : h + 1, :], piece)
+            piece = jnp.where(row == places[s : s + 1, :], own[s][h : h + 1, :], piece)
         left[:, h * LANES : (h + 1) * LANES] = piece
     out[...] = jnp.dot(left[...].astype(BF16), w_out[...], preferred_element_type=F32)[:docs]
-
-
-def gate_up_kernel(kv, states, gains, w, *rest):
+    for copy in w_copies:
+        copy.wait()
+
+
+def gate_up_kernel(kv, states, gains, w, ready_a, ready_b, *rest):
     parts = rest[:kv]
     attn_out, partial_out, w_buf, spread_buf, acc, sems = rest[kv:]
     docs, width = states.shape
     hidden = w.shape[2]
-    blocks, rows = w_buf.shape[:2]
+    rows = w_buf.shape[1]
+    first = ready_a.shape[0] + ready_b.shape[0]
     w_rows = w.reshape(2 * width, hidden)
-
-    def block_copy(b):
-        return pltpu.make_async_copy(
-            w_rows.at[pl.ds(b * rows, rows)], w_buf.at[b], sems.at[b]
-        )
-
-    for b in range(blocks):
-        block_copy(b).start()
+    for copy in weight_copies(w_rows, first, w_buf, sems):
+        copy.start()
     attn = tree_sum([part[...] for part in parts]).astype(BF16)
     attn_out[...] = attn
     resid = (states[...].astype(F32) + attn.astype(F32)).astype(BF16).astype(F32)
@@ -221,13 +261,21 @@
     spread(two_parts(resid * gains[1:2, :]), spread_buf, docs)
     acc[...] = jnp.zeros_like(acc)
 
-    def step(b, carry):
-        block_copy(b).wait()
-        left = spread_buf[:, pl.ds(pl.multiple_of(b * rows, rows), rows)]
-        acc[...] += jnp.dot(left, w_buf[b], preferred_element_type=F32)
-        return carry
-
-    lax.fori_loop(0, blocks, step, 0)
+    def add_blocks(buf, first, wait):
+        def step(b, carry):
+            if wait:
+                weight_copy(w_rows, first + b, buf, b, sems).wait()
+            start = pl.multiple_of((first + b) * rows, rows)
+            acc[...] += jnp.dot(
+                spread_buf[:, pl.ds(start, rows)], buf[b], preferred_element_type=F32
+            )
+            return carry
+
+        lax.fori_loop(0, buf.shape[0], step, 0)
+
+    add_blocks(ready_a, 0, False)
+    add_blocks(ready_b, ready_a.shape[0], False)
+    add_blocks(w_buf, first, True)
     partial_out[:, :hidden] = (acc[: 2 * docs] + acc[2 * docs :]).astype(BF16)
     lane = lax.broadcasted_iota(jnp.int32, (docs, LANES), 1)
     first = squares.astype(BF16).astype(F32)
@@ -263,12 +311,12 @@
     lax.fori_loop(0, hidden // step_rows, step, 0)
 
 
-def cost(flops, nbytes):
-    return pl.CostEstimate(flops=flops, bytes_accessed=nbytes, transcendentals=0)
-
-
-def params(mib):
-    return pltpu.CompilerParams(vmem_limit_bytes=mib * MIB)
+def cost(micros):
+    return pl.CostEstimate(flops=0, bytes_accessed=int(micros * 3.69e6), transcendentals=0)
+
+
+def params(docs, mib):
+    return pltpu.CompilerParams(vmem_limit_bytes=(mib if docs <= 8 else mib + 24) * MIB)
 
 
 def per_device(
@@ -286,12 +334,24 @@
     pairs = heads // 2
     halves = 2
 
-    qkv_parts = pl.pallas_call(
+    half = LANES // 2
+    freq = ROPE_BASE ** (-(np.arange(half, dtype=np.float64) * 2.0 / LANES))
+    freq = jnp.asarray(np.concatenate([freq, freq]).astype(np.float32)[None, :])
+    *qkv_parts, table, places = pl.pallas_call(
         functools.partial(qkv_kernel, tp),
-        out_shape=[jax.ShapeDtypeStruct((packed, LANES), F32)] * tp,
-        in_specs=[smem(), vmem(), vmem(), hbm(), hbm()],
-        out_specs=[vmem()] * tp,
+        out_shape=[jax.ShapeDtypeStruct((packed, LANES), F32)] * tp
+        + [
+            jax.ShapeDtypeStruct((8, LANES), F32),
+            jax.ShapeDtypeStruct((max(tp, 8), LANES), jnp.int32),
+        ],
+        in_specs=[hbm()] * 7,
+        out_specs=[vmem()] * (tp + 2),
         scratch_shapes=[
+            pltpu.SMEM((docs,), jnp.int32),
+            pltpu.SMEM((docs,), jnp.int32),
+            pltpu.VMEM((1, LANES), F32),
+            pltpu.VMEM((docs, width), BF16),
+            pltpu.VMEM((2, width), F32),
             pltpu.VMEM((halves, pairs, width // halves, 2, LANES), BF16),
             pltpu.VMEM((width, 2 * LANES), BF16),
             pltpu.VMEM((4 * docs, 2 * width), BF16),
@@ -299,68 +359,74 @@
             pltpu.VMEM((2 * docs, 2 * LANES), F32),
             pltpu.VMEM((docs, LANES), F32),
             pltpu.SemaphoreType.DMA((halves * pairs + 1,)),
-        ],
-        compiler_params=params(12),
-        cost_estimate=cost(32 * docs * width * LANES, width * heads * 320),
+            pltpu.SemaphoreType.DMA((5,)),
+        ],
+        compiler_params=params(docs, 10),
+        cost_estimate=cost(8),
         name="qkv",
-    )(owner_rows, states, norm_gains, wq, wkv)
+    )(*(in_hbm(a) for a in (owner_rows, lengths, freq, states, norm_gains, wq, wkv)))
     qkv_parts = exchange(qkv_parts, "tp", tp)
 
-    half = LANES // 2
-    freq = ROPE_BASE ** (-(np.arange(half, dtype=np.float64) * 2.0 / LANES))
-    freq = np.concatenate([freq, freq]).astype(np.float32)[None, :]
-    rows = 512
-    head_out, new_kv = pl.pallas_call(
-        functools.partial(attend_kernel, tp, heads),
+    w_gu = in_hbm(w_gate_up)
+    gu_blocks = 2 * width // GU_BLOCK
+    ready_a = max(gu_blocks * 5 // 16, 1)
+    ready_b = max(gu_blocks // 8, 1)
+    head_out, new_kv, w_ready_a = pl.pallas_call(
+        functools.partial(attend_kernel, tp, heads, 512),
         out_shape=[
             jax.ShapeDtypeStruct((heads, LANES), BF16),
             jax.ShapeDtypeStruct((1, 2 * LANES), BF16),
-        ],
-        in_specs=[smem(), smem(), vmem(), hbm()] + [vmem()] * tp,
-        out_specs=[vmem(), vmem()],
+            pltpu.VMEM((ready_a, GU_BLOCK, hidden), BF16),
+        ],
+        in_specs=[vmem(), vmem(), hbm()] + [vmem()] * tp,
+        out_specs=[vmem()] * 3,
         scratch_shapes=[
-            pltpu.VMEM((cache_len // rows, rows, 2 * LANES), BF16),
             pltpu.VMEM((heads, cache_len), F32),
-            pltpu.SemaphoreType.DMA((cache_len // rows,)),
-        ],
-        compiler_params=params(10),
-        cost_estimate=cost(32 * cache_len * LANES, cache_len * 512),
+            pltpu.SemaphoreType.DMA((ready_a,)),
+        ],
+        compiler_params=params(docs, 6),
+        cost_estimate=cost(8),
         name="attend",
-    )(owner_rows, lengths, jnp.asarray(freq), cache, *qkv_parts)
+    )(table, cache, w_gu, *qkv_parts)
 
     head_parts = exchange([head_out] * tp, "tp", tp)
-    out_part = pl.pallas_call(
-        functools.partial(out_kernel, tp),
-        out_shape=jax.ShapeDtypeStruct((docs, width), F32),
-        in_specs=[smem(), vmem()] + [vmem()] * tp,
-        out_specs=vmem(),
-        scratch_shapes=[pltpu.VMEM((max(docs, 8), heads * LANES), F32)],
-        compiler_params=params(8),
-        cost_estimate=cost(2 * docs * heads * LANES * width, heads * LANES * width * 2),
+    out_part, w_ready_b = pl.pallas_call(
+        functools.partial(out_kernel, tp, ready_a),
+        out_shape=[
+            jax.ShapeDtypeStruct((docs, width), F32),
+            pltpu.VMEM((ready_b, GU_BLOCK, hidden), BF16),
+        ],
+        in_specs=[vmem(), vmem(), hbm()] + [vmem()] * tp,
+        out_specs=[vmem()] * 2,
+        scratch_shapes=[
+            pltpu.VMEM((max(docs, 8), heads * LANES), F32),
+            pltpu.SemaphoreType.DMA((ready_b,)),
+        ],
+        compiler_params=params(docs, 6),
+        cost_estimate=cost(6),
         name="attn_project",
-    )(owner_rows, w_out, *head_parts)
+    )(places, w_out, w_gu, *head_parts)
 
     out_parts = exchange([out_part] * kv, "kv", kv)
-    gu_rows = GU_BLOCK
-    gu_blocks = 2 * width // gu_rows
+    gu_rest = gu_blocks - ready_a - ready_b
     attn_out, gu_part = pl.pallas_call(
         functools.partial(gate_up_kernel, kv),
         out_shape=[
             jax.ShapeDtypeStruct((docs, width), BF16),
             jax.ShapeDtypeStruct((2 * docs, hidden + LANES), BF16),
         ],
-        in_specs=[vmem(), vmem(), hbm()] + [vmem()] * kv,
+        in_specs=[vmem(), vmem(), hbm(), vmem(), vmem()] + [vmem()] * kv,
         out_specs=[vmem(), vmem()],
         scratch_shapes=[
-            pltpu.VMEM((gu_blocks, gu_rows, hidden), BF16),
+            pltpu.VMEM((gu_rest, GU_BLOCK, hidden), BF16),
             pltpu.VMEM((4 * docs, 2 * width), BF16),
             pltpu.VMEM((4 * docs, hidden), F32),
-            pltpu.SemaphoreType.DMA((gu_blocks,)),
-        ],
-        compiler_params=params(34),
-        cost_estimate=cost(8 * docs * width * hidden, width * hidden * 4),
+            pltpu.SemaphoreType.DMA((gu_rest,)),
+        ],
+        compiler_params=params(docs, 18),
+        cost_estimate=cost(8),
         name="gate_up",
-    )(states, norm_gains, w_gate_up, *out_parts)
+    )(states, norm_gains, w_gu, w_ready_a, w_ready_b, *out_parts)
 
     gu_parts = exchange([gu_part] * tp, "tp", tp)
     ffn_part = pl.pallas_call(
@@ -369,8 +435,8 @@
         in_specs=[vmem()] + [vmem()] * tp,
         out_specs=vmem(),
         scratch_shapes=[pltpu.VMEM((docs, hidden), BF16)],
-        compiler_params=params(20),
-        cost_estimate=cost(2 * docs * hidden * width, hidden * width * 2),
+        compiler_params=params(docs, 6),
+        cost_estimate=cost(5),
         name="down",
     )(w_down, *gu_parts)
     ffn_out = tree_sum(exchange([ffn_part] * kv, "kv", kv)).astype(BF16)

time: 70.1 us -> 58 us (0.83)
  local copies, waits for them, and re-layouts: 7.16 us -> 0.03 us
  Pallas kernels: 25.9 us -> 21.2 us
    unnamed x30 -> x16, local copies, waits for them, and re-layouts: 7.16 us -> 0.03 us
    pallas_call x1, Pallas kernels: 10.2 us -> 6.61 us  [per_device(): pl.pallas_call(functools.partial(gate_up_kernel, kv), out_shape=[jax.Shap...]
    pallas_call x1, Pallas kernels: 6.47 us -> 5.17 us  [per_device(): pl.pallas_call(functools.partial(qkv_kernel, tp), out_shape=[jax.ShapeDty...]
where the time goes in v2:
time: 58 us; the launch traced here: 57.8 us
  Pallas kernels  21.2 us (37%)
  starting transfers between devices  18.4 us (32%)
  waiting for transfers between devices  16.8 us (29%)
  between operations  0.76 us (1%)
  other arithmetic  0.62 us (1%)
    ppermute x15, starting transfers between devices, exchange(): lax.ppermute(arrays[s], axis, [(i, i ^ s) for i in range(size)])  18.4 us
    ppermute x15, waiting for transfers between devices, exchange(): lax.ppermute(arrays[s], axis, [(i, i ^ s) for i in range(size)])  16.8 us
    pallas_call x1, Pallas kernels, per_device(): pl.pallas_call(functools.partial(gate_up_kernel, kv), out_shape=[jax.Shap...  6.61 us
    pallas_call x1, Pallas kernels, per_device(): pl.pallas_call(functools.partial(qkv_kernel, tp), out_shape=[jax.ShapeDty...  5.17 us
    pallas_call x1, Pallas kernels, per_device(): pl.pallas_call(functools.partial(attend_kernel, tp, heads, 512), out_shap...  4.42 us
    pallas_call x1, Pallas kernels, per_device(): pl.pallas_call(functools.partial(down_kernel, tp), out_shape=jax.ShapeDty...  2.89 us
    pallas_call x1, Pallas kernels, per_device(): pl.pallas_call(functools.partial(out_kernel, tp, ready_a), out_shape=[jax...  2.09 us
  transfers between devices with their start and end apart: 15, of which 10 were waited for; matrix products, arithmetic and copies ran while one was open for 0% of the time, Pallas kernels for 0%

profile of v2, /device:TPU:0, one launch (start us, length us, event | category | flops | bytes accessed | tf_op | source)
XLA Modules:
  0.0 57.8 jit_solution(651266345400694251)
XLA Ops:
  0.6 5.2 %qkv.1 = (f32[16,128]{1,0:T(8,128)S(1)}, f32[16,128]{1,0:T(8,128)S(1)}, f32[16,128]{1,0:T(8,128)S(1)}, f32[16,128]{1,0:T(8,128)S(1)}, f32[8,128]{1,0:T(8,128)S(1)}, /*index=5*/s32[8,128]{1,0:T(8,128)S(1)}) custom-call(s32[4]{0:T(128)} %owner_hbm.1, s32[4]{0:T(128)} %lengths_hbm.1, f32[1,128]{1,0:T(1,128)} %constant.2.clone.frequency_hbm, ...), custom_call_target="tpu_custom_call" | custom-call | bytes 29520000 | tf_op jit(solution)/shard_map/qkv/pallas_call | solution.py:340
  5.8 3.1 %collective-permute-start = (f32[16,128]{1,0:T(8,128)S(1)}, f32[16,128]{1,0:T(8,128)S(1)}, u32[]{:S(2)}, u32[]{:S(2)}) collective-permute-start(f32[16,128]{1,0:T(8,128)S(1)} %get-tuple-element.18), channel_id=1, source_target_pairs={{0,4},{4,0},{8,12},{12,8},{1,5},{5,1},{9,13},{13,9},{2,6},{6,2},{1... | collective-permute-start | bytes 24584 | tf_op jit(solution)/shard_map/ppermute | solution.py:39
  8.9 2.6 %collective-permute-start.1 = (f32[16,128]{1,0:T(8,128)S(1)}, f32[16,128]{1,0:T(8,128)S(1)}, u32[]{:S(2)}, u32[]{:S(2)}) collective-permute-start(f32[16,128]{1,0:T(8,128)S(1)} %get-tuple-element.19), channel_id=1, source_target_pairs={{0,8},{4,12},{8,0},{12,4},{1,9},{5,13},{9,1},{13,5},{2,10},{6,14},... | collective-permute-start | bytes 24584 | tf_op jit(solution)/shard_map/ppermute | solution.py:39
  11.5 0.0 collective-permute-start.2
  11.5 0.0 collective-permute-done.rest_1_
  11.5 2.0 %collective-permute-done.1.rest_2_ = f32[16,128]{1,0:T(8,128)S(1)} collective-permute-done((f32[16,128]{1,0:T(8,128)S(1)}, f32[16,128]{1,0:T(8,128)S(1)}, u32[]{:S(2)}, u32[]{:S(2)}) %collective-permute-start.1) | collective-permute-done | bytes 8224 | tf_op jit(solution)/shard_map/ppermute | solution.py:39
  13.5 3.5 %collective-permute-done.2.rest_3_ = f32[16,128]{1,0:T(8,128)S(1)} collective-permute-done((f32[16,128]{1,0:T(8,128)S(1)}, f32[16,128]{1,0:T(8,128)S(1)}, u32[]{:S(2)}, u32[]{:S(2)}) %collective-permute-start.2) | collective-permute-done | bytes 8224 | tf_op jit(solution)/shard_map/ppermute | solution.py:39
  17.0 4.4 %attend.1 = (bf16[8,128]{1,0:T(8,128)(2,1)S(1)}, bf16[1,256]{1,0:T(2,128)(2,1)}, bf16[5,256,3584]{2,1,0:T(8,128)(2,1)S(1)}) custom-call(f32[8,128]{1,0:T(8,128)S(1)} %get-tuple-element.16.table, bf16[8192,256]{1,0:T(8,128)(2,1)S(1)} %bitcast.6, bf16[2048,2,3584]{2,1,0:T(2,128)(2,1)} %w.5, f32[16,128]{1,0:T(8,128)S(1)} %get-tuple-element.17.rest_0_, ...), custom_call_target="tpu_custom_call" | custom-call | bytes 29520000 | tf_op jit(solution)/shard_map/attend/pallas_call | solution.py:374
  21.4 0.2 collective-permute-start.5
  21.5 0.0 collective-permute-start.4
  21.6 4.3 %collective-permute-start.3 = (bf16[8,128]{1,0:T(8,128)(2,1)S(1)}, bf16[8,128]{1,0:T(8,128)(2,1)S(1)}, u32[]{:S(2)}, u32[]{:S(2)}) collective-permute-start(bf16[8,128]{1,0:T(8,128)(2,1)S(1)} %get-tuple-element.23.rest_0_), channel_id=1, source_target_pairs={{0,4},{4,0},{8,12},{12,8},{1,5},{5,1},{9,13},{13,9},{2,6},{6,2},{1... | collective-permute-start | bytes 6152 | tf_op jit(solution)/shard_map/ppermute | solution.py:39
  25.8 1.0 %collective-permute-done.5.rest_3_ = bf16[8,128]{1,0:T(8,128)(2,1)S(1)} collective-permute-done((bf16[8,128]{1,0:T(8,128)(2,1)S(1)}, bf16[8,128]{1,0:T(8,128)(2,1)S(1)}, u32[]{:S(2)}, u32[]{:S(2)}) %collective-permute-start.5) | collective-permute-done | bytes 2080 | tf_op jit(solution)/shard_map/ppermute | solution.py:39
  26.8 0.6 collective-permute-done.3.rest_1_
  27.4 2.1 %attn_project.1 = (f32[4,2048]{1,0:T(4,128)S(1)}, bf16[2,256,3584]{2,1,0:T(8,128)(2,1)S(1)}) custom-call(s32[8,128]{1,0:T(8,128)S(1)} %get-tuple-element.22.places, bf16[1024,2048]{1,0:T(8,128)(2,1)S(1)} %copy-done.1, bf16[2048,2,3584]{2,1,0:T(2,128)(2,1)} %w.5, bf16[8,128]{1,0:T(8,128)(2,1)S(1)} %get-tuple-element.23.rest_0_, ...), custom_call_target="tpu_custom_call" | custom-call | bytes 22140000 | tf_op jit(solution)/shard_map/attn_project/pallas_call | solution.py:393
  29.5 0.1 collective-permute-start.8
  29.6 1.6 %collective-permute-start.7 = (f32[4,2048]{1,0:T(4,128)S(1)}, f32[4,2048]{1,0:T(4,128)S(1)}, u32[]{:S(2)}, u32[]{:S(2)}) collective-permute-start(f32[4,2048]{1,0:T(4,128)S(1)} %get-tuple-element.25.rest_0_), channel_id=1, source_target_pairs={{0,2},{1,3},{2,0},{3,1},{4,6},{5,7},{6,4},{7,5},{8,10},{9,11},{10,... | collective-permute-start | bytes 98312 | tf_op jit(solution)/shard_map/ppermute | solution.py:39
  31.1 0.3 collective-permute-start.6
  31.4 1.8 %collective-permute-done.8.rest_3_ = f32[4,2048]{1,0:T(4,128)S(1)} collective-permute-done((f32[4,2048]{1,0:T(4,128)S(1)}, f32[4,2048]{1,0:T(4,128)S(1)}, u32[]{:S(2)}, u32[]{:S(2)}) %collective-permute-start.8) | collective-permute-done | bytes 32800 | tf_op jit(solution)/shard_map/ppermute | solution.py:39
  33.2 0.4 collective-permute-done.7.rest_2_
  33.7 6.6 %gate_up.1 = (bf16[4,2048]{1,0:T(4,128)(2,1)}, bf16[8,3712]{1,0:T(8,128)(2,1)S(1)}) custom-call(bf16[4,2048]{1,0:T(4,128)(2,1)S(1)} %copy-done.2, f32[2,2048]{1,0:T(2,128)S(1)} %copy-done.3, bf16[2048,2,3584]{2,1,0:T(2,128)(2,1)} %w.5, bf16[5,256,3584]{2,1,0:T(8,128)(2,1)S(1)} %get-tuple-element.21.ready_a, ...), custom_call_target="tpu_custom_call" | custom-call | bytes 29520000 | tf_op jit(solution)/shard_map/gate_up/pallas_call | solution.py:412
  40.3 2.4 %collective-permute-start.11 = (bf16[8,3712]{1,0:T(8,128)(2,1)S(1)}, bf16[8,3712]{1,0:T(8,128)(2,1)S(1)}, u32[]{:S(2)}, u32[]{:S(2)}) collective-permute-start(bf16[8,3712]{1,0:T(8,128)(2,1)S(1)} %get-tuple-element.27.rest_0_), channel_id=1, source_target_pairs={{0,12},{4,8},{8,4},{12,0},{1,13},{5,9},{9,5},{13,1},{2,14},{6,10},... | collective-permute-start | bytes 178184 | tf_op jit(solution)/shard_map/ppermute | solution.py:39
  42.7 1.1 %collective-permute-start.10 = (bf16[8,3712]{1,0:T(8,128)(2,1)S(1)}, bf16[8,3712]{1,0:T(8,128)(2,1)S(1)}, u32[]{:S(2)}, u32[]{:S(2)}) collective-permute-start(bf16[8,3712]{1,0:T(8,128)(2,1)S(1)} %get-tuple-element.27.rest_0_), channel_id=1, source_target_pairs={{0,8},{4,12},{8,0},{12,4},{1,9},{5,13},{9,1},{13,5},{2,10},{6,14},... | collective-permute-start | bytes 178184 | tf_op jit(solution)/shard_map/ppermute | solution.py:39
  43.8 0.9 %collective-permute-start.9 = (bf16[8,3712]{1,0:T(8,128)(2,1)S(1)}, bf16[8,3712]{1,0:T(8,128)(2,1)S(1)}, u32[]{:S(2)}, u32[]{:S(2)}) collective-permute-start(bf16[8,3712]{1,0:T(8,128)(2,1)S(1)} %get-tuple-element.27.rest_0_), channel_id=1, source_target_pairs={{0,4},{4,0},{8,12},{12,8},{1,5},{5,1},{9,13},{13,9},{2,6},{6,2},{1... | collective-permute-start | bytes 178184 | tf_op jit(solution)/shard_map/ppermute | solution.py:39
  44.7 2.3 %collective-permute-done.11.rest_3_ = bf16[8,3712]{1,0:T(8,128)(2,1)S(1)} collective-permute-done((bf16[8,3712]{1,0:T(8,128)(2,1)S(1)}, bf16[8,3712]{1,0:T(8,128)(2,1)S(1)}, u32[]{:S(2)}, u32[]{:S(2)}) %collective-permute-start.11) | collective-permute-done | bytes 59424 | tf_op jit(solution)/shard_map/ppermute | solution.py:39
  47.1 2.7 %collective-permute-done.10.rest_2_ = bf16[8,3712]{1,0:T(8,128)(2,1)S(1)} collective-permute-done((bf16[8,3712]{1,0:T(8,128)(2,1)S(1)}, bf16[8,3712]{1,0:T(8,128)(2,1)S(1)}, u32[]{:S(2)}, u32[]{:S(2)}) %collective-permute-start.10) | collective-permute-done | bytes 59424 | tf_op jit(solution)/shard_map/ppermute | solution.py:39
  49.9 2.9 %down.1 = f32[4,2048]{1,0:T(4,128)S(1)} custom-call(bf16[3584,2048]{1,0:T(8,128)(2,1)S(1)} %bitcast.5, bf16[8,3712]{1,0:T(8,128)(2,1)S(1)} %get-tuple-element.27.rest_0_, bf16[8,3712]{1,0:T(8,128)(2,1)S(1)} %collective-permute-done.9.rest_1_, bf16[8,3712]{1,0:T(8,128)(2,1)S(1)} %collective-permute-done.10.rest_2_, ...), custom_call_target="tpu_custom_call" | custom-call | bytes 18450000 | tf_op jit(solution)/shard_map/down/pallas_call | solution.py:432
  52.8 0.3 collective-permute-start.14
  53.1 1.1 %collective-permute-start.13 = (f32[4,2048]{1,0:T(4,128)S(1)}, f32[4,2048]{1,0:T(4,128)S(1)}, u32[]{:S(2)}, u32[]{:S(2)}) collective-permute-start(f32[4,2048]{1,0:T(4,128)S(1)} %down.1), channel_id=1, source_target_pairs={{0,2},{1,3},{2,0},{3,1},{4,6},{5,7},{6,4},{7,5},{8,10},{9,11},{10,... | collective-permute-start | bytes 98312 | tf_op jit(solution)/shard_map/ppermute | solution.py:39
  54.1 0.5 collective-permute-start.12
  54.6 1.7 %collective-permute-done.14 = f32[4,2048]{1,0:T(4,128)S(1)} collective-permute-done((f32[4,2048]{1,0:T(4,128)S(1)}, f32[4,2048]{1,0:T(4,128)S(1)}, u32[]{:S(2)}, u32[]{:S(2)}) %collective-permute-start.14) | collective-permute-done | bytes 32800 | tf_op jit(solution)/shard_map/ppermute | solution.py:39
  56.4 0.8 %collective-permute-done.13 = f32[4,2048]{1,0:T(4,128)S(1)} collective-permute-done((f32[4,2048]{1,0:T(4,128)S(1)}, f32[4,2048]{1,0:T(4,128)S(1)}, u32[]{:S(2)}, u32[]{:S(2)}) %collective-permute-start.13) | collective-permute-done | bytes 32800 | tf_op jit(solution)/shard_map/ppermute | solution.py:39
  57.2 0.6 %add_convert_fusion = bf16[4,2048]{1,0:T(4,128)(2,1)} fusion(f32[4,2048]{1,0:T(4,128)S(1)} %collective-permute-done.13, f32[4,2048]{1,0:T(4,128)S(1)} %collective-permute-done.14, f32[4,2048]{1,0:T(4,128)S(1)} %down.1, f32[4,2048]{1,0:T(4,128)S(1)} %collective-permute-done.12), kind=kLoop, calls=%fused_computation | loop fusion | flops 32768 | bytes 147456 | tf_op jit(solution)/shard_map/convert_element_type | solution.py:442
  (21 shorter events, 0.0 us)
Async XLA Ops:
  0.6 16.3 %copy-start = (bf16[1,8192,1,256]{3,1,2,0:T(8,128)(2,1)S(1)}, bf16[1,8192,1,256]{3,1,2,0:T(8,128)(2,1)}, u32[]{:S(2)}) copy-start(bf16[1,8192,1,256]{3,1,2,0:T(8,128)(2,1)} %param.18) | copy-start | bytes 12582916
  5.8 5.7 %collective-permute-start = (f32[16,128]{1,0:T(8,128)S(1)}, f32[16,128]{1,0:T(8,128)S(1)}, u32[]{:S(2)}, u32[]{:S(2)}) collective-permute-start(f32[16,128]{1,0:T(8,128)S(1)} %get-tuple-element.18), channel_id=1, source_target_pairs={{0,4},{4,0},{8,12},{12,8},{1,5},{5,1},{9,13},{13,9},{2,6},{6,2},{1... | collective-permute-start | bytes 24584 | tf_op jit(solution)/shard_map/ppermute | solution.py:39
  8.9 4.5 %collective-permute-start.1 = (f32[16,128]{1,0:T(8,128)S(1)}, f32[16,128]{1,0:T(8,128)S(1)}, u32[]{:S(2)}, u32[]{:S(2)}) collective-permute-start(f32[16,128]{1,0:T(8,128)S(1)} %get-tuple-element.19), channel_id=1, source_target_pairs={{0,8},{4,12},{8,0},{12,4},{1,9},{5,13},{9,1},{13,5},{2,10},{6,14},... | collective-permute-start | bytes 24584 | tf_op jit(solution)/shard_map/ppermute | solution.py:39
  11.5 5.4 %collective-permute-start.2 = (f32[16,128]{1,0:T(8,128)S(1)}, f32[16,128]{1,0:T(8,128)S(1)}, u32[]{:S(2)}, u32[]{:S(2)}) collective-permute-start(f32[16,128]{1,0:T(8,128)S(1)} %get-tuple-element.20), channel_id=1, source_target_pairs={{0,12},{4,8},{8,4},{12,0},{1,13},{5,9},{9,5},{13,1},{2,14},{6,10},... | collective-permute-start | bytes 24584 | tf_op jit(solution)/shard_map/ppermute | solution.py:39
  17.0 10.5 %copy-start.1 = (bf16[1024,2048]{1,0:T(8,128)(2,1)S(1)}, bf16[1024,2048]{1,0:T(8,128)(2,1)}, u32[]{:S(2)}) copy-start(bf16[1024,2048]{1,0:T(8,128)(2,1)} %w_out.1) | copy-start | bytes 12582916
  21.4 5.4 %collective-permute-start.5 = (bf16[8,128]{1,0:T(8,128)(2,1)S(1)}, bf16[8,128]{1,0:T(8,128)(2,1)S(1)}, u32[]{:S(2)}, u32[]{:S(2)}) collective-permute-start(bf16[8,128]{1,0:T(8,128)(2,1)S(1)} %get-tuple-element.23.rest_0_), channel_id=1, source_target_pairs={{0,12},{4,8},{8,4},{12,0},{1,13},{5,9},{9,5},{13,1},{2,14},{6,10},... | collective-permute-start | bytes 6152 | tf_op jit(solution)/shard_map/ppermute | solution.py:39
  21.5 5.3 %collective-permute-start.4 = (bf16[8,128]{1,0:T(8,128)(2,1)S(1)}, bf16[8,128]{1,0:T(8,128)(2,1)S(1)}, u32[]{:S(2)}, u32[]{:S(2)}) collective-permute-start(bf16[8,128]{1,0:T(8,128)(2,1)S(1)} %get-tuple-element.23.rest_0_), channel_id=1, source_target_pairs={{0,8},{4,12},{8,0},{12,4},{1,9},{5,13},{9,1},{13,5},{2,10},{6,14},... | collective-permute-start | bytes 6152 | tf_op jit(solution)/shard_map/ppermute | solution.py:39
  21.6 5.8 %collective-permute-start.3 = (bf16[8,128]{1,0:T(8,128)(2,1)S(1)}, bf16[8,128]{1,0:T(8,128)(2,1)S(1)}, u32[]{:S(2)}, u32[]{:S(2)}) collective-permute-start(bf16[8,128]{1,0:T(8,128)(2,1)S(1)} %get-tuple-element.23.rest_0_), channel_id=1, source_target_pairs={{0,4},{4,0},{8,12},{12,8},{1,5},{5,1},{9,13},{13,9},{2,6},{6,2},{1... | collective-permute-start | bytes 6152 | tf_op jit(solution)/shard_map/ppermute | solution.py:39
  27.4 6.2 %copy-start.2 = (bf16[4,2048]{1,0:T(4,128)(2,1)S(1)}, bf16[4,2048]{1,0:T(4,128)(2,1)}, u32[]{:S(2)}) copy-start(bf16[4,2048]{1,0:T(4,128)(2,1)} %states.1) | copy-start | bytes 49156
  27.4 6.2 %copy-start.3 = (f32[2,2048]{1,0:T(2,128)S(1)}, f32[2,2048]{1,0:T(2,128)}, u32[]{:S(2)}) copy-start(f32[2,2048]{1,0:T(2,128)} %gains.1) | copy-start | bytes 49156
  29.5 3.7 %collective-permute-start.8 = (f32[4,2048]{1,0:T(4,128)S(1)}, f32[4,2048]{1,0:T(4,128)S(1)}, u32[]{:S(2)}, u32[]{:S(2)}) collective-permute-start(f32[4,2048]{1,0:T(4,128)S(1)} %get-tuple-element.25.rest_0_), channel_id=1, source_target_pairs={{0,3},{1,2},{2,1},{3,0},{4,7},{5,6},{6,5},{7,4},{8,11},{9,10},{10,... | collective-permute-start | bytes 98312 | tf_op jit(solution)/shard_map/ppermute | solution.py:39
  29.6 4.0 %collective-permute-start.7 = (f32[4,2048]{1,0:T(4,128)S(1)}, f32[4,2048]{1,0:T(4,128)S(1)}, u32[]{:S(2)}, u32[]{:S(2)}) collective-permute-start(f32[4,2048]{1,0:T(4,128)S(1)} %get-tuple-element.25.rest_0_), channel_id=1, source_target_pairs={{0,2},{1,3},{2,0},{3,1},{4,6},{5,7},{6,4},{7,5},{8,10},{9,11},{10,... | collective-permute-start | bytes 98312 | tf_op jit(solution)/shard_map/ppermute | solution.py:39
  31.1 2.5 %collective-permute-start.6 = (f32[4,2048]{1,0:T(4,128)S(1)}, f32[4,2048]{1,0:T(4,128)S(1)}, u32[]{:S(2)}, u32[]{:S(2)}) collective-permute-start(f32[4,2048]{1,0:T(4,128)S(1)} %get-tuple-element.25.rest_0_), channel_id=1, source_target_pairs={{0,1},{1,0},{2,3},{3,2},{4,5},{5,4},{6,7},{7,6},{8,9},{9,8},{10,11... | collective-permute-start | bytes 98312 | tf_op jit(solution)/shard_map/ppermute | solution.py:39
  33.6 16.2 %slice-start = ((s8[14680064]{0:T(1024)(128)(4,1)}), s8[4194304]{0:T(1024)(128)(4,1)S(1)}, s32[]{:S(2)}) async-start(s8[14680064]{0:T(1024)(128)(4,1)} %bitcast.4), calls=%async_computation | async-start | bytes 8388608
  33.6 16.2 %slice-start.1 = ((s8[14680064]{0:T(1024)(128)(4,1)}), s8[4194304]{0:T(1024)(128)(4,1)S(1)}, s32[]{:S(2)}) async-start(s8[14680064]{0:T(1024)(128)(4,1)} %bitcast.4), calls=%async_computation.1 | async-start | bytes 8388608
  33.6 16.2 %slice-start.2 = ((s8[14680064]{0:T(1024)(128)(4,1)}), s8[4194304]{0:T(1024)(128)(4,1)S(1)}, s32[]{:S(2)}) async-start(s8[14680064]{0:T(1024)(128)(4,1)} %bitcast.4), calls=%async_computation.2 | async-start | bytes 8388608
  33.7 16.2 %slice-start.3 = ((s8[14680064]{0:T(1024)(128)(4,1)}), s8[2097152]{0:T(1024)(128)(4,1)S(1)}, s32[]{:S(2)}) async-start(s8[14680064]{0:T(1024)(128)(4,1)} %bitcast.4), calls=%async_computation.3 | async-start | bytes 4194304
  40.3 6.8 %collective-permute-start.11 = (bf16[8,3712]{1,0:T(8,128)(2,1)S(1)}, bf16[8,3712]{1,0:T(8,128)(2,1)S(1)}, u32[]{:S(2)}, u32[]{:S(2)}) collective-permute-start(bf16[8,3712]{1,0:T(8,128)(2,1)S(1)} %get-tuple-element.27.rest_0_), channel_id=1, source_target_pairs={{0,12},{4,8},{8,4},{12,0},{1,13},{5,9},{9,5},{13,1},{2,14},{6,10},... | collective-permute-start | bytes 178184 | tf_op jit(solution)/shard_map/ppermute | solution.py:39
  42.7 7.1 %collective-permute-start.10 = (bf16[8,3712]{1,0:T(8,128)(2,1)S(1)}, bf16[8,3712]{1,0:T(8,128)(2,1)S(1)}, u32[]{:S(2)}, u32[]{:S(2)}) collective-permute-start(bf16[8,3712]{1,0:T(8,128)(2,1)S(1)} %get-tuple-element.27.rest_0_), channel_id=1, source_target_pairs={{0,8},{4,12},{8,0},{12,4},{1,9},{5,13},{9,1},{13,5},{2,10},{6,14},... | collective-permute-start | bytes 178184 | tf_op jit(solution)/shard_map/ppermute | solution.py:39
  43.8 6.0 %collective-permute-start.9 = (bf16[8,3712]{1,0:T(8,128)(2,1)S(1)}, bf16[8,3712]{1,0:T(8,128)(2,1)S(1)}, u32[]{:S(2)}, u32[]{:S(2)}) collective-permute-start(bf16[8,3712]{1,0:T(8,128)(2,1)S(1)} %get-tuple-element.27.rest_0_), channel_id=1, source_target_pairs={{0,4},{4,0},{8,12},{12,8},{1,5},{5,1},{9,13},{13,9},{2,6},{6,2},{1... | collective-permute-start | bytes 178184 | tf_op jit(solution)/shard_map/ppermute | solution.py:39
  52.8 3.6 %collective-permute-start.14 = (f32[4,2048]{1,0:T(4,128)S(1)}, f32[4,2048]{1,0:T(4,128)S(1)}, u32[]{:S(2)}, u32[]{:S(2)}) collective-permute-start(f32[4,2048]{1,0:T(4,128)S(1)} %down.1), channel_id=1, source_target_pairs={{0,3},{1,2},{2,1},{3,0},{4,7},{5,6},{6,5},{7,4},{8,11},{9,10},{10,... | collective-permute-start | bytes 98312 | tf_op jit(solution)/shard_map/ppermute | solution.py:39
  53.1 4.1 %collective-permute-start.13 = (f32[4,2048]{1,0:T(4,128)S(1)}, f32[4,2048]{1,0:T(4,128)S(1)}, u32[]{:S(2)}, u32[]{:S(2)}) collective-permute-start(f32[4,2048]{1,0:T(4,128)S(1)} %down.1), channel_id=1, source_target_pairs={{0,2},{1,3},{2,0},{3,1},{4,6},{5,7},{6,4},{7,5},{8,10},{9,11},{10,... | collective-permute-start | bytes 98312 | tf_op jit(solution)/shard_map/ppermute | solution.py:39
  54.1 3.1 %collective-permute-start.12 = (f32[4,2048]{1,0:T(4,128)S(1)}, f32[4,2048]{1,0:T(4,128)S(1)}, u32[]{:S(2)}, u32[]{:S(2)}) collective-permute-start(f32[4,2048]{1,0:T(4,128)S(1)} %down.1), channel_id=1, source_target_pairs={{0,1},{1,0},{2,3},{3,2},{4,5},{5,4},{6,7},{7,6},{8,9},{9,8},{10,11... | collective-permute-start | bytes 98312 | tf_op jit(solution)/shard_map/ppermute | solution.py:39

commit v3 on v2

--- a/solution.py
+++ b/solution.py
@@ -94,10 +94,9 @@
 
 
 def qkv_kernel(tp, owner_hbm, lengths_hbm, frequency_hbm, states_hbm, gains_hbm, wq, wkv, *rest):
-    outs = rest[:tp]
-    table, places = rest[tp : tp + 2]
-    owner, lengths, frequency, states, gains = rest[tp + 2 : tp + 7]
-    wq_buf, wkv_buf, spread_buf, res, kv_res, sq_res, sems, small_sems = rest[tp + 7 :]
+    outs, table, places = rest[:3]
+    owner, lengths, frequency, states, gains = rest[3:8]
+    wq_buf, wkv_buf, spread_buf, res, kv_res, sq_res, sems, small_sems = rest[8:]
     docs, width = states.shape
     pairs = wq.shape[1]
     halves = wq_buf.shape[0]
@@ -160,30 +159,30 @@
         )
     res[...] = total[: 2 * docs] + total[2 * docs :]
     for s in range(tp):
-        doc = owner[me ^ s]
+        doc = owner[s]
         for parity in range(2):
             chosen = pick_row(res, parity * docs + doc)
             for p in range(pairs):
-                outs[s][2 * p + parity : 2 * p + parity + 1, :] = chosen[
+                outs[s, 2 * p + parity : 2 * p + parity + 1, :] = chosen[
                     :, p * LANES : (p + 1) * LANES
                 ]
         chosen = pick_row(kv_res, doc)
         h = 2 * pairs
-        outs[s][h : h + 1, :] = chosen[:, :LANES]
-        outs[s][h + 1 : h + 2, :] = chosen[:, LANES:]
-        outs[s][h + 2 : h + 3, :] = pick_row(sq_res, doc)
-        outs[s][h + 3 :, :] = jnp.zeros((outs[s].shape[0] - h - 3, LANES), F32)
-
-
-def attend_kernel(tp, heads, rows, table, cache, w, *rest):
-    parts = rest[:tp]
-    heads_out, new_kv_out, w_ready, scores, w_sems = rest[tp:]
+        outs[s, h : h + 1, :] = chosen[:, :LANES]
+        outs[s, h + 1 : h + 2, :] = chosen[:, LANES:]
+        outs[s, h + 2 : h + 3, :] = pick_row(sq_res, doc)
+        outs[s, h + 3 :, :] = jnp.zeros((outs.shape[1] - h - 3, LANES), F32)
+
+
+def attend_kernel(
+    heads, rows, table, cache, w, parts, heads_out, new_kv_out, w_ready, scores, w_sems
+):
     width, _, hidden = w.shape
     w_copies = weight_copies(w.reshape(2 * width, hidden), 0, w_ready, w_sems)
     for copy in w_copies:
         copy.start()
     blocks = cache.shape[0] // rows
-    sums = tree_sum([part[...] for part in parts])
+    sums = tree_sum([parts[j] for j in range(parts.shape[0])])
     sums = sums * lax.rsqrt(sums[heads + 2 : heads + 3, :] / D + EPS)
     rotated = sums * table[0:1, :] + pltpu.roll(sums, LANES // 2, 1) * table[1:2, :]
     query = rotated[:heads].astype(BF16)
@@ -224,14 +223,10 @@
         copy.wait()
 
 
-def out_kernel(tp, first, places, w_out, w, *rest):
+def out_kernel(tp, places, w_out, *rest):
     parts = rest[:tp]
-    out, w_ready, left, w_sems = rest[tp:]
-    width, _, hidden = w.shape
-    w_copies = weight_copies(w.reshape(2 * width, hidden), first, w_ready, w_sems)
-    for copy in w_copies:
-        copy.start()
-    docs = out.shape[0]
+    out, left = rest[tp:]
+    docs = out.shape[1]
     row = lax.broadcasted_iota(jnp.int32, (left.shape[0], LANES), 0)
     own = [parts[s][...].astype(F32) for s in range(tp)]
     for h in range(own[0].shape[0]):
@@ -239,22 +234,22 @@
         for s in range(tp):
             piece = jnp.where(row == places[s : s + 1, :], own[s][h : h + 1, :], piece)
         left[:, h * LANES : (h + 1) * LANES] = piece
-    out[...] = jnp.dot(left[...].astype(BF16), w_out[...], preferred_element_type=F32)[:docs]
-    for copy in w_copies:
-        copy.wait()
-
-
-def gate_up_kernel(kv, states, gains, w, ready_a, ready_b, *rest):
-    parts = rest[:kv]
-    attn_out, partial_out, w_buf, spread_buf, acc, sems = rest[kv:]
+    terms = jnp.dot(left[...].astype(BF16), w_out[...], preferred_element_type=F32)[:docs]
+    for j in range(out.shape[0]):
+        out[j] = terms
+
+
+def gate_up_kernel(
+    states, gains, w, ready, parts, attn_out, partial_out, w_buf, spread_buf, acc, sems
+):
     docs, width = states.shape
     hidden = w.shape[2]
     rows = w_buf.shape[1]
-    first = ready_a.shape[0] + ready_b.shape[0]
+    first = ready.shape[0]
     w_rows = w.reshape(2 * width, hidden)
     for copy in weight_copies(w_rows, first, w_buf, sems):
         copy.start()
-    attn = tree_sum([part[...] for part in parts]).astype(BF16)
+    attn = tree_sum([parts[j] for j in range(parts.shape[0])]).astype(BF16)
     attn_out[...] = attn
     resid = (states[...].astype(F32) + attn.astype(F32)).astype(BF16).astype(F32)
     squares = jnp.sum(resid * resid, axis=1, keepdims=True)
@@ -273,8 +268,7 @@
 
         lax.fori_loop(0, buf.shape[0], step, 0)
 
-    add_blocks(ready_a, 0, False)
-    add_blocks(ready_b, ready_a.shape[0], False)
+    add_blocks(ready, 0, False)
     add_blocks(w_buf, first, True)
     partial_out[:, :hidden] = (acc[: 2 * docs] + acc[2 * docs :]).astype(BF16)
     lane = lax.broadcasted_iota(jnp.int32, (docs, LANES), 1)
@@ -337,15 +331,15 @@
     half = LANES // 2
     freq = ROPE_BASE ** (-(np.arange(half, dtype=np.float64) * 2.0 / LANES))
     freq = jnp.asarray(np.concatenate([freq, freq]).astype(np.float32)[None, :])
-    *qkv_parts, table, places = pl.pallas_call(
+    qkv_parts, table, places = pl.pallas_call(
         functools.partial(qkv_kernel, tp),
-        out_shape=[jax.ShapeDtypeStruct((packed, LANES), F32)] * tp
-        + [
+        out_shape=[
+            jax.ShapeDtypeStruct((tp, packed, LANES), F32),
             jax.ShapeDtypeStruct((8, LANES), F32),
             jax.ShapeDtypeStruct((max(tp, 8), LANES), jnp.int32),
         ],
         in_specs=[hbm()] * 7,
-        out_specs=[vmem()] * (tp + 2),
+        out_specs=[vmem()] * 3,
         scratch_shapes=[
             pltpu.SMEM((docs,), jnp.int32),
             pltpu.SMEM((docs,), jnp.int32),
@@ -365,57 +359,50 @@
         cost_estimate=cost(8),
         name="qkv",
     )(*(in_hbm(a) for a in (owner_rows, lengths, freq, states, norm_gains, wq, wkv)))
-    qkv_parts = exchange(qkv_parts, "tp", tp)
+    qkv_parts = lax.all_to_all(qkv_parts, "tp", 0, 0, tiled=True)
 
     w_gu = in_hbm(w_gate_up)
     gu_blocks = 2 * width // GU_BLOCK
-    ready_a = max(gu_blocks * 5 // 16, 1)
-    ready_b = max(gu_blocks // 8, 1)
-    head_out, new_kv, w_ready_a = pl.pallas_call(
-        functools.partial(attend_kernel, tp, heads, 512),
+    ready = max(gu_blocks * 6 // 16, 1)
+    head_out, new_kv, w_ready = pl.pallas_call(
+        functools.partial(attend_kernel, heads, 512),
         out_shape=[
             jax.ShapeDtypeStruct((heads, LANES), BF16),
             jax.ShapeDtypeStruct((1, 2 * LANES), BF16),
-            pltpu.VMEM((ready_a, GU_BLOCK, hidden), BF16),
-        ],
-        in_specs=[vmem(), vmem(), hbm()] + [vmem()] * tp,
+            pltpu.VMEM((ready, GU_BLOCK, hidden), BF16),
+        ],
+        in_specs=[vmem(), vmem(), hbm(), vmem()],
         out_specs=[vmem()] * 3,
         scratch_shapes=[
             pltpu.VMEM((heads, cache_len), F32),
-            pltpu.SemaphoreType.DMA((ready_a,)),
+            pltpu.SemaphoreType.DMA((ready,)),
         ],
         compiler_params=params(docs, 6),
         cost_estimate=cost(8),
         name="attend",
-    )(table, cache, w_gu, *qkv_parts)
+    )(table, cache, w_gu, qkv_parts)
 
     head_parts = exchange([head_out] * tp, "tp", tp)
-    out_part, w_ready_b = pl.pallas_call(
-        functools.partial(out_kernel, tp, ready_a),
-        out_shape=[
-            jax.ShapeDtypeStruct((docs, width), F32),
-            pltpu.VMEM((ready_b, GU_BLOCK, hidden), BF16),
-        ],
-        in_specs=[vmem(), vmem(), hbm()] + [vmem()] * tp,
-        out_specs=[vmem()] * 2,
-        scratch_shapes=[
-            pltpu.VMEM((max(docs, 8), heads * LANES), F32),
-            pltpu.SemaphoreType.DMA((ready_b,)),
-        ],
+    out_part = pl.pallas_call(
+        functools.partial(out_kernel, tp),
+        out_shape=jax.ShapeDtypeStruct((kv, docs, width), F32),
+        in_specs=[vmem()] * (tp + 2),
+        out_specs=vmem(),
+        scratch_shapes=[pltpu.VMEM((max(docs, 8), heads * LANES), F32)],
         compiler_params=params(docs, 6),
         cost_estimate=cost(6),
         name="attn_project",
-    )(places, w_out, w_gu, *head_parts)
-
-    out_parts = exchange([out_part] * kv, "kv", kv)
-    gu_rest = gu_blocks - ready_a - ready_b
+    )(places, w_out, *head_parts)
+
+    out_parts = lax.all_to_all(out_part, "kv", 0, 0, tiled=True)
+    gu_rest = gu_blocks - ready
     attn_out, gu_part = pl.pallas_call(
-        functools.partial(gate_up_kernel, kv),
+        gate_up_kernel,
         out_shape=[
             jax.ShapeDtypeStruct((docs, width), BF16),
             jax.ShapeDtypeStruct((2 * docs, hidden + LANES), BF16),
         ],
-        in_specs=[vmem(), vmem(), hbm(), vmem(), vmem()] + [vmem()] * kv,
+        in_specs=[vmem(), vmem(), hbm(), vmem(), vmem()],
         out_specs=[vmem(), vmem()],
         scratch_shapes=[
             pltpu.VMEM((gu_rest, GU_BLOCK, hidden), BF16),
@@ -423,10 +410,10 @@
             pltpu.VMEM((4 * docs, hidden), F32),
             pltpu.SemaphoreType.DMA((gu_rest,)),
         ],
-        compiler_params=params(docs, 18),
+        compiler_params=params(docs, 22),
         cost_estimate=cost(8),
         name="gate_up",
-    )(states, norm_gains, w_gu, w_ready_a, w_ready_b, *out_parts)
+    )(states, norm_gains, w_gu, w_ready, out_parts)
 
     gu_parts = exchange([gu_part] * tp, "tp", tp)
     ffn_part = pl.pallas_call(

time: 58 us -> 62.5 us (1.078)
  blocking collectives: 0 us -> 19.1 us
  waiting for transfers between devices: 16.8 us -> 8.21 us
  starting transfers between devices: 18.4 us -> 10.8 us
  local copies, waits for them, and re-layouts: 0.03 us -> 2.21 us
    all_to_all x0 -> x2, blocking collectives: none -> 19.1 us  [the longest x1 11.8 us: per_device(): qkv_parts = lax.all_to_all(qkv_parts, 'tp', 0, 0, tiled=True)]
    ppermute x15 -> x9, waiting for transfers between devices: 16.8 us -> 8.21 us  [exchange(): lax.ppermute(arrays[s], axis, [(i, i ^ s) for i in range(size)])]
    ppermute x15 -> x9, starting transfers between devices: 18.4 us -> 10.8 us  [exchange(): lax.ppermute(arrays[s], axis, [(i, i ^ s) for i in range(size)])]
    unnamed x16, local copies, waits for them, and re-layouts: 0.03 us -> 2.21 us
  transfers between devices with their start and end apart: 15 -> 9, of which waited for: 10 -> 7; matrix products, arithmetic and copies ran while one was open for 0% -> 0% of each run, Pallas kernels for 0% -> 0%
where the time goes in v3:
time: 62.5 us; the launch traced here: 62.3 us
  Pallas kernels  20.7 us (33%)
  blocking collectives  19.1 us (31%)
  starting transfers between devices  10.8 us (17%)
  waiting for transfers between devices  8.21 us (13%)
  local copies, waits for them, and re-layouts  2.21 us (4%)
  between operations  0.7 us (1%)
    all_to_all x1, blocking collectives, per_device(): qkv_parts = lax.all_to_all(qkv_parts, 'tp', 0, 0, tiled=True)  11.8 us
    ppermute x9, starting transfers between devices, exchange(): lax.ppermute(arrays[s], axis, [(i, i ^ s) for i in range(size)])  10.8 us
    ppermute x9, waiting for transfers between devices, exchange(): lax.ppermute(arrays[s], axis, [(i, i ^ s) for i in range(size)])  8.21 us
    all_to_all x1, blocking collectives, per_device(): out_parts = lax.all_to_all(out_part, 'kv', 0, 0, tiled=True)  7.33 us
    pallas_call x1, Pallas kernels, per_device(): pl.pallas_call(gate_up_kernel, out_shape=[jax.ShapeDtypeStruct((docs, wid...  7.14 us
    pallas_call x1, Pallas kernels, per_device(): pl.pallas_call(functools.partial(qkv_kernel, tp), out_shape=[jax.ShapeDty...  5.02 us
    pallas_call x1, Pallas kernels, per_device(): pl.pallas_call(functools.partial(attend_kernel, heads, 512), out_shape=[j...  4.95 us
    pallas_call x1, Pallas kernels, per_device(): pl.pallas_call(functools.partial(down_kernel, tp), out_shape=jax.ShapeDty...  2.89 us
  transfers between devices with their start and end apart: 9, of which 7 were waited for; matrix products, arithmetic and copies ran while one was open for 0% of the time, Pallas kernels for 0%

profile of v3, /device:TPU:0, one launch (start us, length us, event | category | flops | bytes accessed | tf_op | source)
XLA Modules:
  0.0 62.3 jit_solution(16583126918500866450)
XLA Ops:
  0.6 5.0 %qkv.1 = (f32[4,16,128]{2,1,0:T(8,128)S(1)}, f32[8,128]{1,0:T(8,128)S(1)}, s32[8,128]{1,0:T(8,128)S(1)}) custom-call(s32[4]{0:T(128)} %owner_hbm.1, s32[4]{0:T(128)} %lengths_hbm.1, f32[1,128]{1,0:T(1,128)} %constant.2.clone.frequency_hbm, bf16[4,2048]{1,0:T(4,128)(2,1)} %states.1, f32[2,2048]{1,0:T(2,128)} %gains.1, bf16[2048,4,2,128]{3,2,1,0:T(2,128)(2,1)} %bitcast.7, ...), custom_call_target="tpu_custom_call" | custom-call | bytes 29520000 | tf_op jit(solution)/shard_map/qkv/pallas_call | solution.py:334
  5.7 11.8 %all_to_all.10.parts = f32[4,16,128]{2,1,0:T(8,128)S(1)} all-to-all(f32[4,16,128]{2,1,0:T(8,128)S(1)} %get-tuple-element.12), channel_id=1, replica_groups=mesh['grp'=2,'tp'=4,'kv'=4] {'tp'}, dimensions={0} | all-to-all | bytes 65536 | tf_op jit(solution)/shard_map/all_to_all | solution.py:362
  17.4 2.2 %copy-done = bf16[1,8192,1,256]{3,1,2,0:T(8,128)(2,1)S(1)} copy-done((bf16[1,8192,1,256]{3,1,2,0:T(8,128)(2,1)S(1)}, bf16[1,8192,1,256]{3,1,2,0:T(8,128)(2,1)}, u32[]{:S(2)}) %copy-start) | copy-done | bytes 4194328
  19.6 5.0 %attend.1 = (bf16[8,128]{1,0:T(8,128)(2,1)S(1)}, bf16[1,256]{1,0:T(2,128)(2,1)}, bf16[6,256,3584]{2,1,0:T(8,128)(2,1)S(1)}) custom-call(f32[8,128]{1,0:T(8,128)S(1)} %get-tuple-element.11.table, bf16[8192,256]{1,0:T(8,128)(2,1)S(1)} %bitcast.6, bf16[2048,2,3584]{2,1,0:T(2,128)(2,1)} %w.3, f32[4,16,128]{2,1,0:T(8,128)S(1)} %all_to_all.10.parts), custom_call_target="tpu_custom_call" | custom-call | bytes 29520000 | tf_op jit(solution)/shard_map/attend/pallas_call | solution.py:367
  24.6 0.7 %collective-permute-start.2 = (bf16[8,128]{1,0:T(8,128)(2,1)S(1)}, bf16[8,128]{1,0:T(8,128)(2,1)S(1)}, u32[]{:S(2)}, u32[]{:S(2)}) collective-permute-start(bf16[8,128]{1,0:T(8,128)(2,1)S(1)} %get-tuple-element.15.rest_0_), channel_id=1, source_target_pairs={{0,12},{4,8},{8,4},{12,0},{1,13},{5,9},{9,5},{13,1},{2,14},{6,10},... | collective-permute-start | bytes 6152 | tf_op jit(solution)/shard_map/ppermute | solution.py:39
  25.3 1.6 %collective-permute-start.1 = (bf16[8,128]{1,0:T(8,128)(2,1)S(1)}, bf16[8,128]{1,0:T(8,128)(2,1)S(1)}, u32[]{:S(2)}, u32[]{:S(2)}) collective-permute-start(bf16[8,128]{1,0:T(8,128)(2,1)S(1)} %get-tuple-element.15.rest_0_), channel_id=1, source_target_pairs={{0,8},{4,12},{8,0},{12,4},{1,9},{5,13},{9,1},{13,5},{2,10},{6,14},... | collective-permute-start | bytes 6152 | tf_op jit(solution)/shard_map/ppermute | solution.py:39
  26.9 2.2 %collective-permute-start = (bf16[8,128]{1,0:T(8,128)(2,1)S(1)}, bf16[8,128]{1,0:T(8,128)(2,1)S(1)}, u32[]{:S(2)}, u32[]{:S(2)}) collective-permute-start(bf16[8,128]{1,0:T(8,128)(2,1)S(1)} %get-tuple-element.15.rest_0_), channel_id=1, source_target_pairs={{0,4},{4,0},{8,12},{12,8},{1,5},{5,1},{9,13},{13,9},{2,6},{6,2},{1... | collective-permute-start | bytes 6152 | tf_op jit(solution)/shard_map/ppermute | solution.py:39
  29.0 1.0 %collective-permute-done.2.rest_3_ = bf16[8,128]{1,0:T(8,128)(2,1)S(1)} collective-permute-done((bf16[8,128]{1,0:T(8,128)(2,1)S(1)}, bf16[8,128]{1,0:T(8,128)(2,1)S(1)}, u32[]{:S(2)}, u32[]{:S(2)}) %collective-permute-start.2) | collective-permute-done | bytes 2080 | tf_op jit(solution)/shard_map/ppermute | solution.py:39
  30.0 0.0 collective-permute-done.1.rest_2_
  30.0 0.6 collective-permute-done.rest_1_
  30.6 0.0 copy-done.1
  30.6 0.6 %attn_project.1 = f32[4,4,2048]{2,1,0:T(4,128)S(1)} custom-call(s32[8,128]{1,0:T(8,128)S(1)} %get-tuple-element.14.places, bf16[1024,2048]{1,0:T(8,128)(2,1)S(1)} %copy-done.1, bf16[8,128]{1,0:T(8,128)(2,1)S(1)} %get-tuple-element.15.rest_0_, bf16[8,128]{1,0:T(8,128)(2,1)S(1)} %collective-permute-done.rest_1_, ...), custom_call_target="tpu_custom_call" | custom-call | bytes 22140000 | tf_op jit(solution)/shard_map/attn_project/pallas_call | solution.py:386
  31.3 7.3 %all_to_all.11.parts = f32[4,4,2048]{2,1,0:T(4,128)S(1)} all-to-all(f32[4,4,2048]{2,1,0:T(4,128)S(1)} %attn_project.1), channel_id=1, replica_groups=mesh['grp'=2,'tp'=4,'kv'=4] {'kv'}, dimensions={0} | all-to-all | bytes 262144 | tf_op jit(solution)/shard_map/all_to_all | solution.py:397
  38.6 0.0 copy-done.2
  38.6 0.0 copy-done.3
  38.6 0.0 slice-start.3
  38.6 7.1 %gate_up.1 = (bf16[4,2048]{1,0:T(4,128)(2,1)}, bf16[8,3712]{1,0:T(8,128)(2,1)S(1)}) custom-call(bf16[4,2048]{1,0:T(4,128)(2,1)S(1)} %copy-done.2, f32[2,2048]{1,0:T(2,128)S(1)} %copy-done.3, bf16[2048,2,3584]{2,1,0:T(2,128)(2,1)} %w.3, bf16[6,256,3584]{2,1,0:T(8,128)(2,1)S(1)} %get-tuple-element.13.ready, f32[4,4,2048]{2,1,0:T(4,128)S(1)} %all_to_all.11.parts), custom_call_target="tpu_custom_call" | custom-call | bytes 29520000 | tf_op jit(solution)/shard_map/gate_up/pallas_call | solution.py:399
  45.8 2.4 %collective-permute-start.5 = (bf16[8,3712]{1,0:T(8,128)(2,1)S(1)}, bf16[8,3712]{1,0:T(8,128)(2,1)S(1)}, u32[]{:S(2)}, u32[]{:S(2)}) collective-permute-start(bf16[8,3712]{1,0:T(8,128)(2,1)S(1)} %get-tuple-element.17.rest_0_), channel_id=1, source_target_pairs={{0,12},{4,8},{8,4},{12,0},{1,13},{5,9},{9,5},{13,1},{2,14},{6,10},... | collective-permute-start | bytes 178184 | tf_op jit(solution)/shard_map/ppermute | solution.py:39
  48.2 1.1 %collective-permute-start.4 = (bf16[8,3712]{1,0:T(8,128)(2,1)S(1)}, bf16[8,3712]{1,0:T(8,128)(2,1)S(1)}, u32[]{:S(2)}, u32[]{:S(2)}) collective-permute-start(bf16[8,3712]{1,0:T(8,128)(2,1)S(1)} %get-tuple-element.17.rest_0_), channel_id=1, source_target_pairs={{0,8},{4,12},{8,0},{12,4},{1,9},{5,13},{9,1},{13,5},{2,10},{6,14},... | collective-permute-start | bytes 178184 | tf_op jit(solution)/shard_map/ppermute | solution.py:39
  49.3 0.9 %collective-permute-start.3 = (bf16[8,3712]{1,0:T(8,128)(2,1)S(1)}, bf16[8,3712]{1,0:T(8,128)(2,1)S(1)}, u32[]{:S(2)}, u32[]{:S(2)}) collective-permute-start(bf16[8,3712]{1,0:T(8,128)(2,1)S(1)} %get-tuple-element.17.rest_0_), channel_id=1, source_target_pairs={{0,4},{4,0},{8,12},{12,8},{1,5},{5,1},{9,13},{13,9},{2,6},{6,2},{1... | collective-permute-start | bytes 178184 | tf_op jit(solution)/shard_map/ppermute | solution.py:39
  50.2 1.7 %collective-permute-done.5.rest_3_ = bf16[8,3712]{1,0:T(8,128)(2,1)S(1)} collective-permute-done((bf16[8,3712]{1,0:T(8,128)(2,1)S(1)}, bf16[8,3712]{1,0:T(8,128)(2,1)S(1)}, u32[]{:S(2)}, u32[]{:S(2)}) %collective-permute-start.5) | collective-permute-done | bytes 59424 | tf_op jit(solution)/shard_map/ppermute | solution.py:39
  51.9 2.6 %collective-permute-done.4.rest_2_ = bf16[8,3712]{1,0:T(8,128)(2,1)S(1)} collective-permute-done((bf16[8,3712]{1,0:T(8,128)(2,1)S(1)}, bf16[8,3712]{1,0:T(8,128)(2,1)S(1)}, u32[]{:S(2)}, u32[]{:S(2)}) %collective-permute-start.4) | collective-permute-done | bytes 59424 | tf_op jit(solution)/shard_map/ppermute | solution.py:39
  54.6 0.1 collective-permute-done.3.rest_1_
  54.7 0.0 slice-done.1
  54.7 2.9 %down.1 = f32[4,2048]{1,0:T(4,128)S(1)} custom-call(bf16[3584,2048]{1,0:T(8,128)(2,1)S(1)} %bitcast.5, bf16[8,3712]{1,0:T(8,128)(2,1)S(1)} %get-tuple-element.17.rest_0_, bf16[8,3712]{1,0:T(8,128)(2,1)S(1)} %collective-permute-done.3.rest_1_, bf16[8,3712]{1,0:T(8,128)(2,1)S(1)} %collective-permute-done.4.rest_2_, ...), custom_call_target="tpu_custom_call" | custom-call | bytes 18450000 | tf_op jit(solution)/shard_map/down/pallas_call | solution.py:419
  57.6 0.0 collective-permute-start.8
  57.6 1.0 %collective-permute-start.7 = (f32[4,2048]{1,0:T(4,128)S(1)}, f32[4,2048]{1,0:T(4,128)S(1)}, u32[]{:S(2)}, u32[]{:S(2)}) collective-permute-start(f32[4,2048]{1,0:T(4,128)S(1)} %down.1), channel_id=1, source_target_pairs={{0,2},{1,3},{2,0},{3,1},{4,6},{5,7},{6,4},{7,5},{8,10},{9,11},{10,... | collective-permute-start | bytes 98312 | tf_op jit(solution)/shard_map/ppermute | solution.py:39
  58.6 0.9 %collective-permute-start.6 = (f32[4,2048]{1,0:T(4,128)S(1)}, f32[4,2048]{1,0:T(4,128)S(1)}, u32[]{:S(2)}, u32[]{:S(2)}) collective-permute-start(f32[4,2048]{1,0:T(4,128)S(1)} %down.1), channel_id=1, source_target_pairs={{0,1},{1,0},{2,3},{3,2},{4,5},{5,4},{6,7},{7,6},{8,9},{9,8},{10,11... | collective-permute-start | bytes 98312 | tf_op jit(solution)/shard_map/ppermute | solution.py:39
  59.5 1.5 %collective-permute-done.8 = f32[4,2048]{1,0:T(4,128)S(1)} collective-permute-done((f32[4,2048]{1,0:T(4,128)S(1)}, f32[4,2048]{1,0:T(4,128)S(1)}, u32[]{:S(2)}, u32[]{:S(2)}) %collective-permute-start.8) | collective-permute-done | bytes 32800 | tf_op jit(solution)/shard_map/ppermute | solution.py:39
  61.0 0.7 %collective-permute-done.7 = f32[4,2048]{1,0:T(4,128)S(1)} collective-permute-done((f32[4,2048]{1,0:T(4,128)S(1)}, f32[4,2048]{1,0:T(4,128)S(1)}, u32[]{:S(2)}, u32[]{:S(2)}) %collective-permute-start.7) | collective-permute-done | bytes 32800 | tf_op jit(solution)/shard_map/ppermute | solution.py:39
  61.7 0.0 collective-permute-done.6
  61.7 0.6 %add_convert_fusion = bf16[4,2048]{1,0:T(4,128)(2,1)} fusion(f32[4,2048]{1,0:T(4,128)S(1)} %collective-permute-done.7, f32[4,2048]{1,0:T(4,128)S(1)} %collective-permute-done.8, f32[4,2048]{1,0:T(4,128)S(1)} %down.1, f32[4,2048]{1,0:T(4,128)S(1)} %collective-permute-done.6), kind=kLoop, calls=%fused_computation | loop fusion | flops 32768 | bytes 147456 | tf_op jit(solution)/shard_map/convert_element_type | solution.py:429
  (11 shorter events, 0.0 us)
Async XLA Ops:
  17.4 2.2 %copy-start = (bf16[1,8192,1,256]{3,1,2,0:T(8,128)(2,1)S(1)}, bf16[1,8192,1,256]{3,1,2,0:T(8,128)(2,1)}, u32[]{:S(2)}) copy-start(bf16[1,8192,1,256]{3,1,2,0:T(8,128)(2,1)} %param.18) | copy-start | bytes 12582916
  19.6 11.0 %copy-start.1 = (bf16[1024,2048]{1,0:T(8,128)(2,1)S(1)}, bf16[1024,2048]{1,0:T(8,128)(2,1)}, u32[]{:S(2)}) copy-start(bf16[1024,2048]{1,0:T(8,128)(2,1)} %w_out.1) | copy-start | bytes 12582916
  19.6 19.0 %copy-start.2 = (bf16[4,2048]{1,0:T(4,128)(2,1)S(1)}, bf16[4,2048]{1,0:T(4,128)(2,1)}, u32[]{:S(2)}) copy-start(bf16[4,2048]{1,0:T(4,128)(2,1)} %states.1) | copy-start | bytes 49156
  19.6 19.0 %copy-start.3 = (f32[2,2048]{1,0:T(2,128)S(1)}, f32[2,2048]{1,0:T(2,128)}, u32[]{:S(2)}) copy-start(f32[2,2048]{1,0:T(2,128)} %gains.1) | copy-start | bytes 49156
  24.6 5.4 %collective-permute-start.2 = (bf16[8,128]{1,0:T(8,128)(2,1)S(1)}, bf16[8,128]{1,0:T(8,128)(2,1)S(1)}, u32[]{:S(2)}, u32[]{:S(2)}) collective-permute-start(bf16[8,128]{1,0:T(8,128)(2,1)S(1)} %get-tuple-element.15.rest_0_), channel_id=1, source_target_pairs={{0,12},{4,8},{8,4},{12,0},{1,13},{5,9},{9,5},{13,1},{2,14},{6,10},... | collective-permute-start | bytes 6152 | tf_op jit(solution)/shard_map/ppermute | solution.py:39
  25.3 4.7 %collective-permute-start.1 = (bf16[8,128]{1,0:T(8,128)(2,1)S(1)}, bf16[8,128]{1,0:T(8,128)(2,1)S(1)}, u32[]{:S(2)}, u32[]{:S(2)}) collective-permute-start(bf16[8,128]{1,0:T(8,128)(2,1)S(1)} %get-tuple-element.15.rest_0_), channel_id=1, source_target_pairs={{0,8},{4,12},{8,0},{12,4},{1,9},{5,13},{9,1},{13,5},{2,10},{6,14},... | collective-permute-start | bytes 6152 | tf_op jit(solution)/shard_map/ppermute | solution.py:39
  26.9 3.7 %collective-permute-start = (bf16[8,128]{1,0:T(8,128)(2,1)S(1)}, bf16[8,128]{1,0:T(8,128)(2,1)S(1)}, u32[]{:S(2)}, u32[]{:S(2)}) collective-permute-start(bf16[8,128]{1,0:T(8,128)(2,1)S(1)} %get-tuple-element.15.rest_0_), channel_id=1, source_target_pairs={{0,4},{4,0},{8,12},{12,8},{1,5},{5,1},{9,13},{13,9},{2,6},{6,2},{1... | collective-permute-start | bytes 6152 | tf_op jit(solution)/shard_map/ppermute | solution.py:39
  30.6 24.1 %slice-start = ((s8[14680064]{0:T(1024)(128)(4,1)}), s8[4194304]{0:T(1024)(128)(4,1)S(1)}, s32[]{:S(2)}) async-start(s8[14680064]{0:T(1024)(128)(4,1)} %bitcast.4), calls=%async_computation.2 | async-start | bytes 8388608
  38.6 16.1 %slice-start.1 = ((s8[14680064]{0:T(1024)(128)(4,1)}), s8[4194304]{0:T(1024)(128)(4,1)S(1)}, s32[]{:S(2)}) async-start(s8[14680064]{0:T(1024)(128)(4,1)} %bitcast.4), calls=%async_computation.3 | async-start | bytes 8388608
  38.6 16.1 %slice-start.2 = ((s8[14680064]{0:T(1024)(128)(4,1)}), s8[4194304]{0:T(1024)(128)(4,1)S(1)}, s32[]{:S(2)}) async-start(s8[14680064]{0:T(1024)(128)(4,1)} %bitcast.4), calls=%async_computation.4 | async-start | bytes 8388608
  38.6 16.1 %slice-start.3 = ((s8[14680064]{0:T(1024)(128)(4,1)}), s8[2097152]{0:T(1024)(128)(4,1)S(1)}, s32[]{:S(2)}) async-start(s8[14680064]{0:T(1024)(128)(4,1)} %bitcast.4), calls=%async_computation.5 | async-start | bytes 4194304
  45.8 6.2 %collective-permute-start.5 = (bf16[8,3712]{1,0:T(8,128)(2,1)S(1)}, bf16[8,3712]{1,0:T(8,128)(2,1)S(1)}, u32[]{:S(2)}, u32[]{:S(2)}) collective-permute-start(bf16[8,3712]{1,0:T(8,128)(2,1)S(1)} %get-tuple-element.17.rest_0_), channel_id=1, source_target_pairs={{0,12},{4,8},{8,4},{12,0},{1,13},{5,9},{9,5},{13,1},{2,14},{6,10},... | collective-permute-start | bytes 178184 | tf_op jit(solution)/shard_map/ppermute | solution.py:39
  48.2 6.4 %collective-permute-start.4 = (bf16[8,3712]{1,0:T(8,128)(2,1)S(1)}, bf16[8,3712]{1,0:T(8,128)(2,1)S(1)}, u32[]{:S(2)}, u32[]{:S(2)}) collective-permute-start(bf16[8,3712]{1,0:T(8,128)(2,1)S(1)} %get-tuple-element.17.rest_0_), channel_id=1, source_target_pairs={{0,8},{4,12},{8,0},{12,4},{1,9},{5,13},{9,1},{13,5},{2,10},{6,14},... | collective-permute-start | bytes 178184 | tf_op jit(solution)/shard_map/ppermute | solution.py:39
  49.3 5.4 %collective-permute-start.3 = (bf16[8,3712]{1,0:T(8,128)(2,1)S(1)}, bf16[8,3712]{1,0:T(8,128)(2,1)S(1)}, u32[]{:S(2)}, u32[]{:S(2)}) collective-permute-start(bf16[8,3712]{1,0:T(8,128)(2,1)S(1)} %get-tuple-element.17.rest_0_), channel_id=1, source_target_pairs={{0,4},{4,0},{8,12},{12,8},{1,5},{5,1},{9,13},{13,9},{2,6},{6,2},{1... | collective-permute-start | bytes 178184 | tf_op jit(solution)/shard_map/ppermute | solution.py:39
  57.6 3.4 %collective-permute-start.8 = (f32[4,2048]{1,0:T(4,128)S(1)}, f32[4,2048]{1,0:T(4,128)S(1)}, u32[]{:S(2)}, u32[]{:S(2)}) collective-permute-start(f32[4,2048]{1,0:T(4,128)S(1)} %down.1), channel_id=1, source_target_pairs={{0,3},{1,2},{2,1},{3,0},{4,7},{5,6},{6,5},{7,4},{8,11},{9,10},{10,... | collective-permute-start | bytes 98312 | tf_op jit(solution)/shard_map/ppermute | solution.py:39
  57.6 4.1 %collective-permute-start.7 = (f32[4,2048]{1,0:T(4,128)S(1)}, f32[4,2048]{1,0:T(4,128)S(1)}, u32[]{:S(2)}, u32[]{:S(2)}) collective-permute-start(f32[4,2048]{1,0:T(4,128)S(1)} %down.1), channel_id=1, source_target_pairs={{0,2},{1,3},{2,0},{3,1},{4,6},{5,7},{6,4},{7,5},{8,10},{9,11},{10,... | collective-permute-start | bytes 98312 | tf_op jit(solution)/shard_map/ppermute | solution.py:39
  58.6 3.0 %collective-permute-start.6 = (f32[4,2048]{1,0:T(4,128)S(1)}, f32[4,2048]{1,0:T(4,128)S(1)}, u32[]{:S(2)}, u32[]{:S(2)}) collective-permute-start(f32[4,2048]{1,0:T(4,128)S(1)} %down.1), channel_id=1, source_target_pairs={{0,1},{1,0},{2,3},{3,2},{4,5},{5,4},{6,7},{7,6},{8,9},{9,8},{10,11... | collective-permute-start | bytes 98312 | tf_op jit(solution)/shard_map/ppermute | solution.py:39

commit v4 on v2

--- a/solution.py
+++ b/solution.py
@@ -15,6 +15,7 @@
 LANES = 128
 MIB = 1 << 20
 GU_BLOCK = 256
+DOWN_BLOCK = 512
 F32 = jnp.float32
 BF16 = jnp.bfloat16
 TURN_A = 6.28125
@@ -61,11 +62,14 @@
     row = lax.broadcasted_iota(jnp.int32, (4 * docs, 2 * LANES), 0)
     lane = lax.broadcasted_iota(jnp.int32, (4 * docs, 2 * LANES), 1)
     keep = lax.rem(lax.div(row, docs), 2) == lax.rem(lane, 2)
-    for c in range(width // LANES):
-        doubled = jnp.dot(
-            rows16[:, c * LANES : (c + 1) * LANES], pick, preferred_element_type=F32
-        )
-        out_ref[:, 2 * c * LANES : 2 * (c + 1) * LANES] = jnp.where(keep, doubled, 0.0).astype(BF16)
+    chunks = width // LANES
+    stacked = jnp.concatenate(
+        [rows16[:, c * LANES : (c + 1) * LANES] for c in range(chunks)], axis=0
+    )
+    doubled = jnp.dot(stacked, pick, preferred_element_type=F32)
+    for c in range(chunks):
+        piece = doubled[c * 4 * docs : (c + 1) * 4 * docs]
+        out_ref[:, 2 * c * LANES : 2 * (c + 1) * LANES] = jnp.where(keep, piece, 0.0).astype(BF16)
 
 
 def weight_copy(w_rows, block, buf, slot, sems):
@@ -175,11 +179,11 @@
         outs[s][h + 3 :, :] = jnp.zeros((outs[s].shape[0] - h - 3, LANES), F32)
 
 
-def attend_kernel(tp, heads, rows, table, cache, w, *rest):
+def attend_kernel(tp, heads, rows, first, table, cache, w, *rest):
     parts = rest[:tp]
-    heads_out, new_kv_out, w_ready, scores, w_sems = rest[tp:]
+    heads_out, new_kv_out, w_ready, scores, w_sems = rest[-5:]
     width, _, hidden = w.shape
-    w_copies = weight_copies(w.reshape(2 * width, hidden), 0, w_ready, w_sems)
+    w_copies = weight_copies(w.reshape(2 * width, hidden), first, w_ready, w_sems)
     for copy in w_copies:
         copy.start()
     blocks = cache.shape[0] // rows
@@ -224,13 +228,9 @@
         copy.wait()
 
 
-def out_kernel(tp, first, places, w_out, w, *rest):
+def out_kernel(tp, places, w_out, *rest):
     parts = rest[:tp]
-    out, w_ready, left, w_sems = rest[tp:]
-    width, _, hidden = w.shape
-    w_copies = weight_copies(w.reshape(2 * width, hidden), first, w_ready, w_sems)
-    for copy in w_copies:
-        copy.start()
+    out, left = rest[-2:]
     docs = out.shape[0]
     row = lax.broadcasted_iota(jnp.int32, (left.shape[0], LANES), 0)
     own = [parts[s][...].astype(F32) for s in range(tp)]
@@ -239,43 +239,44 @@
         for s in range(tp):
             piece = jnp.where(row == places[s : s + 1, :], own[s][h : h + 1, :], piece)
         left[:, h * LANES : (h + 1) * LANES] = piece
-    out[...] = jnp.dot(left[...].astype(BF16), w_out[...], preferred_element_type=F32)[:docs]
-    for copy in w_copies:
+    terms = jnp.dot(left[...].astype(BF16), w_out[...], preferred_element_type=F32)
+    out[...] = terms[:docs].astype(BF16)
+
+
+def fetch_kernel(first, token, w, out, sems):
+    if len(w.shape) == 3:
+        w = w.reshape(w.shape[0] * w.shape[1], w.shape[2])
+    copies = weight_copies(w, first, out, sems)
+    for copy in copies:
+        copy.start()
+    for copy in copies:
         copy.wait()
 
 
-def gate_up_kernel(kv, states, gains, w, ready_a, ready_b, *rest):
-    parts = rest[:kv]
-    attn_out, partial_out, w_buf, spread_buf, acc, sems = rest[kv:]
+def gate_up_kernel(kv, groups, states, gains, *rest):
+    blocks, parts = rest[:groups], rest[groups : groups + kv]
+    attn_out, partial_out, spread_buf, acc = rest[groups + kv :]
     docs, width = states.shape
-    hidden = w.shape[2]
-    rows = w_buf.shape[1]
-    first = ready_a.shape[0] + ready_b.shape[0]
-    w_rows = w.reshape(2 * width, hidden)
-    for copy in weight_copies(w_rows, first, w_buf, sems):
-        copy.start()
-    attn = tree_sum([part[...] for part in parts]).astype(BF16)
+    rows, hidden = blocks[0].shape[1:]
+    attn = tree_sum([part[...].astype(F32) for part in parts]).astype(BF16)
     attn_out[...] = attn
     resid = (states[...].astype(F32) + attn.astype(F32)).astype(BF16).astype(F32)
     squares = jnp.sum(resid * resid, axis=1, keepdims=True)
     spread(two_parts(resid * gains[1:2, :]), spread_buf, docs)
     acc[...] = jnp.zeros_like(acc)
 
-    def add_blocks(buf, first, wait):
-        def step(b, carry):
-            if wait:
-                weight_copy(w_rows, first + b, buf, b, sems).wait()
+    first = 0
+    for group in blocks:
+
+        def step(b, carry, group=group, first=first):
             start = pl.multiple_of((first + b) * rows, rows)
             acc[...] += jnp.dot(
-                spread_buf[:, pl.ds(start, rows)], buf[b], preferred_element_type=F32
+                spread_buf[:, pl.ds(start, rows)], group[b], preferred_element_type=F32
             )
             return carry
 
-        lax.fori_loop(0, buf.shape[0], step, 0)
-
-    add_blocks(ready_a, 0, False)
-    add_blocks(ready_b, ready_a.shape[0], False)
-    add_blocks(w_buf, first, True)
+        lax.fori_loop(0, group.shape[0], step, 0)
+        first += group.shape[0]
     partial_out[:, :hidden] = (acc[: 2 * docs] + acc[2 * docs :]).astype(BF16)
     lane = lax.broadcasted_iota(jnp.int32, (docs, LANES), 1)
     first = squares.astype(BF16).astype(F32)
@@ -287,28 +288,29 @@
 
 def down_kernel(tp, w_down, *rest):
     parts = rest[:tp]
-    out, act_buf = rest[tp:]
+    out, act_buf, acc = rest[tp:]
     docs = out.shape[0]
-    hidden = w_down.shape[0]
+    blocks, step_rows = w_down.shape[:2]
+    hidden = blocks * step_rows
     summed = tree_sum([part[...].astype(F32) for part in parts])
     squares = jnp.sum(summed[:docs, hidden:], axis=1, keepdims=True)
     inverse = lax.rsqrt(squares / D + EPS)
     gate = summed[:docs, :hidden] * inverse
     up = summed[docs:, :hidden] * inverse
     act_buf[...] = (gate / (1.0 + jnp.exp(-gate)) * up).astype(BF16)
-    step_rows = 512
-    out[...] = jnp.zeros_like(out)
+    acc[...] = jnp.zeros_like(acc)
 
     def step(b, carry):
         start = pl.multiple_of(b * step_rows, step_rows)
-        out[...] += jnp.dot(
+        acc[...] += jnp.dot(
             act_buf[:, pl.ds(start, step_rows)],
-            w_down[pl.ds(start, step_rows), :],
+            w_down[b],
             preferred_element_type=F32,
         )
         return carry
 
-    lax.fori_loop(0, hidden // step_rows, step, 0)
+    lax.fori_loop(0, blocks, step, 0)
+    out[...] = acc[...].astype(BF16)
 
 
 def cost(micros):
@@ -365,81 +367,97 @@
         cost_estimate=cost(8),
         name="qkv",
     )(*(in_hbm(a) for a in (owner_rows, lengths, freq, states, norm_gains, wq, wkv)))
-    qkv_parts = exchange(qkv_parts, "tp", tp)
-
     w_gu = in_hbm(w_gate_up)
     gu_blocks = 2 * width // GU_BLOCK
-    ready_a = max(gu_blocks * 5 // 16, 1)
-    ready_b = max(gu_blocks // 8, 1)
-    head_out, new_kv, w_ready_a = pl.pallas_call(
-        functools.partial(attend_kernel, tp, heads, 512),
+    bounds = sorted({gu_blocks * i // 16 for i in (0, 5, 8, 13, 16)})
+    shares = list(zip(bounds, bounds[1:]))
+    fetched = []
+
+    def blocks_of(share, rows=GU_BLOCK, columns=hidden):
+        return pltpu.VMEM((share[1] - share[0], rows, columns), BF16)
+
+    def fetch(weights, share, token, *block):
+        return pl.pallas_call(
+            functools.partial(fetch_kernel, share[0]),
+            out_shape=blocks_of(share, *block),
+            in_specs=[hbm(), hbm()],
+            out_specs=vmem(),
+            scratch_shapes=[pltpu.SemaphoreType.DMA((share[1] - share[0],))],
+            compiler_params=params(docs, 2),
+            cost_estimate=cost(0.5 * (share[1] - share[0])),
+            name="fetch",
+        )(token, weights)
+
+    if len(shares) == 4:
+        fetched.append(fetch(w_gu, shares[0], table))
+    qkv_parts = exchange(qkv_parts, "tp", tp)
+    own_share = shares[1] if len(shares) == 4 else shares[0]
+    head_out, new_kv, w_ready = pl.pallas_call(
+        functools.partial(attend_kernel, tp, heads, 512, own_share[0]),
         out_shape=[
             jax.ShapeDtypeStruct((heads, LANES), BF16),
             jax.ShapeDtypeStruct((1, 2 * LANES), BF16),
-            pltpu.VMEM((ready_a, GU_BLOCK, hidden), BF16),
-        ],
-        in_specs=[vmem(), vmem(), hbm()] + [vmem()] * tp,
+            blocks_of(own_share),
+        ],
+        in_specs=[vmem(), vmem(), hbm()] + [vmem()] * tp + [hbm()] * len(fetched),
         out_specs=[vmem()] * 3,
         scratch_shapes=[
             pltpu.VMEM((heads, cache_len), F32),
-            pltpu.SemaphoreType.DMA((ready_a,)),
+            pltpu.SemaphoreType.DMA((own_share[1] - own_share[0],)),
         ],
         compiler_params=params(docs, 6),
         cost_estimate=cost(8),
         name="attend",
-    )(table, cache, w_gu, *qkv_parts)
-
+    )(table, cache, w_gu, *qkv_parts, *fetched)
+    fetched.append(w_ready)
+
+    if len(shares) == 4:
+        fetched.append(fetch(w_gu, shares[2], head_out))
     head_parts = exchange([head_out] * tp, "tp", tp)
-    out_part, w_ready_b = pl.pallas_call(
-        functools.partial(out_kernel, tp, ready_a),
-        out_shape=[
-            jax.ShapeDtypeStruct((docs, width), F32),
-            pltpu.VMEM((ready_b, GU_BLOCK, hidden), BF16),
-        ],
-        in_specs=[vmem(), vmem(), hbm()] + [vmem()] * tp,
-        out_specs=[vmem()] * 2,
-        scratch_shapes=[
-            pltpu.VMEM((max(docs, 8), heads * LANES), F32),
-            pltpu.SemaphoreType.DMA((ready_b,)),
-        ],
+    out_part = pl.pallas_call(
+        functools.partial(out_kernel, tp),
+        out_shape=jax.ShapeDtypeStruct((docs, width), BF16),
+        in_specs=[vmem()] * (tp + 2) + [hbm()],
+        out_specs=vmem(),
+        scratch_shapes=[pltpu.VMEM((max(docs, 8), heads * LANES), F32)],
         compiler_params=params(docs, 6),
         cost_estimate=cost(6),
         name="attn_project",
-    )(places, w_out, w_gu, *head_parts)
-
+    )(places, w_out, *head_parts, fetched[-1])
+
+    fetched.append(fetch(w_gu, shares[-1], out_part))
     out_parts = exchange([out_part] * kv, "kv", kv)
-    gu_rest = gu_blocks - ready_a - ready_b
     attn_out, gu_part = pl.pallas_call(
-        functools.partial(gate_up_kernel, kv),
+        functools.partial(gate_up_kernel, kv, len(fetched)),
         out_shape=[
             jax.ShapeDtypeStruct((docs, width), BF16),
             jax.ShapeDtypeStruct((2 * docs, hidden + LANES), BF16),
         ],
-        in_specs=[vmem(), vmem(), hbm(), vmem(), vmem()] + [vmem()] * kv,
+        in_specs=[vmem()] * (2 + len(fetched) + kv),
         out_specs=[vmem(), vmem()],
         scratch_shapes=[
-            pltpu.VMEM((gu_rest, GU_BLOCK, hidden), BF16),
             pltpu.VMEM((4 * docs, 2 * width), BF16),
             pltpu.VMEM((4 * docs, hidden), F32),
-            pltpu.SemaphoreType.DMA((gu_rest,)),
-        ],
-        compiler_params=params(docs, 18),
-        cost_estimate=cost(8),
+        ],
+        compiler_params=params(docs, 6),
+        cost_estimate=cost(10),
         name="gate_up",
-    )(states, norm_gains, w_gu, w_ready_a, w_ready_b, *out_parts)
-
+    )(states, norm_gains, *fetched, *out_parts)
+
+    w_down_ready = fetch(in_hbm(w_down), (0, hidden // DOWN_BLOCK), gu_part, DOWN_BLOCK, width)
     gu_parts = exchange([gu_part] * tp, "tp", tp)
     ffn_part = pl.pallas_call(
         functools.partial(down_kernel, tp),
-        out_shape=jax.ShapeDtypeStruct((docs, width), F32),
+        out_shape=jax.ShapeDtypeStruct((docs, width), BF16),
         in_specs=[vmem()] + [vmem()] * tp,
         out_specs=vmem(),
-        scratch_shapes=[pltpu.VMEM((docs, hidden), BF16)],
+        scratch_shapes=[pltpu.VMEM((docs, hidden), BF16), pltpu.VMEM((docs, width), F32)],
         compiler_params=params(docs, 6),
         cost_estimate=cost(5),
         name="down",
-    )(w_down, *gu_parts)
-    ffn_out = tree_sum(exchange([ffn_part] * kv, "kv", kv)).astype(BF16)
+    )(w_down_ready, *gu_parts)
+    ffn_parts = exchange([ffn_part] * kv, "kv", kv)
+    ffn_out = tree_sum([part.astype(F32) for part in ffn_parts]).astype(BF16)
     return attn_out, ffn_out, new_kv.reshape(1, 1, 2 * LANES)
 
 

time: 58 us -> 57 us (0.983)
  waiting for transfers between devices: 16.8 us -> 3.72 us
  Pallas kernels: 21.2 us -> 33.4 us
    ppermute x15, waiting for transfers between devices: 16.8 us -> 3.72 us  [exchange(): lax.ppermute(arrays[s], axis, [(i, i ^ s) for i in range(size)])]
    pallas_call x3 -> x7, Pallas kernels: 13.1 us -> 25.5 us  [the longest x4 15.5 us: fetch(): pl.pallas_call(functools.partial(fetch_kernel, share[0]), out_shape=block...]
  transfers between devices with their start and end apart: 15 -> 15, of which waited for: 10 -> 3; matrix products, arithmetic and copies ran while one was open for 0% -> 0% of each run, Pallas kernels for 0% -> 27%
where the time goes in v4:
time: 57 us; the launch traced here: 56.9 us
  Pallas kernels  33.4 us (59%)
  starting transfers between devices  18.3 us (32%)
  waiting for transfers between devices  3.72 us (7%)
  between operations  0.82 us (1%)
  other arithmetic  0.63 us (1%)
    ppermute x15, starting transfers between devices, exchange(): lax.ppermute(arrays[s], axis, [(i, i ^ s) for i in range(size)])  18.3 us
    pallas_call x4, Pallas kernels, fetch(): pl.pallas_call(functools.partial(fetch_kernel, share[0]), out_shape=block...  15.5 us
    pallas_call x1, Pallas kernels, per_device(): pl.pallas_call(functools.partial(gate_up_kernel, kv, len(fetched)), out_s...  6.16 us
    pallas_call x1, Pallas kernels, per_device(): pl.pallas_call(functools.partial(qkv_kernel, tp), out_shape=[jax.ShapeDty...  5 us
    ppermute x15, waiting for transfers between devices, exchange(): lax.ppermute(arrays[s], axis, [(i, i ^ s) for i in range(size)])  3.72 us
    pallas_call x1, Pallas kernels, per_device(): pl.pallas_call(functools.partial(attend_kernel, tp, heads, 512, own_share...  3.2 us
    pallas_call x1, Pallas kernels, per_device(): pl.pallas_call(functools.partial(down_kernel, tp), out_shape=jax.ShapeDty...  2.91 us
  transfers between devices with their start and end apart: 15, of which 3 were waited for; matrix products, arithmetic and copies ran while one was open for 0% of the time, Pallas kernels for 27%

profile of v4, /device:TPU:0, one launch (start us, length us, event | category | flops | bytes accessed | tf_op | source)
XLA Modules:
  0.0 56.9 jit_solution(11593396820678306657)
XLA Ops:
  0.6 5.0 %qkv.1 = (f32[16,128]{1,0:T(8,128)S(1)}, f32[16,128]{1,0:T(8,128)S(1)}, f32[16,128]{1,0:T(8,128)S(1)}, f32[16,128]{1,0:T(8,128)S(1)}, f32[8,128]{1,0:T(8,128)S(1)}, /*index=5*/s32[8,128]{1,0:T(8,128)S(1)}) custom-call(s32[4]{0:T(128)} %owner_hbm.1, s32[4]{0:T(128)} %lengths_hbm.1, f32[1,128]{1,0:T(1,128)} %constant.2.clone.frequency_hbm, ...), custom_call_target="tpu_custom_call" | custom-call | bytes 29520000 | tf_op jit(solution)/shard_map/qkv/pallas_call | solution.py:342
  5.6 3.1 %collective-permute-start = (f32[16,128]{1,0:T(8,128)S(1)}, f32[16,128]{1,0:T(8,128)S(1)}, u32[]{:S(2)}, u32[]{:S(2)}) collective-permute-start(f32[16,128]{1,0:T(8,128)S(1)} %get-tuple-element.16), channel_id=1, source_target_pairs={{0,4},{4,0},{8,12},{12,8},{1,5},{5,1},{9,13},{13,9},{2,6},{6,2},{1... | collective-permute-start | bytes 24584 | tf_op jit(solution)/shard_map/ppermute | solution.py:40
  8.7 2.6 %collective-permute-start.1 = (f32[16,128]{1,0:T(8,128)S(1)}, f32[16,128]{1,0:T(8,128)S(1)}, u32[]{:S(2)}, u32[]{:S(2)}) collective-permute-start(f32[16,128]{1,0:T(8,128)S(1)} %get-tuple-element.17), channel_id=1, source_target_pairs={{0,8},{4,12},{8,0},{12,4},{1,9},{5,13},{9,1},{13,5},{2,10},{6,14},... | collective-permute-start | bytes 24584 | tf_op jit(solution)/shard_map/ppermute | solution.py:40
  11.3 0.0 collective-permute-start.2
  11.3 3.9 %fetch.4.rest_4_.rest_0_ = bf16[5,256,3584]{2,1,0:T(8,128)(2,1)S(1)} custom-call(f32[8,128]{1,0:T(8,128)S(1)} %get-tuple-element.14.token.table, bf16[2048,2,3584]{2,1,0:T(2,128)(2,1)} %w.8), custom_call_target="tpu_custom_call" | custom-call | bytes 9225000 | tf_op jit(solution)/shard_map/fetch/pallas_call | solution.py:380
  15.2 0.0 collective-permute-done.rest_1_
  15.2 0.0 collective-permute-done.1.rest_2_
  15.2 1.6 %collective-permute-done.2.rest_3_ = f32[16,128]{1,0:T(8,128)S(1)} collective-permute-done((f32[16,128]{1,0:T(8,128)S(1)}, f32[16,128]{1,0:T(8,128)S(1)}, u32[]{:S(2)}, u32[]{:S(2)}) %collective-permute-start.2) | collective-permute-done | bytes 8224 | tf_op jit(solution)/shard_map/ppermute | solution.py:40
  16.8 3.2 %attend.1 = (bf16[8,128]{1,0:T(8,128)(2,1)S(1)}, bf16[1,256]{1,0:T(2,128)(2,1)}, bf16[3,256,3584]{2,1,0:T(8,128)(2,1)S(1)}) custom-call(f32[8,128]{1,0:T(8,128)S(1)} %get-tuple-element.14.token.table, bf16[8192,256]{1,0:T(8,128)(2,1)S(1)} %bitcast.4, bf16[2048,2,3584]{2,1,0:T(2,128)(2,1)} %w.8, f32[16,128]{1,0:T(8,128)S(1)} %get-tuple-element.15.rest_0_, ...), custom_call_target="tpu_custom_call" | custom-call | bytes 29520000 | tf_op jit(solution)/shard_map/attend/pallas_call | solution.py:395
  20.0 0.0 copy-start.1
  20.0 3.3 %collective-permute-start.5 = (bf16[8,128]{1,0:T(8,128)(2,1)S(1)}, bf16[8,128]{1,0:T(8,128)(2,1)S(1)}, u32[]{:S(2)}, u32[]{:S(2)}) collective-permute-start(bf16[8,128]{1,0:T(8,128)(2,1)S(1)} %get-tuple-element.20.token.rest_0_), channel_id=1, source_target_pairs={{0,12},{4,8},{8,4},{12,0},{1,13},{5,9},{9,5},{13,1},{2,14},{6,10},... | collective-permute-start | bytes 6152 | tf_op jit(solution)/shard_map/ppermute | solution.py:40
  23.3 0.0 collective-permute-start.4
  23.3 1.1 %collective-permute-start.3 = (bf16[8,128]{1,0:T(8,128)(2,1)S(1)}, bf16[8,128]{1,0:T(8,128)(2,1)S(1)}, u32[]{:S(2)}, u32[]{:S(2)}) collective-permute-start(bf16[8,128]{1,0:T(8,128)(2,1)S(1)} %get-tuple-element.20.token.rest_0_), channel_id=1, source_target_pairs={{0,4},{4,0},{8,12},{12,8},{1,5},{5,1},{9,13},{13,9},{2,6},{6,2},{1... | collective-permute-start | bytes 6152 | tf_op jit(solution)/shard_map/ppermute | solution.py:40
  24.4 3.7 %fetch.5.rest_4_.rest_2_ = bf16[5,256,3584]{2,1,0:T(8,128)(2,1)S(1)} custom-call(bf16[8,128]{1,0:T(8,128)(2,1)S(1)} %get-tuple-element.20.token.rest_0_, bf16[2048,2,3584]{2,1,0:T(2,128)(2,1)} %w.8), custom_call_target="tpu_custom_call" | custom-call | bytes 9225000 | tf_op jit(solution)/shard_map/fetch/pallas_call | solution.py:380
  28.2 0.0 collective-permute-done.3.rest_1_
  28.2 0.7 %attn_project.1.token.rest_4_ = bf16[4,2048]{1,0:T(4,128)(2,1)S(1)} custom-call(s32[8,128]{1,0:T(8,128)S(1)} %get-tuple-element.21.places, bf16[1024,2048]{1,0:T(8,128)(2,1)S(1)} %copy-done.1, bf16[8,128]{1,0:T(8,128)(2,1)S(1)} %get-tuple-element.20.token.rest_0_, bf16[8,128]{1,0:T(8,128)(2,1)S(1)} %collective-permute-done.3.rest_1_, ...), custom_call_target="tpu_custom_call" | custom-call | bytes 22140000 | tf_op jit(solution)/shard_map/attn_project/pallas_call | solution.py:417
  28.9 0.0 collective-permute-start.8
  28.9 1.6 %collective-permute-start.7 = (bf16[4,2048]{1,0:T(4,128)(2,1)S(1)}, bf16[4,2048]{1,0:T(4,128)(2,1)S(1)}, u32[]{:S(2)}, u32[]{:S(2)}) collective-permute-start(bf16[4,2048]{1,0:T(4,128)(2,1)S(1)} %attn_project.1.token.rest_4_), channel_id=1, source_target_pairs={{0,2},{1,3},{2,0},{3,1},{4,6},{5,7},{6,4},{7,5},{8,10},{9,11},{10,... | collective-permute-start | bytes 49160 | tf_op jit(solution)/shard_map/ppermute | solution.py:40
  30.4 0.3 collective-permute-start.6
  30.7 2.6 %fetch.6.rest_3_ = bf16[3,256,3584]{2,1,0:T(8,128)(2,1)S(1)} custom-call(bf16[4,2048]{1,0:T(4,128)(2,1)S(1)} %attn_project.1.token.rest_4_, bf16[2048,2,3584]{2,1,0:T(2,128)(2,1)} %w.8), custom_call_target="tpu_custom_call" | custom-call | bytes 5535000 | tf_op jit(solution)/shard_map/fetch/pallas_call | solution.py:380
  33.4 0.0 collective-permute-done.8.rest_7_
  33.4 6.2 %gate_up.1 = (bf16[4,2048]{1,0:T(4,128)(2,1)}, bf16[8,3712]{1,0:T(8,128)(2,1)S(1)}) custom-call(bf16[4,2048]{1,0:T(4,128)(2,1)S(1)} %copy-done.2, f32[2,2048]{1,0:T(2,128)S(1)} %copy-done.3, bf16[5,256,3584]{2,1,0:T(8,128)(2,1)S(1)} %fetch.4.rest_4_.rest_0_, bf16[3,256,3584]{2,1,0:T(8,128)(2,1)S(1)} %get-tuple-element.19.rest_1_, ...), custom_call_target="tpu_custom_call" | custom-call | bytes 36900000 | tf_op jit(solution)/shard_map/gate_up/pallas_call | solution.py:430
  39.6 3.3 %collective-permute-start.11 = (bf16[8,3712]{1,0:T(8,128)(2,1)S(1)}, bf16[8,3712]{1,0:T(8,128)(2,1)S(1)}, u32[]{:S(2)}, u32[]{:S(2)}) collective-permute-start(bf16[8,3712]{1,0:T(8,128)(2,1)S(1)} %get-tuple-element.23.token.rest_0_), channel_id=1, source_target_pairs={{0,12},{4,8},{8,4},{12,0},{1,13},{5,9},{9,5},{13,1},{2,14},{6,10},... | collective-permute-start | bytes 178184 | tf_op jit(solution)/shard_map/ppermute | solution.py:40
  42.8 1.1 %collective-permute-start.9 = (bf16[8,3712]{1,0:T(8,128)(2,1)S(1)}, bf16[8,3712]{1,0:T(8,128)(2,1)S(1)}, u32[]{:S(2)}, u32[]{:S(2)}) collective-permute-start(bf16[8,3712]{1,0:T(8,128)(2,1)S(1)} %get-tuple-element.23.token.rest_0_), channel_id=1, source_target_pairs={{0,4},{4,0},{8,12},{12,8},{1,5},{5,1},{9,13},{13,9},{2,6},{6,2},{1... | collective-permute-start | bytes 178184 | tf_op jit(solution)/shard_map/ppermute | solution.py:40
  44.0 5.3 %fetch.7.w_down = bf16[7,512,2048]{2,1,0:T(8,128)(2,1)S(1)} custom-call(bf16[8,3712]{1,0:T(8,128)(2,1)S(1)} %get-tuple-element.23.token.rest_0_, bf16[3584,2048]{1,0:T(8,128)(2,1)} %w.9), custom_call_target="tpu_custom_call" | custom-call | bytes 12915000 | tf_op jit(solution)/shard_map/fetch/pallas_call | solution.py:380
  49.3 2.9 %down.1 = bf16[4,2048]{1,0:T(4,128)(2,1)S(1)} custom-call(bf16[7,512,2048]{2,1,0:T(8,128)(2,1)S(1)} %fetch.7.w_down, bf16[8,3712]{1,0:T(8,128)(2,1)S(1)} %get-tuple-element.23.token.rest_0_, bf16[8,3712]{1,0:T(8,128)(2,1)S(1)} %collective-permute-done.9.rest_1_, bf16[8,3712]{1,0:T(8,128)(2,1)S(1)} %collective-permute-done.10.rest_2_, ...), custom_call_target="tpu_custom_call" | custom-call | bytes 18450000 | tf_op jit(solution)/shard_map/down/pallas_call | solution.py:449
  52.2 0.3 collective-permute-start.14
  52.5 1.3 %collective-permute-start.13 = (bf16[4,2048]{1,0:T(4,128)(2,1)S(1)}, bf16[4,2048]{1,0:T(4,128)(2,1)S(1)}, u32[]{:S(2)}, u32[]{:S(2)}) collective-permute-start(bf16[4,2048]{1,0:T(4,128)(2,1)S(1)} %down.1), channel_id=1, source_target_pairs={{0,2},{1,3},{2,0},{3,1},{4,6},{5,7},{6,4},{7,5},{8,10},{9,11},{10,... | collective-permute-start | bytes 49160 | tf_op jit(solution)/shard_map/ppermute | solution.py:40
  53.8 0.3 collective-permute-start.12
  54.1 1.4 %collective-permute-done.14 = bf16[4,2048]{1,0:T(4,128)(2,1)S(1)} collective-permute-done((bf16[4,2048]{1,0:T(4,128)(2,1)S(1)}, bf16[4,2048]{1,0:T(4,128)(2,1)S(1)}, u32[]{:S(2)}, u32[]{:S(2)}) %collective-permute-start.14) | collective-permute-done | bytes 16416 | tf_op jit(solution)/shard_map/ppermute | solution.py:40
  55.5 0.7 %collective-permute-done.13 = bf16[4,2048]{1,0:T(4,128)(2,1)S(1)} collective-permute-done((bf16[4,2048]{1,0:T(4,128)(2,1)S(1)}, bf16[4,2048]{1,0:T(4,128)(2,1)S(1)}, u32[]{:S(2)}, u32[]{:S(2)}) %collective-permute-start.13) | collective-permute-done | bytes 16416 | tf_op jit(solution)/shard_map/ppermute | solution.py:40
  56.3 0.6 %add_convert_fusion = bf16[4,2048]{1,0:T(4,128)(2,1)} fusion(bf16[4,2048]{1,0:T(4,128)(2,1)S(1)} %collective-permute-done.14, bf16[4,2048]{1,0:T(4,128)(2,1)S(1)} %collective-permute-done.13, bf16[4,2048]{1,0:T(4,128)(2,1)S(1)} %collective-permute-done.12, bf16[4,2048]{1,0:T(4,128)(2,1)S(1)} %down.1), kind=kLoop, calls=%fused_computation | loop fusion | flops 65536 | bytes 81920 | tf_op jit(solution)/shard_map/convert_element_type | solution.py:460
  (16 shorter events, 0.0 us)
Async XLA Ops:
  5.6 9.6 %collective-permute-start = (f32[16,128]{1,0:T(8,128)S(1)}, f32[16,128]{1,0:T(8,128)S(1)}, u32[]{:S(2)}, u32[]{:S(2)}) collective-permute-start(f32[16,128]{1,0:T(8,128)S(1)} %get-tuple-element.16), channel_id=1, source_target_pairs={{0,4},{4,0},{8,12},{12,8},{1,5},{5,1},{9,13},{13,9},{2,6},{6,2},{1... | collective-permute-start | bytes 24584 | tf_op jit(solution)/shard_map/ppermute | solution.py:40
  8.7 6.5 %collective-permute-start.1 = (f32[16,128]{1,0:T(8,128)S(1)}, f32[16,128]{1,0:T(8,128)S(1)}, u32[]{:S(2)}, u32[]{:S(2)}) collective-permute-start(f32[16,128]{1,0:T(8,128)S(1)} %get-tuple-element.17), channel_id=1, source_target_pairs={{0,8},{4,12},{8,0},{12,4},{1,9},{5,13},{9,1},{13,5},{2,10},{6,14},... | collective-permute-start | bytes 24584 | tf_op jit(solution)/shard_map/ppermute | solution.py:40
  11.3 5.4 %collective-permute-start.2 = (f32[16,128]{1,0:T(8,128)S(1)}, f32[16,128]{1,0:T(8,128)S(1)}, u32[]{:S(2)}, u32[]{:S(2)}) collective-permute-start(f32[16,128]{1,0:T(8,128)S(1)} %get-tuple-element.18), channel_id=1, source_target_pairs={{0,12},{4,8},{8,4},{12,0},{1,13},{5,9},{9,5},{13,1},{2,14},{6,10},... | collective-permute-start | bytes 24584 | tf_op jit(solution)/shard_map/ppermute | solution.py:40
  11.3 5.4 %copy-start = (bf16[1,8192,1,256]{3,1,2,0:T(8,128)(2,1)S(1)}, bf16[1,8192,1,256]{3,1,2,0:T(8,128)(2,1)}, u32[]{:S(2)}) copy-start(bf16[1,8192,1,256]{3,1,2,0:T(8,128)(2,1)} %param.18) | copy-start | bytes 12582916
  20.0 8.2 %copy-start.1 = (bf16[1024,2048]{1,0:T(8,128)(2,1)S(1)}, bf16[1024,2048]{1,0:T(8,128)(2,1)}, u32[]{:S(2)}) copy-start(bf16[1024,2048]{1,0:T(8,128)(2,1)} %w_out.1) | copy-start | bytes 12582916
  20.0 8.2 %collective-permute-start.5 = (bf16[8,128]{1,0:T(8,128)(2,1)S(1)}, bf16[8,128]{1,0:T(8,128)(2,1)S(1)}, u32[]{:S(2)}, u32[]{:S(2)}) collective-permute-start(bf16[8,128]{1,0:T(8,128)(2,1)S(1)} %get-tuple-element.20.token.rest_0_), channel_id=1, source_target_pairs={{0,12},{4,8},{8,4},{12,0},{1,13},{5,9},{9,5},{13,1},{2,14},{6,10},... | collective-permute-start | bytes 6152 | tf_op jit(solution)/shard_map/ppermute | solution.py:40
  23.3 4.9 %collective-permute-start.4 = (bf16[8,128]{1,0:T(8,128)(2,1)S(1)}, bf16[8,128]{1,0:T(8,128)(2,1)S(1)}, u32[]{:S(2)}, u32[]{:S(2)}) collective-permute-start(bf16[8,128]{1,0:T(8,128)(2,1)S(1)} %get-tuple-element.20.token.rest_0_), channel_id=1, source_target_pairs={{0,8},{4,12},{8,0},{12,4},{1,9},{5,13},{9,1},{13,5},{2,10},{6,14},... | collective-permute-start | bytes 6152 | tf_op jit(solution)/shard_map/ppermute | solution.py:40
  23.3 4.9 %collective-permute-start.3 = (bf16[8,128]{1,0:T(8,128)(2,1)S(1)}, bf16[8,128]{1,0:T(8,128)(2,1)S(1)}, u32[]{:S(2)}, u32[]{:S(2)}) collective-permute-start(bf16[8,128]{1,0:T(8,128)(2,1)S(1)} %get-tuple-element.20.token.rest_0_), channel_id=1, source_target_pairs={{0,4},{4,0},{8,12},{12,8},{1,5},{5,1},{9,13},{13,9},{2,6},{6,2},{1... | collective-permute-start | bytes 6152 | tf_op jit(solution)/shard_map/ppermute | solution.py:40
  28.9 4.6 %copy-start.2 = (bf16[4,2048]{1,0:T(4,128)(2,1)S(1)}, bf16[4,2048]{1,0:T(4,128)(2,1)}, u32[]{:S(2)}) copy-start(bf16[4,2048]{1,0:T(4,128)(2,1)} %states.1) | copy-start | bytes 49156
  28.9 4.6 %copy-start.3 = (f32[2,2048]{1,0:T(2,128)S(1)}, f32[2,2048]{1,0:T(2,128)}, u32[]{:S(2)}) copy-start(f32[2,2048]{1,0:T(2,128)} %gains.1) | copy-start | bytes 49156
  28.9 4.5 %collective-permute-start.8 = (bf16[4,2048]{1,0:T(4,128)(2,1)S(1)}, bf16[4,2048]{1,0:T(4,128)(2,1)S(1)}, u32[]{:S(2)}, u32[]{:S(2)}) collective-permute-start(bf16[4,2048]{1,0:T(4,128)(2,1)S(1)} %attn_project.1.token.rest_4_), channel_id=1, source_target_pairs={{0,3},{1,2},{2,1},{3,0},{4,7},{5,6},{6,5},{7,4},{8,11},{9,10},{10,... | collective-permute-start | bytes 49160 | tf_op jit(solution)/shard_map/ppermute | solution.py:40
  28.9 4.5 %collective-permute-start.7 = (bf16[4,2048]{1,0:T(4,128)(2,1)S(1)}, bf16[4,2048]{1,0:T(4,128)(2,1)S(1)}, u32[]{:S(2)}, u32[]{:S(2)}) collective-permute-start(bf16[4,2048]{1,0:T(4,128)(2,1)S(1)} %attn_project.1.token.rest_4_), channel_id=1, source_target_pairs={{0,2},{1,3},{2,0},{3,1},{4,6},{5,7},{6,4},{7,5},{8,10},{9,11},{10,... | collective-permute-start | bytes 49160 | tf_op jit(solution)/shard_map/ppermute | solution.py:40
  30.4 3.0 %collective-permute-start.6 = (bf16[4,2048]{1,0:T(4,128)(2,1)S(1)}, bf16[4,2048]{1,0:T(4,128)(2,1)S(1)}, u32[]{:S(2)}, u32[]{:S(2)}) collective-permute-start(bf16[4,2048]{1,0:T(4,128)(2,1)S(1)} %attn_project.1.token.rest_4_), channel_id=1, source_target_pairs={{0,1},{1,0},{2,3},{3,2},{4,5},{5,4},{6,7},{7,6},{8,9},{9,8},{10,11... | collective-permute-start | bytes 49160 | tf_op jit(solution)/shard_map/ppermute | solution.py:40
  39.6 9.7 %collective-permute-start.11 = (bf16[8,3712]{1,0:T(8,128)(2,1)S(1)}, bf16[8,3712]{1,0:T(8,128)(2,1)S(1)}, u32[]{:S(2)}, u32[]{:S(2)}) collective-permute-start(bf16[8,3712]{1,0:T(8,128)(2,1)S(1)} %get-tuple-element.23.token.rest_0_), channel_id=1, source_target_pairs={{0,12},{4,8},{8,4},{12,0},{1,13},{5,9},{9,5},{13,1},{2,14},{6,10},... | collective-permute-start | bytes 178184 | tf_op jit(solution)/shard_map/ppermute | solution.py:40
  42.8 6.5 %collective-permute-start.10 = (bf16[8,3712]{1,0:T(8,128)(2,1)S(1)}, bf16[8,3712]{1,0:T(8,128)(2,1)S(1)}, u32[]{:S(2)}, u32[]{:S(2)}) collective-permute-start(bf16[8,3712]{1,0:T(8,128)(2,1)S(1)} %get-tuple-element.23.token.rest_0_), channel_id=1, source_target_pairs={{0,8},{4,12},{8,0},{12,4},{1,9},{5,13},{9,1},{13,5},{2,10},{6,14},... | collective-permute-start | bytes 178184 | tf_op jit(solution)/shard_map/ppermute | solution.py:40
  42.8 6.5 %collective-permute-start.9 = (bf16[8,3712]{1,0:T(8,128)(2,1)S(1)}, bf16[8,3712]{1,0:T(8,128)(2,1)S(1)}, u32[]{:S(2)}, u32[]{:S(2)}) collective-permute-start(bf16[8,3712]{1,0:T(8,128)(2,1)S(1)} %get-tuple-element.23.token.rest_0_), channel_id=1, source_target_pairs={{0,4},{4,0},{8,12},{12,8},{1,5},{5,1},{9,13},{13,9},{2,6},{6,2},{1... | collective-permute-start | bytes 178184 | tf_op jit(solution)/shard_map/ppermute | solution.py:40
  52.2 3.3 %collective-permute-start.14 = (bf16[4,2048]{1,0:T(4,128)(2,1)S(1)}, bf16[4,2048]{1,0:T(4,128)(2,1)S(1)}, u32[]{:S(2)}, u32[]{:S(2)}) collective-permute-start(bf16[4,2048]{1,0:T(4,128)(2,1)S(1)} %down.1), channel_id=1, source_target_pairs={{0,3},{1,2},{2,1},{3,0},{4,7},{5,6},{6,5},{7,4},{8,11},{9,10},{10,... | collective-permute-start | bytes 49160 | tf_op jit(solution)/shard_map/ppermute | solution.py:40
  52.5 3.7 %collective-permute-start.13 = (bf16[4,2048]{1,0:T(4,128)(2,1)S(1)}, bf16[4,2048]{1,0:T(4,128)(2,1)S(1)}, u32[]{:S(2)}, u32[]{:S(2)}) collective-permute-start(bf16[4,2048]{1,0:T(4,128)(2,1)S(1)} %down.1), channel_id=1, source_target_pairs={{0,2},{1,3},{2,0},{3,1},{4,6},{5,7},{6,4},{7,5},{8,10},{9,11},{10,... | collective-permute-start | bytes 49160 | tf_op jit(solution)/shard_map/ppermute | solution.py:40
  53.8 2.4 %collective-permute-start.12 = (bf16[4,2048]{1,0:T(4,128)(2,1)S(1)}, bf16[4,2048]{1,0:T(4,128)(2,1)S(1)}, u32[]{:S(2)}, u32[]{:S(2)}) collective-permute-start(bf16[4,2048]{1,0:T(4,128)(2,1)S(1)} %down.1), channel_id=1, source_target_pairs={{0,1},{1,0},{2,3},{3,2},{4,5},{5,4},{6,7},{7,6},{8,9},{9,8},{10,11... | collective-permute-start | bytes 49160 | tf_op jit(solution)/shard_map/ppermute | solution.py:40

commit v5 on v4

--- a/solution.py
+++ b/solution.py
@@ -14,8 +14,7 @@
 ROPE_BASE = 500000.0
 LANES = 128
 MIB = 1 << 20
-GU_BLOCK = 256
-DOWN_BLOCK = 512
+GU_SHARES = (4, 6, 4, 2, 12)
 F32 = jnp.float32
 BF16 = jnp.bfloat16
 TURN_A = 6.28125
@@ -72,15 +71,29 @@
         out_ref[:, 2 * c * LANES : 2 * (c + 1) * LANES] = jnp.where(keep, piece, 0.0).astype(BF16)
 
 
-def weight_copy(w_rows, block, buf, slot, sems):
-    rows = buf.shape[1]
-    return pltpu.make_async_copy(
-        w_rows.at[pl.ds(block * rows, rows)], buf.at[slot], sems.at[slot]
-    )
-
-
-def weight_copies(w_rows, first, buf, sems):
-    return [weight_copy(w_rows, first + b, buf, b, sems) for b in range(buf.shape[0])]
+def tile_copies(matrix, first, buf, sems):
+    return [
+        pltpu.make_async_copy(
+            matrix.at[:, pl.ds((first + i) * LANES, LANES)], buf.at[i], sems.at[i]
+        )
+        for i in range(buf.shape[0])
+    ]
+
+
+def matrix_of(w):
+    return w if len(w.shape) == 2 else w.reshape(w.shape[0] * w.shape[1], w.shape[2])
+
+
+def times_tiles(left, tiles, store, tile_ready=None):
+    def step(j, carry):
+        if tile_ready is not None:
+            tile_ready(2 * j)
+            tile_ready(2 * j + 1)
+        pair = jnp.concatenate([tiles[2 * j], tiles[2 * j + 1]], axis=1)
+        store(j, jnp.dot(left[...], pair, preferred_element_type=F32))
+        return carry
+
+    lax.fori_loop(0, tiles.shape[0] // 2, step, 0)
 
 
 def pick_row(ref, index):
@@ -97,11 +110,14 @@
     return jnp.cos(angle), jnp.where(lane < LANES // 2, -sine, sine)
 
 
-def qkv_kernel(tp, owner_hbm, lengths_hbm, frequency_hbm, states_hbm, gains_hbm, wq, wkv, *rest):
+def qkv_kernel(
+    tp, owner_hbm, lengths_hbm, frequency_hbm, states_hbm, gains_hbm, wq, wkv, cache, *rest
+):
     outs = rest[:tp]
-    table, places = rest[tp : tp + 2]
-    owner, lengths, frequency, states, gains = rest[tp + 2 : tp + 7]
-    wq_buf, wkv_buf, spread_buf, res, kv_res, sq_res, sems, small_sems = rest[tp + 7 :]
+    table, places, cache_tiles = rest[tp : tp + 3]
+    owner, lengths, frequency, states, gains = rest[tp + 3 : tp + 8]
+    wq_buf, wkv_buf, spread_buf, res, kv_res, sq_res, sems, small_sems, cache_sems = rest[tp + 8 :]
+    cache_copies = tile_copies(cache, 0, cache_tiles, cache_sems)
     docs, width = states.shape
     pairs = wq.shape[1]
     halves = wq_buf.shape[0]
@@ -156,6 +172,9 @@
     for c in range(halves):
         for p in range(pairs):
             copies[c * pairs + p].wait()
+        if c == 0:
+            for copy in cache_copies:
+                copy.start()
         block = jnp.concatenate(
             [wq_buf.at[c, p].reshape(rows, LANES)[...] for p in range(pairs)], axis=1
         )
@@ -177,16 +196,17 @@
         outs[s][h + 1 : h + 2, :] = chosen[:, LANES:]
         outs[s][h + 2 : h + 3, :] = pick_row(sq_res, doc)
         outs[s][h + 3 :, :] = jnp.zeros((outs[s].shape[0] - h - 3, LANES), F32)
+    for copy in cache_copies:
+        copy.wait()
 
 
 def attend_kernel(tp, heads, rows, first, table, cache, w, *rest):
     parts = rest[:tp]
     heads_out, new_kv_out, w_ready, scores, w_sems = rest[-5:]
-    width, _, hidden = w.shape
-    w_copies = weight_copies(w.reshape(2 * width, hidden), first, w_ready, w_sems)
+    w_copies = tile_copies(matrix_of(w), first, w_ready, w_sems)
     for copy in w_copies:
         copy.start()
-    blocks = cache.shape[0] // rows
+    blocks = cache.shape[1] // rows
     sums = tree_sum([part[...] for part in parts])
     sums = sums * lax.rsqrt(sums[heads + 2 : heads + 3, :] / D + EPS)
     rotated = sums * table[0:1, :] + pltpu.roll(sums, LANES // 2, 1) * table[1:2, :]
@@ -205,7 +225,7 @@
     for b in range(blocks):
         block = lax.dot_general(
             query,
-            cache[b * rows : (b + 1) * rows, :LANES],
+            cache[0, b * rows : (b + 1) * rows, :],
             (((1,), (1,)), ((), ())),
             preferred_element_type=F32,
         )
@@ -220,7 +240,7 @@
         total = total + jnp.sum(weights, axis=1, keepdims=True)
         acc = acc + jnp.dot(
             weights.astype(BF16),
-            cache[b * rows : (b + 1) * rows, LANES:],
+            cache[1, b * rows : (b + 1) * rows, :],
             preferred_element_type=F32,
         )
     heads_out[...] = (acc / total).astype(BF16)
@@ -244,40 +264,47 @@
 
 
 def fetch_kernel(first, token, w, out, sems):
-    if len(w.shape) == 3:
-        w = w.reshape(w.shape[0] * w.shape[1], w.shape[2])
-    copies = weight_copies(w, first, out, sems)
+    copies = tile_copies(matrix_of(w), first, out, sems)
     for copy in copies:
         copy.start()
     for copy in copies:
         copy.wait()
 
 
-def gate_up_kernel(kv, groups, states, gains, *rest):
-    blocks, parts = rest[:groups], rest[groups : groups + kv]
-    attn_out, partial_out, spread_buf, acc = rest[groups + kv :]
+def gate_up_kernel(kv, groups, first, states, gains, w, *rest):
+    ready, parts = rest[:groups], rest[groups : groups + kv]
+    attn_out, partial_out, w_tiles, spread_buf, w_sems = rest[groups + kv :]
     docs, width = states.shape
-    rows, hidden = blocks[0].shape[1:]
+    hidden = w.shape[2]
+    w_matrix = matrix_of(w)
+    for copy in tile_copies(w_matrix, first, w_tiles, w_sems):
+        copy.start()
     attn = tree_sum([part[...].astype(F32) for part in parts]).astype(BF16)
     attn_out[...] = attn
     resid = (states[...].astype(F32) + attn.astype(F32)).astype(BF16).astype(F32)
     squares = jnp.sum(resid * resid, axis=1, keepdims=True)
     spread(two_parts(resid * gains[1:2, :]), spread_buf, docs)
-    acc[...] = jnp.zeros_like(acc)
-
-    first = 0
-    for group in blocks:
-
-        def step(b, carry, group=group, first=first):
-            start = pl.multiple_of((first + b) * rows, rows)
-            acc[...] += jnp.dot(
-                spread_buf[:, pl.ds(start, rows)], group[b], preferred_element_type=F32
-            )
-            return carry
-
-        lax.fori_loop(0, group.shape[0], step, 0)
-        first += group.shape[0]
-    partial_out[:, :hidden] = (acc[: 2 * docs] + acc[2 * docs :]).astype(BF16)
+
+    def store_from(tile):
+        def store(j, product):
+            start = pl.multiple_of((tile + 2 * j) * LANES, 2 * LANES)
+            summed = product[: 2 * docs] + product[2 * docs :]
+            partial_out[:, pl.ds(start, 2 * LANES)] = summed.astype(BF16)
+
+        return store
+
+    def tile_ready(i):
+        pltpu.make_async_copy(
+            w_matrix.at[:, pl.ds(pl.multiple_of((first + i) * LANES, LANES), LANES)],
+            w_tiles.at[i],
+            w_sems.at[i],
+        ).wait()
+
+    tile = 0
+    for group in ready:
+        times_tiles(spread_buf, group, store_from(tile))
+        tile += group.shape[0]
+    times_tiles(spread_buf, w_tiles, store_from(tile), tile_ready)
     lane = lax.broadcasted_iota(jnp.int32, (docs, LANES), 1)
     first = squares.astype(BF16).astype(F32)
     second = (squares - first).astype(BF16).astype(F32)
@@ -288,29 +315,21 @@
 
 def down_kernel(tp, w_down, *rest):
     parts = rest[:tp]
-    out, act_buf, acc = rest[tp:]
+    out, act_buf = rest[tp:]
     docs = out.shape[0]
-    blocks, step_rows = w_down.shape[:2]
-    hidden = blocks * step_rows
+    hidden = w_down.shape[1]
     summed = tree_sum([part[...].astype(F32) for part in parts])
     squares = jnp.sum(summed[:docs, hidden:], axis=1, keepdims=True)
     inverse = lax.rsqrt(squares / D + EPS)
     gate = summed[:docs, :hidden] * inverse
     up = summed[docs:, :hidden] * inverse
     act_buf[...] = (gate / (1.0 + jnp.exp(-gate)) * up).astype(BF16)
-    acc[...] = jnp.zeros_like(acc)
-
-    def step(b, carry):
-        start = pl.multiple_of(b * step_rows, step_rows)
-        acc[...] += jnp.dot(
-            act_buf[:, pl.ds(start, step_rows)],
-            w_down[b],
-            preferred_element_type=F32,
-        )
-        return carry
-
-    lax.fori_loop(0, blocks, step, 0)
-    out[...] = acc[...].astype(BF16)
+
+    def store(j, product):
+        start = pl.multiple_of(2 * j * LANES, 2 * LANES)
+        out[:, pl.ds(start, 2 * LANES)] = product.astype(BF16)
+
+    times_tiles(act_buf, w_down, store)
 
 
 def cost(micros):
@@ -339,15 +358,16 @@
     half = LANES // 2
     freq = ROPE_BASE ** (-(np.arange(half, dtype=np.float64) * 2.0 / LANES))
     freq = jnp.asarray(np.concatenate([freq, freq]).astype(np.float32)[None, :])
-    *qkv_parts, table, places = pl.pallas_call(
+    *qkv_parts, table, places, cache_tiles = pl.pallas_call(
         functools.partial(qkv_kernel, tp),
         out_shape=[jax.ShapeDtypeStruct((packed, LANES), F32)] * tp
         + [
             jax.ShapeDtypeStruct((8, LANES), F32),
             jax.ShapeDtypeStruct((max(tp, 8), LANES), jnp.int32),
+            pltpu.VMEM((2, cache_len, LANES), BF16),
         ],
-        in_specs=[hbm()] * 7,
-        out_specs=[vmem()] * (tp + 2),
+        in_specs=[hbm()] * 8,
+        out_specs=[vmem()] * (tp + 3),
         scratch_shapes=[
             pltpu.SMEM((docs,), jnp.int32),
             pltpu.SMEM((docs,), jnp.int32),
@@ -362,57 +382,54 @@
             pltpu.VMEM((docs, LANES), F32),
             pltpu.SemaphoreType.DMA((halves * pairs + 1,)),
             pltpu.SemaphoreType.DMA((5,)),
+            pltpu.SemaphoreType.DMA((2,)),
         ],
         compiler_params=params(docs, 10),
         cost_estimate=cost(8),
         name="qkv",
-    )(*(in_hbm(a) for a in (owner_rows, lengths, freq, states, norm_gains, wq, wkv)))
+    )(*(in_hbm(a) for a in (owner_rows, lengths, freq, states, norm_gains, wq, wkv, cache)))
     w_gu = in_hbm(w_gate_up)
-    gu_blocks = 2 * width // GU_BLOCK
-    bounds = sorted({gu_blocks * i // 16 for i in (0, 5, 8, 13, 16)})
+    bounds = np.cumsum([0] + [hidden // LANES * n // 28 for n in GU_SHARES]).tolist()
     shares = list(zip(bounds, bounds[1:]))
     fetched = []
 
-    def blocks_of(share, rows=GU_BLOCK, columns=hidden):
-        return pltpu.VMEM((share[1] - share[0], rows, columns), BF16)
-
-    def fetch(weights, share, token, *block):
+    def tiles_of(share, rows):
+        return pltpu.VMEM((share[1] - share[0], rows, LANES), BF16)
+
+    def fetch(weights, share, rows, token):
         return pl.pallas_call(
             functools.partial(fetch_kernel, share[0]),
-            out_shape=blocks_of(share, *block),
+            out_shape=tiles_of(share, rows),
             in_specs=[hbm(), hbm()],
             out_specs=vmem(),
             scratch_shapes=[pltpu.SemaphoreType.DMA((share[1] - share[0],))],
             compiler_params=params(docs, 2),
-            cost_estimate=cost(0.5 * (share[1] - share[0])),
+            cost_estimate=cost(0.3 * (share[1] - share[0])),
             name="fetch",
         )(token, weights)
 
-    if len(shares) == 4:
-        fetched.append(fetch(w_gu, shares[0], table))
+    fetched.append(fetch(w_gu, shares[0], 2 * width, table))
     qkv_parts = exchange(qkv_parts, "tp", tp)
-    own_share = shares[1] if len(shares) == 4 else shares[0]
     head_out, new_kv, w_ready = pl.pallas_call(
-        functools.partial(attend_kernel, tp, heads, 512, own_share[0]),
+        functools.partial(attend_kernel, tp, heads, 512, shares[1][0]),
         out_shape=[
             jax.ShapeDtypeStruct((heads, LANES), BF16),
             jax.ShapeDtypeStruct((1, 2 * LANES), BF16),
-            blocks_of(own_share),
+            tiles_of(shares[1], 2 * width),
         ],
         in_specs=[vmem(), vmem(), hbm()] + [vmem()] * tp + [hbm()] * len(fetched),
         out_specs=[vmem()] * 3,
         scratch_shapes=[
             pltpu.VMEM((heads, cache_len), F32),
-            pltpu.SemaphoreType.DMA((own_share[1] - own_share[0],)),
+            pltpu.SemaphoreType.DMA((shares[1][1] - shares[1][0],)),
         ],
         compiler_params=params(docs, 6),
         cost_estimate=cost(8),
         name="attend",
-    )(table, cache, w_gu, *qkv_parts, *fetched)
+    )(table, cache_tiles, w_gu, *qkv_parts, *fetched)
     fetched.append(w_ready)
 
-    if len(shares) == 4:
-        fetched.append(fetch(w_gu, shares[2], head_out))
+    fetched.append(fetch(w_gu, shares[2], 2 * width, head_out))
     head_parts = exchange([head_out] * tp, "tp", tp)
     out_part = pl.pallas_call(
         functools.partial(out_kernel, tp),
@@ -425,33 +442,34 @@
         name="attn_project",
     )(places, w_out, *head_parts, fetched[-1])
 
-    fetched.append(fetch(w_gu, shares[-1], out_part))
+    fetched.append(fetch(w_gu, shares[3], 2 * width, out_part))
     out_parts = exchange([out_part] * kv, "kv", kv)
     attn_out, gu_part = pl.pallas_call(
-        functools.partial(gate_up_kernel, kv, len(fetched)),
+        functools.partial(gate_up_kernel, kv, len(fetched), shares[4][0]),
         out_shape=[
             jax.ShapeDtypeStruct((docs, width), BF16),
             jax.ShapeDtypeStruct((2 * docs, hidden + LANES), BF16),
         ],
-        in_specs=[vmem()] * (2 + len(fetched) + kv),
+        in_specs=[vmem(), vmem(), hbm()] + [vmem()] * (len(fetched) + kv),
         out_specs=[vmem(), vmem()],
         scratch_shapes=[
+            tiles_of(shares[4], 2 * width),
             pltpu.VMEM((4 * docs, 2 * width), BF16),
-            pltpu.VMEM((4 * docs, hidden), F32),
+            pltpu.SemaphoreType.DMA((shares[4][1] - shares[4][0],)),
         ],
-        compiler_params=params(docs, 6),
+        compiler_params=params(docs, 20),
         cost_estimate=cost(10),
         name="gate_up",
-    )(states, norm_gains, *fetched, *out_parts)
-
-    w_down_ready = fetch(in_hbm(w_down), (0, hidden // DOWN_BLOCK), gu_part, DOWN_BLOCK, width)
+    )(states, norm_gains, w_gu, *fetched, *out_parts)
+
+    w_down_ready = fetch(in_hbm(w_down), (0, width // LANES), hidden, gu_part)
     gu_parts = exchange([gu_part] * tp, "tp", tp)
     ffn_part = pl.pallas_call(
         functools.partial(down_kernel, tp),
         out_shape=jax.ShapeDtypeStruct((docs, width), BF16),
         in_specs=[vmem()] + [vmem()] * tp,
         out_specs=vmem(),
-        scratch_shapes=[pltpu.VMEM((docs, hidden), BF16), pltpu.VMEM((docs, width), F32)],
+        scratch_shapes=[pltpu.VMEM((docs, hidden), BF16)],
         compiler_params=params(docs, 6),
         cost_estimate=cost(5),
         name="down",

time: 57 us -> 55.9 us (0.981)
  Pallas kernels: 33.4 us -> 30.5 us
  waiting for transfers between devices: 3.72 us -> 5.46 us
    pallas_call x6, Pallas kernels: 24.9 us -> 21.7 us  [the longest x4 11.7 us: fetch(): pl.pallas_call(functools.partial(fetch_kernel, share[0]), out_shape=tiles...]
    ppermute x15, waiting for transfers between devices: 3.72 us -> 5.46 us  [exchange(): lax.ppermute(arrays[s], axis, [(i, i ^ s) for i in range(size)])]
  transfers between devices with their start and end apart: 15 -> 15, of which waited for: 3 -> 4; matrix products, arithmetic and copies ran while one was open for 0% -> 0% of each run, Pallas kernels for 27% -> 21%
where the time goes in v5:
time: 55.9 us; the launch traced here: 55.7 us
  Pallas kernels  30.5 us (55%)
  starting transfers between devices  18.3 us (33%)
  waiting for transfers between devices  5.46 us (10%)
  between operations  0.8 us (1%)
  other arithmetic  0.63 us (1%)
    ppermute x15, starting transfers between devices, exchange(): lax.ppermute(arrays[s], axis, [(i, i ^ s) for i in range(size)])  18.3 us
    pallas_call x4, Pallas kernels, fetch(): pl.pallas_call(functools.partial(fetch_kernel, share[0]), out_shape=tiles...  11.7 us
    pallas_call x1, Pallas kernels, per_device(): pl.pallas_call(functools.partial(gate_up_kernel, kv, len(fetched), shares...  5.98 us
    ppermute x15, waiting for transfers between devices, exchange(): lax.ppermute(arrays[s], axis, [(i, i ^ s) for i in range(size)])  5.46 us
    pallas_call x1, Pallas kernels, per_device(): pl.pallas_call(functools.partial(qkv_kernel, tp), out_shape=[jax.ShapeDty...  5.08 us
    pallas_call x1, Pallas kernels, per_device(): pl.pallas_call(functools.partial(attend_kernel, tp, heads, 512, shares[1]...  4.09 us
    pallas_call x1, Pallas kernels, per_device(): pl.pallas_call(functools.partial(down_kernel, tp), out_shape=jax.ShapeDty...  3.02 us
  transfers between devices with their start and end apart: 15, of which 4 were waited for; matrix products, arithmetic and copies ran while one was open for 0% of the time, Pallas kernels for 21%

profile of v5, /device:TPU:0, one launch (start us, length us, event | category | flops | bytes accessed | tf_op | source)
XLA Modules:
  0.0 55.7 jit_solution(3986267463713972067)
XLA Ops:
  0.6 5.1 %qkv.1 = (f32[16,128]{1,0:T(8,128)S(1)}, f32[16,128]{1,0:T(8,128)S(1)}, f32[16,128]{1,0:T(8,128)S(1)}, f32[16,128]{1,0:T(8,128)S(1)}, f32[8,128]{1,0:T(8,128)S(1...) custom-call(s32[4]{0:T(128)} %owner_hbm.1, s32[4]{0:T(128)} %lengths_hbm.1, ...), custom_call_target="tpu_custom_call" | custom-call | bytes 29520000 | tf_op jit(solution)/shard_map/qkv/pallas_call | solution.py:361
  5.7 3.1 %collective-permute-start = (f32[16,128]{1,0:T(8,128)S(1)}, f32[16,128]{1,0:T(8,128)S(1)}, u32[]{:S(2)}, u32[]{:S(2)}) collective-permute-start(f32[16,128]{1,0:T(8,128)S(1)} %get-tuple-element.18), channel_id=1, source_target_pairs={{0,4},{4,0},{8,12},{12,8},{1,5},{5,1},{9,13},{13,9},{2,6},{6,2},{1... | collective-permute-start | bytes 24584 | tf_op jit(solution)/shard_map/ppermute | solution.py:39
  8.8 2.6 %collective-permute-start.1 = (f32[16,128]{1,0:T(8,128)S(1)}, f32[16,128]{1,0:T(8,128)S(1)}, u32[]{:S(2)}, u32[]{:S(2)}) collective-permute-start(f32[16,128]{1,0:T(8,128)S(1)} %get-tuple-element.19), channel_id=1, source_target_pairs={{0,8},{4,12},{8,0},{12,4},{1,9},{5,13},{9,1},{13,5},{2,10},{6,14},... | collective-permute-start | bytes 24584 | tf_op jit(solution)/shard_map/ppermute | solution.py:39
  11.4 2.3 %fetch.4.rest_4_.rest_0_ = bf16[4,4096,128]{2,1,0:T(8,128)(2,1)S(1)} custom-call(f32[8,128]{1,0:T(8,128)S(1)} %get-tuple-element.15.token.table, bf16[2048,2,3584]{2,1,0:T(2,128)(2,1)} %w.10), custom_call_target="tpu_custom_call" | custom-call | bytes 4428000 | tf_op jit(solution)/shard_map/fetch/pallas_call | solution.py:400
  13.7 3.1 %collective-permute-done.2.rest_3_ = f32[16,128]{1,0:T(8,128)S(1)} collective-permute-done((f32[16,128]{1,0:T(8,128)S(1)}, f32[16,128]{1,0:T(8,128)S(1)}, u32[]{:S(2)}, u32[]{:S(2)}) %collective-permute-start.2) | collective-permute-done | bytes 8224 | tf_op jit(solution)/shard_map/ppermute | solution.py:39
  16.9 4.1 %attend.1 = (bf16[8,128]{1,0:T(8,128)(2,1)S(1)}, bf16[1,256]{1,0:T(2,128)(2,1)}, bf16[6,4096,128]{2,1,0:T(8,128)(2,1)S(1)}) custom-call(f32[8,128]{1,0:T(8,128)S(1)} %get-tuple-element.15.token.table, bf16[2,8192,128]{2,1,0:T(8,128)(2,1)S(1)} %get-tuple-element.16.cache, bf16[2048,2,3584]{2,1,0:T(2,128)(2,1)} %w.10, ...), custom_call_target="tpu_custom_call" | custom-call | bytes 29520000 | tf_op jit(solution)/shard_map/attend/pallas_call | solution.py:413
  21.0 0.0 copy-start
  21.0 0.7 %collective-permute-start.5 = (bf16[8,128]{1,0:T(8,128)(2,1)S(1)}, bf16[8,128]{1,0:T(8,128)(2,1)S(1)}, u32[]{:S(2)}, u32[]{:S(2)}) collective-permute-start(bf16[8,128]{1,0:T(8,128)(2,1)S(1)} %get-tuple-element.22.token.rest_0_), channel_id=1, source_target_pairs={{0,12},{4,8},{8,4},{12,0},{1,13},{5,9},{9,5},{13,1},{2,14},{6,10},... | collective-permute-start | bytes 6152 | tf_op jit(solution)/shard_map/ppermute | solution.py:39
  21.7 3.7 %collective-permute-start.3 = (bf16[8,128]{1,0:T(8,128)(2,1)S(1)}, bf16[8,128]{1,0:T(8,128)(2,1)S(1)}, u32[]{:S(2)}, u32[]{:S(2)}) collective-permute-start(bf16[8,128]{1,0:T(8,128)(2,1)S(1)} %get-tuple-element.22.token.rest_0_), channel_id=1, source_target_pairs={{0,4},{4,0},{8,12},{12,8},{1,5},{5,1},{9,13},{13,9},{2,6},{6,2},{1... | collective-permute-start | bytes 6152 | tf_op jit(solution)/shard_map/ppermute | solution.py:39
  25.4 2.3 %fetch.5.rest_4_.rest_2_ = bf16[4,4096,128]{2,1,0:T(8,128)(2,1)S(1)} custom-call(bf16[8,128]{1,0:T(8,128)(2,1)S(1)} %get-tuple-element.22.token.rest_0_, bf16[2048,2,3584]{2,1,0:T(2,128)(2,1)} %w.10), custom_call_target="tpu_custom_call" | custom-call | bytes 4428000 | tf_op jit(solution)/shard_map/fetch/pallas_call | solution.py:400
  27.7 0.0 collective-permute-done.5.rest_3_
  27.7 0.0 collective-permute-done.3.rest_1_
  27.7 0.7 %attn_project.1.token.rest_4_ = bf16[4,2048]{1,0:T(4,128)(2,1)S(1)} custom-call(s32[8,128]{1,0:T(8,128)S(1)} %get-tuple-element.23.places, bf16[1024,2048]{1,0:T(8,128)(2,1)S(1)} %copy-done, bf16[8,128]{1,0:T(8,128)(2,1)S(1)} %get-tuple-element.22.token.rest_0_, bf16[8,128]{1,0:T(8,128)(2,1)S(1)} %collective-permute-done.3.rest_1_, ...), custom_call_target="tpu_custom_call" | custom-call | bytes 22140000 | tf_op jit(solution)/shard_map/attn_project/pallas_call | solution.py:434
  28.4 0.0 collective-permute-start.8
  28.4 1.6 %collective-permute-start.7 = (bf16[4,2048]{1,0:T(4,128)(2,1)S(1)}, bf16[4,2048]{1,0:T(4,128)(2,1)S(1)}, u32[]{:S(2)}, u32[]{:S(2)}) collective-permute-start(bf16[4,2048]{1,0:T(4,128)(2,1)S(1)} %attn_project.1.token.rest_4_), channel_id=1, source_target_pairs={{0,2},{1,3},{2,0},{3,1},{4,6},{5,7},{6,4},{7,5},{8,10},{9,11},{10,... | collective-permute-start | bytes 49160 | tf_op jit(solution)/shard_map/ppermute | solution.py:39
  30.0 0.3 collective-permute-start.6
  30.3 1.6 %fetch.6.rest_3_ = bf16[2,4096,128]{2,1,0:T(8,128)(2,1)S(1)} custom-call(bf16[4,2048]{1,0:T(4,128)(2,1)S(1)} %attn_project.1.token.rest_4_, bf16[2048,2,3584]{2,1,0:T(2,128)(2,1)} %w.10), custom_call_target="tpu_custom_call" | custom-call | bytes 2214000 | tf_op jit(solution)/shard_map/fetch/pallas_call | solution.py:400
  31.8 0.0 collective-permute-done.8.rest_7_
  31.8 0.4 collective-permute-done.7.rest_6_
  32.2 6.0 %gate_up.1 = (bf16[4,2048]{1,0:T(4,128)(2,1)}, bf16[8,3712]{1,0:T(8,128)(2,1)S(1)}) custom-call(bf16[4,2048]{1,0:T(4,128)(2,1)S(1)} %copy-done.1, f32[2,2048]{1,0:T(2,128)S(1)} %copy-done.2, bf16[2048,2,3584]{2,1,0:T(2,128)(2,1)} %w.10, bf16[4,4096,128]{2,1,0:T(8,128)(2,1)S(1)} %fetch.4.rest_4_.rest_0_, bf16[6,4096,128]{2,1,0:T(8,128)(2,1)S(1)} %get-tuple-element.21.rest_1_, ...), custom_call_target="tpu_custom_call" | custom-call | bytes 36900000 | tf_op jit(solution)/shard_map/gate_up/pallas_call | solution.py:447
  38.2 1.7 %collective-permute-start.11 = (bf16[8,3712]{1,0:T(8,128)(2,1)S(1)}, bf16[8,3712]{1,0:T(8,128)(2,1)S(1)}, u32[]{:S(2)}, u32[]{:S(2)}) collective-permute-start(bf16[8,3712]{1,0:T(8,128)(2,1)S(1)} %get-tuple-element.25.token.rest_0_), channel_id=1, source_target_pairs={{0,12},{4,8},{8,4},{12,0},{1,13},{5,9},{9,5},{13,1},{2,14},{6,10},... | collective-permute-start | bytes 178184 | tf_op jit(solution)/shard_map/ppermute | solution.py:39
  39.9 1.1 %collective-permute-start.10 = (bf16[8,3712]{1,0:T(8,128)(2,1)S(1)}, bf16[8,3712]{1,0:T(8,128)(2,1)S(1)}, u32[]{:S(2)}, u32[]{:S(2)}) collective-permute-start(bf16[8,3712]{1,0:T(8,128)(2,1)S(1)} %get-tuple-element.25.token.rest_0_), channel_id=1, source_target_pairs={{0,8},{4,12},{8,0},{12,4},{1,9},{5,13},{9,1},{13,5},{2,10},{6,14},... | collective-permute-start | bytes 178184 | tf_op jit(solution)/shard_map/ppermute | solution.py:39
  41.0 1.6 %collective-permute-start.9 = (bf16[8,3712]{1,0:T(8,128)(2,1)S(1)}, bf16[8,3712]{1,0:T(8,128)(2,1)S(1)}, u32[]{:S(2)}, u32[]{:S(2)}) collective-permute-start(bf16[8,3712]{1,0:T(8,128)(2,1)S(1)} %get-tuple-element.25.token.rest_0_), channel_id=1, source_target_pairs={{0,4},{4,0},{8,12},{12,8},{1,5},{5,1},{9,13},{13,9},{2,6},{6,2},{1... | collective-permute-start | bytes 178184 | tf_op jit(solution)/shard_map/ppermute | solution.py:39
  42.7 5.6 %fetch.7.w_down = bf16[16,3584,128]{2,1,0:T(8,128)(2,1)S(1)} custom-call(bf16[8,3712]{1,0:T(8,128)(2,1)S(1)} %get-tuple-element.25.token.rest_0_, bf16[3584,2048]{1,0:T(8,128)(2,1)} %w.11), custom_call_target="tpu_custom_call" | custom-call | bytes 17712000 | tf_op jit(solution)/shard_map/fetch/pallas_call | solution.py:400
  48.3 0.0 collective-permute-done.11.rest_3_
  48.3 0.0 collective-permute-done.10.rest_2_
  48.3 3.0 %down.1 = bf16[4,2048]{1,0:T(4,128)(2,1)S(1)} custom-call(bf16[16,3584,128]{2,1,0:T(8,128)(2,1)S(1)} %fetch.7.w_down, bf16[8,3712]{1,0:T(8,128)(2,1)S(1)} %get-tuple-element.25.token.rest_0_, bf16[8,3712]{1,0:T(8,128)(2,1)S(1)} %collective-permute-done.9.rest_1_, bf16[8,3712]{1,0:T(8,128)(2,1)S(1)} %collective-permute-done.10.rest_2_, ...), custom_call_target="tpu_custom_call" | custom-call | bytes 18450000 | tf_op jit(solution)/shard_map/down/pallas_call | solution.py:467
  51.3 1.5 %collective-permute-start.13 = (bf16[4,2048]{1,0:T(4,128)(2,1)S(1)}, bf16[4,2048]{1,0:T(4,128)(2,1)S(1)}, u32[]{:S(2)}, u32[]{:S(2)}) collective-permute-start(bf16[4,2048]{1,0:T(4,128)(2,1)S(1)} %down.1), channel_id=1, source_target_pairs={{0,2},{1,3},{2,0},{3,1},{4,6},{5,7},{6,4},{7,5},{8,10},{9,11},{10,... | collective-permute-start | bytes 49160 | tf_op jit(solution)/shard_map/ppermute | solution.py:39
  52.8 0.3 collective-permute-start.12
  53.2 1.5 %collective-permute-done.14 = bf16[4,2048]{1,0:T(4,128)(2,1)S(1)} collective-permute-done((bf16[4,2048]{1,0:T(4,128)(2,1)S(1)}, bf16[4,2048]{1,0:T(4,128)(2,1)S(1)}, u32[]{:S(2)}, u32[]{:S(2)}) %collective-permute-start.14) | collective-permute-done | bytes 16416 | tf_op jit(solution)/shard_map/ppermute | solution.py:39
  54.6 0.5 collective-permute-done.13
  55.1 0.6 %add_convert_fusion = bf16[4,2048]{1,0:T(4,128)(2,1)} fusion(bf16[4,2048]{1,0:T(4,128)(2,1)S(1)} %collective-permute-done.14, bf16[4,2048]{1,0:T(4,128)(2,1)S(1)} %collective-permute-done.13, bf16[4,2048]{1,0:T(4,128)(2,1)S(1)} %collective-permute-done.12, bf16[4,2048]{1,0:T(4,128)(2,1)S(1)} %down.1), kind=kLoop, calls=%fused_computation | loop fusion | flops 65536 | bytes 81920 | tf_op jit(solution)/shard_map/convert_element_type | solution.py:478
  (14 shorter events, 0.0 us)
Async XLA Ops:
  5.7 8.0 %collective-permute-start = (f32[16,128]{1,0:T(8,128)S(1)}, f32[16,128]{1,0:T(8,128)S(1)}, u32[]{:S(2)}, u32[]{:S(2)}) collective-permute-start(f32[16,128]{1,0:T(8,128)S(1)} %get-tuple-element.18), channel_id=1, source_target_pairs={{0,4},{4,0},{8,12},{12,8},{1,5},{5,1},{9,13},{13,9},{2,6},{6,2},{1... | collective-permute-start | bytes 24584 | tf_op jit(solution)/shard_map/ppermute | solution.py:39
  8.8 4.9 %collective-permute-start.1 = (f32[16,128]{1,0:T(8,128)S(1)}, f32[16,128]{1,0:T(8,128)S(1)}, u32[]{:S(2)}, u32[]{:S(2)}) collective-permute-start(f32[16,128]{1,0:T(8,128)S(1)} %get-tuple-element.19), channel_id=1, source_target_pairs={{0,8},{4,12},{8,0},{12,4},{1,9},{5,13},{9,1},{13,5},{2,10},{6,14},... | collective-permute-start | bytes 24584 | tf_op jit(solution)/shard_map/ppermute | solution.py:39
  11.4 5.4 %collective-permute-start.2 = (f32[16,128]{1,0:T(8,128)S(1)}, f32[16,128]{1,0:T(8,128)S(1)}, u32[]{:S(2)}, u32[]{:S(2)}) collective-permute-start(f32[16,128]{1,0:T(8,128)S(1)} %get-tuple-element.20), channel_id=1, source_target_pairs={{0,12},{4,8},{8,4},{12,0},{1,13},{5,9},{9,5},{13,1},{2,14},{6,10},... | collective-permute-start | bytes 24584 | tf_op jit(solution)/shard_map/ppermute | solution.py:39
  21.0 6.8 %copy-start = (bf16[1024,2048]{1,0:T(8,128)(2,1)S(1)}, bf16[1024,2048]{1,0:T(8,128)(2,1)}, u32[]{:S(2)}) copy-start(bf16[1024,2048]{1,0:T(8,128)(2,1)} %w_out.1) | copy-start | bytes 12582916
  21.0 6.7 %collective-permute-start.5 = (bf16[8,128]{1,0:T(8,128)(2,1)S(1)}, bf16[8,128]{1,0:T(8,128)(2,1)S(1)}, u32[]{:S(2)}, u32[]{:S(2)}) collective-permute-start(bf16[8,128]{1,0:T(8,128)(2,1)S(1)} %get-tuple-element.22.token.rest_0_), channel_id=1, source_target_pairs={{0,12},{4,8},{8,4},{12,0},{1,13},{5,9},{9,5},{13,1},{2,14},{6,10},... | collective-permute-start | bytes 6152 | tf_op jit(solution)/shard_map/ppermute | solution.py:39
  21.7 6.0 %collective-permute-start.4 = (bf16[8,128]{1,0:T(8,128)(2,1)S(1)}, bf16[8,128]{1,0:T(8,128)(2,1)S(1)}, u32[]{:S(2)}, u32[]{:S(2)}) collective-permute-start(bf16[8,128]{1,0:T(8,128)(2,1)S(1)} %get-tuple-element.22.token.rest_0_), channel_id=1, source_target_pairs={{0,8},{4,12},{8,0},{12,4},{1,9},{5,13},{9,1},{13,5},{2,10},{6,14},... | collective-permute-start | bytes 6152 | tf_op jit(solution)/shard_map/ppermute | solution.py:39
  21.7 6.0 %collective-permute-start.3 = (bf16[8,128]{1,0:T(8,128)(2,1)S(1)}, bf16[8,128]{1,0:T(8,128)(2,1)S(1)}, u32[]{:S(2)}, u32[]{:S(2)}) collective-permute-start(bf16[8,128]{1,0:T(8,128)(2,1)S(1)} %get-tuple-element.22.token.rest_0_), channel_id=1, source_target_pairs={{0,4},{4,0},{8,12},{12,8},{1,5},{5,1},{9,13},{13,9},{2,6},{6,2},{1... | collective-permute-start | bytes 6152 | tf_op jit(solution)/shard_map/ppermute | solution.py:39
  28.4 3.8 %copy-start.1 = (bf16[4,2048]{1,0:T(4,128)(2,1)S(1)}, bf16[4,2048]{1,0:T(4,128)(2,1)}, u32[]{:S(2)}) copy-start(bf16[4,2048]{1,0:T(4,128)(2,1)} %states.1) | copy-start | bytes 49156
  28.4 3.8 %copy-start.2 = (f32[2,2048]{1,0:T(2,128)S(1)}, f32[2,2048]{1,0:T(2,128)}, u32[]{:S(2)}) copy-start(f32[2,2048]{1,0:T(2,128)} %gains.1) | copy-start | bytes 49156
  28.4 3.5 %collective-permute-start.8 = (bf16[4,2048]{1,0:T(4,128)(2,1)S(1)}, bf16[4,2048]{1,0:T(4,128)(2,1)S(1)}, u32[]{:S(2)}, u32[]{:S(2)}) collective-permute-start(bf16[4,2048]{1,0:T(4,128)(2,1)S(1)} %attn_project.1.token.rest_4_), channel_id=1, source_target_pairs={{0,3},{1,2},{2,1},{3,0},{4,7},{5,6},{6,5},{7,4},{8,11},{9,10},{10,... | collective-permute-start | bytes 49160 | tf_op jit(solution)/shard_map/ppermute | solution.py:39
  28.4 3.8 %collective-permute-start.7 = (bf16[4,2048]{1,0:T(4,128)(2,1)S(1)}, bf16[4,2048]{1,0:T(4,128)(2,1)S(1)}, u32[]{:S(2)}, u32[]{:S(2)}) collective-permute-start(bf16[4,2048]{1,0:T(4,128)(2,1)S(1)} %attn_project.1.token.rest_4_), channel_id=1, source_target_pairs={{0,2},{1,3},{2,0},{3,1},{4,6},{5,7},{6,4},{7,5},{8,10},{9,11},{10,... | collective-permute-start | bytes 49160 | tf_op jit(solution)/shard_map/ppermute | solution.py:39
  30.0 2.3 %collective-permute-start.6 = (bf16[4,2048]{1,0:T(4,128)(2,1)S(1)}, bf16[4,2048]{1,0:T(4,128)(2,1)S(1)}, u32[]{:S(2)}, u32[]{:S(2)}) collective-permute-start(bf16[4,2048]{1,0:T(4,128)(2,1)S(1)} %attn_project.1.token.rest_4_), channel_id=1, source_target_pairs={{0,1},{1,0},{2,3},{3,2},{4,5},{5,4},{6,7},{7,6},{8,9},{9,8},{10,11... | collective-permute-start | bytes 49160 | tf_op jit(solution)/shard_map/ppermute | solution.py:39
  38.2 10.1 %collective-permute-start.11 = (bf16[8,3712]{1,0:T(8,128)(2,1)S(1)}, bf16[8,3712]{1,0:T(8,128)(2,1)S(1)}, u32[]{:S(2)}, u32[]{:S(2)}) collective-permute-start(bf16[8,3712]{1,0:T(8,128)(2,1)S(1)} %get-tuple-element.25.token.rest_0_), channel_id=1, source_target_pairs={{0,12},{4,8},{8,4},{12,0},{1,13},{5,9},{9,5},{13,1},{2,14},{6,10},... | collective-permute-start | bytes 178184 | tf_op jit(solution)/shard_map/ppermute | solution.py:39
  39.9 8.4 %collective-permute-start.10 = (bf16[8,3712]{1,0:T(8,128)(2,1)S(1)}, bf16[8,3712]{1,0:T(8,128)(2,1)S(1)}, u32[]{:S(2)}, u32[]{:S(2)}) collective-permute-start(bf16[8,3712]{1,0:T(8,128)(2,1)S(1)} %get-tuple-element.25.token.rest_0_), channel_id=1, source_target_pairs={{0,8},{4,12},{8,0},{12,4},{1,9},{5,13},{9,1},{13,5},{2,10},{6,14},... | collective-permute-start | bytes 178184 | tf_op jit(solution)/shard_map/ppermute | solution.py:39
  41.0 7.2 %collective-permute-start.9 = (bf16[8,3712]{1,0:T(8,128)(2,1)S(1)}, bf16[8,3712]{1,0:T(8,128)(2,1)S(1)}, u32[]{:S(2)}, u32[]{:S(2)}) collective-permute-start(bf16[8,3712]{1,0:T(8,128)(2,1)S(1)} %get-tuple-element.25.token.rest_0_), channel_id=1, source_target_pairs={{0,4},{4,0},{8,12},{12,8},{1,5},{5,1},{9,13},{13,9},{2,6},{6,2},{1... | collective-permute-start | bytes 178184 | tf_op jit(solution)/shard_map/ppermute | solution.py:39
  51.3 3.3 %collective-permute-start.14 = (bf16[4,2048]{1,0:T(4,128)(2,1)S(1)}, bf16[4,2048]{1,0:T(4,128)(2,1)S(1)}, u32[]{:S(2)}, u32[]{:S(2)}) collective-permute-start(bf16[4,2048]{1,0:T(4,128)(2,1)S(1)} %down.1), channel_id=1, source_target_pairs={{0,3},{1,2},{2,1},{3,0},{4,7},{5,6},{6,5},{7,4},{8,11},{9,10},{10,... | collective-permute-start | bytes 49160 | tf_op jit(solution)/shard_map/ppermute | solution.py:39
  51.3 3.8 %collective-permute-start.13 = (bf16[4,2048]{1,0:T(4,128)(2,1)S(1)}, bf16[4,2048]{1,0:T(4,128)(2,1)S(1)}, u32[]{:S(2)}, u32[]{:S(2)}) collective-permute-start(bf16[4,2048]{1,0:T(4,128)(2,1)S(1)} %down.1), channel_id=1, source_target_pairs={{0,2},{1,3},{2,0},{3,1},{4,6},{5,7},{6,4},{7,5},{8,10},{9,11},{10,... | collective-permute-start | bytes 49160 | tf_op jit(solution)/shard_map/ppermute | solution.py:39
  52.8 2.3 %collective-permute-start.12 = (bf16[4,2048]{1,0:T(4,128)(2,1)S(1)}, bf16[4,2048]{1,0:T(4,128)(2,1)S(1)}, u32[]{:S(2)}, u32[]{:S(2)}) collective-permute-start(bf16[4,2048]{1,0:T(4,128)(2,1)S(1)} %down.1), channel_id=1, source_target_pairs={{0,1},{1,0},{2,3},{3,2},{4,5},{5,4},{6,7},{7,6},{8,9},{9,8},{10,11... | collective-permute-start | bytes 49160 | tf_op jit(solution)/shard_map/ppermute | solution.py:39

commit v6 on v5

--- a/solution.py
+++ b/solution.py
@@ -14,12 +14,12 @@
 ROPE_BASE = 500000.0
 LANES = 128
 MIB = 1 << 20
-GU_SHARES = (4, 6, 4, 2, 12)
+GU_SHARES = (6, 4, 6, 4, 8)
 F32 = jnp.float32
 BF16 = jnp.bfloat16
-TURN_A = 6.28125
-TURN_B = 0.0019340515136718750
-TURN_C = 2.0 * math.pi - TURN_A - TURN_B
+QUARTER = (1.5703125, 4.837512969970703125e-4, 7.549789948768648e-8)
+SIN = (-1.9515295891e-4, 8.3321608736e-3, -1.6666654611e-1)
+COS = (2.443315711809948e-5, -1.388731625493765e-3, 4.166664568298827e-2)
 
 
 def vmem():
@@ -35,10 +35,11 @@
 
 
 def exchange(arrays, axis, size):
-    return [arrays[0]] + [
+    got = [
         lax.ppermute(arrays[s], axis, [(i, i ^ s) for i in range(size)])
-        for s in range(1, size)
+        for s in reversed(range(1, size))
     ]
+    return [arrays[0]] + got[::-1]
 
 
 def tree_sum(parts):
@@ -49,15 +50,12 @@
 
 def two_parts(scaled):
     high = scaled.astype(BF16).astype(F32)
-    low = scaled - high
-    return jnp.concatenate([high, high, low, low], axis=0).astype(BF16)
+    return high, scaled - high
 
 
 def spread(rows16, out_ref, docs):
     width = rows16.shape[1]
-    source = lax.broadcasted_iota(jnp.int32, (LANES, 2 * LANES), 0)
-    target = lax.broadcasted_iota(jnp.int32, (LANES, 2 * LANES), 1)
-    pick = (lax.shift_right_logical(target, 1) == source).astype(F32).astype(BF16)
+    pick = one_hot_spread(2)
     row = lax.broadcasted_iota(jnp.int32, (4 * docs, 2 * LANES), 0)
     lane = lax.broadcasted_iota(jnp.int32, (4 * docs, 2 * LANES), 1)
     keep = lax.rem(lax.div(row, docs), 2) == lax.rem(lane, 2)
@@ -96,18 +94,55 @@
     lax.fori_loop(0, tiles.shape[0] // 2, step, 0)
 
 
-def pick_row(ref, index):
-    row = lax.broadcasted_iota(jnp.int32, ref.shape, 0)
-    return jnp.sum(jnp.where(row == index, ref[...], 0.0), axis=0, keepdims=True)
+def pick_doc(value, doc, docs):
+    axis = value.ndim - 2
+    row = lax.broadcasted_iota(jnp.int32, value.shape, axis)
+    return jnp.sum(jnp.where(lax.rem(row, docs) == doc, value, 0.0), axis=axis)
+
+
+def sine_cosine(angle):
+    turns = jnp.floor(angle * (2.0 / math.pi) + 0.5)
+    rest = ((angle - turns * QUARTER[0]) - turns * QUARTER[1]) - turns * QUARTER[2]
+    square = rest * rest
+    sine = rest + rest * square * ((SIN[0] * square + SIN[1]) * square + SIN[2])
+    cosine = 1.0 - 0.5 * square + square * square * (
+        (COS[0] * square + COS[1]) * square + COS[2]
+    )
+    quadrant = turns - 4.0 * jnp.floor(turns * 0.25)
+    odd = (quadrant == 1.0) | (quadrant == 3.0)
+    sine, cosine = jnp.where(odd, cosine, sine), jnp.where(odd, sine, cosine)
+    return (
+        jnp.where(quadrant >= 2.0, -sine, sine),
+        jnp.where((quadrant == 1.0) | (quadrant == 2.0), -cosine, cosine),
+    )
 
 
 def rope_rows(length, frequency):
-    angle = length * frequency
-    turns = jnp.floor(angle * (0.5 / math.pi) + 0.5)
-    angle = ((angle - turns * TURN_A) - turns * TURN_B) - turns * TURN_C
+    sine, cosine = sine_cosine(length * frequency)
     lane = lax.broadcasted_iota(jnp.int32, (1, LANES), 1)
-    sine = jnp.sin(angle)
-    return jnp.cos(angle), jnp.where(lane < LANES // 2, -sine, sine)
+    return cosine, jnp.where(lane < LANES // 2, -sine, sine)
+
+
+def one_hot_spread(fold):
+    source = lax.broadcasted_iota(jnp.int32, (LANES, fold * LANES), 0)
+    target = lax.broadcasted_iota(jnp.int32, (LANES, fold * LANES), 1)
+    return (lax.div(target, fold) == source).astype(F32).astype(BF16)
+
+
+def spread_heads(rows, out_ref, heads):
+    count, width = rows.shape
+    chunks = width // LANES
+    stacked = jnp.concatenate([rows[:, c * LANES : (c + 1) * LANES] for c in range(chunks)], axis=0)
+    wide = jnp.dot(stacked.astype(BF16), one_hot_spread(heads), preferred_element_type=F32)
+    columns = heads * LANES
+    lane = lax.rem(lax.broadcasted_iota(jnp.int32, (count, columns), 1), heads)
+    for c in range(chunks):
+        piece = wide[c * count : (c + 1) * count]
+        for h in range(0, heads, 2):
+            pair = [jnp.where(lane == h + i, piece, 0.0) for i in range(2)]
+            out_ref[h * count : (h + 2) * count, c * columns : (c + 1) * columns] = (
+                jnp.concatenate(pair, axis=0).astype(BF16)
+            )
 
 
 def qkv_kernel(
@@ -116,12 +151,11 @@
     outs = rest[:tp]
     table, places, cache_tiles = rest[tp : tp + 3]
     owner, lengths, frequency, states, gains = rest[tp + 3 : tp + 8]
-    wq_buf, wkv_buf, spread_buf, res, kv_res, sq_res, sems, small_sems, cache_sems = rest[tp + 8 :]
-    cache_copies = tile_copies(cache, 0, cache_tiles, cache_sems)
+    wq_buf, wkv_buf, spread_buf, sems, small_sems, cache_sems = rest[tp + 8 :]
     docs, width = states.shape
-    pairs = wq.shape[1]
-    halves = wq_buf.shape[0]
-    rows = 2 * width // halves
+    heads = wq.shape[0] // width
+    parts = wq_buf.shape[0]
+    rows = wq_buf.shape[1]
     small = [
         pltpu.make_async_copy(source, target, small_sems.at[i])
         for i, (source, target) in enumerate(
@@ -134,29 +168,21 @@
             ]
         )
     ]
-    for copy in small:
-        copy.start()
-    kv_copy = pltpu.make_async_copy(wkv, wkv_buf, sems.at[halves * pairs])
-    kv_copy.start()
-    copies = []
-    for c in range(halves):
-        for p in range(pairs):
-            copies.append(
-                pltpu.make_async_copy(
-                    wq.at[pl.ds(c * rows // 2, rows // 2), p],
-                    wq_buf.at[c, p],
-                    sems.at[c * pairs + p],
-                )
-            )
-    for copy in copies:
+    copies = [
+        pltpu.make_async_copy(wq.at[pl.ds(c * rows, rows)], wq_buf.at[c], sems.at[c])
+        for c in range(parts)
+    ]
+    kv_copy = pltpu.make_async_copy(wkv, wkv_buf, sems.at[parts])
+    cache_copies = tile_copies(cache, 0, cache_tiles, cache_sems)
+    for copy in small + [kv_copy] + copies:
         copy.start()
     for copy in small:
         copy.wait()
     me = lax.axis_index("tp")
     x = states[...].astype(F32)
-    sq_res[...] = jnp.broadcast_to(jnp.sum(x * x, axis=1, keepdims=True), sq_res.shape)
-    rows16 = two_parts(x * gains[0:1, :])
-    spread(rows16, spread_buf, docs)
+    squares = jnp.broadcast_to(jnp.sum(x * x, axis=1, keepdims=True), (docs, LANES))
+    both = jnp.concatenate(two_parts(x * gains[0:1, :]), axis=0)
+    spread_heads(both, spread_buf, heads)
     length = lengths[owner[me]].astype(F32)
     cosine, sine = rope_rows(length, frequency[...])
     table[0:1, :] = cosine
@@ -166,36 +192,26 @@
     for s in range(tp):
         places[s : s + 1, :] = jnp.full((1, LANES), owner[me ^ s], jnp.int32)
     kv_copy.wait()
-    kv_total = jnp.dot(rows16, wkv_buf[...], preferred_element_type=F32)
-    kv_res[...] = kv_total[: 2 * docs] + kv_total[2 * docs :]
-    total = jnp.zeros((4 * docs, pairs * LANES), F32)
-    for c in range(halves):
-        for p in range(pairs):
-            copies[c * pairs + p].wait()
-        if c == 0:
+    kv_total = jnp.dot(both.astype(BF16), wkv_buf[...], preferred_element_type=F32)
+    total = jnp.zeros((heads * 2 * docs, LANES), F32)
+    for c in range(parts):
+        copies[c].wait()
+        if c == parts // 2:
             for copy in cache_copies:
                 copy.start()
-        block = jnp.concatenate(
-            [wq_buf.at[c, p].reshape(rows, LANES)[...] for p in range(pairs)], axis=1
+        total = total + jnp.dot(
+            spread_buf[:, c * rows : (c + 1) * rows], wq_buf[c], preferred_element_type=F32
         )
-        total = total + jnp.dot(
-            spread_buf[:, c * rows : (c + 1) * rows], block, preferred_element_type=F32
-        )
-    res[...] = total[: 2 * docs] + total[2 * docs :]
+    total = total.reshape(heads, 2 * docs, LANES)
     for s in range(tp):
         doc = owner[me ^ s]
-        for parity in range(2):
-            chosen = pick_row(res, parity * docs + doc)
-            for p in range(pairs):
-                outs[s][2 * p + parity : 2 * p + parity + 1, :] = chosen[
-                    :, p * LANES : (p + 1) * LANES
-                ]
-        chosen = pick_row(kv_res, doc)
-        h = 2 * pairs
-        outs[s][h : h + 1, :] = chosen[:, :LANES]
-        outs[s][h + 1 : h + 2, :] = chosen[:, LANES:]
-        outs[s][h + 2 : h + 3, :] = pick_row(sq_res, doc)
-        outs[s][h + 3 :, :] = jnp.zeros((outs[s].shape[0] - h - 3, LANES), F32)
+        out = outs[-s]
+        out[:heads, :] = pick_doc(total, doc, docs)
+        kv_row = pick_doc(kv_total, doc, docs)[None]
+        out[heads : heads + 1, :] = kv_row[:, :LANES]
+        out[heads + 1 : heads + 2, :] = kv_row[:, LANES:]
+        out[heads + 2 : heads + 3, :] = pick_doc(squares, doc, docs)[None]
+        out[heads + 3 :, :] = jnp.zeros((out.shape[0] - heads - 3, LANES), F32)
     for copy in cache_copies:
         copy.wait()
 
@@ -219,9 +235,9 @@
     value = value.astype(F32)
     scale = LANES ** (-0.5)
     own = jnp.sum(query.astype(F32) * key, axis=1, keepdims=True) * scale
-    column = lax.broadcasted_iota(jnp.int32, (heads, rows), 1).astype(F32)
-    length = table[2:3, 0:1]
-    top = own
+    column = lax.broadcasted_iota(jnp.int32, (heads, LANES), 1).astype(F32)
+    length = table[2:3, :]
+    tops = jnp.full((heads, LANES), -jnp.inf, F32)
     for b in range(blocks):
         block = lax.dot_general(
             query,
@@ -229,20 +245,26 @@
             (((1,), (1,)), ((), ())),
             preferred_element_type=F32,
         )
-        block = jnp.where(column < length - b * rows, block * scale, -jnp.inf)
-        top = jnp.maximum(top, jnp.max(block, axis=1, keepdims=True))
-        scores[:, b * rows : (b + 1) * rows] = block
+        for start in range(0, rows, LANES):
+            at = b * rows + start
+            piece = block[:, start : start + LANES] * scale
+            piece = jnp.where(column < length - at, piece, -jnp.inf)
+            tops = jnp.maximum(tops, piece)
+            scores[:, at : at + LANES] = piece
+    top = jnp.maximum(jnp.max(tops, axis=1, keepdims=True), own)
     own = jnp.exp(own - top)
-    total = own
+    sums_by_lane = jnp.zeros((heads, LANES), F32)
     acc = own.astype(BF16).astype(F32) * value
     for b in range(blocks):
         weights = jnp.exp(scores[:, b * rows : (b + 1) * rows] - top)
-        total = total + jnp.sum(weights, axis=1, keepdims=True)
+        for start in range(0, rows, LANES):
+            sums_by_lane = sums_by_lane + weights[:, start : start + LANES]
         acc = acc + jnp.dot(
             weights.astype(BF16),
             cache[1, b * rows : (b + 1) * rows, :],
             preferred_element_type=F32,
         )
+    total = own + jnp.sum(sums_by_lane, axis=1, keepdims=True)
     heads_out[...] = (acc / total).astype(BF16)
     for copy in w_copies:
         copy.wait()
@@ -271,19 +293,24 @@
         copy.wait()
 
 
-def gate_up_kernel(kv, groups, first, states, gains, w, *rest):
+def gate_up_kernel(kv, groups, first, states, gains, w, w_down, *rest):
     ready, parts = rest[:groups], rest[groups : groups + kv]
-    attn_out, partial_out, w_tiles, spread_buf, w_sems = rest[groups + kv :]
+    attn_out, partial_out, *down_tiles = rest[groups + kv : -4]
+    w_tiles, spread_buf, w_sems, down_sems = rest[-4:]
     docs, width = states.shape
     hidden = w.shape[2]
     w_matrix = matrix_of(w)
     for copy in tile_copies(w_matrix, first, w_tiles, w_sems):
         copy.start()
+    down_copies = [c for tiles in down_tiles for c in tile_copies(w_down, 0, tiles, down_sems)]
+    for copy in down_copies:
+        copy.start()
     attn = tree_sum([part[...].astype(F32) for part in parts]).astype(BF16)
     attn_out[...] = attn
     resid = (states[...].astype(F32) + attn.astype(F32)).astype(BF16).astype(F32)
     squares = jnp.sum(resid * resid, axis=1, keepdims=True)
-    spread(two_parts(resid * gains[1:2, :]), spread_buf, docs)
+    high, low = two_parts(resid * gains[1:2, :])
+    spread(jnp.concatenate([high, high, low, low], axis=0).astype(BF16), spread_buf, docs)
 
     def store_from(tile):
         def store(j, product):
@@ -311,13 +338,15 @@
     third = squares - first - second
     terms = jnp.where(lane == 0, first, jnp.where(lane == 1, second, jnp.where(lane == 2, third, 0.0)))
     partial_out[:, hidden:] = jnp.concatenate([terms, terms], axis=0).astype(BF16)
-
-
-def down_kernel(tp, w_down, *rest):
-    parts = rest[:tp]
-    out, act_buf = rest[tp:]
+    for copy in down_copies:
+        copy.wait()
+
+
+def down_kernel(tp, groups, *rest):
+    ready, parts = rest[:groups], rest[groups : groups + tp]
+    out, act_buf = rest[groups + tp :]
     docs = out.shape[0]
-    hidden = w_down.shape[1]
+    hidden = ready[0].shape[1]
     summed = tree_sum([part[...].astype(F32) for part in parts])
     squares = jnp.sum(summed[:docs, hidden:], axis=1, keepdims=True)
     inverse = lax.rsqrt(squares / D + EPS)
@@ -325,11 +354,17 @@
     up = summed[docs:, :hidden] * inverse
     act_buf[...] = (gate / (1.0 + jnp.exp(-gate)) * up).astype(BF16)
 
-    def store(j, product):
-        start = pl.multiple_of(2 * j * LANES, 2 * LANES)
-        out[:, pl.ds(start, 2 * LANES)] = product.astype(BF16)
-
-    times_tiles(act_buf, w_down, store)
+    def store_from(tile):
+        def store(j, product):
+            start = pl.multiple_of((tile + 2 * j) * LANES, 2 * LANES)
+            out[:, pl.ds(start, 2 * LANES)] = product.astype(BF16)
+
+        return store
+
+    tile = 0
+    for group in ready:
+        times_tiles(act_buf, group, store_from(tile))
+        tile += group.shape[0]
 
 
 def cost(micros):
@@ -348,12 +383,11 @@
     heads = w_query.shape[1]
     cache_len = kv_cache.shape[1]
     hidden = w_gate_up.shape[2]
-    wq = w_query.reshape(width, heads // 2, 2, LANES)
+    wq = w_query.reshape(width * heads, LANES)
     wkv = w_keyval.reshape(width, 2 * LANES)
     cache = kv_cache.reshape(cache_len, 2 * LANES)
     packed = 2 * heads
-    pairs = heads // 2
-    halves = 2
+    wq_parts = 4
 
     half = LANES // 2
     freq = ROPE_BASE ** (-(np.arange(half, dtype=np.float64) * 2.0 / LANES))
@@ -374,13 +408,10 @@
             pltpu.VMEM((1, LANES), F32),
             pltpu.VMEM((docs, width), BF16),
             pltpu.VMEM((2, width), F32),
-            pltpu.VMEM((halves, pairs, width // halves, 2, LANES), BF16),
+            pltpu.VMEM((wq_parts, width * heads // wq_parts, LANES), BF16),
             pltpu.VMEM((width, 2 * LANES), BF16),
-            pltpu.VMEM((4 * docs, 2 * width), BF16),
-            pltpu.VMEM((2 * docs, pairs * LANES), F32),
-            pltpu.VMEM((2 * docs, 2 * LANES), F32),
-            pltpu.VMEM((docs, LANES), F32),
-            pltpu.SemaphoreType.DMA((halves * pairs + 1,)),
+            pltpu.VMEM((heads * 2 * docs, width * heads), BF16),
+            pltpu.SemaphoreType.DMA((wq_parts + 1,)),
             pltpu.SemaphoreType.DMA((5,)),
             pltpu.SemaphoreType.DMA((2,)),
         ],
@@ -409,7 +440,7 @@
         )(token, weights)
 
     fetched.append(fetch(w_gu, shares[0], 2 * width, table))
-    qkv_parts = exchange(qkv_parts, "tp", tp)
+    qkv_parts = exchange([qkv_parts[-s] for s in range(tp)], "tp", tp)
     head_out, new_kv, w_ready = pl.pallas_call(
         functools.partial(attend_kernel, tp, heads, 512, shares[1][0]),
         out_shape=[
@@ -444,36 +475,40 @@
 
     fetched.append(fetch(w_gu, shares[3], 2 * width, out_part))
     out_parts = exchange([out_part] * kv, "kv", kv)
-    attn_out, gu_part = pl.pallas_call(
+    down_cut = width // LANES // 4 * 2
+    w_down = in_hbm(w_down)
+    attn_out, gu_part, *down_ready = pl.pallas_call(
         functools.partial(gate_up_kernel, kv, len(fetched), shares[4][0]),
         out_shape=[
             jax.ShapeDtypeStruct((docs, width), BF16),
             jax.ShapeDtypeStruct((2 * docs, hidden + LANES), BF16),
-        ],
-        in_specs=[vmem(), vmem(), hbm()] + [vmem()] * (len(fetched) + kv),
-        out_specs=[vmem(), vmem()],
+        ]
+        + [tiles_of((0, down_cut), hidden)] * (down_cut > 0),
+        in_specs=[vmem(), vmem(), hbm(), hbm()] + [vmem()] * (len(fetched) + kv),
+        out_specs=[vmem()] * (2 + (down_cut > 0)),
         scratch_shapes=[
             tiles_of(shares[4], 2 * width),
             pltpu.VMEM((4 * docs, 2 * width), BF16),
             pltpu.SemaphoreType.DMA((shares[4][1] - shares[4][0],)),
+            pltpu.SemaphoreType.DMA((max(down_cut, 1),)),
         ],
         compiler_params=params(docs, 20),
         cost_estimate=cost(10),
         name="gate_up",
-    )(states, norm_gains, w_gu, *fetched, *out_parts)
-
-    w_down_ready = fetch(in_hbm(w_down), (0, width // LANES), hidden, gu_part)
+    )(states, norm_gains, w_gu, w_down, *fetched, *out_parts)
+
+    down_ready.append(fetch(w_down, (down_cut, width // LANES), hidden, gu_part))
     gu_parts = exchange([gu_part] * tp, "tp", tp)
     ffn_part = pl.pallas_call(
-        functools.partial(down_kernel, tp),
+        functools.partial(down_kernel, tp, len(down_ready)),
         out_shape=jax.ShapeDtypeStruct((docs, width), BF16),
-        in_specs=[vmem()] + [vmem()] * tp,
+        in_specs=[vmem()] * (len(down_ready) + tp),
         out_specs=vmem(),
         scratch_shapes=[pltpu.VMEM((docs, hidden), BF16)],
         compiler_params=params(docs, 6),
         cost_estimate=cost(5),
         name="down",
-    )(w_down_ready, *gu_parts)
+    )(*down_ready, *gu_parts)
     ffn_parts = exchange([ffn_part] * kv, "kv", kv)
     ffn_out = tree_sum([part.astype(F32) for part in ffn_parts]).astype(BF16)
     return attn_out, ffn_out, new_kv.reshape(1, 1, 2 * LANES)

time: 55.9 us -> 56.7 us (1.014)
  waiting for transfers between devices: 5.46 us -> 6.03 us
    pallas_call x1, Pallas kernels: 4.09 us -> 3.4 us  [per_device(): pl.pallas_call(functools.partial(attend_kernel, tp, heads, 512, shares[1]...]
    pallas_call x1, Pallas kernels: 5.98 us -> 6.64 us  [per_device(): pl.pallas_call(functools.partial(gate_up_kernel, kv, len(fetched), shares...]
  transfers between devices with their start and end apart: 15 -> 15, of which waited for: 4 -> 4; matrix products, arithmetic and copies ran while one was open for 0% -> 0% of each run, Pallas kernels for 21% -> 20%
where the time goes in v6:
time: 56.7 us; the launch traced here: 56.5 us
  Pallas kernels  30.7 us (54%)
  starting transfers between devices  18.3 us (32%)
  waiting for transfers between devices  6.03 us (11%)
  between operations  0.81 us (1%)
  other arithmetic  0.63 us (1%)
    ppermute x15, starting transfers between devices, exchange(): lax.ppermute(arrays[s], axis, [(i, i ^ s) for i in range(size)])  18.3 us
    pallas_call x4, Pallas kernels, fetch(): pl.pallas_call(functools.partial(fetch_kernel, share[0]), out_shape=tiles...  11.4 us
    pallas_call x1, Pallas kernels, per_device(): pl.pallas_call(functools.partial(gate_up_kernel, kv, len(fetched), shares...  6.64 us
    ppermute x15, waiting for transfers between devices, exchange(): lax.ppermute(arrays[s], axis, [(i, i ^ s) for i in range(size)])  6.03 us
    pallas_call x1, Pallas kernels, per_device(): pl.pallas_call(functools.partial(qkv_kernel, tp), out_shape=[jax.ShapeDty...  5.56 us
    pallas_call x1, Pallas kernels, per_device(): pl.pallas_call(functools.partial(attend_kernel, tp, heads, 512, shares[1]...  3.4 us
    pallas_call x1, Pallas kernels, per_device(): pl.pallas_call(functools.partial(down_kernel, tp, len(down_ready)), out_s...  3.02 us
  transfers between devices with their start and end apart: 15, of which 4 were waited for; matrix products, arithmetic and copies ran while one was open for 0% of the time, Pallas kernels for 20%

profile of v6, /device:TPU:0, one launch (start us, length us, event | category | flops | bytes accessed | tf_op | source)
XLA Modules:
  0.0 56.5 jit_solution(13481842323458130821)
XLA Ops:
  0.6 5.6 %qkv.1 = (f32[16,128]{1,0:T(8,128)S(1)}, f32[16,128]{1,0:T(8,128)S(1)}, f32[16,128]{1,0:T(8,128)S(1)}, f32[16,128]{1,0:T(8,128)S(1)}, f32[8,128]{1,0:T(8,128)S(1...) custom-call(s32[4]{0:T(128)} %owner_hbm.1, s32[4]{0:T(128)} %lengths_hbm.1, ...), custom_call_target="tpu_custom_call" | custom-call | bytes 29520000 | tf_op jit(solution)/shard_map/qkv/pallas_call | solution.py:395
  6.2 3.1 %collective-permute-start = (f32[16,128]{1,0:T(8,128)S(1)}, f32[16,128]{1,0:T(8,128)S(1)}, u32[]{:S(2)}, u32[]{:S(2)}) collective-permute-start(f32[16,128]{1,0:T(8,128)S(1)} %get-tuple-element.19), channel_id=1, source_target_pairs={{0,4},{4,0},{8,12},{12,8},{1,5},{5,1},{9,13},{13,9},{2,6},{6,2},{1... | collective-permute-start | bytes 24584 | tf_op jit(solution)/shard_map/ppermute | solution.py:39
  9.3 2.6 %collective-permute-start.1 = (f32[16,128]{1,0:T(8,128)S(1)}, f32[16,128]{1,0:T(8,128)S(1)}, u32[]{:S(2)}, u32[]{:S(2)}) collective-permute-start(f32[16,128]{1,0:T(8,128)S(1)} %get-tuple-element.20), channel_id=1, source_target_pairs={{0,8},{4,12},{8,0},{12,4},{1,9},{5,13},{9,1},{13,5},{2,10},{6,14},... | collective-permute-start | bytes 24584 | tf_op jit(solution)/shard_map/ppermute | solution.py:39
  11.9 2.9 %fetch.4.rest_4_.rest_0_ = bf16[6,4096,128]{2,1,0:T(8,128)(2,1)S(1)} custom-call(f32[8,128]{1,0:T(8,128)S(1)} %get-tuple-element.16.token.table, bf16[2048,2,3584]{2,1,0:T(2,128)(2,1)} %w.10), custom_call_target="tpu_custom_call" | custom-call | bytes 6641999 | tf_op jit(solution)/shard_map/fetch/pallas_call | solution.py:431
  14.8 0.0 collective-permute-done.rest_1_
  14.8 2.5 %collective-permute-done.2.rest_3_ = f32[16,128]{1,0:T(8,128)S(1)} collective-permute-done((f32[16,128]{1,0:T(8,128)S(1)}, f32[16,128]{1,0:T(8,128)S(1)}, u32[]{:S(2)}, u32[]{:S(2)}) %collective-permute-start.2) | collective-permute-done | bytes 8224 | tf_op jit(solution)/shard_map/ppermute | solution.py:39
  17.3 3.4 %attend.1 = (bf16[8,128]{1,0:T(8,128)(2,1)S(1)}, bf16[1,256]{1,0:T(2,128)(2,1)}, bf16[4,4096,128]{2,1,0:T(8,128)(2,1)S(1)}) custom-call(f32[8,128]{1,0:T(8,128)S(1)} %get-tuple-element.16.token.table, bf16[2,8192,128]{2,1,0:T(8,128)(2,1)S(1)} %get-tuple-element.17.cache, bf16[2048,2,3584]{2,1,0:T(2,128)(2,1)} %w.10, ...), custom_call_target="tpu_custom_call" | custom-call | bytes 29520000 | tf_op jit(solution)/shard_map/attend/pallas_call | solution.py:444
  20.7 0.0 copy-start
  20.7 1.4 %collective-permute-start.5 = (bf16[8,128]{1,0:T(8,128)(2,1)S(1)}, bf16[8,128]{1,0:T(8,128)(2,1)S(1)}, u32[]{:S(2)}, u32[]{:S(2)}) collective-permute-start(bf16[8,128]{1,0:T(8,128)(2,1)S(1)} %get-tuple-element.23.token.rest_0_), channel_id=1, source_target_pairs={{0,12},{4,8},{8,4},{12,0},{1,13},{5,9},{9,5},{13,1},{2,14},{6,10},... | collective-permute-start | bytes 6152 | tf_op jit(solution)/shard_map/ppermute | solution.py:39
  22.2 3.0 %collective-permute-start.3 = (bf16[8,128]{1,0:T(8,128)(2,1)S(1)}, bf16[8,128]{1,0:T(8,128)(2,1)S(1)}, u32[]{:S(2)}, u32[]{:S(2)}) collective-permute-start(bf16[8,128]{1,0:T(8,128)(2,1)S(1)} %get-tuple-element.23.token.rest_0_), channel_id=1, source_target_pairs={{0,4},{4,0},{8,12},{12,8},{1,5},{5,1},{9,13},{13,9},{2,6},{6,2},{1... | collective-permute-start | bytes 6152 | tf_op jit(solution)/shard_map/ppermute | solution.py:39
  25.2 2.9 %fetch.5.rest_4_.rest_2_ = bf16[6,4096,128]{2,1,0:T(8,128)(2,1)S(1)} custom-call(bf16[8,128]{1,0:T(8,128)(2,1)S(1)} %get-tuple-element.23.token.rest_0_, bf16[2048,2,3584]{2,1,0:T(2,128)(2,1)} %w.10), custom_call_target="tpu_custom_call" | custom-call | bytes 6641999 | tf_op jit(solution)/shard_map/fetch/pallas_call | solution.py:431
  28.1 0.0 collective-permute-done.5.rest_3_
  28.1 0.0 collective-permute-done.4.rest_2_
  28.2 0.7 %attn_project.1.token.rest_4_ = bf16[4,2048]{1,0:T(4,128)(2,1)S(1)} custom-call(s32[8,128]{1,0:T(8,128)S(1)} %get-tuple-element.24.places, bf16[1024,2048]{1,0:T(8,128)(2,1)S(1)} %copy-done, bf16[8,128]{1,0:T(8,128)(2,1)S(1)} %get-tuple-element.23.token.rest_0_, bf16[8,128]{1,0:T(8,128)(2,1)S(1)} %collective-permute-done.3.rest_1_, ...), custom_call_target="tpu_custom_call" | custom-call | bytes 22140000 | tf_op jit(solution)/shard_map/attn_project/pallas_call | solution.py:465
  28.8 0.0 collective-permute-start.8
  28.9 1.6 %collective-permute-start.7 = (bf16[4,2048]{1,0:T(4,128)(2,1)S(1)}, bf16[4,2048]{1,0:T(4,128)(2,1)S(1)}, u32[]{:S(2)}, u32[]{:S(2)}) collective-permute-start(bf16[4,2048]{1,0:T(4,128)(2,1)S(1)} %attn_project.1.token.rest_4_), channel_id=1, source_target_pairs={{0,2},{1,3},{2,0},{3,1},{4,6},{5,7},{6,4},{7,5},{8,10},{9,11},{10,... | collective-permute-start | bytes 49160 | tf_op jit(solution)/shard_map/ppermute | solution.py:39
  30.4 0.3 collective-permute-start.6
  30.7 2.3 %fetch.6.rest_3_ = bf16[4,4096,128]{2,1,0:T(8,128)(2,1)S(1)} custom-call(bf16[4,2048]{1,0:T(4,128)(2,1)S(1)} %attn_project.1.token.rest_4_, bf16[2048,2,3584]{2,1,0:T(2,128)(2,1)} %w.10), custom_call_target="tpu_custom_call" | custom-call | bytes 4428000 | tf_op jit(solution)/shard_map/fetch/pallas_call | solution.py:431
  33.0 0.0 collective-permute-done.7.rest_6_
  33.0 6.6 %gate_up.1 = (bf16[4,2048]{1,0:T(4,128)(2,1)}, bf16[8,3712]{1,0:T(8,128)(2,1)S(1)}, bf16[8,3584,128]{2,1,0:T(8,128)(2,1)S(1)}) custom-call(bf16[4,2048]{1,0:T(4,128)(2,1)S(1)} %copy-done.1, f32[2,2048]{1,0:T(2,128)S(1)} %copy-done.2, bf16[2048,2,3584]{2,1,0:T(2,128)(2,1)} %w.10, bf16[3584,2048]{1,0:T(8,128)(2,1)} %w.11, ...), custom_call_target="tpu_custom_call" | custom-call | bytes 36900000 | tf_op jit(solution)/shard_map/gate_up/pallas_call | solution.py:480
  39.7 1.4 %collective-permute-start.11 = (bf16[8,3712]{1,0:T(8,128)(2,1)S(1)}, bf16[8,3712]{1,0:T(8,128)(2,1)S(1)}, u32[]{:S(2)}, u32[]{:S(2)}) collective-permute-start(bf16[8,3712]{1,0:T(8,128)(2,1)S(1)} %get-tuple-element.27.token.rest_2_), channel_id=1, source_target_pairs={{0,12},{4,8},{8,4},{12,0},{1,13},{5,9},{9,5},{13,1},{2,14},{6,10},... | collective-permute-start | bytes 178184 | tf_op jit(solution)/shard_map/ppermute | solution.py:39
  41.1 0.7 %collective-permute-start.10 = (bf16[8,3712]{1,0:T(8,128)(2,1)S(1)}, bf16[8,3712]{1,0:T(8,128)(2,1)S(1)}, u32[]{:S(2)}, u32[]{:S(2)}) collective-permute-start(bf16[8,3712]{1,0:T(8,128)(2,1)S(1)} %get-tuple-element.27.token.rest_2_), channel_id=1, source_target_pairs={{0,8},{4,12},{8,0},{12,4},{1,9},{5,13},{9,1},{13,5},{2,10},{6,14},... | collective-permute-start | bytes 178184 | tf_op jit(solution)/shard_map/ppermute | solution.py:39
  41.8 2.3 %collective-permute-start.9 = (bf16[8,3712]{1,0:T(8,128)(2,1)S(1)}, bf16[8,3712]{1,0:T(8,128)(2,1)S(1)}, u32[]{:S(2)}, u32[]{:S(2)}) collective-permute-start(bf16[8,3712]{1,0:T(8,128)(2,1)S(1)} %get-tuple-element.27.token.rest_2_), channel_id=1, source_target_pairs={{0,4},{4,0},{8,12},{12,8},{1,5},{5,1},{9,13},{13,9},{2,6},{6,2},{1... | collective-permute-start | bytes 178184 | tf_op jit(solution)/shard_map/ppermute | solution.py:39
  44.1 3.3 %fetch.7.rest_1_ = bf16[8,3584,128]{2,1,0:T(8,128)(2,1)S(1)} custom-call(bf16[8,3712]{1,0:T(8,128)(2,1)S(1)} %get-tuple-element.27.token.rest_2_, bf16[3584,2048]{1,0:T(8,128)(2,1)} %w.11), custom_call_target="tpu_custom_call" | custom-call | bytes 8856000 | tf_op jit(solution)/shard_map/fetch/pallas_call | solution.py:431
  47.4 0.7 %collective-permute-done.10.rest_4_ = bf16[8,3712]{1,0:T(8,128)(2,1)S(1)} collective-permute-done((bf16[8,3712]{1,0:T(8,128)(2,1)S(1)}, bf16[8,3712]{1,0:T(8,128)(2,1)S(1)}, u32[]{:S(2)}, u32[]{:S(2)}) %collective-permute-start.10) | collective-permute-done | bytes 59424 | tf_op jit(solution)/shard_map/ppermute | solution.py:39
  48.2 3.0 %down.1 = bf16[4,2048]{1,0:T(4,128)(2,1)S(1)} custom-call(bf16[8,3584,128]{2,1,0:T(8,128)(2,1)S(1)} %get-tuple-element.26.rest_0_, bf16[8,3584,128]{2,1,0:T(8,128)(2,1)S(1)} %fetch.7.rest_1_, bf16[8,3712]{1,0:T(8,128)(2,1)S(1)} %get-tuple-element.27.token.rest_2_, bf16[8,3712]{1,0:T(8,128)(2,1)S(1)} %collective-permute-done.9.rest_3_, ...), custom_call_target="tpu_custom_call" | custom-call | bytes 18450000 | tf_op jit(solution)/shard_map/down/pallas_call | solution.py:502
  51.2 0.9 %collective-permute-start.14 = (bf16[4,2048]{1,0:T(4,128)(2,1)S(1)}, bf16[4,2048]{1,0:T(4,128)(2,1)S(1)}, u32[]{:S(2)}, u32[]{:S(2)}) collective-permute-start(bf16[4,2048]{1,0:T(4,128)(2,1)S(1)} %down.1), channel_id=1, source_target_pairs={{0,3},{1,2},{2,1},{3,0},{4,7},{5,6},{6,5},{7,4},{8,11},{9,10},{10,... | collective-permute-start | bytes 49160 | tf_op jit(solution)/shard_map/ppermute | solution.py:39
  52.1 0.7 %collective-permute-start.13 = (bf16[4,2048]{1,0:T(4,128)(2,1)S(1)}, bf16[4,2048]{1,0:T(4,128)(2,1)S(1)}, u32[]{:S(2)}, u32[]{:S(2)}) collective-permute-start(bf16[4,2048]{1,0:T(4,128)(2,1)S(1)} %down.1), channel_id=1, source_target_pairs={{0,2},{1,3},{2,0},{3,1},{4,6},{5,7},{6,4},{7,5},{8,10},{9,11},{10,... | collective-permute-start | bytes 49160 | tf_op jit(solution)/shard_map/ppermute | solution.py:39
  52.8 0.2 collective-permute-start.12
  53.1 1.3 %collective-permute-done.14 = bf16[4,2048]{1,0:T(4,128)(2,1)S(1)} collective-permute-done((bf16[4,2048]{1,0:T(4,128)(2,1)S(1)}, bf16[4,2048]{1,0:T(4,128)(2,1)S(1)}, u32[]{:S(2)}, u32[]{:S(2)}) %collective-permute-start.14) | collective-permute-done | bytes 16416 | tf_op jit(solution)/shard_map/ppermute | solution.py:39
  54.4 1.5 %collective-permute-done.13 = bf16[4,2048]{1,0:T(4,128)(2,1)S(1)} collective-permute-done((bf16[4,2048]{1,0:T(4,128)(2,1)S(1)}, bf16[4,2048]{1,0:T(4,128)(2,1)S(1)}, u32[]{:S(2)}, u32[]{:S(2)}) %collective-permute-start.13) | collective-permute-done | bytes 16416 | tf_op jit(solution)/shard_map/ppermute | solution.py:39
  55.8 0.6 %add_convert_fusion = bf16[4,2048]{1,0:T(4,128)(2,1)} fusion(bf16[4,2048]{1,0:T(4,128)(2,1)S(1)} %collective-permute-done.14, bf16[4,2048]{1,0:T(4,128)(2,1)S(1)} %collective-permute-done.13, bf16[4,2048]{1,0:T(4,128)(2,1)S(1)} %collective-permute-done.12, bf16[4,2048]{1,0:T(4,128)(2,1)S(1)} %down.1), kind=kLoop, calls=%fused_computation | loop fusion | flops 65536 | bytes 81920 | tf_op jit(solution)/shard_map/convert_element_type | solution.py:513
  (14 shorter events, 0.0 us)
Async XLA Ops:
  6.2 8.6 %collective-permute-start = (f32[16,128]{1,0:T(8,128)S(1)}, f32[16,128]{1,0:T(8,128)S(1)}, u32[]{:S(2)}, u32[]{:S(2)}) collective-permute-start(f32[16,128]{1,0:T(8,128)S(1)} %get-tuple-element.19), channel_id=1, source_target_pairs={{0,4},{4,0},{8,12},{12,8},{1,5},{5,1},{9,13},{13,9},{2,6},{6,2},{1... | collective-permute-start | bytes 24584 | tf_op jit(solution)/shard_map/ppermute | solution.py:39
  9.3 5.5 %collective-permute-start.1 = (f32[16,128]{1,0:T(8,128)S(1)}, f32[16,128]{1,0:T(8,128)S(1)}, u32[]{:S(2)}, u32[]{:S(2)}) collective-permute-start(f32[16,128]{1,0:T(8,128)S(1)} %get-tuple-element.20), channel_id=1, source_target_pairs={{0,8},{4,12},{8,0},{12,4},{1,9},{5,13},{9,1},{13,5},{2,10},{6,14},... | collective-permute-start | bytes 24584 | tf_op jit(solution)/shard_map/ppermute | solution.py:39
  11.9 5.4 %collective-permute-start.2 = (f32[16,128]{1,0:T(8,128)S(1)}, f32[16,128]{1,0:T(8,128)S(1)}, u32[]{:S(2)}, u32[]{:S(2)}) collective-permute-start(f32[16,128]{1,0:T(8,128)S(1)} %get-tuple-element.21), channel_id=1, source_target_pairs={{0,12},{4,8},{8,4},{12,0},{1,13},{5,9},{9,5},{13,1},{2,14},{6,10},... | collective-permute-start | bytes 24584 | tf_op jit(solution)/shard_map/ppermute | solution.py:39
  20.7 7.4 %copy-start = (bf16[1024,2048]{1,0:T(8,128)(2,1)S(1)}, bf16[1024,2048]{1,0:T(8,128)(2,1)}, u32[]{:S(2)}) copy-start(bf16[1024,2048]{1,0:T(8,128)(2,1)} %w_out.1) | copy-start | bytes 12582916
  20.7 7.4 %collective-permute-start.5 = (bf16[8,128]{1,0:T(8,128)(2,1)S(1)}, bf16[8,128]{1,0:T(8,128)(2,1)S(1)}, u32[]{:S(2)}, u32[]{:S(2)}) collective-permute-start(bf16[8,128]{1,0:T(8,128)(2,1)S(1)} %get-tuple-element.23.token.rest_0_), channel_id=1, source_target_pairs={{0,12},{4,8},{8,4},{12,0},{1,13},{5,9},{9,5},{13,1},{2,14},{6,10},... | collective-permute-start | bytes 6152 | tf_op jit(solution)/shard_map/ppermute | solution.py:39
  22.2 6.0 %collective-permute-start.4 = (bf16[8,128]{1,0:T(8,128)(2,1)S(1)}, bf16[8,128]{1,0:T(8,128)(2,1)S(1)}, u32[]{:S(2)}, u32[]{:S(2)}) collective-permute-start(bf16[8,128]{1,0:T(8,128)(2,1)S(1)} %get-tuple-element.23.token.rest_0_), channel_id=1, source_target_pairs={{0,8},{4,12},{8,0},{12,4},{1,9},{5,13},{9,1},{13,5},{2,10},{6,14},... | collective-permute-start | bytes 6152 | tf_op jit(solution)/shard_map/ppermute | solution.py:39
  22.2 6.0 %collective-permute-start.3 = (bf16[8,128]{1,0:T(8,128)(2,1)S(1)}, bf16[8,128]{1,0:T(8,128)(2,1)S(1)}, u32[]{:S(2)}, u32[]{:S(2)}) collective-permute-start(bf16[8,128]{1,0:T(8,128)(2,1)S(1)} %get-tuple-element.23.token.rest_0_), channel_id=1, source_target_pairs={{0,4},{4,0},{8,12},{12,8},{1,5},{5,1},{9,13},{13,9},{2,6},{6,2},{1... | collective-permute-start | bytes 6152 | tf_op jit(solution)/shard_map/ppermute | solution.py:39
  28.8 4.2 %copy-start.1 = (bf16[4,2048]{1,0:T(4,128)(2,1)S(1)}, bf16[4,2048]{1,0:T(4,128)(2,1)}, u32[]{:S(2)}) copy-start(bf16[4,2048]{1,0:T(4,128)(2,1)} %states.1) | copy-start | bytes 49156
  28.8 4.2 %copy-start.2 = (f32[2,2048]{1,0:T(2,128)S(1)}, f32[2,2048]{1,0:T(2,128)}, u32[]{:S(2)}) copy-start(f32[2,2048]{1,0:T(2,128)} %gains.1) | copy-start | bytes 49156
  28.8 4.1 %collective-permute-start.8 = (bf16[4,2048]{1,0:T(4,128)(2,1)S(1)}, bf16[4,2048]{1,0:T(4,128)(2,1)S(1)}, u32[]{:S(2)}, u32[]{:S(2)}) collective-permute-start(bf16[4,2048]{1,0:T(4,128)(2,1)S(1)} %attn_project.1.token.rest_4_), channel_id=1, source_target_pairs={{0,3},{1,2},{2,1},{3,0},{4,7},{5,6},{6,5},{7,4},{8,11},{9,10},{10,... | collective-permute-start | bytes 49160 | tf_op jit(solution)/shard_map/ppermute | solution.py:39
  28.9 4.1 %collective-permute-start.7 = (bf16[4,2048]{1,0:T(4,128)(2,1)S(1)}, bf16[4,2048]{1,0:T(4,128)(2,1)S(1)}, u32[]{:S(2)}, u32[]{:S(2)}) collective-permute-start(bf16[4,2048]{1,0:T(4,128)(2,1)S(1)} %attn_project.1.token.rest_4_), channel_id=1, source_target_pairs={{0,2},{1,3},{2,0},{3,1},{4,6},{5,7},{6,4},{7,5},{8,10},{9,11},{10,... | collective-permute-start | bytes 49160 | tf_op jit(solution)/shard_map/ppermute | solution.py:39
  30.4 2.6 %collective-permute-start.6 = (bf16[4,2048]{1,0:T(4,128)(2,1)S(1)}, bf16[4,2048]{1,0:T(4,128)(2,1)S(1)}, u32[]{:S(2)}, u32[]{:S(2)}) collective-permute-start(bf16[4,2048]{1,0:T(4,128)(2,1)S(1)} %attn_project.1.token.rest_4_), channel_id=1, source_target_pairs={{0,1},{1,0},{2,3},{3,2},{4,5},{5,4},{6,7},{7,6},{8,9},{9,8},{10,11... | collective-permute-start | bytes 49160 | tf_op jit(solution)/shard_map/ppermute | solution.py:39
  39.7 7.7 %collective-permute-start.11 = (bf16[8,3712]{1,0:T(8,128)(2,1)S(1)}, bf16[8,3712]{1,0:T(8,128)(2,1)S(1)}, u32[]{:S(2)}, u32[]{:S(2)}) collective-permute-start(bf16[8,3712]{1,0:T(8,128)(2,1)S(1)} %get-tuple-element.27.token.rest_2_), channel_id=1, source_target_pairs={{0,12},{4,8},{8,4},{12,0},{1,13},{5,9},{9,5},{13,1},{2,14},{6,10},... | collective-permute-start | bytes 178184 | tf_op jit(solution)/shard_map/ppermute | solution.py:39
  41.1 7.1 %collective-permute-start.10 = (bf16[8,3712]{1,0:T(8,128)(2,1)S(1)}, bf16[8,3712]{1,0:T(8,128)(2,1)S(1)}, u32[]{:S(2)}, u32[]{:S(2)}) collective-permute-start(bf16[8,3712]{1,0:T(8,128)(2,1)S(1)} %get-tuple-element.27.token.rest_2_), channel_id=1, source_target_pairs={{0,8},{4,12},{8,0},{12,4},{1,9},{5,13},{9,1},{13,5},{2,10},{6,14},... | collective-permute-start | bytes 178184 | tf_op jit(solution)/shard_map/ppermute | solution.py:39
  41.8 6.4 %collective-permute-start.9 = (bf16[8,3712]{1,0:T(8,128)(2,1)S(1)}, bf16[8,3712]{1,0:T(8,128)(2,1)S(1)}, u32[]{:S(2)}, u32[]{:S(2)}) collective-permute-start(bf16[8,3712]{1,0:T(8,128)(2,1)S(1)} %get-tuple-element.27.token.rest_2_), channel_id=1, source_target_pairs={{0,4},{4,0},{8,12},{12,8},{1,5},{5,1},{9,13},{13,9},{2,6},{6,2},{1... | collective-permute-start | bytes 178184 | tf_op jit(solution)/shard_map/ppermute | solution.py:39
  51.2 3.2 %collective-permute-start.14 = (bf16[4,2048]{1,0:T(4,128)(2,1)S(1)}, bf16[4,2048]{1,0:T(4,128)(2,1)S(1)}, u32[]{:S(2)}, u32[]{:S(2)}) collective-permute-start(bf16[4,2048]{1,0:T(4,128)(2,1)S(1)} %down.1), channel_id=1, source_target_pairs={{0,3},{1,2},{2,1},{3,0},{4,7},{5,6},{6,5},{7,4},{8,11},{9,10},{10,... | collective-permute-start | bytes 49160 | tf_op jit(solution)/shard_map/ppermute | solution.py:39
  52.1 3.7 %collective-permute-start.13 = (bf16[4,2048]{1,0:T(4,128)(2,1)S(1)}, bf16[4,2048]{1,0:T(4,128)(2,1)S(1)}, u32[]{:S(2)}, u32[]{:S(2)}) collective-permute-start(bf16[4,2048]{1,0:T(4,128)(2,1)S(1)} %down.1), channel_id=1, source_target_pairs={{0,2},{1,3},{2,0},{3,1},{4,6},{5,7},{6,4},{7,5},{8,10},{9,11},{10,... | collective-permute-start | bytes 49160 | tf_op jit(solution)/shard_map/ppermute | solution.py:39
  52.8 3.0 %collective-permute-start.12 = (bf16[4,2048]{1,0:T(4,128)(2,1)S(1)}, bf16[4,2048]{1,0:T(4,128)(2,1)S(1)}, u32[]{:S(2)}, u32[]{:S(2)}) collective-permute-start(bf16[4,2048]{1,0:T(4,128)(2,1)S(1)} %down.1), channel_id=1, source_target_pairs={{0,1},{1,0},{2,3},{3,2},{4,5},{5,4},{6,7},{7,6},{8,9},{9,8},{10,11... | collective-permute-start | bytes 49160 | tf_op jit(solution)/shard_map/ppermute | solution.py:39

commit v7 on v6

--- a/solution.py
+++ b/solution.py
@@ -14,7 +14,7 @@
 ROPE_BASE = 500000.0
 LANES = 128
 MIB = 1 << 20
-GU_SHARES = (6, 4, 6, 4, 8)
+GU_SHARES = (4, 4, 4, 2, 14)
 F32 = jnp.float32
 BF16 = jnp.bfloat16
 QUARTER = (1.5703125, 4.837512969970703125e-4, 7.549789948768648e-8)
@@ -35,11 +35,10 @@
 
 
 def exchange(arrays, axis, size):
-    got = [
+    return [arrays[0]] + [
         lax.ppermute(arrays[s], axis, [(i, i ^ s) for i in range(size)])
-        for s in reversed(range(1, size))
+        for s in range(1, size)
     ]
-    return [arrays[0]] + got[::-1]
 
 
 def tree_sum(parts):
@@ -58,7 +57,7 @@
     pick = one_hot_spread(2)
     row = lax.broadcasted_iota(jnp.int32, (4 * docs, 2 * LANES), 0)
     lane = lax.broadcasted_iota(jnp.int32, (4 * docs, 2 * LANES), 1)
-    keep = lax.rem(lax.div(row, docs), 2) == lax.rem(lane, 2)
+    keep = (lax.shift_right_logical(row, docs.bit_length() - 1) & 1) == (lane & 1)
     chunks = width // LANES
     stacked = jnp.concatenate(
         [rows16[:, c * LANES : (c + 1) * LANES] for c in range(chunks)], axis=0
@@ -97,7 +96,7 @@
 def pick_doc(value, doc, docs):
     axis = value.ndim - 2
     row = lax.broadcasted_iota(jnp.int32, value.shape, axis)
-    return jnp.sum(jnp.where(lax.rem(row, docs) == doc, value, 0.0), axis=axis)
+    return jnp.sum(jnp.where(row & (docs - 1) == doc, value, 0.0), axis=axis)
 
 
 def sine_cosine(angle):
@@ -126,7 +125,7 @@
 def one_hot_spread(fold):
     source = lax.broadcasted_iota(jnp.int32, (LANES, fold * LANES), 0)
     target = lax.broadcasted_iota(jnp.int32, (LANES, fold * LANES), 1)
-    return (lax.div(target, fold) == source).astype(F32).astype(BF16)
+    return (lax.shift_right_logical(target, fold.bit_length() - 1) == source).astype(F32).astype(BF16)
 
 
 def spread_heads(rows, out_ref, heads):
@@ -135,7 +134,7 @@
     stacked = jnp.concatenate([rows[:, c * LANES : (c + 1) * LANES] for c in range(chunks)], axis=0)
     wide = jnp.dot(stacked.astype(BF16), one_hot_spread(heads), preferred_element_type=F32)
     columns = heads * LANES
-    lane = lax.rem(lax.broadcasted_iota(jnp.int32, (count, columns), 1), heads)
+    lane = lax.broadcasted_iota(jnp.int32, (count, columns), 1) & (heads - 1)
     for c in range(chunks):
         piece = wide[c * count : (c + 1) * count]
         for h in range(0, heads, 2):
@@ -293,17 +292,13 @@
         copy.wait()
 
 
-def gate_up_kernel(kv, groups, first, states, gains, w, w_down, *rest):
+def gate_up_kernel(kv, groups, first, states, gains, w, *rest):
     ready, parts = rest[:groups], rest[groups : groups + kv]
-    attn_out, partial_out, *down_tiles = rest[groups + kv : -4]
-    w_tiles, spread_buf, w_sems, down_sems = rest[-4:]
+    attn_out, partial_out, w_tiles, spread_buf, w_sems = rest[groups + kv :]
     docs, width = states.shape
     hidden = w.shape[2]
     w_matrix = matrix_of(w)
     for copy in tile_copies(w_matrix, first, w_tiles, w_sems):
-        copy.start()
-    down_copies = [c for tiles in down_tiles for c in tile_copies(w_down, 0, tiles, down_sems)]
-    for copy in down_copies:
         copy.start()
     attn = tree_sum([part[...].astype(F32) for part in parts]).astype(BF16)
     attn_out[...] = attn
@@ -338,15 +333,13 @@
     third = squares - first - second
     terms = jnp.where(lane == 0, first, jnp.where(lane == 1, second, jnp.where(lane == 2, third, 0.0)))
     partial_out[:, hidden:] = jnp.concatenate([terms, terms], axis=0).astype(BF16)
-    for copy in down_copies:
-        copy.wait()
-
-
-def down_kernel(tp, groups, *rest):
-    ready, parts = rest[:groups], rest[groups : groups + tp]
-    out, act_buf = rest[groups + tp :]
-    docs = out.shape[0]
-    hidden = ready[0].shape[1]
+
+
+def down_kernel(tp, w_down, *rest):
+    parts = rest[:tp]
+    out, act_buf = rest[tp:]
+    docs, width = out.shape
+    hidden = w_down.shape[0]
     summed = tree_sum([part[...].astype(F32) for part in parts])
     squares = jnp.sum(summed[:docs, hidden:], axis=1, keepdims=True)
     inverse = lax.rsqrt(squares / D + EPS)
@@ -354,17 +347,13 @@
     up = summed[docs:, :hidden] * inverse
     act_buf[...] = (gate / (1.0 + jnp.exp(-gate)) * up).astype(BF16)
 
-    def store_from(tile):
-        def store(j, product):
-            start = pl.multiple_of((tile + 2 * j) * LANES, 2 * LANES)
-            out[:, pl.ds(start, 2 * LANES)] = product.astype(BF16)
-
-        return store
-
-    tile = 0
-    for group in ready:
-        times_tiles(act_buf, group, store_from(tile))
-        tile += group.shape[0]
+    def step(j, carry):
+        columns = pl.ds(pl.multiple_of(2 * j * LANES, 2 * LANES), 2 * LANES)
+        product = jnp.dot(act_buf[...], w_down[:, columns], preferred_element_type=F32)
+        out[:, columns] = product.astype(BF16)
+        return carry
+
+    lax.fori_loop(0, width // (2 * LANES), step, 0)
 
 
 def cost(micros):
@@ -475,40 +464,35 @@
 
     fetched.append(fetch(w_gu, shares[3], 2 * width, out_part))
     out_parts = exchange([out_part] * kv, "kv", kv)
-    down_cut = width // LANES // 4 * 2
-    w_down = in_hbm(w_down)
-    attn_out, gu_part, *down_ready = pl.pallas_call(
+    attn_out, gu_part = pl.pallas_call(
         functools.partial(gate_up_kernel, kv, len(fetched), shares[4][0]),
         out_shape=[
             jax.ShapeDtypeStruct((docs, width), BF16),
             jax.ShapeDtypeStruct((2 * docs, hidden + LANES), BF16),
-        ]
-        + [tiles_of((0, down_cut), hidden)] * (down_cut > 0),
-        in_specs=[vmem(), vmem(), hbm(), hbm()] + [vmem()] * (len(fetched) + kv),
-        out_specs=[vmem()] * (2 + (down_cut > 0)),
+        ],
+        in_specs=[vmem(), vmem(), hbm()] + [vmem()] * (len(fetched) + kv),
+        out_specs=[vmem()] * 2,
         scratch_shapes=[
             tiles_of(shares[4], 2 * width),
             pltpu.VMEM((4 * docs, 2 * width), BF16),
             pltpu.SemaphoreType.DMA((shares[4][1] - shares[4][0],)),
-            pltpu.SemaphoreType.DMA((max(down_cut, 1),)),
         ],
         compiler_params=params(docs, 20),
         cost_estimate=cost(10),
         name="gate_up",
-    )(states, norm_gains, w_gu, w_down, *fetched, *out_parts)
-
-    down_ready.append(fetch(w_down, (down_cut, width // LANES), hidden, gu_part))
+    )(states, norm_gains, w_gu, *fetched, *out_parts)
+
     gu_parts = exchange([gu_part] * tp, "tp", tp)
     ffn_part = pl.pallas_call(
-        functools.partial(down_kernel, tp, len(down_ready)),
+        functools.partial(down_kernel, tp),
         out_shape=jax.ShapeDtypeStruct((docs, width), BF16),
-        in_specs=[vmem()] * (len(down_ready) + tp),
+        in_specs=[vmem()] * (1 + tp),
         out_specs=vmem(),
         scratch_shapes=[pltpu.VMEM((docs, hidden), BF16)],
         compiler_params=params(docs, 6),
         cost_estimate=cost(5),
         name="down",
-    )(*down_ready, *gu_parts)
+    )(w_down, *gu_parts)
     ffn_parts = exchange([ffn_part] * kv, "kv", kv)
     ffn_out = tree_sum([part.astype(F32) for part in ffn_parts]).astype(BF16)
     return attn_out, ffn_out, new_kv.reshape(1, 1, 2 * LANES)

time: 56.7 us -> 55.3 us (0.975)
  Pallas kernels: 30.7 us -> 25 us
  waiting for transfers between devices: 6.03 us -> 10.2 us
    pallas_call x4 -> x3, Pallas kernels: 11.4 us -> 6.1 us  [fetch(): pl.pallas_call(functools.partial(fetch_kernel, share[0]), out_shape=tiles...]
    ppermute x15, waiting for transfers between devices: 6.03 us -> 10.2 us  [exchange(): lax.ppermute(arrays[s], axis, [(i, i ^ s) for i in range(size)])]
  transfers between devices with their start and end apart: 15 -> 15, of which waited for: 4 -> 6; matrix products, arithmetic and copies ran while one was open for 0% -> 0% of each run, Pallas kernels for 20% -> 11%
where the time goes in v7:
time: 55.3 us; the launch traced here: 55.1 us
  Pallas kernels  25 us (45%)
  starting transfers between devices  18.3 us (33%)
  waiting for transfers between devices  10.2 us (18%)
  between operations  0.83 us (2%)
  other arithmetic  0.63 us (1%)
    ppermute x15, starting transfers between devices, exchange(): lax.ppermute(arrays[s], axis, [(i, i ^ s) for i in range(size)])  18.3 us
    ppermute x15, waiting for transfers between devices, exchange(): lax.ppermute(arrays[s], axis, [(i, i ^ s) for i in range(size)])  10.2 us
    pallas_call x1, Pallas kernels, per_device(): pl.pallas_call(functools.partial(gate_up_kernel, kv, len(fetched), shares...  6.35 us
    pallas_call x3, Pallas kernels, fetch(): pl.pallas_call(functools.partial(fetch_kernel, share[0]), out_shape=tiles...  6.1 us
    pallas_call x1, Pallas kernels, per_device(): pl.pallas_call(functools.partial(qkv_kernel, tp), out_shape=[jax.ShapeDty...  5.56 us
    pallas_call x1, Pallas kernels, per_device(): pl.pallas_call(functools.partial(attend_kernel, tp, heads, 512, shares[1]...  3.3 us
    pallas_call x1, Pallas kernels, per_device(): pl.pallas_call(functools.partial(down_kernel, tp), out_shape=jax.ShapeDty...  3.04 us
  transfers between devices with their start and end apart: 15, of which 6 were waited for; matrix products, arithmetic and copies ran while one was open for 0% of the time, Pallas kernels for 11%

profile of v7, /device:TPU:0, one launch (start us, length us, event | category | flops | bytes accessed | tf_op | source)
XLA Modules:
  0.0 55.1 jit_solution(4787104339781422044)
XLA Ops:
  0.6 5.6 %qkv.1 = (f32[16,128]{1,0:T(8,128)S(1)}, f32[16,128]{1,0:T(8,128)S(1)}, f32[16,128]{1,0:T(8,128)S(1)}, f32[16,128]{1,0:T(8,128)S(1)}, f32[8,128]{1,0:T(8,128)S(1...) custom-call(s32[4]{0:T(128)} %owner_hbm.1, s32[4]{0:T(128)} %lengths_hbm.1, ...), custom_call_target="tpu_custom_call" | custom-call | bytes 29520000 | tf_op jit(solution)/shard_map/qkv/pallas_call | solution.py:384
  6.2 3.1 %collective-permute-start = (f32[16,128]{1,0:T(8,128)S(1)}, f32[16,128]{1,0:T(8,128)S(1)}, u32[]{:S(2)}, u32[]{:S(2)}) collective-permute-start(f32[16,128]{1,0:T(8,128)S(1)} %get-tuple-element.18), channel_id=1, source_target_pairs={{0,4},{4,0},{8,12},{12,8},{1,5},{5,1},{9,13},{13,9},{2,6},{6,2},{1... | collective-permute-start | bytes 24584 | tf_op jit(solution)/shard_map/ppermute | solution.py:39
  9.3 2.6 %collective-permute-start.1 = (f32[16,128]{1,0:T(8,128)S(1)}, f32[16,128]{1,0:T(8,128)S(1)}, u32[]{:S(2)}, u32[]{:S(2)}) collective-permute-start(f32[16,128]{1,0:T(8,128)S(1)} %get-tuple-element.19), channel_id=1, source_target_pairs={{0,8},{4,12},{8,0},{12,4},{1,9},{5,13},{9,1},{13,5},{2,10},{6,14},... | collective-permute-start | bytes 24584 | tf_op jit(solution)/shard_map/ppermute | solution.py:39
  11.9 2.3 %fetch.3.rest_4_.rest_0_ = bf16[4,4096,128]{2,1,0:T(8,128)(2,1)S(1)} custom-call(f32[8,128]{1,0:T(8,128)S(1)} %get-tuple-element.15.token.table, bf16[2048,2,3584]{2,1,0:T(2,128)(2,1)} %w.9), custom_call_target="tpu_custom_call" | custom-call | bytes 4428000 | tf_op jit(solution)/shard_map/fetch/pallas_call | solution.py:420
  14.2 3.1 %collective-permute-done.2.rest_3_ = f32[16,128]{1,0:T(8,128)S(1)} collective-permute-done((f32[16,128]{1,0:T(8,128)S(1)}, f32[16,128]{1,0:T(8,128)S(1)}, u32[]{:S(2)}, u32[]{:S(2)}) %collective-permute-start.2) | collective-permute-done | bytes 8224 | tf_op jit(solution)/shard_map/ppermute | solution.py:39
  17.3 3.3 %attend.1 = (bf16[8,128]{1,0:T(8,128)(2,1)S(1)}, bf16[1,256]{1,0:T(2,128)(2,1)}, bf16[4,4096,128]{2,1,0:T(8,128)(2,1)S(1)}) custom-call(f32[8,128]{1,0:T(8,128)S(1)} %get-tuple-element.15.token.table, bf16[2,8192,128]{2,1,0:T(8,128)(2,1)S(1)} %get-tuple-element.16.cache, bf16[2048,2,3584]{2,1,0:T(2,128)(2,1)} %w.9, f32[16,128]{1,0:T(8,128)S(1)} %get-tuple-element.17.rest_0_, ...), custom_call_target="tpu_custom_call" | custom-call | bytes 29520000 | tf_op jit(solution)/shard_map/attend/pallas_call | solution.py:433
  20.6 0.0 copy-start
  20.6 0.7 %collective-permute-start.5 = (bf16[8,128]{1,0:T(8,128)(2,1)S(1)}, bf16[8,128]{1,0:T(8,128)(2,1)S(1)}, u32[]{:S(2)}, u32[]{:S(2)}) collective-permute-start(bf16[8,128]{1,0:T(8,128)(2,1)S(1)} %get-tuple-element.22.token.rest_0_), channel_id=1, source_target_pairs={{0,12},{4,8},{8,4},{12,0},{1,13},{5,9},{9,5},{13,1},{2,14},{6,10},... | collective-permute-start | bytes 6152 | tf_op jit(solution)/shard_map/ppermute | solution.py:39
  21.4 3.7 %collective-permute-start.3 = (bf16[8,128]{1,0:T(8,128)(2,1)S(1)}, bf16[8,128]{1,0:T(8,128)(2,1)S(1)}, u32[]{:S(2)}, u32[]{:S(2)}) collective-permute-start(bf16[8,128]{1,0:T(8,128)(2,1)S(1)} %get-tuple-element.22.token.rest_0_), channel_id=1, source_target_pairs={{0,4},{4,0},{8,12},{12,8},{1,5},{5,1},{9,13},{13,9},{2,6},{6,2},{1... | collective-permute-start | bytes 6152 | tf_op jit(solution)/shard_map/ppermute | solution.py:39
  25.1 2.3 %fetch.4.rest_4_.rest_2_ = bf16[4,4096,128]{2,1,0:T(8,128)(2,1)S(1)} custom-call(bf16[8,128]{1,0:T(8,128)(2,1)S(1)} %get-tuple-element.22.token.rest_0_, bf16[2048,2,3584]{2,1,0:T(2,128)(2,1)} %w.9), custom_call_target="tpu_custom_call" | custom-call | bytes 4428000 | tf_op jit(solution)/shard_map/fetch/pallas_call | solution.py:420
  27.4 0.0 collective-permute-done.3.rest_1_
  27.4 0.7 %attn_project.1.token.rest_4_ = bf16[4,2048]{1,0:T(4,128)(2,1)S(1)} custom-call(s32[8,128]{1,0:T(8,128)S(1)} %get-tuple-element.23.places, bf16[1024,2048]{1,0:T(8,128)(2,1)S(1)} %copy-done, bf16[8,128]{1,0:T(8,128)(2,1)S(1)} %get-tuple-element.22.token.rest_0_, bf16[8,128]{1,0:T(8,128)(2,1)S(1)} %collective-permute-done.3.rest_1_, ...), custom_call_target="tpu_custom_call" | custom-call | bytes 22140000 | tf_op jit(solution)/shard_map/attn_project/pallas_call | solution.py:454
  28.1 0.0 collective-permute-start.8
  28.1 1.6 %collective-permute-start.7 = (bf16[4,2048]{1,0:T(4,128)(2,1)S(1)}, bf16[4,2048]{1,0:T(4,128)(2,1)S(1)}, u32[]{:S(2)}, u32[]{:S(2)}) collective-permute-start(bf16[4,2048]{1,0:T(4,128)(2,1)S(1)} %attn_project.1.token.rest_4_), channel_id=1, source_target_pairs={{0,2},{1,3},{2,0},{3,1},{4,6},{5,7},{6,4},{7,5},{8,10},{9,11},{10,... | collective-permute-start | bytes 49160 | tf_op jit(solution)/shard_map/ppermute | solution.py:39
  29.6 0.3 collective-permute-start.6
  29.9 1.6 %fetch.5.rest_3_ = bf16[2,4096,128]{2,1,0:T(8,128)(2,1)S(1)} custom-call(bf16[4,2048]{1,0:T(4,128)(2,1)S(1)} %attn_project.1.token.rest_4_, bf16[2048,2,3584]{2,1,0:T(2,128)(2,1)} %w.9), custom_call_target="tpu_custom_call" | custom-call | bytes 2214000 | tf_op jit(solution)/shard_map/fetch/pallas_call | solution.py:420
  31.5 0.0 collective-permute-done.8.rest_7_
  31.5 0.4 collective-permute-done.7.rest_6_
  31.9 0.0 slice-start.1
  31.9 6.3 %gate_up.1 = (bf16[4,2048]{1,0:T(4,128)(2,1)}, bf16[8,3712]{1,0:T(8,128)(2,1)S(1)}) custom-call(bf16[4,2048]{1,0:T(4,128)(2,1)S(1)} %copy-done.1, f32[2,2048]{1,0:T(2,128)S(1)} %copy-done.2, bf16[2048,2,3584]{2,1,0:T(2,128)(2,1)} %w.9, bf16[4,4096,128]{2,1,0:T(8,128)(2,1)S(1)} %fetch.3.rest_4_.rest_0_, bf16[4,4096,128]{2,1,0:T(8,128)(2,1)S(1)} %get-tuple-element.21.rest_1_, ...), custom_call_target="tpu_custom_call" | custom-call | bytes 36900000 | tf_op jit(solution)/shard_map/gate_up/pallas_call | solution.py:467
  38.3 1.7 %collective-permute-start.11 = (bf16[8,3712]{1,0:T(8,128)(2,1)S(1)}, bf16[8,3712]{1,0:T(8,128)(2,1)S(1)}, u32[]{:S(2)}, u32[]{:S(2)}) collective-permute-start(bf16[8,3712]{1,0:T(8,128)(2,1)S(1)} %get-tuple-element.25.rest_0_), channel_id=1, source_target_pairs={{0,12},{4,8},{8,4},{12,0},{1,13},{5,9},{9,5},{13,1},{2,14},{6,10},... | collective-permute-start | bytes 178184 | tf_op jit(solution)/shard_map/ppermute | solution.py:39
  40.0 1.1 %collective-permute-start.10 = (bf16[8,3712]{1,0:T(8,128)(2,1)S(1)}, bf16[8,3712]{1,0:T(8,128)(2,1)S(1)}, u32[]{:S(2)}, u32[]{:S(2)}) collective-permute-start(bf16[8,3712]{1,0:T(8,128)(2,1)S(1)} %get-tuple-element.25.rest_0_), channel_id=1, source_target_pairs={{0,8},{4,12},{8,0},{12,4},{1,9},{5,13},{9,1},{13,5},{2,10},{6,14},... | collective-permute-start | bytes 178184 | tf_op jit(solution)/shard_map/ppermute | solution.py:39
  41.1 1.6 %collective-permute-start.9 = (bf16[8,3712]{1,0:T(8,128)(2,1)S(1)}, bf16[8,3712]{1,0:T(8,128)(2,1)S(1)}, u32[]{:S(2)}, u32[]{:S(2)}) collective-permute-start(bf16[8,3712]{1,0:T(8,128)(2,1)S(1)} %get-tuple-element.25.rest_0_), channel_id=1, source_target_pairs={{0,4},{4,0},{8,12},{12,8},{1,5},{5,1},{9,13},{13,9},{2,6},{6,2},{1... | collective-permute-start | bytes 178184 | tf_op jit(solution)/shard_map/ppermute | solution.py:39
  42.8 2.3 %collective-permute-done.11.rest_3_ = bf16[8,3712]{1,0:T(8,128)(2,1)S(1)} collective-permute-done((bf16[8,3712]{1,0:T(8,128)(2,1)S(1)}, bf16[8,3712]{1,0:T(8,128)(2,1)S(1)}, u32[]{:S(2)}, u32[]{:S(2)}) %collective-permute-start.11) | collective-permute-done | bytes 59424 | tf_op jit(solution)/shard_map/ppermute | solution.py:39
  45.1 2.1 %collective-permute-done.10.rest_2_ = bf16[8,3712]{1,0:T(8,128)(2,1)S(1)} collective-permute-done((bf16[8,3712]{1,0:T(8,128)(2,1)S(1)}, bf16[8,3712]{1,0:T(8,128)(2,1)S(1)}, u32[]{:S(2)}, u32[]{:S(2)}) %collective-permute-start.10) | collective-permute-done | bytes 59424 | tf_op jit(solution)/shard_map/ppermute | solution.py:39
  47.2 3.0 %down.1 = bf16[4,2048]{1,0:T(4,128)(2,1)S(1)} custom-call(bf16[3584,2048]{1,0:T(8,128)(2,1)S(1)} %bitcast.5, bf16[8,3712]{1,0:T(8,128)(2,1)S(1)} %get-tuple-element.25.rest_0_, bf16[8,3712]{1,0:T(8,128)(2,1)S(1)} %collective-permute-done.9.rest_1_, bf16[8,3712]{1,0:T(8,128)(2,1)S(1)} %collective-permute-done.10.rest_2_, ...), custom_call_target="tpu_custom_call" | custom-call | bytes 18450000 | tf_op jit(solution)/shard_map/down/pallas_call | solution.py:486
  50.2 0.3 collective-permute-start.14
  50.6 1.3 %collective-permute-start.13 = (bf16[4,2048]{1,0:T(4,128)(2,1)S(1)}, bf16[4,2048]{1,0:T(4,128)(2,1)S(1)}, u32[]{:S(2)}, u32[]{:S(2)}) collective-permute-start(bf16[4,2048]{1,0:T(4,128)(2,1)S(1)} %down.1), channel_id=1, source_target_pairs={{0,2},{1,3},{2,0},{3,1},{4,6},{5,7},{6,4},{7,5},{8,10},{9,11},{10,... | collective-permute-start | bytes 49160 | tf_op jit(solution)/shard_map/ppermute | solution.py:39
  51.9 0.2 collective-permute-start.12
  52.1 1.3 %collective-permute-done.14 = bf16[4,2048]{1,0:T(4,128)(2,1)S(1)} collective-permute-done((bf16[4,2048]{1,0:T(4,128)(2,1)S(1)}, bf16[4,2048]{1,0:T(4,128)(2,1)S(1)}, u32[]{:S(2)}, u32[]{:S(2)}) %collective-permute-start.14) | collective-permute-done | bytes 16416 | tf_op jit(solution)/shard_map/ppermute | solution.py:39
  53.4 1.0 %collective-permute-done.13 = bf16[4,2048]{1,0:T(4,128)(2,1)S(1)} collective-permute-done((bf16[4,2048]{1,0:T(4,128)(2,1)S(1)}, bf16[4,2048]{1,0:T(4,128)(2,1)S(1)}, u32[]{:S(2)}, u32[]{:S(2)}) %collective-permute-start.13) | collective-permute-done | bytes 16416 | tf_op jit(solution)/shard_map/ppermute | solution.py:39
  54.4 0.6 %add_convert_fusion = bf16[4,2048]{1,0:T(4,128)(2,1)} fusion(bf16[4,2048]{1,0:T(4,128)(2,1)S(1)} %collective-permute-done.14, bf16[4,2048]{1,0:T(4,128)(2,1)S(1)} %collective-permute-done.13, bf16[4,2048]{1,0:T(4,128)(2,1)S(1)} %collective-permute-done.12, bf16[4,2048]{1,0:T(4,128)(2,1)S(1)} %down.1), kind=kLoop, calls=%fused_computation | loop fusion | flops 65536 | bytes 81920 | tf_op jit(solution)/shard_map/convert_element_type | solution.py:497
  (22 shorter events, 0.0 us)
Async XLA Ops:
  6.2 8.0 %collective-permute-start = (f32[16,128]{1,0:T(8,128)S(1)}, f32[16,128]{1,0:T(8,128)S(1)}, u32[]{:S(2)}, u32[]{:S(2)}) collective-permute-start(f32[16,128]{1,0:T(8,128)S(1)} %get-tuple-element.18), channel_id=1, source_target_pairs={{0,4},{4,0},{8,12},{12,8},{1,5},{5,1},{9,13},{13,9},{2,6},{6,2},{1... | collective-permute-start | bytes 24584 | tf_op jit(solution)/shard_map/ppermute | solution.py:39
  9.3 4.9 %collective-permute-start.1 = (f32[16,128]{1,0:T(8,128)S(1)}, f32[16,128]{1,0:T(8,128)S(1)}, u32[]{:S(2)}, u32[]{:S(2)}) collective-permute-start(f32[16,128]{1,0:T(8,128)S(1)} %get-tuple-element.19), channel_id=1, source_target_pairs={{0,8},{4,12},{8,0},{12,4},{1,9},{5,13},{9,1},{13,5},{2,10},{6,14},... | collective-permute-start | bytes 24584 | tf_op jit(solution)/shard_map/ppermute | solution.py:39
  11.9 5.4 %collective-permute-start.2 = (f32[16,128]{1,0:T(8,128)S(1)}, f32[16,128]{1,0:T(8,128)S(1)}, u32[]{:S(2)}, u32[]{:S(2)}) collective-permute-start(f32[16,128]{1,0:T(8,128)S(1)} %get-tuple-element.20), channel_id=1, source_target_pairs={{0,12},{4,8},{8,4},{12,0},{1,13},{5,9},{9,5},{13,1},{2,14},{6,10},... | collective-permute-start | bytes 24584 | tf_op jit(solution)/shard_map/ppermute | solution.py:39
  20.6 6.8 %copy-start = (bf16[1024,2048]{1,0:T(8,128)(2,1)S(1)}, bf16[1024,2048]{1,0:T(8,128)(2,1)}, u32[]{:S(2)}) copy-start(bf16[1024,2048]{1,0:T(8,128)(2,1)} %w_out.1) | copy-start | bytes 12582916
  20.6 6.7 %collective-permute-start.5 = (bf16[8,128]{1,0:T(8,128)(2,1)S(1)}, bf16[8,128]{1,0:T(8,128)(2,1)S(1)}, u32[]{:S(2)}, u32[]{:S(2)}) collective-permute-start(bf16[8,128]{1,0:T(8,128)(2,1)S(1)} %get-tuple-element.22.token.rest_0_), channel_id=1, source_target_pairs={{0,12},{4,8},{8,4},{12,0},{1,13},{5,9},{9,5},{13,1},{2,14},{6,10},... | collective-permute-start | bytes 6152 | tf_op jit(solution)/shard_map/ppermute | solution.py:39
  21.4 6.0 %collective-permute-start.4 = (bf16[8,128]{1,0:T(8,128)(2,1)S(1)}, bf16[8,128]{1,0:T(8,128)(2,1)S(1)}, u32[]{:S(2)}, u32[]{:S(2)}) collective-permute-start(bf16[8,128]{1,0:T(8,128)(2,1)S(1)} %get-tuple-element.22.token.rest_0_), channel_id=1, source_target_pairs={{0,8},{4,12},{8,0},{12,4},{1,9},{5,13},{9,1},{13,5},{2,10},{6,14},... | collective-permute-start | bytes 6152 | tf_op jit(solution)/shard_map/ppermute | solution.py:39
  21.4 6.0 %collective-permute-start.3 = (bf16[8,128]{1,0:T(8,128)(2,1)S(1)}, bf16[8,128]{1,0:T(8,128)(2,1)S(1)}, u32[]{:S(2)}, u32[]{:S(2)}) collective-permute-start(bf16[8,128]{1,0:T(8,128)(2,1)S(1)} %get-tuple-element.22.token.rest_0_), channel_id=1, source_target_pairs={{0,4},{4,0},{8,12},{12,8},{1,5},{5,1},{9,13},{13,9},{2,6},{6,2},{1... | collective-permute-start | bytes 6152 | tf_op jit(solution)/shard_map/ppermute | solution.py:39
  28.1 3.8 %copy-start.1 = (bf16[4,2048]{1,0:T(4,128)(2,1)S(1)}, bf16[4,2048]{1,0:T(4,128)(2,1)}, u32[]{:S(2)}) copy-start(bf16[4,2048]{1,0:T(4,128)(2,1)} %states.1) | copy-start | bytes 49156
  28.1 3.8 %copy-start.2 = (f32[2,2048]{1,0:T(2,128)S(1)}, f32[2,2048]{1,0:T(2,128)}, u32[]{:S(2)}) copy-start(f32[2,2048]{1,0:T(2,128)} %gains.1) | copy-start | bytes 49156
  28.1 3.5 %collective-permute-start.8 = (bf16[4,2048]{1,0:T(4,128)(2,1)S(1)}, bf16[4,2048]{1,0:T(4,128)(2,1)S(1)}, u32[]{:S(2)}, u32[]{:S(2)}) collective-permute-start(bf16[4,2048]{1,0:T(4,128)(2,1)S(1)} %attn_project.1.token.rest_4_), channel_id=1, source_target_pairs={{0,3},{1,2},{2,1},{3,0},{4,7},{5,6},{6,5},{7,4},{8,11},{9,10},{10,... | collective-permute-start | bytes 49160 | tf_op jit(solution)/shard_map/ppermute | solution.py:39
  28.1 3.8 %collective-permute-start.7 = (bf16[4,2048]{1,0:T(4,128)(2,1)S(1)}, bf16[4,2048]{1,0:T(4,128)(2,1)S(1)}, u32[]{:S(2)}, u32[]{:S(2)}) collective-permute-start(bf16[4,2048]{1,0:T(4,128)(2,1)S(1)} %attn_project.1.token.rest_4_), channel_id=1, source_target_pairs={{0,2},{1,3},{2,0},{3,1},{4,6},{5,7},{6,4},{7,5},{8,10},{9,11},{10,... | collective-permute-start | bytes 49160 | tf_op jit(solution)/shard_map/ppermute | solution.py:39
  29.6 2.2 %collective-permute-start.6 = (bf16[4,2048]{1,0:T(4,128)(2,1)S(1)}, bf16[4,2048]{1,0:T(4,128)(2,1)S(1)}, u32[]{:S(2)}, u32[]{:S(2)}) collective-permute-start(bf16[4,2048]{1,0:T(4,128)(2,1)S(1)} %attn_project.1.token.rest_4_), channel_id=1, source_target_pairs={{0,1},{1,0},{2,3},{3,2},{4,5},{5,4},{6,7},{7,6},{8,9},{9,8},{10,11... | collective-permute-start | bytes 49160 | tf_op jit(solution)/shard_map/ppermute | solution.py:39
  31.9 15.3 %slice-start = ((s8[14680064]{0:T(1024)(128)(4,1)}), s8[4194304]{0:T(1024)(128)(4,1)S(1)}, s32[]{:S(2)}) async-start(s8[14680064]{0:T(1024)(128)(4,1)} %bitcast.4), calls=%async_computation | async-start | bytes 8388608
  31.9 15.2 %slice-start.1 = ((s8[14680064]{0:T(1024)(128)(4,1)}), s8[4194304]{0:T(1024)(128)(4,1)S(1)}, s32[]{:S(2)}) async-start(s8[14680064]{0:T(1024)(128)(4,1)} %bitcast.4), calls=%async_computation.1 | async-start | bytes 8388608
  31.9 15.2 %slice-start.2 = ((s8[14680064]{0:T(1024)(128)(4,1)}), s8[4194304]{0:T(1024)(128)(4,1)S(1)}, s32[]{:S(2)}) async-start(s8[14680064]{0:T(1024)(128)(4,1)} %bitcast.4), calls=%async_computation.2 | async-start | bytes 8388608
  31.9 15.2 %slice-start.3 = ((s8[14680064]{0:T(1024)(128)(4,1)}), s8[2097152]{0:T(1024)(128)(4,1)S(1)}, s32[]{:S(2)}) async-start(s8[14680064]{0:T(1024)(128)(4,1)} %bitcast.4), calls=%async_computation.3 | async-start | bytes 4194304
  38.3 6.8 %collective-permute-start.11 = (bf16[8,3712]{1,0:T(8,128)(2,1)S(1)}, bf16[8,3712]{1,0:T(8,128)(2,1)S(1)}, u32[]{:S(2)}, u32[]{:S(2)}) collective-permute-start(bf16[8,3712]{1,0:T(8,128)(2,1)S(1)} %get-tuple-element.25.rest_0_), channel_id=1, source_target_pairs={{0,12},{4,8},{8,4},{12,0},{1,13},{5,9},{9,5},{13,1},{2,14},{6,10},... | collective-permute-start | bytes 178184 | tf_op jit(solution)/shard_map/ppermute | solution.py:39
  40.0 7.1 %collective-permute-start.10 = (bf16[8,3712]{1,0:T(8,128)(2,1)S(1)}, bf16[8,3712]{1,0:T(8,128)(2,1)S(1)}, u32[]{:S(2)}, u32[]{:S(2)}) collective-permute-start(bf16[8,3712]{1,0:T(8,128)(2,1)S(1)} %get-tuple-element.25.rest_0_), channel_id=1, source_target_pairs={{0,8},{4,12},{8,0},{12,4},{1,9},{5,13},{9,1},{13,5},{2,10},{6,14},... | collective-permute-start | bytes 178184 | tf_op jit(solution)/shard_map/ppermute | solution.py:39
  41.1 6.0 %collective-permute-start.9 = (bf16[8,3712]{1,0:T(8,128)(2,1)S(1)}, bf16[8,3712]{1,0:T(8,128)(2,1)S(1)}, u32[]{:S(2)}, u32[]{:S(2)}) collective-permute-start(bf16[8,3712]{1,0:T(8,128)(2,1)S(1)} %get-tuple-element.25.rest_0_), channel_id=1, source_target_pairs={{0,4},{4,0},{8,12},{12,8},{1,5},{5,1},{9,13},{13,9},{2,6},{6,2},{1... | collective-permute-start | bytes 178184 | tf_op jit(solution)/shard_map/ppermute | solution.py:39
  50.2 3.2 %collective-permute-start.14 = (bf16[4,2048]{1,0:T(4,128)(2,1)S(1)}, bf16[4,2048]{1,0:T(4,128)(2,1)S(1)}, u32[]{:S(2)}, u32[]{:S(2)}) collective-permute-start(bf16[4,2048]{1,0:T(4,128)(2,1)S(1)} %down.1), channel_id=1, source_target_pairs={{0,3},{1,2},{2,1},{3,0},{4,7},{5,6},{6,5},{7,4},{8,11},{9,10},{10,... | collective-permute-start | bytes 49160 | tf_op jit(solution)/shard_map/ppermute | solution.py:39
  50.6 3.9 %collective-permute-start.13 = (bf16[4,2048]{1,0:T(4,128)(2,1)S(1)}, bf16[4,2048]{1,0:T(4,128)(2,1)S(1)}, u32[]{:S(2)}, u32[]{:S(2)}) collective-permute-start(bf16[4,2048]{1,0:T(4,128)(2,1)S(1)} %down.1), channel_id=1, source_target_pairs={{0,2},{1,3},{2,0},{3,1},{4,6},{5,7},{6,4},{7,5},{8,10},{9,11},{10,... | collective-permute-start | bytes 49160 | tf_op jit(solution)/shard_map/ppermute | solution.py:39
  51.9 2.6 %collective-permute-start.12 = (bf16[4,2048]{1,0:T(4,128)(2,1)S(1)}, bf16[4,2048]{1,0:T(4,128)(2,1)S(1)}, u32[]{:S(2)}, u32[]{:S(2)}) collective-permute-start(bf16[4,2048]{1,0:T(4,128)(2,1)S(1)} %down.1), channel_id=1, source_target_pairs={{0,1},{1,0},{2,3},{3,2},{4,5},{5,4},{6,7},{7,6},{8,9},{9,8},{10,11... | collective-permute-start | bytes 49160 | tf_op jit(solution)/shard_map/ppermute | solution.py:39

commit v8 on v7

--- a/solution.py
+++ b/solution.py
@@ -14,7 +14,8 @@
 ROPE_BASE = 500000.0
 LANES = 128
 MIB = 1 << 20
-GU_SHARES = (4, 4, 4, 2, 14)
+TILE_GROUP = 4
+GU_SHARES = (4, 6, 6, 2, 10)
 F32 = jnp.float32
 BF16 = jnp.bfloat16
 QUARTER = (1.5703125, 4.837512969970703125e-4, 7.549789948768648e-8)
@@ -81,16 +82,15 @@
     return w if len(w.shape) == 2 else w.reshape(w.shape[0] * w.shape[1], w.shape[2])
 
 
-def times_tiles(left, tiles, store, tile_ready=None):
-    def step(j, carry):
+def times_tiles(left, tiles, first, store, tile_ready=None):
+    count = tiles.shape[0]
+    for start in range(0, count, TILE_GROUP):
+        group = range(start, min(start + TILE_GROUP, count))
         if tile_ready is not None:
-            tile_ready(2 * j)
-            tile_ready(2 * j + 1)
-        pair = jnp.concatenate([tiles[2 * j], tiles[2 * j + 1]], axis=1)
-        store(j, jnp.dot(left[...], pair, preferred_element_type=F32))
-        return carry
-
-    lax.fori_loop(0, tiles.shape[0] // 2, step, 0)
+            for i in group:
+                tile_ready(i)
+        columns = jnp.concatenate([tiles[i] for i in group], axis=1)
+        store(first + start, jnp.dot(left[...], columns, preferred_element_type=F32))
 
 
 def pick_doc(value, doc, docs):
@@ -177,6 +177,8 @@
         copy.start()
     for copy in small:
         copy.wait()
+    for copy in cache_copies:
+        copy.start()
     me = lax.axis_index("tp")
     x = states[...].astype(F32)
     squares = jnp.broadcast_to(jnp.sum(x * x, axis=1, keepdims=True), (docs, LANES))
@@ -195,9 +197,6 @@
     total = jnp.zeros((heads * 2 * docs, LANES), F32)
     for c in range(parts):
         copies[c].wait()
-        if c == parts // 2:
-            for copy in cache_copies:
-                copy.start()
         total = total + jnp.dot(
             spread_buf[:, c * rows : (c + 1) * rows], wq_buf[c], preferred_element_type=F32
         )
@@ -298,7 +297,8 @@
     docs, width = states.shape
     hidden = w.shape[2]
     w_matrix = matrix_of(w)
-    for copy in tile_copies(w_matrix, first, w_tiles, w_sems):
+    copies = tile_copies(w_matrix, first, w_tiles, w_sems)
+    for copy in copies:
         copy.start()
     attn = tree_sum([part[...].astype(F32) for part in parts]).astype(BF16)
     attn_out[...] = attn
@@ -307,26 +307,16 @@
     high, low = two_parts(resid * gains[1:2, :])
     spread(jnp.concatenate([high, high, low, low], axis=0).astype(BF16), spread_buf, docs)
 
-    def store_from(tile):
-        def store(j, product):
-            start = pl.multiple_of((tile + 2 * j) * LANES, 2 * LANES)
-            summed = product[: 2 * docs] + product[2 * docs :]
-            partial_out[:, pl.ds(start, 2 * LANES)] = summed.astype(BF16)
-
-        return store
-
-    def tile_ready(i):
-        pltpu.make_async_copy(
-            w_matrix.at[:, pl.ds(pl.multiple_of((first + i) * LANES, LANES), LANES)],
-            w_tiles.at[i],
-            w_sems.at[i],
-        ).wait()
+    def store(tile, product):
+        summed = product[: 2 * docs] + product[2 * docs :]
+        columns = slice(tile * LANES, tile * LANES + summed.shape[1])
+        partial_out[:, columns] = summed.astype(BF16)
 
     tile = 0
     for group in ready:
-        times_tiles(spread_buf, group, store_from(tile))
+        times_tiles(spread_buf, group, tile, store)
         tile += group.shape[0]
-    times_tiles(spread_buf, w_tiles, store_from(tile), tile_ready)
+    times_tiles(spread_buf, w_tiles, tile, store, lambda i: copies[i].wait())
     lane = lax.broadcasted_iota(jnp.int32, (docs, LANES), 1)
     first = squares.astype(BF16).astype(F32)
     second = (squares - first).astype(BF16).astype(F32)
@@ -347,13 +337,7 @@
     up = summed[docs:, :hidden] * inverse
     act_buf[...] = (gate / (1.0 + jnp.exp(-gate)) * up).astype(BF16)
 
-    def step(j, carry):
-        columns = pl.ds(pl.multiple_of(2 * j * LANES, 2 * LANES), 2 * LANES)
-        product = jnp.dot(act_buf[...], w_down[:, columns], preferred_element_type=F32)
-        out[:, columns] = product.astype(BF16)
-        return carry
-
-    lax.fori_loop(0, width // (2 * LANES), step, 0)
+    out[...] = jnp.dot(act_buf[...], w_down[...], preferred_element_type=F32).astype(BF16)
 
 
 def cost(micros):

time: 55.3 us -> 56 us (1.013)
  Pallas kernels: 25 us -> 26 us
    pallas_call x1, Pallas kernels: 6.35 us -> 8.11 us  [per_device(): pl.pallas_call(functools.partial(gate_up_kernel, kv, len(fetched), shares...]
    pallas_call x1, Pallas kernels: 5.56 us -> 4.43 us  [per_device(): pl.pallas_call(functools.partial(qkv_kernel, tp), out_shape=[jax.ShapeDty...]
    pallas_call x1, Pallas kernels: 3.04 us -> 2.09 us  [per_device(): pl.pallas_call(functools.partial(down_kernel, tp), out_shape=jax.ShapeDty...]
    pallas_call x3, Pallas kernels: 6.1 us -> 6.77 us  [fetch(): pl.pallas_call(functools.partial(fetch_kernel, share[0]), out_shape=tiles...]
    pallas_call x1, Pallas kernels: 3.3 us -> 3.98 us  [per_device(): pl.pallas_call(functools.partial(attend_kernel, tp, heads, 512, shares[1]...]
  transfers between devices with their start and end apart: 15 -> 15, of which waited for: 6 -> 6; matrix products, arithmetic and copies ran while one was open for 0% -> 0% of each run, Pallas kernels for 11% -> 12%
where the time goes in v8:
time: 56 us; the launch traced here: 55.7 us
  Pallas kernels  26 us (46%)
  starting transfers between devices  18.3 us (33%)
  waiting for transfers between devices  9.87 us (18%)
  between operations  0.83 us (1%)
  other arithmetic  0.63 us (1%)
    ppermute x15, starting transfers between devices, exchange(): lax.ppermute(arrays[s], axis, [(i, i ^ s) for i in range(size)])  18.3 us
    ppermute x15, waiting for transfers between devices, exchange(): lax.ppermute(arrays[s], axis, [(i, i ^ s) for i in range(size)])  9.87 us
    pallas_call x1, Pallas kernels, per_device(): pl.pallas_call(functools.partial(gate_up_kernel, kv, len(fetched), shares...  8.11 us
    pallas_call x3, Pallas kernels, fetch(): pl.pallas_call(functools.partial(fetch_kernel, share[0]), out_shape=tiles...  6.77 us
    pallas_call x1, Pallas kernels, per_device(): pl.pallas_call(functools.partial(qkv_kernel, tp), out_shape=[jax.ShapeDty...  4.43 us
    pallas_call x1, Pallas kernels, per_device(): pl.pallas_call(functools.partial(attend_kernel, tp, heads, 512, shares[1]...  3.98 us
    pallas_call x1, Pallas kernels, per_device(): pl.pallas_call(functools.partial(down_kernel, tp), out_shape=jax.ShapeDty...  2.09 us
  transfers between devices with their start and end apart: 15, of which 6 were waited for; matrix products, arithmetic and copies ran while one was open for 0% of the time, Pallas kernels for 12%

profile of v8, /device:TPU:0, one launch (start us, length us, event | category | flops | bytes accessed | tf_op | source)
XLA Modules:
  0.0 55.7 jit_solution(1079756423229999828)
XLA Ops:
  0.6 4.4 %qkv.1 = (f32[16,128]{1,0:T(8,128)S(1)}, f32[16,128]{1,0:T(8,128)S(1)}, f32[16,128]{1,0:T(8,128)S(1)}, f32[16,128]{1,0:T(8,128)S(1)}, f32[8,128]{1,0:T(8,128)S(1...) custom-call(s32[4]{0:T(128)} %owner_hbm.1, s32[4]{0:T(128)} %lengths_hbm.1, ...), custom_call_target="tpu_custom_call" | custom-call | bytes 29520000 | tf_op jit(solution)/shard_map/qkv/pallas_call | solution.py:368
  5.1 3.1 %collective-permute-start = (f32[16,128]{1,0:T(8,128)S(1)}, f32[16,128]{1,0:T(8,128)S(1)}, u32[]{:S(2)}, u32[]{:S(2)}) collective-permute-start(f32[16,128]{1,0:T(8,128)S(1)} %get-tuple-element.18), channel_id=1, source_target_pairs={{0,4},{4,0},{8,12},{12,8},{1,5},{5,1},{9,13},{13,9},{2,6},{6,2},{1... | collective-permute-start | bytes 24584 | tf_op jit(solution)/shard_map/ppermute | solution.py:40
  8.2 2.6 %collective-permute-start.1 = (f32[16,128]{1,0:T(8,128)S(1)}, f32[16,128]{1,0:T(8,128)S(1)}, u32[]{:S(2)}, u32[]{:S(2)}) collective-permute-start(f32[16,128]{1,0:T(8,128)S(1)} %get-tuple-element.19), channel_id=1, source_target_pairs={{0,8},{4,12},{8,0},{12,4},{1,9},{5,13},{9,1},{13,5},{2,10},{6,14},... | collective-permute-start | bytes 24584 | tf_op jit(solution)/shard_map/ppermute | solution.py:40
  10.8 2.3 %fetch.3.rest_4_.rest_0_ = bf16[4,4096,128]{2,1,0:T(8,128)(2,1)S(1)} custom-call(f32[8,128]{1,0:T(8,128)S(1)} %get-tuple-element.15.token.table, bf16[2048,2,3584]{2,1,0:T(2,128)(2,1)} %w.9), custom_call_target="tpu_custom_call" | custom-call | bytes 4428000 | tf_op jit(solution)/shard_map/fetch/pallas_call | solution.py:404
  13.0 0.0 collective-permute-done.rest_1_
  13.1 3.1 %collective-permute-done.2.rest_3_ = f32[16,128]{1,0:T(8,128)S(1)} collective-permute-done((f32[16,128]{1,0:T(8,128)S(1)}, f32[16,128]{1,0:T(8,128)S(1)}, u32[]{:S(2)}, u32[]{:S(2)}) %collective-permute-start.2) | collective-permute-done | bytes 8224 | tf_op jit(solution)/shard_map/ppermute | solution.py:40
  16.2 4.0 %attend.1 = (bf16[8,128]{1,0:T(8,128)(2,1)S(1)}, bf16[1,256]{1,0:T(2,128)(2,1)}, bf16[6,4096,128]{2,1,0:T(8,128)(2,1)S(1)}) custom-call(f32[8,128]{1,0:T(8,128)S(1)} %get-tuple-element.15.token.table, bf16[2,8192,128]{2,1,0:T(8,128)(2,1)S(1)} %get-tuple-element.16.cache, bf16[2048,2,3584]{2,1,0:T(2,128)(2,1)} %w.9, f32[16,128]{1,0:T(8,128)S(1)} %get-tuple-element.17.rest_0_, ...), custom_call_target="tpu_custom_call" | custom-call | bytes 29520000 | tf_op jit(solution)/shard_map/attend/pallas_call | solution.py:417
  20.2 0.0 copy-start
  20.2 0.7 %collective-permute-start.5 = (bf16[8,128]{1,0:T(8,128)(2,1)S(1)}, bf16[8,128]{1,0:T(8,128)(2,1)S(1)}, u32[]{:S(2)}, u32[]{:S(2)}) collective-permute-start(bf16[8,128]{1,0:T(8,128)(2,1)S(1)} %get-tuple-element.22.token.rest_0_), channel_id=1, source_target_pairs={{0,12},{4,8},{8,4},{12,0},{1,13},{5,9},{9,5},{13,1},{2,14},{6,10},... | collective-permute-start | bytes 6152 | tf_op jit(solution)/shard_map/ppermute | solution.py:40
  20.9 0.0 collective-permute-start.4
  20.9 3.7 %collective-permute-start.3 = (bf16[8,128]{1,0:T(8,128)(2,1)S(1)}, bf16[8,128]{1,0:T(8,128)(2,1)S(1)}, u32[]{:S(2)}, u32[]{:S(2)}) collective-permute-start(bf16[8,128]{1,0:T(8,128)(2,1)S(1)} %get-tuple-element.22.token.rest_0_), channel_id=1, source_target_pairs={{0,4},{4,0},{8,12},{12,8},{1,5},{5,1},{9,13},{13,9},{2,6},{6,2},{1... | collective-permute-start | bytes 6152 | tf_op jit(solution)/shard_map/ppermute | solution.py:40
  24.7 2.9 %fetch.4.rest_4_.rest_2_ = bf16[6,4096,128]{2,1,0:T(8,128)(2,1)S(1)} custom-call(bf16[8,128]{1,0:T(8,128)(2,1)S(1)} %get-tuple-element.22.token.rest_0_, bf16[2048,2,3584]{2,1,0:T(2,128)(2,1)} %w.9), custom_call_target="tpu_custom_call" | custom-call | bytes 6641999 | tf_op jit(solution)/shard_map/fetch/pallas_call | solution.py:404
  27.6 0.0 collective-permute-done.5.rest_3_
  27.6 0.7 %attn_project.1.token.rest_4_ = bf16[4,2048]{1,0:T(4,128)(2,1)S(1)} custom-call(s32[8,128]{1,0:T(8,128)S(1)} %get-tuple-element.23.places, bf16[1024,2048]{1,0:T(8,128)(2,1)S(1)} %copy-done, bf16[8,128]{1,0:T(8,128)(2,1)S(1)} %get-tuple-element.22.token.rest_0_, bf16[8,128]{1,0:T(8,128)(2,1)S(1)} %collective-permute-done.3.rest_1_, ...), custom_call_target="tpu_custom_call" | custom-call | bytes 22140000 | tf_op jit(solution)/shard_map/attn_project/pallas_call | solution.py:438
  28.3 0.0 collective-permute-start.8
  28.3 1.6 %collective-permute-start.7 = (bf16[4,2048]{1,0:T(4,128)(2,1)S(1)}, bf16[4,2048]{1,0:T(4,128)(2,1)S(1)}, u32[]{:S(2)}, u32[]{:S(2)}) collective-permute-start(bf16[4,2048]{1,0:T(4,128)(2,1)S(1)} %attn_project.1.token.rest_4_), channel_id=1, source_target_pairs={{0,2},{1,3},{2,0},{3,1},{4,6},{5,7},{6,4},{7,5},{8,10},{9,11},{10,... | collective-permute-start | bytes 49160 | tf_op jit(solution)/shard_map/ppermute | solution.py:40
  29.9 0.3 collective-permute-start.6
  30.2 1.6 %fetch.5.rest_3_ = bf16[2,4096,128]{2,1,0:T(8,128)(2,1)S(1)} custom-call(bf16[4,2048]{1,0:T(4,128)(2,1)S(1)} %attn_project.1.token.rest_4_, bf16[2048,2,3584]{2,1,0:T(2,128)(2,1)} %w.9), custom_call_target="tpu_custom_call" | custom-call | bytes 2214000 | tf_op jit(solution)/shard_map/fetch/pallas_call | solution.py:404
  31.8 0.4 collective-permute-done.7.rest_6_
  32.2 8.1 %gate_up.1 = (bf16[4,2048]{1,0:T(4,128)(2,1)}, bf16[8,3712]{1,0:T(8,128)(2,1)S(1)}) custom-call(bf16[4,2048]{1,0:T(4,128)(2,1)S(1)} %copy-done.1, f32[2,2048]{1,0:T(2,128)S(1)} %copy-done.2, bf16[2048,2,3584]{2,1,0:T(2,128)(2,1)} %w.9, bf16[4,4096,128]{2,1,0:T(8,128)(2,1)S(1)} %fetch.3.rest_4_.rest_0_, bf16[6,4096,128]{2,1,0:T(8,128)(2,1)S(1)} %get-tuple-element.21.rest_1_, ...), custom_call_target="tpu_custom_call" | custom-call | bytes 36900000 | tf_op jit(solution)/shard_map/gate_up/pallas_call | solution.py:451
  40.3 1.0 %collective-permute-start.11 = (bf16[8,3712]{1,0:T(8,128)(2,1)S(1)}, bf16[8,3712]{1,0:T(8,128)(2,1)S(1)}, u32[]{:S(2)}, u32[]{:S(2)}) collective-permute-start(bf16[8,3712]{1,0:T(8,128)(2,1)S(1)} %get-tuple-element.25.rest_0_), channel_id=1, source_target_pairs={{0,12},{4,8},{8,4},{12,0},{1,13},{5,9},{9,5},{13,1},{2,14},{6,10},... | collective-permute-start | bytes 178184 | tf_op jit(solution)/shard_map/ppermute | solution.py:40
  41.3 1.1 %collective-permute-start.10 = (bf16[8,3712]{1,0:T(8,128)(2,1)S(1)}, bf16[8,3712]{1,0:T(8,128)(2,1)S(1)}, u32[]{:S(2)}, u32[]{:S(2)}) collective-permute-start(bf16[8,3712]{1,0:T(8,128)(2,1)S(1)} %get-tuple-element.25.rest_0_), channel_id=1, source_target_pairs={{0,8},{4,12},{8,0},{12,4},{1,9},{5,13},{9,1},{13,5},{2,10},{6,14},... | collective-permute-start | bytes 178184 | tf_op jit(solution)/shard_map/ppermute | solution.py:40
  42.4 2.3 %collective-permute-start.9 = (bf16[8,3712]{1,0:T(8,128)(2,1)S(1)}, bf16[8,3712]{1,0:T(8,128)(2,1)S(1)}, u32[]{:S(2)}, u32[]{:S(2)}) collective-permute-start(bf16[8,3712]{1,0:T(8,128)(2,1)S(1)} %get-tuple-element.25.rest_0_), channel_id=1, source_target_pairs={{0,4},{4,0},{8,12},{12,8},{1,5},{5,1},{9,13},{13,9},{2,6},{6,2},{1... | collective-permute-start | bytes 178184 | tf_op jit(solution)/shard_map/ppermute | solution.py:40
  44.8 2.3 %collective-permute-done.11.rest_3_ = bf16[8,3712]{1,0:T(8,128)(2,1)S(1)} collective-permute-done((bf16[8,3712]{1,0:T(8,128)(2,1)S(1)}, bf16[8,3712]{1,0:T(8,128)(2,1)S(1)}, u32[]{:S(2)}, u32[]{:S(2)}) %collective-permute-start.11) | collective-permute-done | bytes 59424 | tf_op jit(solution)/shard_map/ppermute | solution.py:40
  47.0 1.7 %collective-permute-done.10.rest_2_ = bf16[8,3712]{1,0:T(8,128)(2,1)S(1)} collective-permute-done((bf16[8,3712]{1,0:T(8,128)(2,1)S(1)}, bf16[8,3712]{1,0:T(8,128)(2,1)S(1)}, u32[]{:S(2)}, u32[]{:S(2)}) %collective-permute-start.10) | collective-permute-done | bytes 59424 | tf_op jit(solution)/shard_map/ppermute | solution.py:40
  48.8 2.1 %down.1 = bf16[4,2048]{1,0:T(4,128)(2,1)S(1)} custom-call(bf16[3584,2048]{1,0:T(8,128)(2,1)S(1)} %bitcast.5, bf16[8,3712]{1,0:T(8,128)(2,1)S(1)} %get-tuple-element.25.rest_0_, bf16[8,3712]{1,0:T(8,128)(2,1)S(1)} %collective-permute-done.9.rest_1_, bf16[8,3712]{1,0:T(8,128)(2,1)S(1)} %collective-permute-done.10.rest_2_, ...), custom_call_target="tpu_custom_call" | custom-call | bytes 18450000 | tf_op jit(solution)/shard_map/down/pallas_call | solution.py:470
  50.8 0.5 collective-permute-start.14
  51.4 0.9 %collective-permute-start.13 = (bf16[4,2048]{1,0:T(4,128)(2,1)S(1)}, bf16[4,2048]{1,0:T(4,128)(2,1)S(1)}, u32[]{:S(2)}, u32[]{:S(2)}) collective-permute-start(bf16[4,2048]{1,0:T(4,128)(2,1)S(1)} %down.1), channel_id=1, source_target_pairs={{0,2},{1,3},{2,0},{3,1},{4,6},{5,7},{6,4},{7,5},{8,10},{9,11},{10,... | collective-permute-start | bytes 49160 | tf_op jit(solution)/shard_map/ppermute | solution.py:40
  52.3 0.5 collective-permute-start.12
  52.7 1.4 %collective-permute-done.14 = bf16[4,2048]{1,0:T(4,128)(2,1)S(1)} collective-permute-done((bf16[4,2048]{1,0:T(4,128)(2,1)S(1)}, bf16[4,2048]{1,0:T(4,128)(2,1)S(1)}, u32[]{:S(2)}, u32[]{:S(2)}) %collective-permute-start.14) | collective-permute-done | bytes 16416 | tf_op jit(solution)/shard_map/ppermute | solution.py:40
  54.1 1.0 %collective-permute-done.13 = bf16[4,2048]{1,0:T(4,128)(2,1)S(1)} collective-permute-done((bf16[4,2048]{1,0:T(4,128)(2,1)S(1)}, bf16[4,2048]{1,0:T(4,128)(2,1)S(1)}, u32[]{:S(2)}, u32[]{:S(2)}) %collective-permute-start.13) | collective-permute-done | bytes 16416 | tf_op jit(solution)/shard_map/ppermute | solution.py:40
  55.1 0.6 %add_convert_fusion = bf16[4,2048]{1,0:T(4,128)(2,1)} fusion(bf16[4,2048]{1,0:T(4,128)(2,1)S(1)} %collective-permute-done.14, bf16[4,2048]{1,0:T(4,128)(2,1)S(1)} %collective-permute-done.13, bf16[4,2048]{1,0:T(4,128)(2,1)S(1)} %collective-permute-done.12, bf16[4,2048]{1,0:T(4,128)(2,1)S(1)} %down.1), kind=kLoop, calls=%fused_computation | loop fusion | flops 65536 | bytes 81920 | tf_op jit(solution)/shard_map/convert_element_type | solution.py:481
  (22 shorter events, 0.0 us)
Async XLA Ops:
  5.1 8.0 %collective-permute-start = (f32[16,128]{1,0:T(8,128)S(1)}, f32[16,128]{1,0:T(8,128)S(1)}, u32[]{:S(2)}, u32[]{:S(2)}) collective-permute-start(f32[16,128]{1,0:T(8,128)S(1)} %get-tuple-element.18), channel_id=1, source_target_pairs={{0,4},{4,0},{8,12},{12,8},{1,5},{5,1},{9,13},{13,9},{2,6},{6,2},{1... | collective-permute-start | bytes 24584 | tf_op jit(solution)/shard_map/ppermute | solution.py:40
  8.2 4.9 %collective-permute-start.1 = (f32[16,128]{1,0:T(8,128)S(1)}, f32[16,128]{1,0:T(8,128)S(1)}, u32[]{:S(2)}, u32[]{:S(2)}) collective-permute-start(f32[16,128]{1,0:T(8,128)S(1)} %get-tuple-element.19), channel_id=1, source_target_pairs={{0,8},{4,12},{8,0},{12,4},{1,9},{5,13},{9,1},{13,5},{2,10},{6,14},... | collective-permute-start | bytes 24584 | tf_op jit(solution)/shard_map/ppermute | solution.py:40
  10.8 5.4 %collective-permute-start.2 = (f32[16,128]{1,0:T(8,128)S(1)}, f32[16,128]{1,0:T(8,128)S(1)}, u32[]{:S(2)}, u32[]{:S(2)}) collective-permute-start(f32[16,128]{1,0:T(8,128)S(1)} %get-tuple-element.20), channel_id=1, source_target_pairs={{0,12},{4,8},{8,4},{12,0},{1,13},{5,9},{9,5},{13,1},{2,14},{6,10},... | collective-permute-start | bytes 24584 | tf_op jit(solution)/shard_map/ppermute | solution.py:40
  20.2 7.4 %copy-start = (bf16[1024,2048]{1,0:T(8,128)(2,1)S(1)}, bf16[1024,2048]{1,0:T(8,128)(2,1)}, u32[]{:S(2)}) copy-start(bf16[1024,2048]{1,0:T(8,128)(2,1)} %w_out.1) | copy-start | bytes 12582916
  20.2 7.4 %collective-permute-start.5 = (bf16[8,128]{1,0:T(8,128)(2,1)S(1)}, bf16[8,128]{1,0:T(8,128)(2,1)S(1)}, u32[]{:S(2)}, u32[]{:S(2)}) collective-permute-start(bf16[8,128]{1,0:T(8,128)(2,1)S(1)} %get-tuple-element.22.token.rest_0_), channel_id=1, source_target_pairs={{0,12},{4,8},{8,4},{12,0},{1,13},{5,9},{9,5},{13,1},{2,14},{6,10},... | collective-permute-start | bytes 6152 | tf_op jit(solution)/shard_map/ppermute | solution.py:40
  20.9 6.7 %collective-permute-start.4 = (bf16[8,128]{1,0:T(8,128)(2,1)S(1)}, bf16[8,128]{1,0:T(8,128)(2,1)S(1)}, u32[]{:S(2)}, u32[]{:S(2)}) collective-permute-start(bf16[8,128]{1,0:T(8,128)(2,1)S(1)} %get-tuple-element.22.token.rest_0_), channel_id=1, source_target_pairs={{0,8},{4,12},{8,0},{12,4},{1,9},{5,13},{9,1},{13,5},{2,10},{6,14},... | collective-permute-start | bytes 6152 | tf_op jit(solution)/shard_map/ppermute | solution.py:40
  20.9 6.7 %collective-permute-start.3 = (bf16[8,128]{1,0:T(8,128)(2,1)S(1)}, bf16[8,128]{1,0:T(8,128)(2,1)S(1)}, u32[]{:S(2)}, u32[]{:S(2)}) collective-permute-start(bf16[8,128]{1,0:T(8,128)(2,1)S(1)} %get-tuple-element.22.token.rest_0_), channel_id=1, source_target_pairs={{0,4},{4,0},{8,12},{12,8},{1,5},{5,1},{9,13},{13,9},{2,6},{6,2},{1... | collective-permute-start | bytes 6152 | tf_op jit(solution)/shard_map/ppermute | solution.py:40
  28.3 3.8 %copy-start.1 = (bf16[4,2048]{1,0:T(4,128)(2,1)S(1)}, bf16[4,2048]{1,0:T(4,128)(2,1)}, u32[]{:S(2)}) copy-start(bf16[4,2048]{1,0:T(4,128)(2,1)} %states.1) | copy-start | bytes 49156
  28.3 3.8 %copy-start.2 = (f32[2,2048]{1,0:T(2,128)S(1)}, f32[2,2048]{1,0:T(2,128)}, u32[]{:S(2)}) copy-start(f32[2,2048]{1,0:T(2,128)} %gains.1) | copy-start | bytes 49156
  28.3 3.5 %collective-permute-start.8 = (bf16[4,2048]{1,0:T(4,128)(2,1)S(1)}, bf16[4,2048]{1,0:T(4,128)(2,1)S(1)}, u32[]{:S(2)}, u32[]{:S(2)}) collective-permute-start(bf16[4,2048]{1,0:T(4,128)(2,1)S(1)} %attn_project.1.token.rest_4_), channel_id=1, source_target_pairs={{0,3},{1,2},{2,1},{3,0},{4,7},{5,6},{6,5},{7,4},{8,11},{9,10},{10,... | collective-permute-start | bytes 49160 | tf_op jit(solution)/shard_map/ppermute | solution.py:40
  28.3 3.8 %collective-permute-start.7 = (bf16[4,2048]{1,0:T(4,128)(2,1)S(1)}, bf16[4,2048]{1,0:T(4,128)(2,1)S(1)}, u32[]{:S(2)}, u32[]{:S(2)}) collective-permute-start(bf16[4,2048]{1,0:T(4,128)(2,1)S(1)} %attn_project.1.token.rest_4_), channel_id=1, source_target_pairs={{0,2},{1,3},{2,0},{3,1},{4,6},{5,7},{6,4},{7,5},{8,10},{9,11},{10,... | collective-permute-start | bytes 49160 | tf_op jit(solution)/shard_map/ppermute | solution.py:40
  29.9 2.3 %collective-permute-start.6 = (bf16[4,2048]{1,0:T(4,128)(2,1)S(1)}, bf16[4,2048]{1,0:T(4,128)(2,1)S(1)}, u32[]{:S(2)}, u32[]{:S(2)}) collective-permute-start(bf16[4,2048]{1,0:T(4,128)(2,1)S(1)} %attn_project.1.token.rest_4_), channel_id=1, source_target_pairs={{0,1},{1,0},{2,3},{3,2},{4,5},{5,4},{6,7},{7,6},{8,9},{9,8},{10,11... | collective-permute-start | bytes 49160 | tf_op jit(solution)/shard_map/ppermute | solution.py:40
  32.1 16.6 %slice-start = ((s8[14680064]{0:T(1024)(128)(4,1)}), s8[4194304]{0:T(1024)(128)(4,1)S(1)}, s32[]{:S(2)}) async-start(s8[14680064]{0:T(1024)(128)(4,1)} %bitcast.4), calls=%async_computation | async-start | bytes 8388608
  32.1 16.6 %slice-start.1 = ((s8[14680064]{0:T(1024)(128)(4,1)}), s8[4194304]{0:T(1024)(128)(4,1)S(1)}, s32[]{:S(2)}) async-start(s8[14680064]{0:T(1024)(128)(4,1)} %bitcast.4), calls=%async_computation.1 | async-start | bytes 8388608
  32.1 16.6 %slice-start.2 = ((s8[14680064]{0:T(1024)(128)(4,1)}), s8[4194304]{0:T(1024)(128)(4,1)S(1)}, s32[]{:S(2)}) async-start(s8[14680064]{0:T(1024)(128)(4,1)} %bitcast.4), calls=%async_computation.2 | async-start | bytes 8388608
  32.2 16.6 %slice-start.3 = ((s8[14680064]{0:T(1024)(128)(4,1)}), s8[2097152]{0:T(1024)(128)(4,1)S(1)}, s32[]{:S(2)}) async-start(s8[14680064]{0:T(1024)(128)(4,1)} %bitcast.4), calls=%async_computation.3 | async-start | bytes 4194304
  40.3 6.8 %collective-permute-start.11 = (bf16[8,3712]{1,0:T(8,128)(2,1)S(1)}, bf16[8,3712]{1,0:T(8,128)(2,1)S(1)}, u32[]{:S(2)}, u32[]{:S(2)}) collective-permute-start(bf16[8,3712]{1,0:T(8,128)(2,1)S(1)} %get-tuple-element.25.rest_0_), channel_id=1, source_target_pairs={{0,12},{4,8},{8,4},{12,0},{1,13},{5,9},{9,5},{13,1},{2,14},{6,10},... | collective-permute-start | bytes 178184 | tf_op jit(solution)/shard_map/ppermute | solution.py:40
  41.3 7.4 %collective-permute-start.10 = (bf16[8,3712]{1,0:T(8,128)(2,1)S(1)}, bf16[8,3712]{1,0:T(8,128)(2,1)S(1)}, u32[]{:S(2)}, u32[]{:S(2)}) collective-permute-start(bf16[8,3712]{1,0:T(8,128)(2,1)S(1)} %get-tuple-element.25.rest_0_), channel_id=1, source_target_pairs={{0,8},{4,12},{8,0},{12,4},{1,9},{5,13},{9,1},{13,5},{2,10},{6,14},... | collective-permute-start | bytes 178184 | tf_op jit(solution)/shard_map/ppermute | solution.py:40
  42.4 6.3 %collective-permute-start.9 = (bf16[8,3712]{1,0:T(8,128)(2,1)S(1)}, bf16[8,3712]{1,0:T(8,128)(2,1)S(1)}, u32[]{:S(2)}, u32[]{:S(2)}) collective-permute-start(bf16[8,3712]{1,0:T(8,128)(2,1)S(1)} %get-tuple-element.25.rest_0_), channel_id=1, source_target_pairs={{0,4},{4,0},{8,12},{12,8},{1,5},{5,1},{9,13},{13,9},{2,6},{6,2},{1... | collective-permute-start | bytes 178184 | tf_op jit(solution)/shard_map/ppermute | solution.py:40
  50.8 3.3 %collective-permute-start.14 = (bf16[4,2048]{1,0:T(4,128)(2,1)S(1)}, bf16[4,2048]{1,0:T(4,128)(2,1)S(1)}, u32[]{:S(2)}, u32[]{:S(2)}) collective-permute-start(bf16[4,2048]{1,0:T(4,128)(2,1)S(1)} %down.1), channel_id=1, source_target_pairs={{0,3},{1,2},{2,1},{3,0},{4,7},{5,6},{6,5},{7,4},{8,11},{9,10},{10,... | collective-permute-start | bytes 49160 | tf_op jit(solution)/shard_map/ppermute | solution.py:40
  51.4 3.7 %collective-permute-start.13 = (bf16[4,2048]{1,0:T(4,128)(2,1)S(1)}, bf16[4,2048]{1,0:T(4,128)(2,1)S(1)}, u32[]{:S(2)}, u32[]{:S(2)}) collective-permute-start(bf16[4,2048]{1,0:T(4,128)(2,1)S(1)} %down.1), channel_id=1, source_target_pairs={{0,2},{1,3},{2,0},{3,1},{4,6},{5,7},{6,4},{7,5},{8,10},{9,11},{10,... | collective-permute-start | bytes 49160 | tf_op jit(solution)/shard_map/ppermute | solution.py:40
  52.3 2.8 %collective-permute-start.12 = (bf16[4,2048]{1,0:T(4,128)(2,1)S(1)}, bf16[4,2048]{1,0:T(4,128)(2,1)S(1)}, u32[]{:S(2)}, u32[]{:S(2)}) collective-permute-start(bf16[4,2048]{1,0:T(4,128)(2,1)S(1)} %down.1), channel_id=1, source_target_pairs={{0,1},{1,0},{2,3},{3,2},{4,5},{5,4},{6,7},{7,6},{8,9},{9,8},{10,11... | collective-permute-start | bytes 49160 | tf_op jit(solution)/shard_map/ppermute | solution.py:40

commit v9 on v8

--- a/solution.py
+++ b/solution.py
@@ -14,8 +14,9 @@
 ROPE_BASE = 500000.0
 LANES = 128
 MIB = 1 << 20
-TILE_GROUP = 4
-GU_SHARES = (4, 6, 6, 2, 10)
+COPY_ROWS = 512
+KEY_ROWS = 512
+GU_SHARES = (8, 6, 2, 2, 4, 4, 2)
 F32 = jnp.float32
 BF16 = jnp.bfloat16
 QUARTER = (1.5703125, 4.837512969970703125e-4, 7.549789948768648e-8)
@@ -82,15 +83,17 @@
     return w if len(w.shape) == 2 else w.reshape(w.shape[0] * w.shape[1], w.shape[2])
 
 
-def times_tiles(left, tiles, first, store, tile_ready=None):
-    count = tiles.shape[0]
-    for start in range(0, count, TILE_GROUP):
-        group = range(start, min(start + TILE_GROUP, count))
-        if tile_ready is not None:
-            for i in group:
-                tile_ready(i)
-        columns = jnp.concatenate([tiles[i] for i in group], axis=1)
-        store(first + start, jnp.dot(left[...], columns, preferred_element_type=F32))
+def block_copies(matrix, first, buf, sems):
+    rows, columns = buf.shape
+    chunk = min(rows, COPY_ROWS)
+    return [
+        pltpu.make_async_copy(
+            matrix.at[pl.ds(start, chunk), pl.ds(first * LANES, columns)],
+            buf.at[pl.ds(start, chunk)],
+            sems.at[start // chunk],
+        )
+        for start in range(0, rows, chunk)
+    ]
 
 
 def pick_doc(value, doc, docs):
@@ -214,10 +217,10 @@
         copy.wait()
 
 
-def attend_kernel(tp, heads, rows, first, table, cache, w, *rest):
+def attend_kernel(tp, heads, rows, first, table, keys, cache, w, *rest):
     parts = rest[:tp]
     heads_out, new_kv_out, w_ready, scores, w_sems = rest[-5:]
-    w_copies = tile_copies(matrix_of(w), first, w_ready, w_sems)
+    w_copies = block_copies(matrix_of(w), first, w_ready, w_sems)
     for copy in w_copies:
         copy.start()
     blocks = cache.shape[1] // rows
@@ -237,11 +240,8 @@
     length = table[2:3, :]
     tops = jnp.full((heads, LANES), -jnp.inf, F32)
     for b in range(blocks):
-        block = lax.dot_general(
-            query,
-            cache[0, b * rows : (b + 1) * rows, :],
-            (((1,), (1,)), ((), ())),
-            preferred_element_type=F32,
+        block = jnp.dot(
+            query, keys[:, b * rows : (b + 1) * rows], preferred_element_type=F32
         )
         for start in range(0, rows, LANES):
             at = b * rows + start
@@ -284,22 +284,35 @@
 
 
 def fetch_kernel(first, token, w, out, sems):
-    copies = tile_copies(matrix_of(w), first, out, sems)
+    copies = block_copies(matrix_of(w), first, out, sems)
     for copy in copies:
         copy.start()
     for copy in copies:
         copy.wait()
 
 
+def fetch_and_turn_kernel(first, token, w, cache, out, turned, sems):
+    copies = block_copies(matrix_of(w), first, out, sems)
+    for copy in copies:
+        copy.start()
+    for start in range(0, cache.shape[1], KEY_ROWS):
+        turned[:, start : start + KEY_ROWS] = cache[0, start : start + KEY_ROWS, :].T
+    for copy in copies:
+        copy.wait()
+
+
 def gate_up_kernel(kv, groups, first, states, gains, w, *rest):
     ready, parts = rest[:groups], rest[groups : groups + kv]
-    attn_out, partial_out, w_tiles, spread_buf, w_sems = rest[groups + kv :]
+    attn_out, partial_out, *blocks, spread_buf, w_sems = rest[groups + kv :]
     docs, width = states.shape
     hidden = w.shape[2]
     w_matrix = matrix_of(w)
-    copies = tile_copies(w_matrix, first, w_tiles, w_sems)
-    for copy in copies:
-        copy.start()
+    copies = []
+    for i, block in enumerate(blocks):
+        copies.append(block_copies(w_matrix, first, block, w_sems.at[i]))
+        first += block.shape[1] // LANES
+        for copy in copies[-1]:
+            copy.start()
     attn = tree_sum([part[...].astype(F32) for part in parts]).astype(BF16)
     attn_out[...] = attn
     resid = (states[...].astype(F32) + attn.astype(F32)).astype(BF16).astype(F32)
@@ -307,16 +320,15 @@
     high, low = two_parts(resid * gains[1:2, :])
     spread(jnp.concatenate([high, high, low, low], axis=0).astype(BF16), spread_buf, docs)
 
-    def store(tile, product):
-        summed = product[: 2 * docs] + product[2 * docs :]
-        columns = slice(tile * LANES, tile * LANES + summed.shape[1])
-        partial_out[:, columns] = summed.astype(BF16)
-
-    tile = 0
-    for group in ready:
-        times_tiles(spread_buf, group, tile, store)
-        tile += group.shape[0]
-    times_tiles(spread_buf, w_tiles, tile, store, lambda i: copies[i].wait())
+    at = 0
+    for i, block in enumerate([*ready, *blocks]):
+        if i >= groups:
+            for copy in copies[i - groups]:
+                copy.wait()
+        product = jnp.dot(spread_buf[...], block[...], preferred_element_type=F32)
+        columns = slice(at, at + block.shape[1])
+        partial_out[:, columns] = (product[: 2 * docs] + product[2 * docs :]).astype(BF16)
+        at += block.shape[1]
     lane = lax.broadcasted_iota(jnp.int32, (docs, LANES), 1)
     first = squares.astype(BF16).astype(F32)
     second = (squares - first).astype(BF16).astype(F32)
@@ -397,43 +409,55 @@
     shares = list(zip(bounds, bounds[1:]))
     fetched = []
 
-    def tiles_of(share, rows):
-        return pltpu.VMEM((share[1] - share[0], rows, LANES), BF16)
-
-    def fetch(weights, share, rows, token):
+    chunks = max(2 * width // COPY_ROWS, 1)
+
+    def block_of(share):
+        return pltpu.VMEM((2 * width, (share[1] - share[0]) * LANES), BF16)
+
+    def fetch(share, token):
         return pl.pallas_call(
             functools.partial(fetch_kernel, share[0]),
-            out_shape=tiles_of(share, rows),
+            out_shape=block_of(share),
             in_specs=[hbm(), hbm()],
             out_specs=vmem(),
-            scratch_shapes=[pltpu.SemaphoreType.DMA((share[1] - share[0],))],
+            scratch_shapes=[pltpu.SemaphoreType.DMA((chunks,))],
             compiler_params=params(docs, 2),
             cost_estimate=cost(0.3 * (share[1] - share[0])),
             name="fetch",
-        )(token, weights)
-
-    fetched.append(fetch(w_gu, shares[0], 2 * width, table))
+        )(token, w_gu)
+
+    w_ready, turned = pl.pallas_call(
+        functools.partial(fetch_and_turn_kernel, shares[0][0]),
+        out_shape=[block_of(shares[0]), pltpu.VMEM((LANES, cache_len), BF16)],
+        in_specs=[hbm(), hbm(), vmem()],
+        out_specs=[vmem(), vmem()],
+        scratch_shapes=[pltpu.SemaphoreType.DMA((chunks,))],
+        compiler_params=params(docs, 4),
+        cost_estimate=cost(3),
+        name="fetch_and_turn_keys",
+    )(table, w_gu, cache_tiles)
+    fetched.append(w_ready)
     qkv_parts = exchange([qkv_parts[-s] for s in range(tp)], "tp", tp)
     head_out, new_kv, w_ready = pl.pallas_call(
         functools.partial(attend_kernel, tp, heads, 512, shares[1][0]),
         out_shape=[
             jax.ShapeDtypeStruct((heads, LANES), BF16),
             jax.ShapeDtypeStruct((1, 2 * LANES), BF16),
-            tiles_of(shares[1], 2 * width),
+            block_of(shares[1]),
         ],
-        in_specs=[vmem(), vmem(), hbm()] + [vmem()] * tp + [hbm()] * len(fetched),
+        in_specs=[vmem(), vmem(), vmem(), hbm()] + [vmem()] * tp + [hbm()] * len(fetched),
         out_specs=[vmem()] * 3,
         scratch_shapes=[
             pltpu.VMEM((heads, cache_len), F32),
-            pltpu.SemaphoreType.DMA((shares[1][1] - shares[1][0],)),
+            pltpu.SemaphoreType.DMA((chunks,)),
         ],
         compiler_params=params(docs, 6),
         cost_estimate=cost(8),
         name="attend",
-    )(table, cache_tiles, w_gu, *qkv_parts, *fetched)
+    )(table, turned, cache_tiles, w_gu, *qkv_parts, *fetched)
     fetched.append(w_ready)
 
-    fetched.append(fetch(w_gu, shares[2], 2 * width, head_out))
+    fetched.append(fetch(shares[2], head_out))
     head_parts = exchange([head_out] * tp, "tp", tp)
     out_part = pl.pallas_call(
         functools.partial(out_kernel, tp),
@@ -446,7 +470,7 @@
         name="attn_project",
     )(places, w_out, *head_parts, fetched[-1])
 
-    fetched.append(fetch(w_gu, shares[3], 2 * width, out_part))
+    fetched.append(fetch(shares[3], out_part))
     out_parts = exchange([out_part] * kv, "kv", kv)
     attn_out, gu_part = pl.pallas_call(
         functools.partial(gate_up_kernel, kv, len(fetched), shares[4][0]),
@@ -457,9 +481,9 @@
         in_specs=[vmem(), vmem(), hbm()] + [vmem()] * (len(fetched) + kv),
         out_specs=[vmem()] * 2,
         scratch_shapes=[
-            tiles_of(shares[4], 2 * width),
+            *(block_of(share) for share in shares[4:]),
             pltpu.VMEM((4 * docs, 2 * width), BF16),
-            pltpu.SemaphoreType.DMA((shares[4][1] - shares[4][0],)),
+            pltpu.SemaphoreType.DMA((len(shares) - 4, chunks)),
         ],
         compiler_params=params(docs, 20),
         cost_estimate=cost(10),

time: 56 us -> 52.6 us (0.939)
  Pallas kernels: 26 us -> 23.2 us
    pallas_call x1, Pallas kernels: 8.11 us -> 5.4 us  [per_device(): pl.pallas_call(functools.partial(gate_up_kernel, kv, len(fetched), shares...]
  transfers between devices with their start and end apart: 15 -> 15, of which waited for: 6 -> 7; matrix products, arithmetic and copies ran while one was open for 0% -> 0% of each run, Pallas kernels for 12% -> 14%
where the time goes in v9:
time: 52.6 us; the launch traced here: 52.3 us
  Pallas kernels  23.2 us (44%)
  starting transfers between devices  18.3 us (35%)
  waiting for transfers between devices  9.31 us (18%)
  between operations  0.81 us (2%)
  other arithmetic  0.63 us (1%)
    ppermute x15, starting transfers between devices, exchange(): lax.ppermute(arrays[s], axis, [(i, i ^ s) for i in range(size)])  18.3 us
    ppermute x15, waiting for transfers between devices, exchange(): lax.ppermute(arrays[s], axis, [(i, i ^ s) for i in range(size)])  9.31 us
    pallas_call x1, Pallas kernels, per_device(): pl.pallas_call(functools.partial(gate_up_kernel, kv, len(fetched), shares...  5.4 us
    pallas_call x1, Pallas kernels, per_device(): pl.pallas_call(functools.partial(qkv_kernel, tp), out_shape=[jax.ShapeDty...  4.43 us
    pallas_call x1, Pallas kernels, per_device(): pl.pallas_call(functools.partial(fetch_and_turn_kernel, shares[0][0]), ou...  3.62 us
    pallas_call x1, Pallas kernels, per_device(): pl.pallas_call(functools.partial(attend_kernel, tp, heads, 512, shares[1]...  3.57 us
    pallas_call x2, Pallas kernels, fetch(): pl.pallas_call(functools.partial(fetch_kernel, share[0]), out_shape=block...  3.44 us
    pallas_call x1, Pallas kernels, per_device(): pl.pallas_call(functools.partial(down_kernel, tp), out_shape=jax.ShapeDty...  2.09 us
  transfers between devices with their start and end apart: 15, of which 7 were waited for; matrix products, arithmetic and copies ran while one was open for 0% of the time, Pallas kernels for 14%

profile of v9, /device:TPU:0, one launch (start us, length us, event | category | flops | bytes accessed | tf_op | source)
XLA Modules:
  0.0 52.3 jit_solution(6813964461663840097)
XLA Ops:
  0.6 4.4 %qkv.1 = (f32[16,128]{1,0:T(8,128)S(1)}, f32[16,128]{1,0:T(8,128)S(1)}, f32[16,128]{1,0:T(8,128)S(1)}, f32[16,128]{1,0:T(8,128)S(1)}, f32[8,128]{1,0:T(8,128)S(1...) custom-call(s32[4]{0:T(128)} %owner_hbm.1, s32[4]{0:T(128)} %lengths_hbm.1, ...), custom_call_target="tpu_custom_call" | custom-call | bytes 29520000 | tf_op jit(solution)/shard_map/qkv/pallas_call | solution.py:380
  5.1 3.1 %collective-permute-start = (f32[16,128]{1,0:T(8,128)S(1)}, f32[16,128]{1,0:T(8,128)S(1)}, u32[]{:S(2)}, u32[]{:S(2)}) collective-permute-start(f32[16,128]{1,0:T(8,128)S(1)} %get-tuple-element.22), channel_id=1, source_target_pairs={{0,4},{4,0},{8,12},{12,8},{1,5},{5,1},{9,13},{13,9},{2,6},{6,2},{1... | collective-permute-start | bytes 24584 | tf_op jit(solution)/shard_map/ppermute | solution.py:41
  8.2 2.6 %collective-permute-start.1 = (f32[16,128]{1,0:T(8,128)S(1)}, f32[16,128]{1,0:T(8,128)S(1)}, u32[]{:S(2)}, u32[]{:S(2)}) collective-permute-start(f32[16,128]{1,0:T(8,128)S(1)} %get-tuple-element.23), channel_id=1, source_target_pairs={{0,8},{4,12},{8,0},{12,4},{1,9},{5,13},{9,1},{13,5},{2,10},{6,14},... | collective-permute-start | bytes 24584 | tf_op jit(solution)/shard_map/ppermute | solution.py:41
  10.8 3.6 %fetch_and_turn_keys.1 = (bf16[4096,1024]{1,0:T(8,128)(2,1)S(1)}, bf16[128,8192]{1,0:T(8,128)(2,1)S(1)}) custom-call(f32[8,128]{1,0:T(8,128)S(1)} %get-tuple-element.17.token.table, bf16[2048,2,3584]{2,1,0:T(2,128)(2,1)} %w.9, bf16[2,8192,128]{2,1,0:T(8,128)(2,1)S(1)} %get-tuple-element.18.cache), custom_call_target="tpu_custom_call" | custom-call | bytes 11070000 | tf_op jit(solution)/shard_map/fetch_and_turn_keys/pallas_call | solution.py:429
  14.4 0.0 collective-permute-done.rest_1_
  14.4 0.0 collective-permute-done.1.rest_2_
  14.4 1.8 %collective-permute-done.2.rest_3_ = f32[16,128]{1,0:T(8,128)S(1)} collective-permute-done((f32[16,128]{1,0:T(8,128)S(1)}, f32[16,128]{1,0:T(8,128)S(1)}, u32[]{:S(2)}, u32[]{:S(2)}) %collective-permute-start.2) | collective-permute-done | bytes 8224 | tf_op jit(solution)/shard_map/ppermute | solution.py:41
  16.2 3.6 %attend.1 = (bf16[8,128]{1,0:T(8,128)(2,1)S(1)}, bf16[1,256]{1,0:T(2,128)(2,1)}, bf16[4096,768]{1,0:T(8,128)(2,1)S(1)}) custom-call(f32[8,128]{1,0:T(8,128)S(1)} %get-tuple-element.17.token.table, bf16[128,8192]{1,0:T(8,128)(2,1)S(1)} %get-tuple-element.20.keys, bf16[2,8192,128]{2,1,0:T(8,128)(2,1)S(1)} %get-tuple-element.18.cache, ...), custom_call_target="tpu_custom_call" | custom-call | bytes 29520000 | tf_op jit(solution)/shard_map/attend/pallas_call | solution.py:441
  19.8 0.0 copy-start
  19.8 2.1 %collective-permute-start.5 = (bf16[8,128]{1,0:T(8,128)(2,1)S(1)}, bf16[8,128]{1,0:T(8,128)(2,1)S(1)}, u32[]{:S(2)}, u32[]{:S(2)}) collective-permute-start(bf16[8,128]{1,0:T(8,128)(2,1)S(1)} %get-tuple-element.26.token.rest_0_), channel_id=1, source_target_pairs={{0,12},{4,8},{8,4},{12,0},{1,13},{5,9},{9,5},{13,1},{2,14},{6,10},... | collective-permute-start | bytes 6152 | tf_op jit(solution)/shard_map/ppermute | solution.py:41
  21.9 2.3 %collective-permute-start.3 = (bf16[8,128]{1,0:T(8,128)(2,1)S(1)}, bf16[8,128]{1,0:T(8,128)(2,1)S(1)}, u32[]{:S(2)}, u32[]{:S(2)}) collective-permute-start(bf16[8,128]{1,0:T(8,128)(2,1)S(1)} %get-tuple-element.26.token.rest_0_), channel_id=1, source_target_pairs={{0,4},{4,0},{8,12},{12,8},{1,5},{5,1},{9,13},{13,9},{2,6},{6,2},{1... | collective-permute-start | bytes 6152 | tf_op jit(solution)/shard_map/ppermute | solution.py:41
  24.2 1.7 %fetch.2.rest_4_.rest_2_ = bf16[4096,256]{1,0:T(8,128)(2,1)S(1)} custom-call(bf16[8,128]{1,0:T(8,128)(2,1)S(1)} %get-tuple-element.26.token.rest_0_, bf16[2048,2,3584]{2,1,0:T(2,128)(2,1)} %w.9), custom_call_target="tpu_custom_call" | custom-call | bytes 2214000 | tf_op jit(solution)/shard_map/fetch/pallas_call | solution.py:418
  26.0 0.4 collective-permute-done.4.rest_2_
  26.4 0.7 %attn_project.1.token.rest_4_ = bf16[4,2048]{1,0:T(4,128)(2,1)S(1)} custom-call(s32[8,128]{1,0:T(8,128)S(1)} %get-tuple-element.27.places, bf16[1024,2048]{1,0:T(8,128)(2,1)S(1)} %copy-done, bf16[8,128]{1,0:T(8,128)(2,1)S(1)} %get-tuple-element.26.token.rest_0_, bf16[8,128]{1,0:T(8,128)(2,1)S(1)} %collective-permute-done.3.rest_1_, ...), custom_call_target="tpu_custom_call" | custom-call | bytes 22140000 | tf_op jit(solution)/shard_map/attn_project/pallas_call | solution.py:462
  27.1 0.0 collective-permute-start.8
  27.1 1.6 %collective-permute-start.7 = (bf16[4,2048]{1,0:T(4,128)(2,1)S(1)}, bf16[4,2048]{1,0:T(4,128)(2,1)S(1)}, u32[]{:S(2)}, u32[]{:S(2)}) collective-permute-start(bf16[4,2048]{1,0:T(4,128)(2,1)S(1)} %attn_project.1.token.rest_4_), channel_id=1, source_target_pairs={{0,2},{1,3},{2,0},{3,1},{4,6},{5,7},{6,4},{7,5},{8,10},{9,11},{10,... | collective-permute-start | bytes 49160 | tf_op jit(solution)/shard_map/ppermute | solution.py:41
  28.6 0.3 collective-permute-start.6
  28.9 1.7 %fetch.3.rest_3_ = bf16[4096,256]{1,0:T(8,128)(2,1)S(1)} custom-call(bf16[4,2048]{1,0:T(4,128)(2,1)S(1)} %attn_project.1.token.rest_4_, bf16[2048,2,3584]{2,1,0:T(2,128)(2,1)} %w.9), custom_call_target="tpu_custom_call" | custom-call | bytes 2214000 | tf_op jit(solution)/shard_map/fetch/pallas_call | solution.py:418
  30.7 0.2 collective-permute-done.7.rest_6_
  30.9 5.4 %gate_up.1 = (bf16[4,2048]{1,0:T(4,128)(2,1)}, bf16[8,3712]{1,0:T(8,128)(2,1)S(1)}) custom-call(bf16[4,2048]{1,0:T(4,128)(2,1)S(1)} %copy-done.1, f32[2,2048]{1,0:T(2,128)S(1)} %copy-done.2, bf16[2048,2,3584]{2,1,0:T(2,128)(2,1)} %w.9, bf16[4096,1024]{1,0:T(8,128)(2,1)S(1)} %get-tuple-element.19.rest_4_.rest_0_, ...), custom_call_target="tpu_custom_call" | custom-call | bytes 36900000 | tf_op jit(solution)/shard_map/gate_up/pallas_call | solution.py:475
  36.3 1.9 %collective-permute-start.11 = (bf16[8,3712]{1,0:T(8,128)(2,1)S(1)}, bf16[8,3712]{1,0:T(8,128)(2,1)S(1)}, u32[]{:S(2)}, u32[]{:S(2)}) collective-permute-start(bf16[8,3712]{1,0:T(8,128)(2,1)S(1)} %get-tuple-element.29.rest_0_), channel_id=1, source_target_pairs={{0,12},{4,8},{8,4},{12,0},{1,13},{5,9},{9,5},{13,1},{2,14},{6,10},... | collective-permute-start | bytes 178184 | tf_op jit(solution)/shard_map/ppermute | solution.py:41
  38.2 1.1 %collective-permute-start.10 = (bf16[8,3712]{1,0:T(8,128)(2,1)S(1)}, bf16[8,3712]{1,0:T(8,128)(2,1)S(1)}, u32[]{:S(2)}, u32[]{:S(2)}) collective-permute-start(bf16[8,3712]{1,0:T(8,128)(2,1)S(1)} %get-tuple-element.29.rest_0_), channel_id=1, source_target_pairs={{0,8},{4,12},{8,0},{12,4},{1,9},{5,13},{9,1},{13,5},{2,10},{6,14},... | collective-permute-start | bytes 178184 | tf_op jit(solution)/shard_map/ppermute | solution.py:41
  39.3 1.5 %collective-permute-start.9 = (bf16[8,3712]{1,0:T(8,128)(2,1)S(1)}, bf16[8,3712]{1,0:T(8,128)(2,1)S(1)}, u32[]{:S(2)}, u32[]{:S(2)}) collective-permute-start(bf16[8,3712]{1,0:T(8,128)(2,1)S(1)} %get-tuple-element.29.rest_0_), channel_id=1, source_target_pairs={{0,4},{4,0},{8,12},{12,8},{1,5},{5,1},{9,13},{13,9},{2,6},{6,2},{1... | collective-permute-start | bytes 178184 | tf_op jit(solution)/shard_map/ppermute | solution.py:41
  40.8 2.2 %collective-permute-done.11.rest_3_ = bf16[8,3712]{1,0:T(8,128)(2,1)S(1)} collective-permute-done((bf16[8,3712]{1,0:T(8,128)(2,1)S(1)}, bf16[8,3712]{1,0:T(8,128)(2,1)S(1)}, u32[]{:S(2)}, u32[]{:S(2)}) %collective-permute-start.11) | collective-permute-done | bytes 59424 | tf_op jit(solution)/shard_map/ppermute | solution.py:41
  43.0 2.4 %collective-permute-done.10.rest_2_ = bf16[8,3712]{1,0:T(8,128)(2,1)S(1)} collective-permute-done((bf16[8,3712]{1,0:T(8,128)(2,1)S(1)}, bf16[8,3712]{1,0:T(8,128)(2,1)S(1)}, u32[]{:S(2)}, u32[]{:S(2)}) %collective-permute-start.10) | collective-permute-done | bytes 59424 | tf_op jit(solution)/shard_map/ppermute | solution.py:41
  45.4 2.1 %down.1 = bf16[4,2048]{1,0:T(4,128)(2,1)S(1)} custom-call(bf16[3584,2048]{1,0:T(8,128)(2,1)S(1)} %bitcast.5, bf16[8,3712]{1,0:T(8,128)(2,1)S(1)} %get-tuple-element.29.rest_0_, bf16[8,3712]{1,0:T(8,128)(2,1)S(1)} %collective-permute-done.9.rest_1_, bf16[8,3712]{1,0:T(8,128)(2,1)S(1)} %collective-permute-done.10.rest_2_, ...), custom_call_target="tpu_custom_call" | custom-call | bytes 18450000 | tf_op jit(solution)/shard_map/down/pallas_call | solution.py:494
  47.5 0.3 collective-permute-start.14
  47.8 1.1 %collective-permute-start.13 = (bf16[4,2048]{1,0:T(4,128)(2,1)S(1)}, bf16[4,2048]{1,0:T(4,128)(2,1)S(1)}, u32[]{:S(2)}, u32[]{:S(2)}) collective-permute-start(bf16[4,2048]{1,0:T(4,128)(2,1)S(1)} %down.1), channel_id=1, source_target_pairs={{0,2},{1,3},{2,0},{3,1},{4,6},{5,7},{6,4},{7,5},{8,10},{9,11},{10,... | collective-permute-start | bytes 49160 | tf_op jit(solution)/shard_map/ppermute | solution.py:41
  49.0 0.4 collective-permute-start.12
  49.3 1.4 %collective-permute-done.14 = bf16[4,2048]{1,0:T(4,128)(2,1)S(1)} collective-permute-done((bf16[4,2048]{1,0:T(4,128)(2,1)S(1)}, bf16[4,2048]{1,0:T(4,128)(2,1)S(1)}, u32[]{:S(2)}, u32[]{:S(2)}) %collective-permute-start.14) | collective-permute-done | bytes 16416 | tf_op jit(solution)/shard_map/ppermute | solution.py:41
  50.8 0.9 %collective-permute-done.13 = bf16[4,2048]{1,0:T(4,128)(2,1)S(1)} collective-permute-done((bf16[4,2048]{1,0:T(4,128)(2,1)S(1)}, bf16[4,2048]{1,0:T(4,128)(2,1)S(1)}, u32[]{:S(2)}, u32[]{:S(2)}) %collective-permute-start.13) | collective-permute-done | bytes 16416 | tf_op jit(solution)/shard_map/ppermute | solution.py:41
  51.7 0.6 %add_convert_fusion = bf16[4,2048]{1,0:T(4,128)(2,1)} fusion(bf16[4,2048]{1,0:T(4,128)(2,1)S(1)} %collective-permute-done.14, bf16[4,2048]{1,0:T(4,128)(2,1)S(1)} %collective-permute-done.13, bf16[4,2048]{1,0:T(4,128)(2,1)S(1)} %collective-permute-done.12, bf16[4,2048]{1,0:T(4,128)(2,1)S(1)} %down.1), kind=kLoop, calls=%fused_computation | loop fusion | flops 65536 | bytes 81920 | tf_op jit(solution)/shard_map/convert_element_type | solution.py:505
  (22 shorter events, 0.0 us)
Async XLA Ops:
  5.1 9.3 %collective-permute-start = (f32[16,128]{1,0:T(8,128)S(1)}, f32[16,128]{1,0:T(8,128)S(1)}, u32[]{:S(2)}, u32[]{:S(2)}) collective-permute-start(f32[16,128]{1,0:T(8,128)S(1)} %get-tuple-element.22), channel_id=1, source_target_pairs={{0,4},{4,0},{8,12},{12,8},{1,5},{5,1},{9,13},{13,9},{2,6},{6,2},{1... | collective-permute-start | bytes 24584 | tf_op jit(solution)/shard_map/ppermute | solution.py:41
  8.2 6.2 %collective-permute-start.1 = (f32[16,128]{1,0:T(8,128)S(1)}, f32[16,128]{1,0:T(8,128)S(1)}, u32[]{:S(2)}, u32[]{:S(2)}) collective-permute-start(f32[16,128]{1,0:T(8,128)S(1)} %get-tuple-element.23), channel_id=1, source_target_pairs={{0,8},{4,12},{8,0},{12,4},{1,9},{5,13},{9,1},{13,5},{2,10},{6,14},... | collective-permute-start | bytes 24584 | tf_op jit(solution)/shard_map/ppermute | solution.py:41
  10.8 5.4 %collective-permute-start.2 = (f32[16,128]{1,0:T(8,128)S(1)}, f32[16,128]{1,0:T(8,128)S(1)}, u32[]{:S(2)}, u32[]{:S(2)}) collective-permute-start(f32[16,128]{1,0:T(8,128)S(1)} %get-tuple-element.24), channel_id=1, source_target_pairs={{0,12},{4,8},{8,4},{12,0},{1,13},{5,9},{9,5},{13,1},{2,14},{6,10},... | collective-permute-start | bytes 24584 | tf_op jit(solution)/shard_map/ppermute | solution.py:41
  19.8 6.6 %copy-start = (bf16[1024,2048]{1,0:T(8,128)(2,1)S(1)}, bf16[1024,2048]{1,0:T(8,128)(2,1)}, u32[]{:S(2)}) copy-start(bf16[1024,2048]{1,0:T(8,128)(2,1)} %w_out.1) | copy-start | bytes 12582916
  19.8 6.2 %collective-permute-start.5 = (bf16[8,128]{1,0:T(8,128)(2,1)S(1)}, bf16[8,128]{1,0:T(8,128)(2,1)S(1)}, u32[]{:S(2)}, u32[]{:S(2)}) collective-permute-start(bf16[8,128]{1,0:T(8,128)(2,1)S(1)} %get-tuple-element.26.token.rest_0_), channel_id=1, source_target_pairs={{0,12},{4,8},{8,4},{12,0},{1,13},{5,9},{9,5},{13,1},{2,14},{6,10},... | collective-permute-start | bytes 6152 | tf_op jit(solution)/shard_map/ppermute | solution.py:41
  21.9 4.5 %collective-permute-start.4 = (bf16[8,128]{1,0:T(8,128)(2,1)S(1)}, bf16[8,128]{1,0:T(8,128)(2,1)S(1)}, u32[]{:S(2)}, u32[]{:S(2)}) collective-permute-start(bf16[8,128]{1,0:T(8,128)(2,1)S(1)} %get-tuple-element.26.token.rest_0_), channel_id=1, source_target_pairs={{0,8},{4,12},{8,0},{12,4},{1,9},{5,13},{9,1},{13,5},{2,10},{6,14},... | collective-permute-start | bytes 6152 | tf_op jit(solution)/shard_map/ppermute | solution.py:41
  21.9 4.5 %collective-permute-start.3 = (bf16[8,128]{1,0:T(8,128)(2,1)S(1)}, bf16[8,128]{1,0:T(8,128)(2,1)S(1)}, u32[]{:S(2)}, u32[]{:S(2)}) collective-permute-start(bf16[8,128]{1,0:T(8,128)(2,1)S(1)} %get-tuple-element.26.token.rest_0_), channel_id=1, source_target_pairs={{0,4},{4,0},{8,12},{12,8},{1,5},{5,1},{9,13},{13,9},{2,6},{6,2},{1... | collective-permute-start | bytes 6152 | tf_op jit(solution)/shard_map/ppermute | solution.py:41
  27.0 3.8 %copy-start.1 = (bf16[4,2048]{1,0:T(4,128)(2,1)S(1)}, bf16[4,2048]{1,0:T(4,128)(2,1)}, u32[]{:S(2)}) copy-start(bf16[4,2048]{1,0:T(4,128)(2,1)} %states.1) | copy-start | bytes 49156
  27.0 3.8 %copy-start.2 = (f32[2,2048]{1,0:T(2,128)S(1)}, f32[2,2048]{1,0:T(2,128)}, u32[]{:S(2)}) copy-start(f32[2,2048]{1,0:T(2,128)} %gains.1) | copy-start | bytes 49156
  27.1 3.6 %collective-permute-start.8 = (bf16[4,2048]{1,0:T(4,128)(2,1)S(1)}, bf16[4,2048]{1,0:T(4,128)(2,1)S(1)}, u32[]{:S(2)}, u32[]{:S(2)}) collective-permute-start(bf16[4,2048]{1,0:T(4,128)(2,1)S(1)} %attn_project.1.token.rest_4_), channel_id=1, source_target_pairs={{0,3},{1,2},{2,1},{3,0},{4,7},{5,6},{6,5},{7,4},{8,11},{9,10},{10,... | collective-permute-start | bytes 49160 | tf_op jit(solution)/shard_map/ppermute | solution.py:41
  27.1 3.8 %collective-permute-start.7 = (bf16[4,2048]{1,0:T(4,128)(2,1)S(1)}, bf16[4,2048]{1,0:T(4,128)(2,1)S(1)}, u32[]{:S(2)}, u32[]{:S(2)}) collective-permute-start(bf16[4,2048]{1,0:T(4,128)(2,1)S(1)} %attn_project.1.token.rest_4_), channel_id=1, source_target_pairs={{0,2},{1,3},{2,0},{3,1},{4,6},{5,7},{6,4},{7,5},{8,10},{9,11},{10,... | collective-permute-start | bytes 49160 | tf_op jit(solution)/shard_map/ppermute | solution.py:41
  28.6 2.3 %collective-permute-start.6 = (bf16[4,2048]{1,0:T(4,128)(2,1)S(1)}, bf16[4,2048]{1,0:T(4,128)(2,1)S(1)}, u32[]{:S(2)}, u32[]{:S(2)}) collective-permute-start(bf16[4,2048]{1,0:T(4,128)(2,1)S(1)} %attn_project.1.token.rest_4_), channel_id=1, source_target_pairs={{0,1},{1,0},{2,3},{3,2},{4,5},{5,4},{6,7},{7,6},{8,9},{9,8},{10,11... | collective-permute-start | bytes 49160 | tf_op jit(solution)/shard_map/ppermute | solution.py:41
  30.9 14.5 %slice-start = ((s8[14680064]{0:T(1024)(128)(4,1)}), s8[4194304]{0:T(1024)(128)(4,1)S(1)}, s32[]{:S(2)}) async-start(s8[14680064]{0:T(1024)(128)(4,1)} %bitcast.4), calls=%async_computation | async-start | bytes 8388608
  30.9 14.4 %slice-start.1 = ((s8[14680064]{0:T(1024)(128)(4,1)}), s8[4194304]{0:T(1024)(128)(4,1)S(1)}, s32[]{:S(2)}) async-start(s8[14680064]{0:T(1024)(128)(4,1)} %bitcast.4), calls=%async_computation.1 | async-start | bytes 8388608
  30.9 14.4 %slice-start.2 = ((s8[14680064]{0:T(1024)(128)(4,1)}), s8[4194304]{0:T(1024)(128)(4,1)S(1)}, s32[]{:S(2)}) async-start(s8[14680064]{0:T(1024)(128)(4,1)} %bitcast.4), calls=%async_computation.2 | async-start | bytes 8388608
  30.9 14.4 %slice-start.3 = ((s8[14680064]{0:T(1024)(128)(4,1)}), s8[2097152]{0:T(1024)(128)(4,1)S(1)}, s32[]{:S(2)}) async-start(s8[14680064]{0:T(1024)(128)(4,1)} %bitcast.4), calls=%async_computation.3 | async-start | bytes 4194304
  36.3 6.6 %collective-permute-start.11 = (bf16[8,3712]{1,0:T(8,128)(2,1)S(1)}, bf16[8,3712]{1,0:T(8,128)(2,1)S(1)}, u32[]{:S(2)}, u32[]{:S(2)}) collective-permute-start(bf16[8,3712]{1,0:T(8,128)(2,1)S(1)} %get-tuple-element.29.rest_0_), channel_id=1, source_target_pairs={{0,12},{4,8},{8,4},{12,0},{1,13},{5,9},{9,5},{13,1},{2,14},{6,10},... | collective-permute-start | bytes 178184 | tf_op jit(solution)/shard_map/ppermute | solution.py:41
  38.2 7.1 %collective-permute-start.10 = (bf16[8,3712]{1,0:T(8,128)(2,1)S(1)}, bf16[8,3712]{1,0:T(8,128)(2,1)S(1)}, u32[]{:S(2)}, u32[]{:S(2)}) collective-permute-start(bf16[8,3712]{1,0:T(8,128)(2,1)S(1)} %get-tuple-element.29.rest_0_), channel_id=1, source_target_pairs={{0,8},{4,12},{8,0},{12,4},{1,9},{5,13},{9,1},{13,5},{2,10},{6,14},... | collective-permute-start | bytes 178184 | tf_op jit(solution)/shard_map/ppermute | solution.py:41
  39.3 6.0 %collective-permute-start.9 = (bf16[8,3712]{1,0:T(8,128)(2,1)S(1)}, bf16[8,3712]{1,0:T(8,128)(2,1)S(1)}, u32[]{:S(2)}, u32[]{:S(2)}) collective-permute-start(bf16[8,3712]{1,0:T(8,128)(2,1)S(1)} %get-tuple-element.29.rest_0_), channel_id=1, source_target_pairs={{0,4},{4,0},{8,12},{12,8},{1,5},{5,1},{9,13},{13,9},{2,6},{6,2},{1... | collective-permute-start | bytes 178184 | tf_op jit(solution)/shard_map/ppermute | solution.py:41
  47.5 3.3 %collective-permute-start.14 = (bf16[4,2048]{1,0:T(4,128)(2,1)S(1)}, bf16[4,2048]{1,0:T(4,128)(2,1)S(1)}, u32[]{:S(2)}, u32[]{:S(2)}) collective-permute-start(bf16[4,2048]{1,0:T(4,128)(2,1)S(1)} %down.1), channel_id=1, source_target_pairs={{0,3},{1,2},{2,1},{3,0},{4,7},{5,6},{6,5},{7,4},{8,11},{9,10},{10,... | collective-permute-start | bytes 49160 | tf_op jit(solution)/shard_map/ppermute | solution.py:41
  47.8 3.9 %collective-permute-start.13 = (bf16[4,2048]{1,0:T(4,128)(2,1)S(1)}, bf16[4,2048]{1,0:T(4,128)(2,1)S(1)}, u32[]{:S(2)}, u32[]{:S(2)}) collective-permute-start(bf16[4,2048]{1,0:T(4,128)(2,1)S(1)} %down.1), channel_id=1, source_target_pairs={{0,2},{1,3},{2,0},{3,1},{4,6},{5,7},{6,4},{7,5},{8,10},{9,11},{10,... | collective-permute-start | bytes 49160 | tf_op jit(solution)/shard_map/ppermute | solution.py:41
  49.0 2.7 %collective-permute-start.12 = (bf16[4,2048]{1,0:T(4,128)(2,1)S(1)}, bf16[4,2048]{1,0:T(4,128)(2,1)S(1)}, u32[]{:S(2)}, u32[]{:S(2)}) collective-permute-start(bf16[4,2048]{1,0:T(4,128)(2,1)S(1)} %down.1), channel_id=1, source_target_pairs={{0,1},{1,0},{2,3},{3,2},{4,5},{5,4},{6,7},{7,6},{8,9},{9,8},{10,11... | collective-permute-start | bytes 49160 | tf_op jit(solution)/shard_map/ppermute | solution.py:41

commit v10 on v9

--- a/solution.py
+++ b/solution.py
@@ -283,7 +283,8 @@
     out[...] = terms[:docs].astype(BF16)
 
 
-def fetch_kernel(first, token, w, out, sems):
+def fetch_kernel(first, token, w, *rest):
+    out, sems = rest[-2:]
     copies = block_copies(matrix_of(w), first, out, sems)
     for copy in copies:
         copy.start()
@@ -414,17 +415,17 @@
     def block_of(share):
         return pltpu.VMEM((2 * width, (share[1] - share[0]) * LANES), BF16)
 
-    def fetch(share, token):
+    def fetch(share, token, *keep):
         return pl.pallas_call(
             functools.partial(fetch_kernel, share[0]),
             out_shape=block_of(share),
-            in_specs=[hbm(), hbm()],
+            in_specs=[hbm(), hbm()] + [vmem()] * len(keep),
             out_specs=vmem(),
             scratch_shapes=[pltpu.SemaphoreType.DMA((chunks,))],
             compiler_params=params(docs, 2),
             cost_estimate=cost(0.3 * (share[1] - share[0])),
             name="fetch",
-        )(token, w_gu)
+        )(token, w_gu, *keep)
 
     w_ready, turned = pl.pallas_call(
         functools.partial(fetch_and_turn_kernel, shares[0][0]),
@@ -445,7 +446,7 @@
             jax.ShapeDtypeStruct((1, 2 * LANES), BF16),
             block_of(shares[1]),
         ],
-        in_specs=[vmem(), vmem(), vmem(), hbm()] + [vmem()] * tp + [hbm()] * len(fetched),
+        in_specs=[vmem(), vmem(), vmem(), hbm()] + [vmem()] * tp + [hbm()] * len(fetched) + [vmem()],
         out_specs=[vmem()] * 3,
         scratch_shapes=[
             pltpu.VMEM((heads, cache_len), F32),
@@ -454,7 +455,7 @@
         compiler_params=params(docs, 6),
         cost_estimate=cost(8),
         name="attend",
-    )(table, turned, cache_tiles, w_gu, *qkv_parts, *fetched)
+    )(table, turned, cache_tiles, w_gu, *qkv_parts, *fetched, w_out)
     fetched.append(w_ready)
 
     fetched.append(fetch(shares[2], head_out))
@@ -470,7 +471,7 @@
         name="attn_project",
     )(places, w_out, *head_parts, fetched[-1])
 
-    fetched.append(fetch(shares[3], out_part))
+    fetched.append(fetch(shares[3], out_part, w_down))
     out_parts = exchange([out_part] * kv, "kv", kv)
     attn_out, gu_part = pl.pallas_call(
         functools.partial(gate_up_kernel, kv, len(fetched), shares[4][0]),

time: 52.6 us -> 53.2 us (1.011)
  waiting for transfers between devices: 9.31 us -> 9.91 us
    ppermute x15, waiting for transfers between devices: 9.31 us -> 9.91 us  [exchange(): lax.ppermute(arrays[s], axis, [(i, i ^ s) for i in range(size)])]
where the time goes in v10:
time: 53.2 us; the launch traced here: 53 us
  Pallas kernels  23.3 us (44%)
  starting transfers between devices  18.3 us (34%)
  waiting for transfers between devices  9.91 us (19%)
  between operations  0.78 us (1%)
  other arithmetic  0.63 us (1%)
    ppermute x15, starting transfers between devices, exchange(): lax.ppermute(arrays[s], axis, [(i, i ^ s) for i in range(size)])  18.3 us
    ppermute x15, waiting for transfers between devices, exchange(): lax.ppermute(arrays[s], axis, [(i, i ^ s) for i in range(size)])  9.91 us
    pallas_call x1, Pallas kernels, per_device(): pl.pallas_call(functools.partial(gate_up_kernel, kv, len(fetched), shares...  5.31 us
    pallas_call x1, Pallas kernels, per_device(): pl.pallas_call(functools.partial(qkv_kernel, tp), out_shape=[jax.ShapeDty...  4.43 us
    pallas_call x1, Pallas kernels, per_device(): pl.pallas_call(functools.partial(fetch_and_turn_kernel, shares[0][0]), ou...  3.77 us
    pallas_call x1, Pallas kernels, per_device(): pl.pallas_call(functools.partial(attend_kernel, tp, heads, 512, shares[1]...  3.57 us
    pallas_call x2, Pallas kernels, fetch(): pl.pallas_call(functools.partial(fetch_kernel, share[0]), out_shape=block...  3.46 us
    pallas_call x1, Pallas kernels, per_device(): pl.pallas_call(functools.partial(down_kernel, tp), out_shape=jax.ShapeDty...  2.09 us
  transfers between devices with their start and end apart: 15, of which 7 were waited for; matrix products, arithmetic and copies ran while one was open for 0% of the time, Pallas kernels for 14%

profile of v10, /device:TPU:0, one launch (start us, length us, event | category | flops | bytes accessed | tf_op | source)
XLA Modules:
  0.0 53.0 jit_solution(13374242747854152834)
XLA Ops:
  0.6 4.4 %qkv.1 = (f32[16,128]{1,0:T(8,128)S(1)}, f32[16,128]{1,0:T(8,128)S(1)}, f32[16,128]{1,0:T(8,128)S(1)}, f32[16,128]{1,0:T(8,128)S(1)}, f32[8,128]{1,0:T(8,128)S(1...) custom-call(s32[4]{0:T(128)} %owner_hbm.1, s32[4]{0:T(128)} %lengths_hbm.1, ...), custom_call_target="tpu_custom_call" | custom-call | bytes 29520000 | tf_op jit(solution)/shard_map/qkv/pallas_call | solution.py:381
  5.1 3.1 %collective-permute-start = (f32[16,128]{1,0:T(8,128)S(1)}, f32[16,128]{1,0:T(8,128)S(1)}, u32[]{:S(2)}, u32[]{:S(2)}) collective-permute-start(f32[16,128]{1,0:T(8,128)S(1)} %get-tuple-element.22), channel_id=1, source_target_pairs={{0,4},{4,0},{8,12},{12,8},{1,5},{5,1},{9,13},{13,9},{2,6},{6,2},{1... | collective-permute-start | bytes 24584 | tf_op jit(solution)/shard_map/ppermute | solution.py:41
  8.2 2.6 %collective-permute-start.1 = (f32[16,128]{1,0:T(8,128)S(1)}, f32[16,128]{1,0:T(8,128)S(1)}, u32[]{:S(2)}, u32[]{:S(2)}) collective-permute-start(f32[16,128]{1,0:T(8,128)S(1)} %get-tuple-element.23), channel_id=1, source_target_pairs={{0,8},{4,12},{8,0},{12,4},{1,9},{5,13},{9,1},{13,5},{2,10},{6,14},... | collective-permute-start | bytes 24584 | tf_op jit(solution)/shard_map/ppermute | solution.py:41
  10.8 0.0 collective-permute-start.2
  10.8 3.8 %fetch_and_turn_keys.1 = (bf16[4096,1024]{1,0:T(8,128)(2,1)S(1)}, bf16[128,8192]{1,0:T(8,128)(2,1)S(1)}) custom-call(f32[8,128]{1,0:T(8,128)S(1)} %get-tuple-element.17.token.table, bf16[2048,2,3584]{2,1,0:T(2,128)(2,1)} %w.9, bf16[2,8192,128]{2,1,0:T(8,128)(2,1)S(1)} %get-tuple-element.18.cache), custom_call_target="tpu_custom_call" | custom-call | bytes 11070000 | tf_op jit(solution)/shard_map/fetch_and_turn_keys/pallas_call | solution.py:430
  14.5 0.0 collective-permute-done.rest_1_
  14.6 1.6 %collective-permute-done.2.rest_3_ = f32[16,128]{1,0:T(8,128)S(1)} collective-permute-done((f32[16,128]{1,0:T(8,128)S(1)}, f32[16,128]{1,0:T(8,128)S(1)}, u32[]{:S(2)}, u32[]{:S(2)}) %collective-permute-start.2) | collective-permute-done | bytes 8224 | tf_op jit(solution)/shard_map/ppermute | solution.py:41
  16.2 3.6 %attend.1 = (bf16[8,128]{1,0:T(8,128)(2,1)S(1)}, bf16[1,256]{1,0:T(2,128)(2,1)}, bf16[4096,768]{1,0:T(8,128)(2,1)S(1)}) custom-call(f32[8,128]{1,0:T(8,128)S(1)} %get-tuple-element.17.token.table, bf16[128,8192]{1,0:T(8,128)(2,1)S(1)} %get-tuple-element.20.keys, bf16[2,8192,128]{2,1,0:T(8,128)(2,1)S(1)} %get-tuple-element.18.cache, ...), custom_call_target="tpu_custom_call" | custom-call | bytes 29520000 | tf_op jit(solution)/shard_map/attend/pallas_call | solution.py:442
  19.8 0.0 slice-start
  19.8 3.2 %collective-permute-start.5 = (bf16[8,128]{1,0:T(8,128)(2,1)S(1)}, bf16[8,128]{1,0:T(8,128)(2,1)S(1)}, u32[]{:S(2)}, u32[]{:S(2)}) collective-permute-start(bf16[8,128]{1,0:T(8,128)(2,1)S(1)} %get-tuple-element.26.token.rest_0_), channel_id=1, source_target_pairs={{0,12},{4,8},{8,4},{12,0},{1,13},{5,9},{9,5},{13,1},{2,14},{6,10},... | collective-permute-start | bytes 6152 | tf_op jit(solution)/shard_map/ppermute | solution.py:41
  23.1 1.2 %collective-permute-start.3 = (bf16[8,128]{1,0:T(8,128)(2,1)S(1)}, bf16[8,128]{1,0:T(8,128)(2,1)S(1)}, u32[]{:S(2)}, u32[]{:S(2)}) collective-permute-start(bf16[8,128]{1,0:T(8,128)(2,1)S(1)} %get-tuple-element.26.token.rest_0_), channel_id=1, source_target_pairs={{0,4},{4,0},{8,12},{12,8},{1,5},{5,1},{9,13},{13,9},{2,6},{6,2},{1... | collective-permute-start | bytes 6152 | tf_op jit(solution)/shard_map/ppermute | solution.py:41
  24.3 1.7 %fetch.2.rest_4_.rest_2_ = bf16[4096,256]{1,0:T(8,128)(2,1)S(1)} custom-call(bf16[8,128]{1,0:T(8,128)(2,1)S(1)} %get-tuple-element.26.token.rest_0_, bf16[2048,2,3584]{2,1,0:T(2,128)(2,1)} %w.9), custom_call_target="tpu_custom_call" | custom-call | bytes 2214000 | tf_op jit(solution)/shard_map/fetch/pallas_call | solution.py:419
  26.0 1.5 %collective-permute-done.4.rest_2_ = bf16[8,128]{1,0:T(8,128)(2,1)S(1)} collective-permute-done((bf16[8,128]{1,0:T(8,128)(2,1)S(1)}, bf16[8,128]{1,0:T(8,128)(2,1)S(1)}, u32[]{:S(2)}, u32[]{:S(2)}) %collective-permute-start.4) | collective-permute-done | bytes 2080 | tf_op jit(solution)/shard_map/ppermute | solution.py:41
  27.5 0.7 %attn_project.1.token.rest_4_ = bf16[4,2048]{1,0:T(4,128)(2,1)S(1)} custom-call(s32[8,128]{1,0:T(8,128)S(1)} %get-tuple-element.27.places, bf16[1024,2048]{1,0:T(8,128)(2,1)S(1)} %copy-done, bf16[8,128]{1,0:T(8,128)(2,1)S(1)} %get-tuple-element.26.token.rest_0_, bf16[8,128]{1,0:T(8,128)(2,1)S(1)} %collective-permute-done.3.rest_1_, ...), custom_call_target="tpu_custom_call" | custom-call | bytes 22140000 | tf_op jit(solution)/shard_map/attn_project/pallas_call | solution.py:463
  28.2 0.0 collective-permute-start.8
  28.2 1.6 %collective-permute-start.7 = (bf16[4,2048]{1,0:T(4,128)(2,1)S(1)}, bf16[4,2048]{1,0:T(4,128)(2,1)S(1)}, u32[]{:S(2)}, u32[]{:S(2)}) collective-permute-start(bf16[4,2048]{1,0:T(4,128)(2,1)S(1)} %attn_project.1.token.rest_4_), channel_id=1, source_target_pairs={{0,2},{1,3},{2,0},{3,1},{4,6},{5,7},{6,4},{7,5},{8,10},{9,11},{10,... | collective-permute-start | bytes 49160 | tf_op jit(solution)/shard_map/ppermute | solution.py:41
  29.8 0.3 collective-permute-start.6
  30.1 1.7 %fetch.3.rest_3_ = bf16[4096,256]{1,0:T(8,128)(2,1)S(1)} custom-call(bf16[4,2048]{1,0:T(4,128)(2,1)S(1)} %attn_project.1.token.rest_4_, bf16[2048,2,3584]{2,1,0:T(2,128)(2,1)} %w.9, bf16[3584,2048]{1,0:T(8,128)(2,1)S(1)} %bitcast.5), custom_call_target="tpu_custom_call" | custom-call | bytes 2214000 | tf_op jit(solution)/shard_map/fetch/pallas_call | solution.py:419
  31.9 0.2 collective-permute-done.7.rest_6_
  32.0 5.3 %gate_up.1 = (bf16[4,2048]{1,0:T(4,128)(2,1)}, bf16[8,3712]{1,0:T(8,128)(2,1)S(1)}) custom-call(bf16[4,2048]{1,0:T(4,128)(2,1)S(1)} %copy-done.1, f32[2,2048]{1,0:T(2,128)S(1)} %copy-done.2, bf16[2048,2,3584]{2,1,0:T(2,128)(2,1)} %w.9, bf16[4096,1024]{1,0:T(8,128)(2,1)S(1)} %get-tuple-element.19.rest_4_.rest_0_, ...), custom_call_target="tpu_custom_call" | custom-call | bytes 36900000 | tf_op jit(solution)/shard_map/gate_up/pallas_call | solution.py:476
  37.4 1.7 %collective-permute-start.11 = (bf16[8,3712]{1,0:T(8,128)(2,1)S(1)}, bf16[8,3712]{1,0:T(8,128)(2,1)S(1)}, u32[]{:S(2)}, u32[]{:S(2)}) collective-permute-start(bf16[8,3712]{1,0:T(8,128)(2,1)S(1)} %get-tuple-element.29.rest_0_), channel_id=1, source_target_pairs={{0,12},{4,8},{8,4},{12,0},{1,13},{5,9},{9,5},{13,1},{2,14},{6,10},... | collective-permute-start | bytes 178184 | tf_op jit(solution)/shard_map/ppermute | solution.py:41
  39.1 0.4 collective-permute-start.10
  39.5 2.3 %collective-permute-start.9 = (bf16[8,3712]{1,0:T(8,128)(2,1)S(1)}, bf16[8,3712]{1,0:T(8,128)(2,1)S(1)}, u32[]{:S(2)}, u32[]{:S(2)}) collective-permute-start(bf16[8,3712]{1,0:T(8,128)(2,1)S(1)} %get-tuple-element.29.rest_0_), channel_id=1, source_target_pairs={{0,4},{4,0},{8,12},{12,8},{1,5},{5,1},{9,13},{13,9},{2,6},{6,2},{1... | collective-permute-start | bytes 178184 | tf_op jit(solution)/shard_map/ppermute | solution.py:41
  41.8 2.2 %collective-permute-done.11.rest_3_ = bf16[8,3712]{1,0:T(8,128)(2,1)S(1)} collective-permute-done((bf16[8,3712]{1,0:T(8,128)(2,1)S(1)}, bf16[8,3712]{1,0:T(8,128)(2,1)S(1)}, u32[]{:S(2)}, u32[]{:S(2)}) %collective-permute-start.11) | collective-permute-done | bytes 59424 | tf_op jit(solution)/shard_map/ppermute | solution.py:41
  44.0 2.0 %collective-permute-done.10.rest_2_ = bf16[8,3712]{1,0:T(8,128)(2,1)S(1)} collective-permute-done((bf16[8,3712]{1,0:T(8,128)(2,1)S(1)}, bf16[8,3712]{1,0:T(8,128)(2,1)S(1)}, u32[]{:S(2)}, u32[]{:S(2)}) %collective-permute-start.10) | collective-permute-done | bytes 59424 | tf_op jit(solution)/shard_map/ppermute | solution.py:41
  46.0 2.1 %down.1 = bf16[4,2048]{1,0:T(4,128)(2,1)S(1)} custom-call(bf16[3584,2048]{1,0:T(8,128)(2,1)S(1)} %bitcast.5, bf16[8,3712]{1,0:T(8,128)(2,1)S(1)} %get-tuple-element.29.rest_0_, bf16[8,3712]{1,0:T(8,128)(2,1)S(1)} %collective-permute-done.9.rest_1_, bf16[8,3712]{1,0:T(8,128)(2,1)S(1)} %collective-permute-done.10.rest_2_, ...), custom_call_target="tpu_custom_call" | custom-call | bytes 18450000 | tf_op jit(solution)/shard_map/down/pallas_call | solution.py:495
  48.1 0.5 collective-permute-start.14
  48.6 1.2 %collective-permute-start.13 = (bf16[4,2048]{1,0:T(4,128)(2,1)S(1)}, bf16[4,2048]{1,0:T(4,128)(2,1)S(1)}, u32[]{:S(2)}, u32[]{:S(2)}) collective-permute-start(bf16[4,2048]{1,0:T(4,128)(2,1)S(1)} %down.1), channel_id=1, source_target_pairs={{0,2},{1,3},{2,0},{3,1},{4,6},{5,7},{6,4},{7,5},{8,10},{9,11},{10,... | collective-permute-start | bytes 49160 | tf_op jit(solution)/shard_map/ppermute | solution.py:41
  49.8 0.2 collective-permute-start.12
  50.0 1.3 %collective-permute-done.14 = bf16[4,2048]{1,0:T(4,128)(2,1)S(1)} collective-permute-done((bf16[4,2048]{1,0:T(4,128)(2,1)S(1)}, bf16[4,2048]{1,0:T(4,128)(2,1)S(1)}, u32[]{:S(2)}, u32[]{:S(2)}) %collective-permute-start.14) | collective-permute-done | bytes 16416 | tf_op jit(solution)/shard_map/ppermute | solution.py:41
  51.3 1.1 %collective-permute-done.13 = bf16[4,2048]{1,0:T(4,128)(2,1)S(1)} collective-permute-done((bf16[4,2048]{1,0:T(4,128)(2,1)S(1)}, bf16[4,2048]{1,0:T(4,128)(2,1)S(1)}, u32[]{:S(2)}, u32[]{:S(2)}) %collective-permute-start.13) | collective-permute-done | bytes 16416 | tf_op jit(solution)/shard_map/ppermute | solution.py:41
  52.3 0.6 %add_convert_fusion = bf16[4,2048]{1,0:T(4,128)(2,1)} fusion(bf16[4,2048]{1,0:T(4,128)(2,1)S(1)} %collective-permute-done.14, bf16[4,2048]{1,0:T(4,128)(2,1)S(1)} %collective-permute-done.13, bf16[4,2048]{1,0:T(4,128)(2,1)S(1)} %collective-permute-done.12, bf16[4,2048]{1,0:T(4,128)(2,1)S(1)} %down.1), kind=kLoop, calls=%fused_computation | loop fusion | flops 65536 | bytes 81920 | tf_op jit(solution)/shard_map/convert_element_type | solution.py:506
  (22 shorter events, 0.0 us)
Async XLA Ops:
  5.1 9.5 %collective-permute-start = (f32[16,128]{1,0:T(8,128)S(1)}, f32[16,128]{1,0:T(8,128)S(1)}, u32[]{:S(2)}, u32[]{:S(2)}) collective-permute-start(f32[16,128]{1,0:T(8,128)S(1)} %get-tuple-element.22), channel_id=1, source_target_pairs={{0,4},{4,0},{8,12},{12,8},{1,5},{5,1},{9,13},{13,9},{2,6},{6,2},{1... | collective-permute-start | bytes 24584 | tf_op jit(solution)/shard_map/ppermute | solution.py:41
  8.2 6.4 %collective-permute-start.1 = (f32[16,128]{1,0:T(8,128)S(1)}, f32[16,128]{1,0:T(8,128)S(1)}, u32[]{:S(2)}, u32[]{:S(2)}) collective-permute-start(f32[16,128]{1,0:T(8,128)S(1)} %get-tuple-element.23), channel_id=1, source_target_pairs={{0,8},{4,12},{8,0},{12,4},{1,9},{5,13},{9,1},{13,5},{2,10},{6,14},... | collective-permute-start | bytes 24584 | tf_op jit(solution)/shard_map/ppermute | solution.py:41
  10.8 5.4 %collective-permute-start.2 = (f32[16,128]{1,0:T(8,128)S(1)}, f32[16,128]{1,0:T(8,128)S(1)}, u32[]{:S(2)}, u32[]{:S(2)}) collective-permute-start(f32[16,128]{1,0:T(8,128)S(1)} %get-tuple-element.24), channel_id=1, source_target_pairs={{0,12},{4,8},{8,4},{12,0},{1,13},{5,9},{9,5},{13,1},{2,14},{6,10},... | collective-permute-start | bytes 24584 | tf_op jit(solution)/shard_map/ppermute | solution.py:41
  10.8 5.4 %copy-start = (bf16[1024,2048]{1,0:T(8,128)(2,1)S(1)}, bf16[1024,2048]{1,0:T(8,128)(2,1)}, u32[]{:S(2)}) copy-start(bf16[1024,2048]{1,0:T(8,128)(2,1)} %w_out.1) | copy-start | bytes 12582916
  19.8 10.3 %slice-start = ((s8[14680064]{0:T(1024)(128)(4,1)}), s8[4194304]{0:T(1024)(128)(4,1)S(1)}, s32[]{:S(2)}) async-start(s8[14680064]{0:T(1024)(128)(4,1)} %bitcast.4), calls=%async_computation | async-start | bytes 8388608
  19.8 10.3 %slice-start.1 = ((s8[14680064]{0:T(1024)(128)(4,1)}), s8[4194304]{0:T(1024)(128)(4,1)S(1)}, s32[]{:S(2)}) async-start(s8[14680064]{0:T(1024)(128)(4,1)} %bitcast.4), calls=%async_computation.1 | async-start | bytes 8388608
  19.8 10.3 %slice-start.2 = ((s8[14680064]{0:T(1024)(128)(4,1)}), s8[4194304]{0:T(1024)(128)(4,1)S(1)}, s32[]{:S(2)}) async-start(s8[14680064]{0:T(1024)(128)(4,1)} %bitcast.4), calls=%async_computation.2 | async-start | bytes 8388608
  19.8 10.3 %slice-start.3 = ((s8[14680064]{0:T(1024)(128)(4,1)}), s8[2097152]{0:T(1024)(128)(4,1)S(1)}, s32[]{:S(2)}) async-start(s8[14680064]{0:T(1024)(128)(4,1)} %bitcast.4), calls=%async_computation.3 | async-start | bytes 4194304
  19.8 6.2 %collective-permute-start.5 = (bf16[8,128]{1,0:T(8,128)(2,1)S(1)}, bf16[8,128]{1,0:T(8,128)(2,1)S(1)}, u32[]{:S(2)}, u32[]{:S(2)}) collective-permute-start(bf16[8,128]{1,0:T(8,128)(2,1)S(1)} %get-tuple-element.26.token.rest_0_), channel_id=1, source_target_pairs={{0,12},{4,8},{8,4},{12,0},{1,13},{5,9},{9,5},{13,1},{2,14},{6,10},... | collective-permute-start | bytes 6152 | tf_op jit(solution)/shard_map/ppermute | solution.py:41
  23.1 4.5 %collective-permute-start.4 = (bf16[8,128]{1,0:T(8,128)(2,1)S(1)}, bf16[8,128]{1,0:T(8,128)(2,1)S(1)}, u32[]{:S(2)}, u32[]{:S(2)}) collective-permute-start(bf16[8,128]{1,0:T(8,128)(2,1)S(1)} %get-tuple-element.26.token.rest_0_), channel_id=1, source_target_pairs={{0,8},{4,12},{8,0},{12,4},{1,9},{5,13},{9,1},{13,5},{2,10},{6,14},... | collective-permute-start | bytes 6152 | tf_op jit(solution)/shard_map/ppermute | solution.py:41
  23.1 4.5 %collective-permute-start.3 = (bf16[8,128]{1,0:T(8,128)(2,1)S(1)}, bf16[8,128]{1,0:T(8,128)(2,1)S(1)}, u32[]{:S(2)}, u32[]{:S(2)}) collective-permute-start(bf16[8,128]{1,0:T(8,128)(2,1)S(1)} %get-tuple-element.26.token.rest_0_), channel_id=1, source_target_pairs={{0,4},{4,0},{8,12},{12,8},{1,5},{5,1},{9,13},{13,9},{2,6},{6,2},{1... | collective-permute-start | bytes 6152 | tf_op jit(solution)/shard_map/ppermute | solution.py:41
  28.2 3.8 %copy-start.1 = (bf16[4,2048]{1,0:T(4,128)(2,1)S(1)}, bf16[4,2048]{1,0:T(4,128)(2,1)}, u32[]{:S(2)}) copy-start(bf16[4,2048]{1,0:T(4,128)(2,1)} %states.1) | copy-start | bytes 49156
  28.2 3.8 %copy-start.2 = (f32[2,2048]{1,0:T(2,128)S(1)}, f32[2,2048]{1,0:T(2,128)}, u32[]{:S(2)}) copy-start(f32[2,2048]{1,0:T(2,128)} %gains.1) | copy-start | bytes 49156
  28.2 3.6 %collective-permute-start.8 = (bf16[4,2048]{1,0:T(4,128)(2,1)S(1)}, bf16[4,2048]{1,0:T(4,128)(2,1)S(1)}, u32[]{:S(2)}, u32[]{:S(2)}) collective-permute-start(bf16[4,2048]{1,0:T(4,128)(2,1)S(1)} %attn_project.1.token.rest_4_), channel_id=1, source_target_pairs={{0,3},{1,2},{2,1},{3,0},{4,7},{5,6},{6,5},{7,4},{8,11},{9,10},{10,... | collective-permute-start | bytes 49160 | tf_op jit(solution)/shard_map/ppermute | solution.py:41
  28.2 3.8 %collective-permute-start.7 = (bf16[4,2048]{1,0:T(4,128)(2,1)S(1)}, bf16[4,2048]{1,0:T(4,128)(2,1)S(1)}, u32[]{:S(2)}, u32[]{:S(2)}) collective-permute-start(bf16[4,2048]{1,0:T(4,128)(2,1)S(1)} %attn_project.1.token.rest_4_), channel_id=1, source_target_pairs={{0,2},{1,3},{2,0},{3,1},{4,6},{5,7},{6,4},{7,5},{8,10},{9,11},{10,... | collective-permute-start | bytes 49160 | tf_op jit(solution)/shard_map/ppermute | solution.py:41
  29.8 2.3 %collective-permute-start.6 = (bf16[4,2048]{1,0:T(4,128)(2,1)S(1)}, bf16[4,2048]{1,0:T(4,128)(2,1)S(1)}, u32[]{:S(2)}, u32[]{:S(2)}) collective-permute-start(bf16[4,2048]{1,0:T(4,128)(2,1)S(1)} %attn_project.1.token.rest_4_), channel_id=1, source_target_pairs={{0,1},{1,0},{2,3},{3,2},{4,5},{5,4},{6,7},{7,6},{8,9},{9,8},{10,11... | collective-permute-start | bytes 49160 | tf_op jit(solution)/shard_map/ppermute | solution.py:41
  37.4 6.6 %collective-permute-start.11 = (bf16[8,3712]{1,0:T(8,128)(2,1)S(1)}, bf16[8,3712]{1,0:T(8,128)(2,1)S(1)}, u32[]{:S(2)}, u32[]{:S(2)}) collective-permute-start(bf16[8,3712]{1,0:T(8,128)(2,1)S(1)} %get-tuple-element.29.rest_0_), channel_id=1, source_target_pairs={{0,12},{4,8},{8,4},{12,0},{1,13},{5,9},{9,5},{13,1},{2,14},{6,10},... | collective-permute-start | bytes 178184 | tf_op jit(solution)/shard_map/ppermute | solution.py:41
  39.1 6.9 %collective-permute-start.10 = (bf16[8,3712]{1,0:T(8,128)(2,1)S(1)}, bf16[8,3712]{1,0:T(8,128)(2,1)S(1)}, u32[]{:S(2)}, u32[]{:S(2)}) collective-permute-start(bf16[8,3712]{1,0:T(8,128)(2,1)S(1)} %get-tuple-element.29.rest_0_), channel_id=1, source_target_pairs={{0,8},{4,12},{8,0},{12,4},{1,9},{5,13},{9,1},{13,5},{2,10},{6,14},... | collective-permute-start | bytes 178184 | tf_op jit(solution)/shard_map/ppermute | solution.py:41
  39.5 6.5 %collective-permute-start.9 = (bf16[8,3712]{1,0:T(8,128)(2,1)S(1)}, bf16[8,3712]{1,0:T(8,128)(2,1)S(1)}, u32[]{:S(2)}, u32[]{:S(2)}) collective-permute-start(bf16[8,3712]{1,0:T(8,128)(2,1)S(1)} %get-tuple-element.29.rest_0_), channel_id=1, source_target_pairs={{0,4},{4,0},{8,12},{12,8},{1,5},{5,1},{9,13},{13,9},{2,6},{6,2},{1... | collective-permute-start | bytes 178184 | tf_op jit(solution)/shard_map/ppermute | solution.py:41
  48.1 3.2 %collective-permute-start.14 = (bf16[4,2048]{1,0:T(4,128)(2,1)S(1)}, bf16[4,2048]{1,0:T(4,128)(2,1)S(1)}, u32[]{:S(2)}, u32[]{:S(2)}) collective-permute-start(bf16[4,2048]{1,0:T(4,128)(2,1)S(1)} %down.1), channel_id=1, source_target_pairs={{0,3},{1,2},{2,1},{3,0},{4,7},{5,6},{6,5},{7,4},{8,11},{9,10},{10,... | collective-permute-start | bytes 49160 | tf_op jit(solution)/shard_map/ppermute | solution.py:41
  48.6 3.7 %collective-permute-start.13 = (bf16[4,2048]{1,0:T(4,128)(2,1)S(1)}, bf16[4,2048]{1,0:T(4,128)(2,1)S(1)}, u32[]{:S(2)}, u32[]{:S(2)}) collective-permute-start(bf16[4,2048]{1,0:T(4,128)(2,1)S(1)} %down.1), channel_id=1, source_target_pairs={{0,2},{1,3},{2,0},{3,1},{4,6},{5,7},{6,4},{7,5},{8,10},{9,11},{10,... | collective-permute-start | bytes 49160 | tf_op jit(solution)/shard_map/ppermute | solution.py:41
  49.8 2.6 %collective-permute-start.12 = (bf16[4,2048]{1,0:T(4,128)(2,1)S(1)}, bf16[4,2048]{1,0:T(4,128)(2,1)S(1)}, u32[]{:S(2)}, u32[]{:S(2)}) collective-permute-start(bf16[4,2048]{1,0:T(4,128)(2,1)S(1)} %down.1), channel_id=1, source_target_pairs={{0,1},{1,0},{2,3},{3,2},{4,5},{5,4},{6,7},{7,6},{8,9},{9,8},{10,11... | collective-permute-start | bytes 49160 | tf_op jit(solution)/shard_map/ppermute | solution.py:41

commit v11 on v10

--- a/solution.py
+++ b/solution.py
@@ -14,9 +14,9 @@
 ROPE_BASE = 500000.0
 LANES = 128
 MIB = 1 << 20
-COPY_ROWS = 512
+COPY_ROWS = 2048
 KEY_ROWS = 512
-GU_SHARES = (8, 6, 2, 2, 4, 4, 2)
+GU_SHARES = (4, 6, 2, 2, 4, 4, 4, 2)
 F32 = jnp.float32
 BF16 = jnp.bfloat16
 QUARTER = (1.5703125, 4.837512969970703125e-4, 7.549789948768648e-8)
@@ -206,7 +206,7 @@
     total = total.reshape(heads, 2 * docs, LANES)
     for s in range(tp):
         doc = owner[me ^ s]
-        out = outs[-s]
+        out = outs[s]
         out[:heads, :] = pick_doc(total, doc, docs)
         kv_row = pick_doc(kv_total, doc, docs)[None]
         out[heads : heads + 1, :] = kv_row[:, :LANES]
@@ -438,7 +438,7 @@
         name="fetch_and_turn_keys",
     )(table, w_gu, cache_tiles)
     fetched.append(w_ready)
-    qkv_parts = exchange([qkv_parts[-s] for s in range(tp)], "tp", tp)
+    qkv_parts = exchange(qkv_parts, "tp", tp)[::-1]
     head_out, new_kv, w_ready = pl.pallas_call(
         functools.partial(attend_kernel, tp, heads, 512, shares[1][0]),
         out_shape=[
@@ -446,7 +446,7 @@
             jax.ShapeDtypeStruct((1, 2 * LANES), BF16),
             block_of(shares[1]),
         ],
-        in_specs=[vmem(), vmem(), vmem(), hbm()] + [vmem()] * tp + [hbm()] * len(fetched) + [vmem()],
+        in_specs=[vmem(), vmem(), vmem(), hbm()] + [vmem()] * tp + [hbm()] * len(fetched),
         out_specs=[vmem()] * 3,
         scratch_shapes=[
             pltpu.VMEM((heads, cache_len), F32),
@@ -455,7 +455,7 @@
         compiler_params=params(docs, 6),
         cost_estimate=cost(8),
         name="attend",
-    )(table, turned, cache_tiles, w_gu, *qkv_parts, *fetched, w_out)
+    )(table, turned, cache_tiles, w_gu, *qkv_parts, *fetched)
     fetched.append(w_ready)
 
     fetched.append(fetch(shares[2], head_out))
@@ -486,7 +486,7 @@
             pltpu.VMEM((4 * docs, 2 * width), BF16),
             pltpu.SemaphoreType.DMA((len(shares) - 4, chunks)),
         ],
-        compiler_params=params(docs, 20),
+        compiler_params=params(docs, 19),
         cost_estimate=cost(10),
         name="gate_up",
     )(states, norm_gains, w_gu, *fetched, *out_parts)

time: 53.2 us -> 52.1 us (0.979)
  waiting for transfers between devices: 9.91 us -> 8.78 us
    pallas_call x1, Pallas kernels: 3.77 us -> 2.29 us  [per_device(): pl.pallas_call(functools.partial(fetch_and_turn_kernel, shares[0][0]), ou...]
    ppermute x15, waiting for transfers between devices: 9.91 us -> 8.78 us  [exchange(): lax.ppermute(arrays[s], axis, [(i, i ^ s) for i in range(size)])]
    pallas_call x1, Pallas kernels: 5.31 us -> 6.18 us  [per_device(): pl.pallas_call(functools.partial(gate_up_kernel, kv, len(fetched), shares...]
    pallas_call x2, Pallas kernels: 3.46 us -> 4.02 us  [fetch(): pl.pallas_call(functools.partial(fetch_kernel, share[0]), out_shape=block...]
  transfers between devices with their start and end apart: 15 -> 15, of which waited for: 7 -> 6; matrix products, arithmetic and copies ran while one was open for 0% -> 0% of each run, Pallas kernels for 14% -> 12%
where the time goes in v11:
time: 52.1 us; the launch traced here: 51.8 us
  Pallas kernels  23.1 us (44%)
  starting transfers between devices  18.4 us (35%)
  waiting for transfers between devices  8.78 us (17%)
  between operations  0.81 us (2%)
  other arithmetic  0.63 us (1%)
    ppermute x15, starting transfers between devices, exchange(): lax.ppermute(arrays[s], axis, [(i, i ^ s) for i in range(size)])  18.4 us
    ppermute x15, waiting for transfers between devices, exchange(): lax.ppermute(arrays[s], axis, [(i, i ^ s) for i in range(size)])  8.78 us
    pallas_call x1, Pallas kernels, per_device(): pl.pallas_call(functools.partial(gate_up_kernel, kv, len(fetched), shares...  6.18 us
    pallas_call x1, Pallas kernels, per_device(): pl.pallas_call(functools.partial(qkv_kernel, tp), out_shape=[jax.ShapeDty...  4.43 us
    pallas_call x2, Pallas kernels, fetch(): pl.pallas_call(functools.partial(fetch_kernel, share[0]), out_shape=block...  4.02 us
    pallas_call x1, Pallas kernels, per_device(): pl.pallas_call(functools.partial(attend_kernel, tp, heads, 512, shares[1]...  3.47 us
    pallas_call x1, Pallas kernels, per_device(): pl.pallas_call(functools.partial(fetch_and_turn_kernel, shares[0][0]), ou...  2.29 us
    pallas_call x1, Pallas kernels, per_device(): pl.pallas_call(functools.partial(down_kernel, tp), out_shape=jax.ShapeDty...  2.09 us
  transfers between devices with their start and end apart: 15, of which 6 were waited for; matrix products, arithmetic and copies ran while one was open for 0% of the time, Pallas kernels for 12%

profile of v11, /device:TPU:0, one launch (start us, length us, event | category | flops | bytes accessed | tf_op | source)
XLA Modules:
  0.0 51.8 jit_solution(17912422215886864922)
XLA Ops:
  0.6 4.4 %qkv.1 = (f32[16,128]{1,0:T(8,128)S(1)}, f32[16,128]{1,0:T(8,128)S(1)}, f32[16,128]{1,0:T(8,128)S(1)}, f32[16,128]{1,0:T(8,128)S(1)}, f32[8,128]{1,0:T(8,128)S(1...) custom-call(s32[4]{0:T(128)} %owner_hbm.1, s32[4]{0:T(128)} %lengths_hbm.1, ...), custom_call_target="tpu_custom_call" | custom-call | bytes 29520000 | tf_op jit(solution)/shard_map/qkv/pallas_call | solution.py:381
  5.1 5.1 %collective-permute-start = (f32[16,128]{1,0:T(8,128)S(1)}, f32[16,128]{1,0:T(8,128)S(1)}, u32[]{:S(2)}, u32[]{:S(2)}) collective-permute-start(f32[16,128]{1,0:T(8,128)S(1)} %get-tuple-element.21), channel_id=1, source_target_pairs={{0,12},{4,8},{8,4},{12,0},{1,13},{5,9},{9,5},{13,1},{2,14},{6,10},... | collective-permute-start | bytes 24584 | tf_op jit(solution)/shard_map/ppermute | solution.py:41
  10.2 0.0 collective-permute-start.1
  10.2 0.6 %collective-permute-start.2 = (f32[16,128]{1,0:T(8,128)S(1)}, f32[16,128]{1,0:T(8,128)S(1)}, u32[]{:S(2)}, u32[]{:S(2)}) collective-permute-start(f32[16,128]{1,0:T(8,128)S(1)} %get-tuple-element.23), channel_id=1, source_target_pairs={{0,4},{4,0},{8,12},{12,8},{1,5},{5,1},{9,13},{13,9},{2,6},{6,2},{1... | collective-permute-start | bytes 24584 | tf_op jit(solution)/shard_map/ppermute | solution.py:41
  10.8 2.3 %fetch_and_turn_keys.1 = (bf16[4096,512]{1,0:T(8,128)(2,1)S(1)}, bf16[128,8192]{1,0:T(8,128)(2,1)S(1)}) custom-call(f32[8,128]{1,0:T(8,128)S(1)} %get-tuple-element.17.token.table, bf16[2048,2,3584]{2,1,0:T(2,128)(2,1)} %w.9, bf16[2,8192,128]{2,1,0:T(8,128)(2,1)S(1)} %get-tuple-element.18.cache), custom_call_target="tpu_custom_call" | custom-call | bytes 11070000 | tf_op jit(solution)/shard_map/fetch_and_turn_keys/pallas_call | solution.py:430
  13.1 1.6 %collective-permute-done.1.rest_1_ = f32[16,128]{1,0:T(8,128)S(1)} collective-permute-done((f32[16,128]{1,0:T(8,128)S(1)}, f32[16,128]{1,0:T(8,128)S(1)}, u32[]{:S(2)}, u32[]{:S(2)}) %collective-permute-start.1) | collective-permute-done | bytes 8224 | tf_op jit(solution)/shard_map/ppermute | solution.py:41
  14.7 0.0 collective-permute-done.2.rest_2_
  14.7 3.5 %attend.1 = (bf16[8,128]{1,0:T(8,128)(2,1)S(1)}, bf16[1,256]{1,0:T(2,128)(2,1)}, bf16[4096,768]{1,0:T(8,128)(2,1)S(1)}) custom-call(f32[8,128]{1,0:T(8,128)S(1)} %get-tuple-element.17.token.table, bf16[128,8192]{1,0:T(8,128)(2,1)S(1)} %get-tuple-element.20.keys, bf16[2,8192,128]{2,1,0:T(8,128)(2,1)S(1)} %get-tuple-element.18.cache, ...), custom_call_target="tpu_custom_call" | custom-call | bytes 29520000 | tf_op jit(solution)/shard_map/attend/pallas_call | solution.py:442
  18.2 0.0 slice-start
  18.2 0.0 copy-start
  18.3 2.2 %collective-permute-start.5 = (bf16[8,128]{1,0:T(8,128)(2,1)S(1)}, bf16[8,128]{1,0:T(8,128)(2,1)S(1)}, u32[]{:S(2)}, u32[]{:S(2)}) collective-permute-start(bf16[8,128]{1,0:T(8,128)(2,1)S(1)} %get-tuple-element.26.token.rest_0_), channel_id=1, source_target_pairs={{0,12},{4,8},{8,4},{12,0},{1,13},{5,9},{9,5},{13,1},{2,14},{6,10},... | collective-permute-start | bytes 6152 | tf_op jit(solution)/shard_map/ppermute | solution.py:41
  20.5 2.2 %collective-permute-start.3 = (bf16[8,128]{1,0:T(8,128)(2,1)S(1)}, bf16[8,128]{1,0:T(8,128)(2,1)S(1)}, u32[]{:S(2)}, u32[]{:S(2)}) collective-permute-start(bf16[8,128]{1,0:T(8,128)(2,1)S(1)} %get-tuple-element.26.token.rest_0_), channel_id=1, source_target_pairs={{0,4},{4,0},{8,12},{12,8},{1,5},{5,1},{9,13},{13,9},{2,6},{6,2},{1... | collective-permute-start | bytes 6152 | tf_op jit(solution)/shard_map/ppermute | solution.py:41
  22.7 2.4 %fetch.2.rest_4_.rest_2_ = bf16[4096,256]{1,0:T(8,128)(2,1)S(1)} custom-call(bf16[8,128]{1,0:T(8,128)(2,1)S(1)} %get-tuple-element.26.token.rest_0_, bf16[2048,2,3584]{2,1,0:T(2,128)(2,1)} %w.9), custom_call_target="tpu_custom_call" | custom-call | bytes 2214000 | tf_op jit(solution)/shard_map/fetch/pallas_call | solution.py:419
  25.2 0.7 %attn_project.1.token.rest_4_ = bf16[4,2048]{1,0:T(4,128)(2,1)S(1)} custom-call(s32[8,128]{1,0:T(8,128)S(1)} %get-tuple-element.27.places, bf16[1024,2048]{1,0:T(8,128)(2,1)S(1)} %copy-done, bf16[8,128]{1,0:T(8,128)(2,1)S(1)} %get-tuple-element.26.token.rest_0_, bf16[8,128]{1,0:T(8,128)(2,1)S(1)} %collective-permute-done.3.rest_1_, ...), custom_call_target="tpu_custom_call" | custom-call | bytes 22140000 | tf_op jit(solution)/shard_map/attn_project/pallas_call | solution.py:463
  25.8 0.0 collective-permute-start.8
  25.9 1.6 %collective-permute-start.7 = (bf16[4,2048]{1,0:T(4,128)(2,1)S(1)}, bf16[4,2048]{1,0:T(4,128)(2,1)S(1)}, u32[]{:S(2)}, u32[]{:S(2)}) collective-permute-start(bf16[4,2048]{1,0:T(4,128)(2,1)S(1)} %attn_project.1.token.rest_4_), channel_id=1, source_target_pairs={{0,2},{1,3},{2,0},{3,1},{4,6},{5,7},{6,4},{7,5},{8,10},{9,11},{10,... | collective-permute-start | bytes 49160 | tf_op jit(solution)/shard_map/ppermute | solution.py:41
  27.4 0.3 collective-permute-start.6
  27.7 1.6 %fetch.3.rest_3_ = bf16[4096,256]{1,0:T(8,128)(2,1)S(1)} custom-call(bf16[4,2048]{1,0:T(4,128)(2,1)S(1)} %attn_project.1.token.rest_4_, bf16[2048,2,3584]{2,1,0:T(2,128)(2,1)} %w.9, bf16[3584,2048]{1,0:T(8,128)(2,1)S(1)} %bitcast.5), custom_call_target="tpu_custom_call" | custom-call | bytes 2214000 | tf_op jit(solution)/shard_map/fetch/pallas_call | solution.py:419
  29.4 0.3 collective-permute-done.7.rest_6_
  29.7 6.2 %gate_up.1 = (bf16[4,2048]{1,0:T(4,128)(2,1)}, bf16[8,3712]{1,0:T(8,128)(2,1)S(1)}) custom-call(bf16[4,2048]{1,0:T(4,128)(2,1)S(1)} %copy-done.1, f32[2,2048]{1,0:T(2,128)S(1)} %copy-done.2, bf16[2048,2,3584]{2,1,0:T(2,128)(2,1)} %w.9, bf16[4096,512]{1,0:T(8,128)(2,1)S(1)} %get-tuple-element.19.rest_4_.rest_0_, ...), custom_call_target="tpu_custom_call" | custom-call | bytes 36900000 | tf_op jit(solution)/shard_map/gate_up/pallas_call | solution.py:476
  35.9 2.3 %collective-permute-start.11 = (bf16[8,3712]{1,0:T(8,128)(2,1)S(1)}, bf16[8,3712]{1,0:T(8,128)(2,1)S(1)}, u32[]{:S(2)}, u32[]{:S(2)}) collective-permute-start(bf16[8,3712]{1,0:T(8,128)(2,1)S(1)} %get-tuple-element.29.rest_0_), channel_id=1, source_target_pairs={{0,12},{4,8},{8,4},{12,0},{1,13},{5,9},{9,5},{13,1},{2,14},{6,10},... | collective-permute-start | bytes 178184 | tf_op jit(solution)/shard_map/ppermute | solution.py:41
  38.1 0.4 collective-permute-start.10
  38.6 1.8 %collective-permute-start.9 = (bf16[8,3712]{1,0:T(8,128)(2,1)S(1)}, bf16[8,3712]{1,0:T(8,128)(2,1)S(1)}, u32[]{:S(2)}, u32[]{:S(2)}) collective-permute-start(bf16[8,3712]{1,0:T(8,128)(2,1)S(1)} %get-tuple-element.29.rest_0_), channel_id=1, source_target_pairs={{0,4},{4,0},{8,12},{12,8},{1,5},{5,1},{9,13},{13,9},{2,6},{6,2},{1... | collective-permute-start | bytes 178184 | tf_op jit(solution)/shard_map/ppermute | solution.py:41
  40.3 2.3 %collective-permute-done.11.rest_3_ = bf16[8,3712]{1,0:T(8,128)(2,1)S(1)} collective-permute-done((bf16[8,3712]{1,0:T(8,128)(2,1)S(1)}, bf16[8,3712]{1,0:T(8,128)(2,1)S(1)}, u32[]{:S(2)}, u32[]{:S(2)}) %collective-permute-start.11) | collective-permute-done | bytes 59424 | tf_op jit(solution)/shard_map/ppermute | solution.py:41
  42.6 1.9 %collective-permute-done.10.rest_2_ = bf16[8,3712]{1,0:T(8,128)(2,1)S(1)} collective-permute-done((bf16[8,3712]{1,0:T(8,128)(2,1)S(1)}, bf16[8,3712]{1,0:T(8,128)(2,1)S(1)}, u32[]{:S(2)}, u32[]{:S(2)}) %collective-permute-start.10) | collective-permute-done | bytes 59424 | tf_op jit(solution)/shard_map/ppermute | solution.py:41
  44.6 2.1 %down.1 = bf16[4,2048]{1,0:T(4,128)(2,1)S(1)} custom-call(bf16[3584,2048]{1,0:T(8,128)(2,1)S(1)} %bitcast.5, bf16[8,3712]{1,0:T(8,128)(2,1)S(1)} %get-tuple-element.29.rest_0_, bf16[8,3712]{1,0:T(8,128)(2,1)S(1)} %collective-permute-done.9.rest_1_, bf16[8,3712]{1,0:T(8,128)(2,1)S(1)} %collective-permute-done.10.rest_2_, ...), custom_call_target="tpu_custom_call" | custom-call | bytes 18450000 | tf_op jit(solution)/shard_map/down/pallas_call | solution.py:495
  46.7 0.6 %collective-permute-start.14 = (bf16[4,2048]{1,0:T(4,128)(2,1)S(1)}, bf16[4,2048]{1,0:T(4,128)(2,1)S(1)}, u32[]{:S(2)}, u32[]{:S(2)}) collective-permute-start(bf16[4,2048]{1,0:T(4,128)(2,1)S(1)} %down.1), channel_id=1, source_target_pairs={{0,3},{1,2},{2,1},{3,0},{4,7},{5,6},{6,5},{7,4},{8,11},{9,10},{10,... | collective-permute-start | bytes 49160 | tf_op jit(solution)/shard_map/ppermute | solution.py:41
  47.3 1.1 %collective-permute-start.13 = (bf16[4,2048]{1,0:T(4,128)(2,1)S(1)}, bf16[4,2048]{1,0:T(4,128)(2,1)S(1)}, u32[]{:S(2)}, u32[]{:S(2)}) collective-permute-start(bf16[4,2048]{1,0:T(4,128)(2,1)S(1)} %down.1), channel_id=1, source_target_pairs={{0,2},{1,3},{2,0},{3,1},{4,6},{5,7},{6,4},{7,5},{8,10},{9,11},{10,... | collective-permute-start | bytes 49160 | tf_op jit(solution)/shard_map/ppermute | solution.py:41
  48.4 0.2 collective-permute-start.12
  48.5 1.3 %collective-permute-done.14 = bf16[4,2048]{1,0:T(4,128)(2,1)S(1)} collective-permute-done((bf16[4,2048]{1,0:T(4,128)(2,1)S(1)}, bf16[4,2048]{1,0:T(4,128)(2,1)S(1)}, u32[]{:S(2)}, u32[]{:S(2)}) %collective-permute-start.14) | collective-permute-done | bytes 16416 | tf_op jit(solution)/shard_map/ppermute | solution.py:41
  49.8 1.3 %collective-permute-done.13 = bf16[4,2048]{1,0:T(4,128)(2,1)S(1)} collective-permute-done((bf16[4,2048]{1,0:T(4,128)(2,1)S(1)}, bf16[4,2048]{1,0:T(4,128)(2,1)S(1)}, u32[]{:S(2)}, u32[]{:S(2)}) %collective-permute-start.13) | collective-permute-done | bytes 16416 | tf_op jit(solution)/shard_map/ppermute | solution.py:41
  51.2 0.6 %add_convert_fusion = bf16[4,2048]{1,0:T(4,128)(2,1)} fusion(bf16[4,2048]{1,0:T(4,128)(2,1)S(1)} %collective-permute-done.14, bf16[4,2048]{1,0:T(4,128)(2,1)S(1)} %collective-permute-done.13, bf16[4,2048]{1,0:T(4,128)(2,1)S(1)} %collective-permute-done.12, bf16[4,2048]{1,0:T(4,128)(2,1)S(1)} %down.1), kind=kLoop, calls=%fused_computation | loop fusion | flops 65536 | bytes 81920 | tf_op jit(solution)/shard_map/convert_element_type | solution.py:506
  (22 shorter events, 0.1 us)
Async XLA Ops:
  5.1 8.1 %collective-permute-start = (f32[16,128]{1,0:T(8,128)S(1)}, f32[16,128]{1,0:T(8,128)S(1)}, u32[]{:S(2)}, u32[]{:S(2)}) collective-permute-start(f32[16,128]{1,0:T(8,128)S(1)} %get-tuple-element.21), channel_id=1, source_target_pairs={{0,12},{4,8},{8,4},{12,0},{1,13},{5,9},{9,5},{13,1},{2,14},{6,10},... | collective-permute-start | bytes 24584 | tf_op jit(solution)/shard_map/ppermute | solution.py:41
  10.2 4.5 %collective-permute-start.1 = (f32[16,128]{1,0:T(8,128)S(1)}, f32[16,128]{1,0:T(8,128)S(1)}, u32[]{:S(2)}, u32[]{:S(2)}) collective-permute-start(f32[16,128]{1,0:T(8,128)S(1)} %get-tuple-element.22), channel_id=1, source_target_pairs={{0,8},{4,12},{8,0},{12,4},{1,9},{5,13},{9,1},{13,5},{2,10},{6,14},... | collective-permute-start | bytes 24584 | tf_op jit(solution)/shard_map/ppermute | solution.py:41
  10.2 4.5 %collective-permute-start.2 = (f32[16,128]{1,0:T(8,128)S(1)}, f32[16,128]{1,0:T(8,128)S(1)}, u32[]{:S(2)}, u32[]{:S(2)}) collective-permute-start(f32[16,128]{1,0:T(8,128)S(1)} %get-tuple-element.23), channel_id=1, source_target_pairs={{0,4},{4,0},{8,12},{12,8},{1,5},{5,1},{9,13},{13,9},{2,6},{6,2},{1... | collective-permute-start | bytes 24584 | tf_op jit(solution)/shard_map/ppermute | solution.py:41
  18.2 9.5 %slice-start = ((s8[14680064]{0:T(1024)(128)(4,1)}), s8[4194304]{0:T(1024)(128)(4,1)S(1)}, s32[]{:S(2)}) async-start(s8[14680064]{0:T(1024)(128)(4,1)} %bitcast.4), calls=%async_computation | async-start | bytes 8388608
  18.2 6.9 %copy-start = (bf16[1024,2048]{1,0:T(8,128)(2,1)S(1)}, bf16[1024,2048]{1,0:T(8,128)(2,1)}, u32[]{:S(2)}) copy-start(bf16[1024,2048]{1,0:T(8,128)(2,1)} %w_out.1) | copy-start | bytes 12582916
  18.2 9.5 %slice-start.1 = ((s8[14680064]{0:T(1024)(128)(4,1)}), s8[4194304]{0:T(1024)(128)(4,1)S(1)}, s32[]{:S(2)}) async-start(s8[14680064]{0:T(1024)(128)(4,1)} %bitcast.4), calls=%async_computation.1 | async-start | bytes 8388608
  18.3 9.5 %slice-start.2 = ((s8[14680064]{0:T(1024)(128)(4,1)}), s8[4194304]{0:T(1024)(128)(4,1)S(1)}, s32[]{:S(2)}) async-start(s8[14680064]{0:T(1024)(128)(4,1)} %bitcast.4), calls=%async_computation.2 | async-start | bytes 8388608
  18.3 9.5 %slice-start.3 = ((s8[14680064]{0:T(1024)(128)(4,1)}), s8[2097152]{0:T(1024)(128)(4,1)S(1)}, s32[]{:S(2)}) async-start(s8[14680064]{0:T(1024)(128)(4,1)} %bitcast.4), calls=%async_computation.3 | async-start | bytes 4194304
  18.3 6.9 %collective-permute-start.5 = (bf16[8,128]{1,0:T(8,128)(2,1)S(1)}, bf16[8,128]{1,0:T(8,128)(2,1)S(1)}, u32[]{:S(2)}, u32[]{:S(2)}) collective-permute-start(bf16[8,128]{1,0:T(8,128)(2,1)S(1)} %get-tuple-element.26.token.rest_0_), channel_id=1, source_target_pairs={{0,12},{4,8},{8,4},{12,0},{1,13},{5,9},{9,5},{13,1},{2,14},{6,10},... | collective-permute-start | bytes 6152 | tf_op jit(solution)/shard_map/ppermute | solution.py:41
  20.5 4.6 %collective-permute-start.4 = (bf16[8,128]{1,0:T(8,128)(2,1)S(1)}, bf16[8,128]{1,0:T(8,128)(2,1)S(1)}, u32[]{:S(2)}, u32[]{:S(2)}) collective-permute-start(bf16[8,128]{1,0:T(8,128)(2,1)S(1)} %get-tuple-element.26.token.rest_0_), channel_id=1, source_target_pairs={{0,8},{4,12},{8,0},{12,4},{1,9},{5,13},{9,1},{13,5},{2,10},{6,14},... | collective-permute-start | bytes 6152 | tf_op jit(solution)/shard_map/ppermute | solution.py:41
  20.5 4.6 %collective-permute-start.3 = (bf16[8,128]{1,0:T(8,128)(2,1)S(1)}, bf16[8,128]{1,0:T(8,128)(2,1)S(1)}, u32[]{:S(2)}, u32[]{:S(2)}) collective-permute-start(bf16[8,128]{1,0:T(8,128)(2,1)S(1)} %get-tuple-element.26.token.rest_0_), channel_id=1, source_target_pairs={{0,4},{4,0},{8,12},{12,8},{1,5},{5,1},{9,13},{13,9},{2,6},{6,2},{1... | collective-permute-start | bytes 6152 | tf_op jit(solution)/shard_map/ppermute | solution.py:41
  25.8 3.8 %copy-start.1 = (bf16[4,2048]{1,0:T(4,128)(2,1)S(1)}, bf16[4,2048]{1,0:T(4,128)(2,1)}, u32[]{:S(2)}) copy-start(bf16[4,2048]{1,0:T(4,128)(2,1)} %states.1) | copy-start | bytes 49156
  25.8 3.8 %copy-start.2 = (f32[2,2048]{1,0:T(2,128)S(1)}, f32[2,2048]{1,0:T(2,128)}, u32[]{:S(2)}) copy-start(f32[2,2048]{1,0:T(2,128)} %gains.1) | copy-start | bytes 49156
  25.8 3.5 %collective-permute-start.8 = (bf16[4,2048]{1,0:T(4,128)(2,1)S(1)}, bf16[4,2048]{1,0:T(4,128)(2,1)S(1)}, u32[]{:S(2)}, u32[]{:S(2)}) collective-permute-start(bf16[4,2048]{1,0:T(4,128)(2,1)S(1)} %attn_project.1.token.rest_4_), channel_id=1, source_target_pairs={{0,3},{1,2},{2,1},{3,0},{4,7},{5,6},{6,5},{7,4},{8,11},{9,10},{10,... | collective-permute-start | bytes 49160 | tf_op jit(solution)/shard_map/ppermute | solution.py:41
  25.9 3.8 %collective-permute-start.7 = (bf16[4,2048]{1,0:T(4,128)(2,1)S(1)}, bf16[4,2048]{1,0:T(4,128)(2,1)S(1)}, u32[]{:S(2)}, u32[]{:S(2)}) collective-permute-start(bf16[4,2048]{1,0:T(4,128)(2,1)S(1)} %attn_project.1.token.rest_4_), channel_id=1, source_target_pairs={{0,2},{1,3},{2,0},{3,1},{4,6},{5,7},{6,4},{7,5},{8,10},{9,11},{10,... | collective-permute-start | bytes 49160 | tf_op jit(solution)/shard_map/ppermute | solution.py:41
  27.4 2.3 %collective-permute-start.6 = (bf16[4,2048]{1,0:T(4,128)(2,1)S(1)}, bf16[4,2048]{1,0:T(4,128)(2,1)S(1)}, u32[]{:S(2)}, u32[]{:S(2)}) collective-permute-start(bf16[4,2048]{1,0:T(4,128)(2,1)S(1)} %attn_project.1.token.rest_4_), channel_id=1, source_target_pairs={{0,1},{1,0},{2,3},{3,2},{4,5},{5,4},{6,7},{7,6},{8,9},{9,8},{10,11... | collective-permute-start | bytes 49160 | tf_op jit(solution)/shard_map/ppermute | solution.py:41
  35.9 6.8 %collective-permute-start.11 = (bf16[8,3712]{1,0:T(8,128)(2,1)S(1)}, bf16[8,3712]{1,0:T(8,128)(2,1)S(1)}, u32[]{:S(2)}, u32[]{:S(2)}) collective-permute-start(bf16[8,3712]{1,0:T(8,128)(2,1)S(1)} %get-tuple-element.29.rest_0_), channel_id=1, source_target_pairs={{0,12},{4,8},{8,4},{12,0},{1,13},{5,9},{9,5},{13,1},{2,14},{6,10},... | collective-permute-start | bytes 178184 | tf_op jit(solution)/shard_map/ppermute | solution.py:41
  38.1 6.4 %collective-permute-start.10 = (bf16[8,3712]{1,0:T(8,128)(2,1)S(1)}, bf16[8,3712]{1,0:T(8,128)(2,1)S(1)}, u32[]{:S(2)}, u32[]{:S(2)}) collective-permute-start(bf16[8,3712]{1,0:T(8,128)(2,1)S(1)} %get-tuple-element.29.rest_0_), channel_id=1, source_target_pairs={{0,8},{4,12},{8,0},{12,4},{1,9},{5,13},{9,1},{13,5},{2,10},{6,14},... | collective-permute-start | bytes 178184 | tf_op jit(solution)/shard_map/ppermute | solution.py:41
  38.6 6.0 %collective-permute-start.9 = (bf16[8,3712]{1,0:T(8,128)(2,1)S(1)}, bf16[8,3712]{1,0:T(8,128)(2,1)S(1)}, u32[]{:S(2)}, u32[]{:S(2)}) collective-permute-start(bf16[8,3712]{1,0:T(8,128)(2,1)S(1)} %get-tuple-element.29.rest_0_), channel_id=1, source_target_pairs={{0,4},{4,0},{8,12},{12,8},{1,5},{5,1},{9,13},{13,9},{2,6},{6,2},{1... | collective-permute-start | bytes 178184 | tf_op jit(solution)/shard_map/ppermute | solution.py:41
  46.7 3.2 %collective-permute-start.14 = (bf16[4,2048]{1,0:T(4,128)(2,1)S(1)}, bf16[4,2048]{1,0:T(4,128)(2,1)S(1)}, u32[]{:S(2)}, u32[]{:S(2)}) collective-permute-start(bf16[4,2048]{1,0:T(4,128)(2,1)S(1)} %down.1), channel_id=1, source_target_pairs={{0,3},{1,2},{2,1},{3,0},{4,7},{5,6},{6,5},{7,4},{8,11},{9,10},{10,... | collective-permute-start | bytes 49160 | tf_op jit(solution)/shard_map/ppermute | solution.py:41
  47.3 3.9 %collective-permute-start.13 = (bf16[4,2048]{1,0:T(4,128)(2,1)S(1)}, bf16[4,2048]{1,0:T(4,128)(2,1)S(1)}, u32[]{:S(2)}, u32[]{:S(2)}) collective-permute-start(bf16[4,2048]{1,0:T(4,128)(2,1)S(1)} %down.1), channel_id=1, source_target_pairs={{0,2},{1,3},{2,0},{3,1},{4,6},{5,7},{6,4},{7,5},{8,10},{9,11},{10,... | collective-permute-start | bytes 49160 | tf_op jit(solution)/shard_map/ppermute | solution.py:41
  48.4 2.8 %collective-permute-start.12 = (bf16[4,2048]{1,0:T(4,128)(2,1)S(1)}, bf16[4,2048]{1,0:T(4,128)(2,1)S(1)}, u32[]{:S(2)}, u32[]{:S(2)}) collective-permute-start(bf16[4,2048]{1,0:T(4,128)(2,1)S(1)} %down.1), channel_id=1, source_target_pairs={{0,1},{1,0},{2,3},{3,2},{4,5},{5,4},{6,7},{7,6},{8,9},{9,8},{10,11... | collective-permute-start | bytes 49160 | tf_op jit(solution)/shard_map/ppermute | solution.py:41

commit v12 on v11

--- a/solution.py
+++ b/solution.py
@@ -219,7 +219,7 @@
 
 def attend_kernel(tp, heads, rows, first, table, keys, cache, w, *rest):
     parts = rest[:tp]
-    heads_out, new_kv_out, w_ready, scores, w_sems = rest[-5:]
+    heads_out, new_kv_out, w_ready, scores, new_kv, w_sems, out_sem = rest[-7:]
     w_copies = block_copies(matrix_of(w), first, w_ready, w_sems)
     for copy in w_copies:
         copy.start()
@@ -230,8 +230,10 @@
     query = rotated[:heads].astype(BF16)
     key = rotated[heads : heads + 1].astype(BF16)
     value = sums[heads + 1 : heads + 2].astype(BF16)
-    new_kv_out[:, :LANES] = key
-    new_kv_out[:, LANES:] = value
+    new_kv[:, :LANES] = key
+    new_kv[:, LANES:] = value
+    out_copy = pltpu.make_async_copy(new_kv, new_kv_out, out_sem.at[0])
+    out_copy.start()
     key = key.astype(F32)
     value = value.astype(F32)
     scale = LANES ** (-0.5)
@@ -266,6 +268,7 @@
     heads_out[...] = (acc / total).astype(BF16)
     for copy in w_copies:
         copy.wait()
+    out_copy.wait()
 
 
 def out_kernel(tp, places, w_out, *rest):
@@ -304,7 +307,7 @@
 
 def gate_up_kernel(kv, groups, first, states, gains, w, *rest):
     ready, parts = rest[:groups], rest[groups : groups + kv]
-    attn_out, partial_out, *blocks, spread_buf, w_sems = rest[groups + kv :]
+    attn_out, partial_out, *blocks, spread_buf, attn_buf, w_sems, out_sem = rest[groups + kv :]
     docs, width = states.shape
     hidden = w.shape[2]
     w_matrix = matrix_of(w)
@@ -315,7 +318,9 @@
         for copy in copies[-1]:
             copy.start()
     attn = tree_sum([part[...].astype(F32) for part in parts]).astype(BF16)
-    attn_out[...] = attn
+    attn_buf[...] = attn
+    out_copy = pltpu.make_async_copy(attn_buf, attn_out, out_sem.at[0])
+    out_copy.start()
     resid = (states[...].astype(F32) + attn.astype(F32)).astype(BF16).astype(F32)
     squares = jnp.sum(resid * resid, axis=1, keepdims=True)
     high, low = two_parts(resid * gains[1:2, :])
@@ -336,6 +341,7 @@
     third = squares - first - second
     terms = jnp.where(lane == 0, first, jnp.where(lane == 1, second, jnp.where(lane == 2, third, 0.0)))
     partial_out[:, hidden:] = jnp.concatenate([terms, terms], axis=0).astype(BF16)
+    out_copy.wait()
 
 
 def down_kernel(tp, w_down, *rest):
@@ -447,10 +453,12 @@
             block_of(shares[1]),
         ],
         in_specs=[vmem(), vmem(), vmem(), hbm()] + [vmem()] * tp + [hbm()] * len(fetched),
-        out_specs=[vmem()] * 3,
+        out_specs=[vmem(), hbm(), vmem()],
         scratch_shapes=[
             pltpu.VMEM((heads, cache_len), F32),
+            pltpu.VMEM((1, 2 * LANES), BF16),
             pltpu.SemaphoreType.DMA((chunks,)),
+            pltpu.SemaphoreType.DMA((1,)),
         ],
         compiler_params=params(docs, 6),
         cost_estimate=cost(8),
@@ -480,11 +488,13 @@
             jax.ShapeDtypeStruct((2 * docs, hidden + LANES), BF16),
         ],
         in_specs=[vmem(), vmem(), hbm()] + [vmem()] * (len(fetched) + kv),
-        out_specs=[vmem()] * 2,
+        out_specs=[hbm(), vmem()],
         scratch_shapes=[
             *(block_of(share) for share in shares[4:]),
             pltpu.VMEM((4 * docs, 2 * width), BF16),
+            pltpu.VMEM((docs, width), BF16),
             pltpu.SemaphoreType.DMA((len(shares) - 4, chunks)),
+            pltpu.SemaphoreType.DMA((1,)),
         ],
         compiler_params=params(docs, 19),
         cost_estimate=cost(10),

time: 52.1 us -> 51.5 us (0.988)
    pallas_call x1, Pallas kernels: 3.47 us -> 2.92 us  [per_device(): pl.pallas_call(functools.partial(attend_kernel, tp, heads, 512, shares[1]...]
where the time goes in v12:
time: 51.5 us; the launch traced here: 51.3 us
  Pallas kernels  22.6 us (44%)
  starting transfers between devices  18.4 us (36%)
  waiting for transfers between devices  8.78 us (17%)
  between operations  0.81 us (2%)
  other arithmetic  0.63 us (1%)
    ppermute x15, starting transfers between devices, exchange(): lax.ppermute(arrays[s], axis, [(i, i ^ s) for i in range(size)])  18.4 us
    ppermute x15, waiting for transfers between devices, exchange(): lax.ppermute(arrays[s], axis, [(i, i ^ s) for i in range(size)])  8.78 us
    pallas_call x1, Pallas kernels, per_device(): pl.pallas_call(functools.partial(gate_up_kernel, kv, len(fetched), shares...  6.2 us
    pallas_call x1, Pallas kernels, per_device(): pl.pallas_call(functools.partial(qkv_kernel, tp), out_shape=[jax.ShapeDty...  4.43 us
    pallas_call x2, Pallas kernels, fetch(): pl.pallas_call(functools.partial(fetch_kernel, share[0]), out_shape=block...  4.02 us
    pallas_call x1, Pallas kernels, per_device(): pl.pallas_call(functools.partial(attend_kernel, tp, heads, 512, shares[1]...  2.92 us
    pallas_call x1, Pallas kernels, per_device(): pl.pallas_call(functools.partial(fetch_and_turn_kernel, shares[0][0]), ou...  2.29 us
    pallas_call x1, Pallas kernels, per_device(): pl.pallas_call(functools.partial(down_kernel, tp), out_shape=jax.ShapeDty...  2.09 us
  transfers between devices with their start and end apart: 15, of which 6 were waited for; matrix products, arithmetic and copies ran while one was open for 0% of the time, Pallas kernels for 12%

profile of v12, /device:TPU:0, one launch (start us, length us, event | category | flops | bytes accessed | tf_op | source)
XLA Modules:
  0.0 51.3 jit_solution(5362962405939906504)
XLA Ops:
  0.6 4.4 %qkv.1 = (f32[16,128]{1,0:T(8,128)S(1)}, f32[16,128]{1,0:T(8,128)S(1)}, f32[16,128]{1,0:T(8,128)S(1)}, f32[16,128]{1,0:T(8,128)S(1)}, f32[8,128]{1,0:T(8,128)S(1...) custom-call(s32[4]{0:T(128)} %owner_hbm.1, s32[4]{0:T(128)} %lengths_hbm.1, ...), custom_call_target="tpu_custom_call" | custom-call | bytes 29520000 | tf_op jit(solution)/shard_map/qkv/pallas_call | solution.py:387
  5.1 5.1 %collective-permute-start = (f32[16,128]{1,0:T(8,128)S(1)}, f32[16,128]{1,0:T(8,128)S(1)}, u32[]{:S(2)}, u32[]{:S(2)}) collective-permute-start(f32[16,128]{1,0:T(8,128)S(1)} %get-tuple-element.21), channel_id=1, source_target_pairs={{0,12},{4,8},{8,4},{12,0},{1,13},{5,9},{9,5},{13,1},{2,14},{6,10},... | collective-permute-start | bytes 24584 | tf_op jit(solution)/shard_map/ppermute | solution.py:41
  10.2 0.0 collective-permute-start.1
  10.2 0.6 %collective-permute-start.2 = (f32[16,128]{1,0:T(8,128)S(1)}, f32[16,128]{1,0:T(8,128)S(1)}, u32[]{:S(2)}, u32[]{:S(2)}) collective-permute-start(f32[16,128]{1,0:T(8,128)S(1)} %get-tuple-element.23), channel_id=1, source_target_pairs={{0,4},{4,0},{8,12},{12,8},{1,5},{5,1},{9,13},{13,9},{2,6},{6,2},{1... | collective-permute-start | bytes 24584 | tf_op jit(solution)/shard_map/ppermute | solution.py:41
  10.8 2.3 %fetch_and_turn_keys.1 = (bf16[4096,512]{1,0:T(8,128)(2,1)S(1)}, bf16[128,8192]{1,0:T(8,128)(2,1)S(1)}) custom-call(f32[8,128]{1,0:T(8,128)S(1)} %get-tuple-element.17.token.table, bf16[2048,2,3584]{2,1,0:T(2,128)(2,1)} %w.9, bf16[2,8192,128]{2,1,0:T(8,128)(2,1)S(1)} %get-tuple-element.18.cache), custom_call_target="tpu_custom_call" | custom-call | bytes 11070000 | tf_op jit(solution)/shard_map/fetch_and_turn_keys/pallas_call | solution.py:436
  13.1 0.0 collective-permute-done.rest_0_
  13.1 1.6 %collective-permute-done.1.rest_1_ = f32[16,128]{1,0:T(8,128)S(1)} collective-permute-done((f32[16,128]{1,0:T(8,128)S(1)}, f32[16,128]{1,0:T(8,128)S(1)}, u32[]{:S(2)}, u32[]{:S(2)}) %collective-permute-start.1) | collective-permute-done | bytes 8224 | tf_op jit(solution)/shard_map/ppermute | solution.py:41
  14.7 2.9 %attend.1 = (bf16[8,128]{1,0:T(8,128)(2,1)S(1)}, bf16[1,256]{1,0:T(2,128)(2,1)}, bf16[4096,768]{1,0:T(8,128)(2,1)S(1)}) custom-call(f32[8,128]{1,0:T(8,128)S(1)} %get-tuple-element.17.token.table, bf16[128,8192]{1,0:T(8,128)(2,1)S(1)} %get-tuple-element.20.keys, bf16[2,8192,128]{2,1,0:T(8,128)(2,1)S(1)} %get-tuple-element.18.cache, ...), custom_call_target="tpu_custom_call" | custom-call | bytes 29520000 | tf_op jit(solution)/shard_map/attend/pallas_call | solution.py:448
  17.7 0.0 slice-start
  17.7 0.0 copy-start
  17.7 2.2 %collective-permute-start.5 = (bf16[8,128]{1,0:T(8,128)(2,1)S(1)}, bf16[8,128]{1,0:T(8,128)(2,1)S(1)}, u32[]{:S(2)}, u32[]{:S(2)}) collective-permute-start(bf16[8,128]{1,0:T(8,128)(2,1)S(1)} %get-tuple-element.26.token.rest_0_), channel_id=1, source_target_pairs={{0,12},{4,8},{8,4},{12,0},{1,13},{5,9},{9,5},{13,1},{2,14},{6,10},... | collective-permute-start | bytes 6152 | tf_op jit(solution)/shard_map/ppermute | solution.py:41
  20.0 2.2 %collective-permute-start.3 = (bf16[8,128]{1,0:T(8,128)(2,1)S(1)}, bf16[8,128]{1,0:T(8,128)(2,1)S(1)}, u32[]{:S(2)}, u32[]{:S(2)}) collective-permute-start(bf16[8,128]{1,0:T(8,128)(2,1)S(1)} %get-tuple-element.26.token.rest_0_), channel_id=1, source_target_pairs={{0,4},{4,0},{8,12},{12,8},{1,5},{5,1},{9,13},{13,9},{2,6},{6,2},{1... | collective-permute-start | bytes 6152 | tf_op jit(solution)/shard_map/ppermute | solution.py:41
  22.2 2.4 %fetch.2.rest_4_.rest_2_ = bf16[4096,256]{1,0:T(8,128)(2,1)S(1)} custom-call(bf16[8,128]{1,0:T(8,128)(2,1)S(1)} %get-tuple-element.26.token.rest_0_, bf16[2048,2,3584]{2,1,0:T(2,128)(2,1)} %w.9), custom_call_target="tpu_custom_call" | custom-call | bytes 2214000 | tf_op jit(solution)/shard_map/fetch/pallas_call | solution.py:425
  24.6 0.7 %attn_project.1.token.rest_4_ = bf16[4,2048]{1,0:T(4,128)(2,1)S(1)} custom-call(s32[8,128]{1,0:T(8,128)S(1)} %get-tuple-element.27.places, bf16[1024,2048]{1,0:T(8,128)(2,1)S(1)} %copy-done, bf16[8,128]{1,0:T(8,128)(2,1)S(1)} %get-tuple-element.26.token.rest_0_, bf16[8,128]{1,0:T(8,128)(2,1)S(1)} %collective-permute-done.3.rest_1_, ...), custom_call_target="tpu_custom_call" | custom-call | bytes 22140000 | tf_op jit(solution)/shard_map/attn_project/pallas_call | solution.py:471
  25.3 0.0 collective-permute-start.8
  25.3 1.6 %collective-permute-start.7 = (bf16[4,2048]{1,0:T(4,128)(2,1)S(1)}, bf16[4,2048]{1,0:T(4,128)(2,1)S(1)}, u32[]{:S(2)}, u32[]{:S(2)}) collective-permute-start(bf16[4,2048]{1,0:T(4,128)(2,1)S(1)} %attn_project.1.token.rest_4_), channel_id=1, source_target_pairs={{0,2},{1,3},{2,0},{3,1},{4,6},{5,7},{6,4},{7,5},{8,10},{9,11},{10,... | collective-permute-start | bytes 49160 | tf_op jit(solution)/shard_map/ppermute | solution.py:41
  26.9 0.3 collective-permute-start.6
  27.2 1.6 %fetch.3.rest_3_ = bf16[4096,256]{1,0:T(8,128)(2,1)S(1)} custom-call(bf16[4,2048]{1,0:T(4,128)(2,1)S(1)} %attn_project.1.token.rest_4_, bf16[2048,2,3584]{2,1,0:T(2,128)(2,1)} %w.9, bf16[3584,2048]{1,0:T(8,128)(2,1)S(1)} %bitcast.5), custom_call_target="tpu_custom_call" | custom-call | bytes 2214000 | tf_op jit(solution)/shard_map/fetch/pallas_call | solution.py:425
  28.8 0.3 collective-permute-done.7.rest_6_
  29.1 6.2 %gate_up.1 = (bf16[4,2048]{1,0:T(4,128)(2,1)}, bf16[8,3712]{1,0:T(8,128)(2,1)S(1)}) custom-call(bf16[4,2048]{1,0:T(4,128)(2,1)S(1)} %copy-done.1, f32[2,2048]{1,0:T(2,128)S(1)} %copy-done.2, bf16[2048,2,3584]{2,1,0:T(2,128)(2,1)} %w.9, bf16[4096,512]{1,0:T(8,128)(2,1)S(1)} %get-tuple-element.19.rest_4_.rest_0_, ...), custom_call_target="tpu_custom_call" | custom-call | bytes 36900000 | tf_op jit(solution)/shard_map/gate_up/pallas_call | solution.py:484
  35.3 2.3 %collective-permute-start.11 = (bf16[8,3712]{1,0:T(8,128)(2,1)S(1)}, bf16[8,3712]{1,0:T(8,128)(2,1)S(1)}, u32[]{:S(2)}, u32[]{:S(2)}) collective-permute-start(bf16[8,3712]{1,0:T(8,128)(2,1)S(1)} %get-tuple-element.29.rest_0_), channel_id=1, source_target_pairs={{0,12},{4,8},{8,4},{12,0},{1,13},{5,9},{9,5},{13,1},{2,14},{6,10},... | collective-permute-start | bytes 178184 | tf_op jit(solution)/shard_map/ppermute | solution.py:41
  37.6 0.4 collective-permute-start.10
  38.0 1.8 %collective-permute-start.9 = (bf16[8,3712]{1,0:T(8,128)(2,1)S(1)}, bf16[8,3712]{1,0:T(8,128)(2,1)S(1)}, u32[]{:S(2)}, u32[]{:S(2)}) collective-permute-start(bf16[8,3712]{1,0:T(8,128)(2,1)S(1)} %get-tuple-element.29.rest_0_), channel_id=1, source_target_pairs={{0,4},{4,0},{8,12},{12,8},{1,5},{5,1},{9,13},{13,9},{2,6},{6,2},{1... | collective-permute-start | bytes 178184 | tf_op jit(solution)/shard_map/ppermute | solution.py:41
  39.8 2.3 %collective-permute-done.11.rest_3_ = bf16[8,3712]{1,0:T(8,128)(2,1)S(1)} collective-permute-done((bf16[8,3712]{1,0:T(8,128)(2,1)S(1)}, bf16[8,3712]{1,0:T(8,128)(2,1)S(1)}, u32[]{:S(2)}, u32[]{:S(2)}) %collective-permute-start.11) | collective-permute-done | bytes 59424 | tf_op jit(solution)/shard_map/ppermute | solution.py:41
  42.1 1.9 %collective-permute-done.10.rest_2_ = bf16[8,3712]{1,0:T(8,128)(2,1)S(1)} collective-permute-done((bf16[8,3712]{1,0:T(8,128)(2,1)S(1)}, bf16[8,3712]{1,0:T(8,128)(2,1)S(1)}, u32[]{:S(2)}, u32[]{:S(2)}) %collective-permute-start.10) | collective-permute-done | bytes 59424 | tf_op jit(solution)/shard_map/ppermute | solution.py:41
  44.0 2.1 %down.1 = bf16[4,2048]{1,0:T(4,128)(2,1)S(1)} custom-call(bf16[3584,2048]{1,0:T(8,128)(2,1)S(1)} %bitcast.5, bf16[8,3712]{1,0:T(8,128)(2,1)S(1)} %get-tuple-element.29.rest_0_, bf16[8,3712]{1,0:T(8,128)(2,1)S(1)} %collective-permute-done.9.rest_1_, bf16[8,3712]{1,0:T(8,128)(2,1)S(1)} %collective-permute-done.10.rest_2_, ...), custom_call_target="tpu_custom_call" | custom-call | bytes 18450000 | tf_op jit(solution)/shard_map/down/pallas_call | solution.py:505
  46.1 0.6 %collective-permute-start.14 = (bf16[4,2048]{1,0:T(4,128)(2,1)S(1)}, bf16[4,2048]{1,0:T(4,128)(2,1)S(1)}, u32[]{:S(2)}, u32[]{:S(2)}) collective-permute-start(bf16[4,2048]{1,0:T(4,128)(2,1)S(1)} %down.1), channel_id=1, source_target_pairs={{0,3},{1,2},{2,1},{3,0},{4,7},{5,6},{6,5},{7,4},{8,11},{9,10},{10,... | collective-permute-start | bytes 49160 | tf_op jit(solution)/shard_map/ppermute | solution.py:41
  46.8 1.1 %collective-permute-start.13 = (bf16[4,2048]{1,0:T(4,128)(2,1)S(1)}, bf16[4,2048]{1,0:T(4,128)(2,1)S(1)}, u32[]{:S(2)}, u32[]{:S(2)}) collective-permute-start(bf16[4,2048]{1,0:T(4,128)(2,1)S(1)} %down.1), channel_id=1, source_target_pairs={{0,2},{1,3},{2,0},{3,1},{4,6},{5,7},{6,4},{7,5},{8,10},{9,11},{10,... | collective-permute-start | bytes 49160 | tf_op jit(solution)/shard_map/ppermute | solution.py:41
  47.8 0.2 collective-permute-start.12
  48.0 1.3 %collective-permute-done.14 = bf16[4,2048]{1,0:T(4,128)(2,1)S(1)} collective-permute-done((bf16[4,2048]{1,0:T(4,128)(2,1)S(1)}, bf16[4,2048]{1,0:T(4,128)(2,1)S(1)}, u32[]{:S(2)}, u32[]{:S(2)}) %collective-permute-start.14) | collective-permute-done | bytes 16416 | tf_op jit(solution)/shard_map/ppermute | solution.py:41
  49.3 1.3 %collective-permute-done.13 = bf16[4,2048]{1,0:T(4,128)(2,1)S(1)} collective-permute-done((bf16[4,2048]{1,0:T(4,128)(2,1)S(1)}, bf16[4,2048]{1,0:T(4,128)(2,1)S(1)}, u32[]{:S(2)}, u32[]{:S(2)}) %collective-permute-start.13) | collective-permute-done | bytes 16416 | tf_op jit(solution)/shard_map/ppermute | solution.py:41
  50.6 0.6 %add_convert_fusion = bf16[4,2048]{1,0:T(4,128)(2,1)} fusion(bf16[4,2048]{1,0:T(4,128)(2,1)S(1)} %collective-permute-done.14, bf16[4,2048]{1,0:T(4,128)(2,1)S(1)} %collective-permute-done.13, bf16[4,2048]{1,0:T(4,128)(2,1)S(1)} %collective-permute-done.12, bf16[4,2048]{1,0:T(4,128)(2,1)S(1)} %down.1), kind=kLoop, calls=%fused_computation | loop fusion | flops 65536 | bytes 81920 | tf_op jit(solution)/shard_map/convert_element_type | solution.py:516
  (22 shorter events, 0.1 us)
Async XLA Ops:
  5.1 8.1 %collective-permute-start = (f32[16,128]{1,0:T(8,128)S(1)}, f32[16,128]{1,0:T(8,128)S(1)}, u32[]{:S(2)}, u32[]{:S(2)}) collective-permute-start(f32[16,128]{1,0:T(8,128)S(1)} %get-tuple-element.21), channel_id=1, source_target_pairs={{0,12},{4,8},{8,4},{12,0},{1,13},{5,9},{9,5},{13,1},{2,14},{6,10},... | collective-permute-start | bytes 24584 | tf_op jit(solution)/shard_map/ppermute | solution.py:41
  10.2 4.5 %collective-permute-start.1 = (f32[16,128]{1,0:T(8,128)S(1)}, f32[16,128]{1,0:T(8,128)S(1)}, u32[]{:S(2)}, u32[]{:S(2)}) collective-permute-start(f32[16,128]{1,0:T(8,128)S(1)} %get-tuple-element.22), channel_id=1, source_target_pairs={{0,8},{4,12},{8,0},{12,4},{1,9},{5,13},{9,1},{13,5},{2,10},{6,14},... | collective-permute-start | bytes 24584 | tf_op jit(solution)/shard_map/ppermute | solution.py:41
  10.2 4.5 %collective-permute-start.2 = (f32[16,128]{1,0:T(8,128)S(1)}, f32[16,128]{1,0:T(8,128)S(1)}, u32[]{:S(2)}, u32[]{:S(2)}) collective-permute-start(f32[16,128]{1,0:T(8,128)S(1)} %get-tuple-element.23), channel_id=1, source_target_pairs={{0,4},{4,0},{8,12},{12,8},{1,5},{5,1},{9,13},{13,9},{2,6},{6,2},{1... | collective-permute-start | bytes 24584 | tf_op jit(solution)/shard_map/ppermute | solution.py:41
  17.7 9.5 %slice-start = ((s8[14680064]{0:T(1024)(128)(4,1)}), s8[4194304]{0:T(1024)(128)(4,1)S(1)}, s32[]{:S(2)}) async-start(s8[14680064]{0:T(1024)(128)(4,1)} %bitcast.4), calls=%async_computation | async-start | bytes 8388608
  17.7 6.9 %copy-start = (bf16[1024,2048]{1,0:T(8,128)(2,1)S(1)}, bf16[1024,2048]{1,0:T(8,128)(2,1)}, u32[]{:S(2)}) copy-start(bf16[1024,2048]{1,0:T(8,128)(2,1)} %w_out.1) | copy-start | bytes 12582916
  17.7 9.5 %slice-start.1 = ((s8[14680064]{0:T(1024)(128)(4,1)}), s8[4194304]{0:T(1024)(128)(4,1)S(1)}, s32[]{:S(2)}) async-start(s8[14680064]{0:T(1024)(128)(4,1)} %bitcast.4), calls=%async_computation.1 | async-start | bytes 8388608
  17.7 9.5 %slice-start.2 = ((s8[14680064]{0:T(1024)(128)(4,1)}), s8[4194304]{0:T(1024)(128)(4,1)S(1)}, s32[]{:S(2)}) async-start(s8[14680064]{0:T(1024)(128)(4,1)} %bitcast.4), calls=%async_computation.2 | async-start | bytes 8388608
  17.7 9.5 %slice-start.3 = ((s8[14680064]{0:T(1024)(128)(4,1)}), s8[2097152]{0:T(1024)(128)(4,1)S(1)}, s32[]{:S(2)}) async-start(s8[14680064]{0:T(1024)(128)(4,1)} %bitcast.4), calls=%async_computation.3 | async-start | bytes 4194304
  17.7 6.9 %collective-permute-start.5 = (bf16[8,128]{1,0:T(8,128)(2,1)S(1)}, bf16[8,128]{1,0:T(8,128)(2,1)S(1)}, u32[]{:S(2)}, u32[]{:S(2)}) collective-permute-start(bf16[8,128]{1,0:T(8,128)(2,1)S(1)} %get-tuple-element.26.token.rest_0_), channel_id=1, source_target_pairs={{0,12},{4,8},{8,4},{12,0},{1,13},{5,9},{9,5},{13,1},{2,14},{6,10},... | collective-permute-start | bytes 6152 | tf_op jit(solution)/shard_map/ppermute | solution.py:41
  20.0 4.6 %collective-permute-start.4 = (bf16[8,128]{1,0:T(8,128)(2,1)S(1)}, bf16[8,128]{1,0:T(8,128)(2,1)S(1)}, u32[]{:S(2)}, u32[]{:S(2)}) collective-permute-start(bf16[8,128]{1,0:T(8,128)(2,1)S(1)} %get-tuple-element.26.token.rest_0_), channel_id=1, source_target_pairs={{0,8},{4,12},{8,0},{12,4},{1,9},{5,13},{9,1},{13,5},{2,10},{6,14},... | collective-permute-start | bytes 6152 | tf_op jit(solution)/shard_map/ppermute | solution.py:41
  20.0 4.6 %collective-permute-start.3 = (bf16[8,128]{1,0:T(8,128)(2,1)S(1)}, bf16[8,128]{1,0:T(8,128)(2,1)S(1)}, u32[]{:S(2)}, u32[]{:S(2)}) collective-permute-start(bf16[8,128]{1,0:T(8,128)(2,1)S(1)} %get-tuple-element.26.token.rest_0_), channel_id=1, source_target_pairs={{0,4},{4,0},{8,12},{12,8},{1,5},{5,1},{9,13},{13,9},{2,6},{6,2},{1... | collective-permute-start | bytes 6152 | tf_op jit(solution)/shard_map/ppermute | solution.py:41
  25.3 3.8 %copy-start.1 = (bf16[4,2048]{1,0:T(4,128)(2,1)S(1)}, bf16[4,2048]{1,0:T(4,128)(2,1)}, u32[]{:S(2)}) copy-start(bf16[4,2048]{1,0:T(4,128)(2,1)} %states.1) | copy-start | bytes 49156
  25.3 3.8 %copy-start.2 = (f32[2,2048]{1,0:T(2,128)S(1)}, f32[2,2048]{1,0:T(2,128)}, u32[]{:S(2)}) copy-start(f32[2,2048]{1,0:T(2,128)} %gains.1) | copy-start | bytes 49156
  25.3 3.5 %collective-permute-start.8 = (bf16[4,2048]{1,0:T(4,128)(2,1)S(1)}, bf16[4,2048]{1,0:T(4,128)(2,1)S(1)}, u32[]{:S(2)}, u32[]{:S(2)}) collective-permute-start(bf16[4,2048]{1,0:T(4,128)(2,1)S(1)} %attn_project.1.token.rest_4_), channel_id=1, source_target_pairs={{0,3},{1,2},{2,1},{3,0},{4,7},{5,6},{6,5},{7,4},{8,11},{9,10},{10,... | collective-permute-start | bytes 49160 | tf_op jit(solution)/shard_map/ppermute | solution.py:41
  25.3 3.8 %collective-permute-start.7 = (bf16[4,2048]{1,0:T(4,128)(2,1)S(1)}, bf16[4,2048]{1,0:T(4,128)(2,1)S(1)}, u32[]{:S(2)}, u32[]{:S(2)}) collective-permute-start(bf16[4,2048]{1,0:T(4,128)(2,1)S(1)} %attn_project.1.token.rest_4_), channel_id=1, source_target_pairs={{0,2},{1,3},{2,0},{3,1},{4,6},{5,7},{6,4},{7,5},{8,10},{9,11},{10,... | collective-permute-start | bytes 49160 | tf_op jit(solution)/shard_map/ppermute | solution.py:41
  26.9 2.3 %collective-permute-start.6 = (bf16[4,2048]{1,0:T(4,128)(2,1)S(1)}, bf16[4,2048]{1,0:T(4,128)(2,1)S(1)}, u32[]{:S(2)}, u32[]{:S(2)}) collective-permute-start(bf16[4,2048]{1,0:T(4,128)(2,1)S(1)} %attn_project.1.token.rest_4_), channel_id=1, source_target_pairs={{0,1},{1,0},{2,3},{3,2},{4,5},{5,4},{6,7},{7,6},{8,9},{9,8},{10,11... | collective-permute-start | bytes 49160 | tf_op jit(solution)/shard_map/ppermute | solution.py:41
  35.3 6.8 %collective-permute-start.11 = (bf16[8,3712]{1,0:T(8,128)(2,1)S(1)}, bf16[8,3712]{1,0:T(8,128)(2,1)S(1)}, u32[]{:S(2)}, u32[]{:S(2)}) collective-permute-start(bf16[8,3712]{1,0:T(8,128)(2,1)S(1)} %get-tuple-element.29.rest_0_), channel_id=1, source_target_pairs={{0,12},{4,8},{8,4},{12,0},{1,13},{5,9},{9,5},{13,1},{2,14},{6,10},... | collective-permute-start | bytes 178184 | tf_op jit(solution)/shard_map/ppermute | solution.py:41
  37.6 6.4 %collective-permute-start.10 = (bf16[8,3712]{1,0:T(8,128)(2,1)S(1)}, bf16[8,3712]{1,0:T(8,128)(2,1)S(1)}, u32[]{:S(2)}, u32[]{:S(2)}) collective-permute-start(bf16[8,3712]{1,0:T(8,128)(2,1)S(1)} %get-tuple-element.29.rest_0_), channel_id=1, source_target_pairs={{0,8},{4,12},{8,0},{12,4},{1,9},{5,13},{9,1},{13,5},{2,10},{6,14},... | collective-permute-start | bytes 178184 | tf_op jit(solution)/shard_map/ppermute | solution.py:41
  38.0 6.0 %collective-permute-start.9 = (bf16[8,3712]{1,0:T(8,128)(2,1)S(1)}, bf16[8,3712]{1,0:T(8,128)(2,1)S(1)}, u32[]{:S(2)}, u32[]{:S(2)}) collective-permute-start(bf16[8,3712]{1,0:T(8,128)(2,1)S(1)} %get-tuple-element.29.rest_0_), channel_id=1, source_target_pairs={{0,4},{4,0},{8,12},{12,8},{1,5},{5,1},{9,13},{13,9},{2,6},{6,2},{1... | collective-permute-start | bytes 178184 | tf_op jit(solution)/shard_map/ppermute | solution.py:41
  46.1 3.2 %collective-permute-start.14 = (bf16[4,2048]{1,0:T(4,128)(2,1)S(1)}, bf16[4,2048]{1,0:T(4,128)(2,1)S(1)}, u32[]{:S(2)}, u32[]{:S(2)}) collective-permute-start(bf16[4,2048]{1,0:T(4,128)(2,1)S(1)} %down.1), channel_id=1, source_target_pairs={{0,3},{1,2},{2,1},{3,0},{4,7},{5,6},{6,5},{7,4},{8,11},{9,10},{10,... | collective-permute-start | bytes 49160 | tf_op jit(solution)/shard_map/ppermute | solution.py:41
  46.8 3.9 %collective-permute-start.13 = (bf16[4,2048]{1,0:T(4,128)(2,1)S(1)}, bf16[4,2048]{1,0:T(4,128)(2,1)S(1)}, u32[]{:S(2)}, u32[]{:S(2)}) collective-permute-start(bf16[4,2048]{1,0:T(4,128)(2,1)S(1)} %down.1), channel_id=1, source_target_pairs={{0,2},{1,3},{2,0},{3,1},{4,6},{5,7},{6,4},{7,5},{8,10},{9,11},{10,... | collective-permute-start | bytes 49160 | tf_op jit(solution)/shard_map/ppermute | solution.py:41
  47.8 2.8 %collective-permute-start.12 = (bf16[4,2048]{1,0:T(4,128)(2,1)S(1)}, bf16[4,2048]{1,0:T(4,128)(2,1)S(1)}, u32[]{:S(2)}, u32[]{:S(2)}) collective-permute-start(bf16[4,2048]{1,0:T(4,128)(2,1)S(1)} %down.1), channel_id=1, source_target_pairs={{0,1},{1,0},{2,3},{3,2},{4,5},{5,4},{6,7},{7,6},{8,9},{9,8},{10,11... | collective-permute-start | bytes 49160 | tf_op jit(solution)/shard_map/ppermute | solution.py:41

commit v13 on v12

--- a/solution.py
+++ b/solution.py
@@ -15,8 +15,8 @@
 LANES = 128
 MIB = 1 << 20
 COPY_ROWS = 2048
-KEY_ROWS = 512
-GU_SHARES = (4, 6, 2, 2, 4, 4, 4, 2)
+DOWN_ROWS = 1024
+GU_SHARES = (4, 6, 4, 2, 4, 4, 2, 2)
 F32 = jnp.float32
 BF16 = jnp.bfloat16
 QUARTER = (1.5703125, 4.837512969970703125e-4, 7.549789948768648e-8)
@@ -68,15 +68,6 @@
     for c in range(chunks):
         piece = doubled[c * 4 * docs : (c + 1) * 4 * docs]
         out_ref[:, 2 * c * LANES : 2 * (c + 1) * LANES] = jnp.where(keep, piece, 0.0).astype(BF16)
-
-
-def tile_copies(matrix, first, buf, sems):
-    return [
-        pltpu.make_async_copy(
-            matrix.at[:, pl.ds((first + i) * LANES, LANES)], buf.at[i], sems.at[i]
-        )
-        for i in range(buf.shape[0])
-    ]
 
 
 def matrix_of(w):
@@ -147,13 +138,11 @@
             )
 
 
-def qkv_kernel(
-    tp, owner_hbm, lengths_hbm, frequency_hbm, states_hbm, gains_hbm, wq, wkv, cache, *rest
-):
+def qkv_kernel(tp, owner_hbm, lengths_hbm, frequency_hbm, states_hbm, gains_hbm, wq, wkv, *rest):
     outs = rest[:tp]
-    table, places, cache_tiles = rest[tp : tp + 3]
-    owner, lengths, frequency, states, gains = rest[tp + 3 : tp + 8]
-    wq_buf, wkv_buf, spread_buf, sems, small_sems, cache_sems = rest[tp + 8 :]
+    table, places = rest[tp : tp + 2]
+    owner, lengths, frequency, states, gains = rest[tp + 2 : tp + 7]
+    wq_buf, wkv_buf, spread_buf, sems, small_sems = rest[tp + 7 :]
     docs, width = states.shape
     heads = wq.shape[0] // width
     parts = wq_buf.shape[0]
@@ -175,17 +164,16 @@
         for c in range(parts)
     ]
     kv_copy = pltpu.make_async_copy(wkv, wkv_buf, sems.at[parts])
-    cache_copies = tile_copies(cache, 0, cache_tiles, cache_sems)
     for copy in small + [kv_copy] + copies:
         copy.start()
     for copy in small:
         copy.wait()
-    for copy in cache_copies:
-        copy.start()
     me = lax.axis_index("tp")
     x = states[...].astype(F32)
     squares = jnp.broadcast_to(jnp.sum(x * x, axis=1, keepdims=True), (docs, LANES))
     both = jnp.concatenate(two_parts(x * gains[0:1, :]), axis=0)
+    kv_copy.wait()
+    kv_total = jnp.dot(both.astype(BF16), wkv_buf[...], preferred_element_type=F32)
     spread_heads(both, spread_buf, heads)
     length = lengths[owner[me]].astype(F32)
     cosine, sine = rope_rows(length, frequency[...])
@@ -195,8 +183,6 @@
     table[3:, :] = jnp.zeros((table.shape[0] - 3, LANES), F32)
     for s in range(tp):
         places[s : s + 1, :] = jnp.full((1, LANES), owner[me ^ s], jnp.int32)
-    kv_copy.wait()
-    kv_total = jnp.dot(both.astype(BF16), wkv_buf[...], preferred_element_type=F32)
     total = jnp.zeros((heads * 2 * docs, LANES), F32)
     for c in range(parts):
         copies[c].wait()
@@ -213,17 +199,15 @@
         out[heads + 1 : heads + 2, :] = kv_row[:, LANES:]
         out[heads + 2 : heads + 3, :] = pick_doc(squares, doc, docs)[None]
         out[heads + 3 :, :] = jnp.zeros((out.shape[0] - heads - 3, LANES), F32)
-    for copy in cache_copies:
-        copy.wait()
-
-
-def attend_kernel(tp, heads, rows, first, table, keys, cache, w, *rest):
+
+
+def attend_kernel(tp, heads, rows, first, table, cache, w, *rest):
     parts = rest[:tp]
     heads_out, new_kv_out, w_ready, scores, new_kv, w_sems, out_sem = rest[-7:]
     w_copies = block_copies(matrix_of(w), first, w_ready, w_sems)
     for copy in w_copies:
         copy.start()
-    blocks = cache.shape[1] // rows
+    blocks = cache.shape[0] // rows
     sums = tree_sum([part[...] for part in parts])
     sums = sums * lax.rsqrt(sums[heads + 2 : heads + 3, :] / D + EPS)
     rotated = sums * table[0:1, :] + pltpu.roll(sums, LANES // 2, 1) * table[1:2, :]
@@ -242,8 +226,11 @@
     length = table[2:3, :]
     tops = jnp.full((heads, LANES), -jnp.inf, F32)
     for b in range(blocks):
-        block = jnp.dot(
-            query, keys[:, b * rows : (b + 1) * rows], preferred_element_type=F32
+        block = lax.dot_general(
+            query,
+            cache[b * rows : (b + 1) * rows, :LANES],
+            (((1,), (1,)), ((), ())),
+            preferred_element_type=F32,
         )
         for start in range(0, rows, LANES):
             at = b * rows + start
@@ -261,7 +248,7 @@
             sums_by_lane = sums_by_lane + weights[:, start : start + LANES]
         acc = acc + jnp.dot(
             weights.astype(BF16),
-            cache[1, b * rows : (b + 1) * rows, :],
+            cache[b * rows : (b + 1) * rows, LANES:],
             preferred_element_type=F32,
         )
     total = own + jnp.sum(sums_by_lane, axis=1, keepdims=True)
@@ -291,16 +278,6 @@
     copies = block_copies(matrix_of(w), first, out, sems)
     for copy in copies:
         copy.start()
-    for copy in copies:
-        copy.wait()
-
-
-def fetch_and_turn_kernel(first, token, w, cache, out, turned, sems):
-    copies = block_copies(matrix_of(w), first, out, sems)
-    for copy in copies:
-        copy.start()
-    for start in range(0, cache.shape[1], KEY_ROWS):
-        turned[:, start : start + KEY_ROWS] = cache[0, start : start + KEY_ROWS, :].T
     for copy in copies:
         copy.wait()
 
@@ -345,18 +322,26 @@
 
 
 def down_kernel(tp, w_down, *rest):
-    parts = rest[:tp]
-    out, act_buf = rest[tp:]
+    parts, out = rest[:tp], rest[tp]
     docs, width = out.shape
     hidden = w_down.shape[0]
-    summed = tree_sum([part[...].astype(F32) for part in parts])
-    squares = jnp.sum(summed[:docs, hidden:], axis=1, keepdims=True)
+
+    def summed(start, size):
+        return tree_sum([part[:, start : start + size].astype(F32) for part in parts])
+
+    squares = jnp.sum(summed(hidden, LANES)[:docs], axis=1, keepdims=True)
     inverse = lax.rsqrt(squares / D + EPS)
-    gate = summed[:docs, :hidden] * inverse
-    up = summed[docs:, :hidden] * inverse
-    act_buf[...] = (gate / (1.0 + jnp.exp(-gate)) * up).astype(BF16)
-
-    out[...] = jnp.dot(act_buf[...], w_down[...], preferred_element_type=F32).astype(BF16)
+    total = jnp.zeros((docs, width), F32)
+    for start in range(0, hidden, DOWN_ROWS):
+        size = min(DOWN_ROWS, hidden - start)
+        both = summed(start, size)
+        gate = both[:docs] * inverse
+        up = both[docs:] * inverse
+        act = (gate / (1.0 + jnp.exp(-gate)) * up).astype(BF16)
+        total = total + jnp.dot(
+            act, w_down[start : start + size, :], preferred_element_type=F32
+        )
+    out[...] = total.astype(BF16)
 
 
 def cost(micros):
@@ -384,16 +369,15 @@
     half = LANES // 2
     freq = ROPE_BASE ** (-(np.arange(half, dtype=np.float64) * 2.0 / LANES))
     freq = jnp.asarray(np.concatenate([freq, freq]).astype(np.float32)[None, :])
-    *qkv_parts, table, places, cache_tiles = pl.pallas_call(
+    *qkv_parts, table, places = pl.pallas_call(
         functools.partial(qkv_kernel, tp),
         out_shape=[jax.ShapeDtypeStruct((packed, LANES), F32)] * tp
         + [
             jax.ShapeDtypeStruct((8, LANES), F32),
             jax.ShapeDtypeStruct((max(tp, 8), LANES), jnp.int32),
-            pltpu.VMEM((2, cache_len, LANES), BF16),
         ],
-        in_specs=[hbm()] * 8,
-        out_specs=[vmem()] * (tp + 3),
+        in_specs=[hbm()] * 7,
+        out_specs=[vmem()] * (tp + 2),
         scratch_shapes=[
             pltpu.SMEM((docs,), jnp.int32),
             pltpu.SMEM((docs,), jnp.int32),
@@ -405,12 +389,11 @@
             pltpu.VMEM((heads * 2 * docs, width * heads), BF16),
             pltpu.SemaphoreType.DMA((wq_parts + 1,)),
             pltpu.SemaphoreType.DMA((5,)),
-            pltpu.SemaphoreType.DMA((2,)),
         ],
         compiler_params=params(docs, 10),
         cost_estimate=cost(8),
         name="qkv",
-    )(*(in_hbm(a) for a in (owner_rows, lengths, freq, states, norm_gains, wq, wkv, cache)))
+    )(*(in_hbm(a) for a in (owner_rows, lengths, freq, states, norm_gains, wq, wkv)))
     w_gu = in_hbm(w_gate_up)
     bounds = np.cumsum([0] + [hidden // LANES * n // 28 for n in GU_SHARES]).tolist()
     shares = list(zip(bounds, bounds[1:]))
@@ -433,17 +416,7 @@
             name="fetch",
         )(token, w_gu, *keep)
 
-    w_ready, turned = pl.pallas_call(
-        functools.partial(fetch_and_turn_kernel, shares[0][0]),
-        out_shape=[block_of(shares[0]), pltpu.VMEM((LANES, cache_len), BF16)],
-        in_specs=[hbm(), hbm(), vmem()],
-        out_specs=[vmem(), vmem()],
-        scratch_shapes=[pltpu.SemaphoreType.DMA((chunks,))],
-        compiler_params=params(docs, 4),
-        cost_estimate=cost(3),
-        name="fetch_and_turn_keys",
-    )(table, w_gu, cache_tiles)
-    fetched.append(w_ready)
+    fetched.append(fetch(shares[0], table, cache))
     qkv_parts = exchange(qkv_parts, "tp", tp)[::-1]
     head_out, new_kv, w_ready = pl.pallas_call(
         functools.partial(attend_kernel, tp, heads, 512, shares[1][0]),
@@ -452,7 +425,7 @@
             jax.ShapeDtypeStruct((1, 2 * LANES), BF16),
             block_of(shares[1]),
         ],
-        in_specs=[vmem(), vmem(), vmem(), hbm()] + [vmem()] * tp + [hbm()] * len(fetched),
+        in_specs=[vmem(), vmem(), hbm()] + [vmem()] * tp + [hbm()] * len(fetched),
         out_specs=[vmem(), hbm(), vmem()],
         scratch_shapes=[
             pltpu.VMEM((heads, cache_len), F32),
@@ -463,7 +436,7 @@
         compiler_params=params(docs, 6),
         cost_estimate=cost(8),
         name="attend",
-    )(table, turned, cache_tiles, w_gu, *qkv_parts, *fetched)
+    )(table, cache, w_gu, *qkv_parts, *fetched)
     fetched.append(w_ready)
 
     fetched.append(fetch(shares[2], head_out))
@@ -479,7 +452,7 @@
         name="attn_project",
     )(places, w_out, *head_parts, fetched[-1])
 
-    fetched.append(fetch(shares[3], out_part, w_down))
+    fetched.append(fetch(shares[3], out_part))
     out_parts = exchange([out_part] * kv, "kv", kv)
     attn_out, gu_part = pl.pallas_call(
         functools.partial(gate_up_kernel, kv, len(fetched), shares[4][0]),
@@ -507,7 +480,6 @@
         out_shape=jax.ShapeDtypeStruct((docs, width), BF16),
         in_specs=[vmem()] * (1 + tp),
         out_specs=vmem(),
-        scratch_shapes=[pltpu.VMEM((docs, hidden), BF16)],
         compiler_params=params(docs, 6),
         cost_estimate=cost(5),
         name="down",

time: 51.5 us -> 50.4 us (0.979)
  Pallas kernels: 22.6 us -> 21.5 us
    pallas_call x1 -> x0, Pallas kernels: 2.29 us -> none  [per_device(): pl.pallas_call(functools.partial(fetch_and_turn_kernel, shares[0][0]), ou...]
    pallas_call x2 -> x3, Pallas kernels: 4.02 us -> 6.18 us  [fetch(): pl.pallas_call(functools.partial(fetch_kernel, share[0]), out_shape=block...]
    pallas_call x1, Pallas kernels: 4.43 us -> 3.91 us  [per_device(): pl.pallas_call(functools.partial(qkv_kernel, tp), out_shape=[jax.ShapeDty...]
where the time goes in v13:
time: 50.4 us; the launch traced here: 50.2 us
  Pallas kernels  21.5 us (43%)
  starting transfers between devices  18.5 us (37%)
  waiting for transfers between devices  8.75 us (17%)
  between operations  0.83 us (2%)
  other arithmetic  0.63 us (1%)
    ppermute x15, starting transfers between devices, exchange(): lax.ppermute(arrays[s], axis, [(i, i ^ s) for i in range(size)])  18.5 us
    ppermute x15, waiting for transfers between devices, exchange(): lax.ppermute(arrays[s], axis, [(i, i ^ s) for i in range(size)])  8.75 us
    pallas_call x3, Pallas kernels, fetch(): pl.pallas_call(functools.partial(fetch_kernel, share[0]), out_shape=block...  6.18 us
    pallas_call x1, Pallas kernels, per_device(): pl.pallas_call(functools.partial(gate_up_kernel, kv, len(fetched), shares...  5.77 us
    pallas_call x1, Pallas kernels, per_device(): pl.pallas_call(functools.partial(qkv_kernel, tp), out_shape=[jax.ShapeDty...  3.91 us
    pallas_call x1, Pallas kernels, per_device(): pl.pallas_call(functools.partial(attend_kernel, tp, heads, 512, shares[1]...  2.92 us
    pallas_call x1, Pallas kernels, per_device(): pl.pallas_call(functools.partial(down_kernel, tp), out_shape=jax.ShapeDty...  2.07 us
  transfers between devices with their start and end apart: 15, of which 6 were waited for; matrix products, arithmetic and copies ran while one was open for 0% of the time, Pallas kernels for 12%

profile of v13, /device:TPU:0, one launch (start us, length us, event | category | flops | bytes accessed | tf_op | source)
XLA Modules:
  0.0 50.2 jit_solution(13916637161316892652)
XLA Ops:
  0.6 3.9 %qkv.1 = (f32[16,128]{1,0:T(8,128)S(1)}, f32[16,128]{1,0:T(8,128)S(1)}, f32[16,128]{1,0:T(8,128)S(1)}, f32[16,128]{1,0:T(8,128)S(1)}, f32[8,128]{1,0:T(8,128)S(1)}, /*index=5*/s32[8,128]{1,0:T(8,128)S(1)}) custom-call(s32[4]{0:T(128)} %owner_hbm.1, s32[4]{0:T(128)} %lengths_hbm.1, f32[1,128]{1,0:T(1,128)} %constant.2.clone.frequency_hbm, ...), custom_call_target="tpu_custom_call" | custom-call | bytes 29520000 | tf_op jit(solution)/shard_map/qkv/pallas_call | solution.py:372
  4.6 5.1 %collective-permute-start = (f32[16,128]{1,0:T(8,128)S(1)}, f32[16,128]{1,0:T(8,128)S(1)}, u32[]{:S(2)}, u32[]{:S(2)}) collective-permute-start(f32[16,128]{1,0:T(8,128)S(1)} %get-tuple-element.15), channel_id=1, source_target_pairs={{0,12},{4,8},{8,4},{12,0},{1,13},{5,9},{9,5},{13,1},{2,14},{6,10},... | collective-permute-start | bytes 24584 | tf_op jit(solution)/shard_map/ppermute | solution.py:41
  9.7 0.0 collective-permute-start.1
  9.7 0.6 %collective-permute-start.2 = (f32[16,128]{1,0:T(8,128)S(1)}, f32[16,128]{1,0:T(8,128)S(1)}, u32[]{:S(2)}, u32[]{:S(2)}) collective-permute-start(f32[16,128]{1,0:T(8,128)S(1)} %get-tuple-element.17), channel_id=1, source_target_pairs={{0,4},{4,0},{8,12},{12,8},{1,5},{5,1},{9,13},{13,9},{2,6},{6,2},{1... | collective-permute-start | bytes 24584 | tf_op jit(solution)/shard_map/ppermute | solution.py:41
  10.3 2.3 %fetch.3.rest_4_.rest_0_ = bf16[4096,512]{1,0:T(8,128)(2,1)S(1)} custom-call(f32[8,128]{1,0:T(8,128)S(1)} %get-tuple-element.14.token.table, bf16[2048,2,3584]{2,1,0:T(2,128)(2,1)} %w.9, bf16[8192,256]{1,0:T(8,128)(2,1)S(1)} %bitcast.4), custom_call_target="tpu_custom_call" | custom-call | bytes 4428000 | tf_op jit(solution)/shard_map/fetch/pallas_call | solution.py:408
  12.6 0.0 collective-permute-done.rest_0_
  12.6 1.6 %collective-permute-done.1.rest_1_ = f32[16,128]{1,0:T(8,128)S(1)} collective-permute-done((f32[16,128]{1,0:T(8,128)S(1)}, f32[16,128]{1,0:T(8,128)S(1)}, u32[]{:S(2)}, u32[]{:S(2)}) %collective-permute-start.1) | collective-permute-done | bytes 8224 | tf_op jit(solution)/shard_map/ppermute | solution.py:41
  14.2 2.9 %attend.1 = (bf16[8,128]{1,0:T(8,128)(2,1)S(1)}, bf16[1,256]{1,0:T(2,128)(2,1)}, bf16[4096,768]{1,0:T(8,128)(2,1)S(1)}) custom-call(f32[8,128]{1,0:T(8,128)S(1)} %get-tuple-element.14.token.table, bf16[8192,256]{1,0:T(8,128)(2,1)S(1)} %bitcast.5, bf16[2048,2,3584]{2,1,0:T(2,128)(2,1)} %w.9, f32[16,128]{1,0:T(8,128)S(1)} %collective-permute-done.rest_0_, ...), custom_call_target="tpu_custom_call" | custom-call | bytes 29520000 | tf_op jit(solution)/shard_map/attend/pallas_call | solution.py:421
  17.2 0.0 copy-start.1
  17.2 2.2 %collective-permute-start.5 = (bf16[8,128]{1,0:T(8,128)(2,1)S(1)}, bf16[8,128]{1,0:T(8,128)(2,1)S(1)}, u32[]{:S(2)}, u32[]{:S(2)}) collective-permute-start(bf16[8,128]{1,0:T(8,128)(2,1)S(1)} %get-tuple-element.20.token.rest_0_), channel_id=1, source_target_pairs={{0,12},{4,8},{8,4},{12,0},{1,13},{5,9},{9,5},{13,1},{2,14},{6,10},... | collective-permute-start | bytes 6152 | tf_op jit(solution)/shard_map/ppermute | solution.py:41
  19.4 2.2 %collective-permute-start.3 = (bf16[8,128]{1,0:T(8,128)(2,1)S(1)}, bf16[8,128]{1,0:T(8,128)(2,1)S(1)}, u32[]{:S(2)}, u32[]{:S(2)}) collective-permute-start(bf16[8,128]{1,0:T(8,128)(2,1)S(1)} %get-tuple-element.20.token.rest_0_), channel_id=1, source_target_pairs={{0,4},{4,0},{8,12},{12,8},{1,5},{5,1},{9,13},{13,9},{2,6},{6,2},{1... | collective-permute-start | bytes 6152 | tf_op jit(solution)/shard_map/ppermute | solution.py:41
  21.6 2.3 %fetch.4.rest_4_.rest_2_ = bf16[4096,512]{1,0:T(8,128)(2,1)S(1)} custom-call(bf16[8,128]{1,0:T(8,128)(2,1)S(1)} %get-tuple-element.20.token.rest_0_, bf16[2048,2,3584]{2,1,0:T(2,128)(2,1)} %w.9), custom_call_target="tpu_custom_call" | custom-call | bytes 4428000 | tf_op jit(solution)/shard_map/fetch/pallas_call | solution.py:408
  23.9 0.0 collective-permute-done.4.rest_2_
  24.0 0.7 %attn_project.1.token.rest_4_ = bf16[4,2048]{1,0:T(4,128)(2,1)S(1)} custom-call(s32[8,128]{1,0:T(8,128)S(1)} %get-tuple-element.21.places, bf16[1024,2048]{1,0:T(8,128)(2,1)S(1)} %copy-done.1, bf16[8,128]{1,0:T(8,128)(2,1)S(1)} %get-tuple-element.20.token.rest_0_, bf16[8,128]{1,0:T(8,128)(2,1)S(1)} %collective-permute-done.3.rest_1_, ...), custom_call_target="tpu_custom_call" | custom-call | bytes 22140000 | tf_op jit(solution)/shard_map/attn_project/pallas_call | solution.py:444
  24.6 0.0 collective-permute-start.8
  24.6 1.6 %collective-permute-start.7 = (bf16[4,2048]{1,0:T(4,128)(2,1)S(1)}, bf16[4,2048]{1,0:T(4,128)(2,1)S(1)}, u32[]{:S(2)}, u32[]{:S(2)}) collective-permute-start(bf16[4,2048]{1,0:T(4,128)(2,1)S(1)} %attn_project.1.token.rest_4_), channel_id=1, source_target_pairs={{0,2},{1,3},{2,0},{3,1},{4,6},{5,7},{6,4},{7,5},{8,10},{9,11},{10,... | collective-permute-start | bytes 49160 | tf_op jit(solution)/shard_map/ppermute | solution.py:41
  26.2 0.3 collective-permute-start.6
  26.5 1.6 %fetch.5.rest_3_ = bf16[4096,256]{1,0:T(8,128)(2,1)S(1)} custom-call(bf16[4,2048]{1,0:T(4,128)(2,1)S(1)} %attn_project.1.token.rest_4_, bf16[2048,2,3584]{2,1,0:T(2,128)(2,1)} %w.9), custom_call_target="tpu_custom_call" | custom-call | bytes 2214000 | tf_op jit(solution)/shard_map/fetch/pallas_call | solution.py:408
  28.1 0.3 collective-permute-done.7.rest_6_
  28.5 5.8 %gate_up.1 = (bf16[4,2048]{1,0:T(4,128)(2,1)}, bf16[8,3712]{1,0:T(8,128)(2,1)S(1)}) custom-call(bf16[4,2048]{1,0:T(4,128)(2,1)S(1)} %copy-done.2, f32[2,2048]{1,0:T(2,128)S(1)} %copy-done.3, bf16[2048,2,3584]{2,1,0:T(2,128)(2,1)} %w.9, bf16[4096,512]{1,0:T(8,128)(2,1)S(1)} %fetch.3.rest_4_.rest_0_, bf16[4096,768]{1,0:T(8,128)(2,1)S(1)} %get-tuple-element.19.rest_1_, ...), custom_call_target="tpu_custom_call" | custom-call | bytes 36900000 | tf_op jit(solution)/shard_map/gate_up/pallas_call | solution.py:457
  34.3 2.3 %collective-permute-start.11 = (bf16[8,3712]{1,0:T(8,128)(2,1)S(1)}, bf16[8,3712]{1,0:T(8,128)(2,1)S(1)}, u32[]{:S(2)}, u32[]{:S(2)}) collective-permute-start(bf16[8,3712]{1,0:T(8,128)(2,1)S(1)} %get-tuple-element.23.rest_0_), channel_id=1, source_target_pairs={{0,12},{4,8},{8,4},{12,0},{1,13},{5,9},{9,5},{13,1},{2,14},{6,10},... | collective-permute-start | bytes 178184 | tf_op jit(solution)/shard_map/ppermute | solution.py:41
  36.5 0.5 %collective-permute-start.10 = (bf16[8,3712]{1,0:T(8,128)(2,1)S(1)}, bf16[8,3712]{1,0:T(8,128)(2,1)S(1)}, u32[]{:S(2)}, u32[]{:S(2)}) collective-permute-start(bf16[8,3712]{1,0:T(8,128)(2,1)S(1)} %get-tuple-element.23.rest_0_), channel_id=1, source_target_pairs={{0,8},{4,12},{8,0},{12,4},{1,9},{5,13},{9,1},{13,5},{2,10},{6,14},... | collective-permute-start | bytes 178184 | tf_op jit(solution)/shard_map/ppermute | solution.py:41
  37.1 1.7 %collective-permute-start.9 = (bf16[8,3712]{1,0:T(8,128)(2,1)S(1)}, bf16[8,3712]{1,0:T(8,128)(2,1)S(1)}, u32[]{:S(2)}, u32[]{:S(2)}) collective-permute-start(bf16[8,3712]{1,0:T(8,128)(2,1)S(1)} %get-tuple-element.23.rest_0_), channel_id=1, source_target_pairs={{0,4},{4,0},{8,12},{12,8},{1,5},{5,1},{9,13},{13,9},{2,6},{6,2},{1... | collective-permute-start | bytes 178184 | tf_op jit(solution)/shard_map/ppermute | solution.py:41
  38.8 2.2 %collective-permute-done.11.rest_3_ = bf16[8,3712]{1,0:T(8,128)(2,1)S(1)} collective-permute-done((bf16[8,3712]{1,0:T(8,128)(2,1)S(1)}, bf16[8,3712]{1,0:T(8,128)(2,1)S(1)}, u32[]{:S(2)}, u32[]{:S(2)}) %collective-permute-start.11) | collective-permute-done | bytes 59424 | tf_op jit(solution)/shard_map/ppermute | solution.py:41
  41.0 2.1 %collective-permute-done.10.rest_2_ = bf16[8,3712]{1,0:T(8,128)(2,1)S(1)} collective-permute-done((bf16[8,3712]{1,0:T(8,128)(2,1)S(1)}, bf16[8,3712]{1,0:T(8,128)(2,1)S(1)}, u32[]{:S(2)}, u32[]{:S(2)}) %collective-permute-start.10) | collective-permute-done | bytes 59424 | tf_op jit(solution)/shard_map/ppermute | solution.py:41
  43.1 2.1 %down.1 = bf16[4,2048]{1,0:T(4,128)(2,1)S(1)} custom-call(bf16[3584,2048]{1,0:T(8,128)(2,1)S(1)} %bitcast.7, bf16[8,3712]{1,0:T(8,128)(2,1)S(1)} %get-tuple-element.23.rest_0_, bf16[8,3712]{1,0:T(8,128)(2,1)S(1)} %collective-permute-done.9.rest_1_, bf16[8,3712]{1,0:T(8,128)(2,1)S(1)} %collective-permute-done.10.rest_2_, ...), custom_call_target="tpu_custom_call" | custom-call | bytes 18450000 | tf_op jit(solution)/shard_map/down/pallas_call | solution.py:478
  45.2 0.6 %collective-permute-start.14 = (bf16[4,2048]{1,0:T(4,128)(2,1)S(1)}, bf16[4,2048]{1,0:T(4,128)(2,1)S(1)}, u32[]{:S(2)}, u32[]{:S(2)}) collective-permute-start(bf16[4,2048]{1,0:T(4,128)(2,1)S(1)} %down.1), channel_id=1, source_target_pairs={{0,3},{1,2},{2,1},{3,0},{4,7},{5,6},{6,5},{7,4},{8,11},{9,10},{10,... | collective-permute-start | bytes 49160 | tf_op jit(solution)/shard_map/ppermute | solution.py:41
  45.8 1.2 %collective-permute-start.13 = (bf16[4,2048]{1,0:T(4,128)(2,1)S(1)}, bf16[4,2048]{1,0:T(4,128)(2,1)S(1)}, u32[]{:S(2)}, u32[]{:S(2)}) collective-permute-start(bf16[4,2048]{1,0:T(4,128)(2,1)S(1)} %down.1), channel_id=1, source_target_pairs={{0,2},{1,3},{2,0},{3,1},{4,6},{5,7},{6,4},{7,5},{8,10},{9,11},{10,... | collective-permute-start | bytes 49160 | tf_op jit(solution)/shard_map/ppermute | solution.py:41
  47.0 0.1 collective-permute-start.12
  47.1 1.3 %collective-permute-done.14 = bf16[4,2048]{1,0:T(4,128)(2,1)S(1)} collective-permute-done((bf16[4,2048]{1,0:T(4,128)(2,1)S(1)}, bf16[4,2048]{1,0:T(4,128)(2,1)S(1)}, u32[]{:S(2)}, u32[]{:S(2)}) %collective-permute-start.14) | collective-permute-done | bytes 16416 | tf_op jit(solution)/shard_map/ppermute | solution.py:41
  48.4 1.2 %collective-permute-done.13 = bf16[4,2048]{1,0:T(4,128)(2,1)S(1)} collective-permute-done((bf16[4,2048]{1,0:T(4,128)(2,1)S(1)}, bf16[4,2048]{1,0:T(4,128)(2,1)S(1)}, u32[]{:S(2)}, u32[]{:S(2)}) %collective-permute-start.13) | collective-permute-done | bytes 16416 | tf_op jit(solution)/shard_map/ppermute | solution.py:41
  49.6 0.6 %add_convert_fusion = bf16[4,2048]{1,0:T(4,128)(2,1)} fusion(bf16[4,2048]{1,0:T(4,128)(2,1)S(1)} %collective-permute-done.14, bf16[4,2048]{1,0:T(4,128)(2,1)S(1)} %collective-permute-done.13, bf16[4,2048]{1,0:T(4,128)(2,1)S(1)} %collective-permute-done.12, bf16[4,2048]{1,0:T(4,128)(2,1)S(1)} %down.1), kind=kLoop, calls=%fused_computation | loop fusion | flops 65536 | bytes 81920 | tf_op jit(solution)/shard_map/convert_element_type | solution.py:488
  (24 shorter events, 0.1 us)
Async XLA Ops:
  0.6 9.7 %copy-start = (bf16[1,8192,1,256]{3,1,2,0:T(8,128)(2,1)S(1)}, bf16[1,8192,1,256]{3,1,2,0:T(8,128)(2,1)}, u32[]{:S(2)}) copy-start(bf16[1,8192,1,256]{3,1,2,0:T(8,128)(2,1)} %param.18) | copy-start | bytes 12582916
  4.6 8.1 %collective-permute-start = (f32[16,128]{1,0:T(8,128)S(1)}, f32[16,128]{1,0:T(8,128)S(1)}, u32[]{:S(2)}, u32[]{:S(2)}) collective-permute-start(f32[16,128]{1,0:T(8,128)S(1)} %get-tuple-element.15), channel_id=1, source_target_pairs={{0,12},{4,8},{8,4},{12,0},{1,13},{5,9},{9,5},{13,1},{2,14},{6,10},... | collective-permute-start | bytes 24584 | tf_op jit(solution)/shard_map/ppermute | solution.py:41
  9.7 4.5 %collective-permute-start.1 = (f32[16,128]{1,0:T(8,128)S(1)}, f32[16,128]{1,0:T(8,128)S(1)}, u32[]{:S(2)}, u32[]{:S(2)}) collective-permute-start(f32[16,128]{1,0:T(8,128)S(1)} %get-tuple-element.16), channel_id=1, source_target_pairs={{0,8},{4,12},{8,0},{12,4},{1,9},{5,13},{9,1},{13,5},{2,10},{6,14},... | collective-permute-start | bytes 24584 | tf_op jit(solution)/shard_map/ppermute | solution.py:41
  9.7 4.5 %collective-permute-start.2 = (f32[16,128]{1,0:T(8,128)S(1)}, f32[16,128]{1,0:T(8,128)S(1)}, u32[]{:S(2)}, u32[]{:S(2)}) collective-permute-start(f32[16,128]{1,0:T(8,128)S(1)} %get-tuple-element.17), channel_id=1, source_target_pairs={{0,4},{4,0},{8,12},{12,8},{1,5},{5,1},{9,13},{13,9},{2,6},{6,2},{1... | collective-permute-start | bytes 24584 | tf_op jit(solution)/shard_map/ppermute | solution.py:41
  17.2 6.8 %copy-start.1 = (bf16[1024,2048]{1,0:T(8,128)(2,1)S(1)}, bf16[1024,2048]{1,0:T(8,128)(2,1)}, u32[]{:S(2)}) copy-start(bf16[1024,2048]{1,0:T(8,128)(2,1)} %w_out.1) | copy-start | bytes 12582916
  17.2 6.8 %collective-permute-start.5 = (bf16[8,128]{1,0:T(8,128)(2,1)S(1)}, bf16[8,128]{1,0:T(8,128)(2,1)S(1)}, u32[]{:S(2)}, u32[]{:S(2)}) collective-permute-start(bf16[8,128]{1,0:T(8,128)(2,1)S(1)} %get-tuple-element.20.token.rest_0_), channel_id=1, source_target_pairs={{0,12},{4,8},{8,4},{12,0},{1,13},{5,9},{9,5},{13,1},{2,14},{6,10},... | collective-permute-start | bytes 6152 | tf_op jit(solution)/shard_map/ppermute | solution.py:41
  19.4 4.5 %collective-permute-start.4 = (bf16[8,128]{1,0:T(8,128)(2,1)S(1)}, bf16[8,128]{1,0:T(8,128)(2,1)S(1)}, u32[]{:S(2)}, u32[]{:S(2)}) collective-permute-start(bf16[8,128]{1,0:T(8,128)(2,1)S(1)} %get-tuple-element.20.token.rest_0_), channel_id=1, source_target_pairs={{0,8},{4,12},{8,0},{12,4},{1,9},{5,13},{9,1},{13,5},{2,10},{6,14},... | collective-permute-start | bytes 6152 | tf_op jit(solution)/shard_map/ppermute | solution.py:41
  19.4 4.5 %collective-permute-start.3 = (bf16[8,128]{1,0:T(8,128)(2,1)S(1)}, bf16[8,128]{1,0:T(8,128)(2,1)S(1)}, u32[]{:S(2)}, u32[]{:S(2)}) collective-permute-start(bf16[8,128]{1,0:T(8,128)(2,1)S(1)} %get-tuple-element.20.token.rest_0_), channel_id=1, source_target_pairs={{0,4},{4,0},{8,12},{12,8},{1,5},{5,1},{9,13},{13,9},{2,6},{6,2},{1... | collective-permute-start | bytes 6152 | tf_op jit(solution)/shard_map/ppermute | solution.py:41
  24.6 3.8 %copy-start.2 = (bf16[4,2048]{1,0:T(4,128)(2,1)S(1)}, bf16[4,2048]{1,0:T(4,128)(2,1)}, u32[]{:S(2)}) copy-start(bf16[4,2048]{1,0:T(4,128)(2,1)} %states.1) | copy-start | bytes 49156
  24.6 3.8 %copy-start.3 = (f32[2,2048]{1,0:T(2,128)S(1)}, f32[2,2048]{1,0:T(2,128)}, u32[]{:S(2)}) copy-start(f32[2,2048]{1,0:T(2,128)} %gains.1) | copy-start | bytes 49156
  24.6 3.5 %collective-permute-start.8 = (bf16[4,2048]{1,0:T(4,128)(2,1)S(1)}, bf16[4,2048]{1,0:T(4,128)(2,1)S(1)}, u32[]{:S(2)}, u32[]{:S(2)}) collective-permute-start(bf16[4,2048]{1,0:T(4,128)(2,1)S(1)} %attn_project.1.token.rest_4_), channel_id=1, source_target_pairs={{0,3},{1,2},{2,1},{3,0},{4,7},{5,6},{6,5},{7,4},{8,11},{9,10},{10,... | collective-permute-start | bytes 49160 | tf_op jit(solution)/shard_map/ppermute | solution.py:41
  24.6 3.8 %collective-permute-start.7 = (bf16[4,2048]{1,0:T(4,128)(2,1)S(1)}, bf16[4,2048]{1,0:T(4,128)(2,1)S(1)}, u32[]{:S(2)}, u32[]{:S(2)}) collective-permute-start(bf16[4,2048]{1,0:T(4,128)(2,1)S(1)} %attn_project.1.token.rest_4_), channel_id=1, source_target_pairs={{0,2},{1,3},{2,0},{3,1},{4,6},{5,7},{6,4},{7,5},{8,10},{9,11},{10,... | collective-permute-start | bytes 49160 | tf_op jit(solution)/shard_map/ppermute | solution.py:41
  26.2 2.3 %collective-permute-start.6 = (bf16[4,2048]{1,0:T(4,128)(2,1)S(1)}, bf16[4,2048]{1,0:T(4,128)(2,1)S(1)}, u32[]{:S(2)}, u32[]{:S(2)}) collective-permute-start(bf16[4,2048]{1,0:T(4,128)(2,1)S(1)} %attn_project.1.token.rest_4_), channel_id=1, source_target_pairs={{0,1},{1,0},{2,3},{3,2},{4,5},{5,4},{6,7},{7,6},{8,9},{9,8},{10,11... | collective-permute-start | bytes 49160 | tf_op jit(solution)/shard_map/ppermute | solution.py:41
  28.5 14.6 %slice-start = ((s8[14680064]{0:T(1024)(128)(4,1)}), s8[4194304]{0:T(1024)(128)(4,1)S(1)}, s32[]{:S(2)}) async-start(s8[14680064]{0:T(1024)(128)(4,1)} %bitcast.6), calls=%async_computation | async-start | bytes 8388608
  28.5 14.6 %slice-start.1 = ((s8[14680064]{0:T(1024)(128)(4,1)}), s8[4194304]{0:T(1024)(128)(4,1)S(1)}, s32[]{:S(2)}) async-start(s8[14680064]{0:T(1024)(128)(4,1)} %bitcast.6), calls=%async_computation.1 | async-start | bytes 8388608
  28.5 14.6 %slice-start.2 = ((s8[14680064]{0:T(1024)(128)(4,1)}), s8[4194304]{0:T(1024)(128)(4,1)S(1)}, s32[]{:S(2)}) async-start(s8[14680064]{0:T(1024)(128)(4,1)} %bitcast.6), calls=%async_computation.2 | async-start | bytes 8388608
  28.5 14.6 %slice-start.3 = ((s8[14680064]{0:T(1024)(128)(4,1)}), s8[2097152]{0:T(1024)(128)(4,1)S(1)}, s32[]{:S(2)}) async-start(s8[14680064]{0:T(1024)(128)(4,1)} %bitcast.6), calls=%async_computation.3 | async-start | bytes 4194304
  34.3 6.7 %collective-permute-start.11 = (bf16[8,3712]{1,0:T(8,128)(2,1)S(1)}, bf16[8,3712]{1,0:T(8,128)(2,1)S(1)}, u32[]{:S(2)}, u32[]{:S(2)}) collective-permute-start(bf16[8,3712]{1,0:T(8,128)(2,1)S(1)} %get-tuple-element.23.rest_0_), channel_id=1, source_target_pairs={{0,12},{4,8},{8,4},{12,0},{1,13},{5,9},{9,5},{13,1},{2,14},{6,10},... | collective-permute-start | bytes 178184 | tf_op jit(solution)/shard_map/ppermute | solution.py:41
  36.5 6.5 %collective-permute-start.10 = (bf16[8,3712]{1,0:T(8,128)(2,1)S(1)}, bf16[8,3712]{1,0:T(8,128)(2,1)S(1)}, u32[]{:S(2)}, u32[]{:S(2)}) collective-permute-start(bf16[8,3712]{1,0:T(8,128)(2,1)S(1)} %get-tuple-element.23.rest_0_), channel_id=1, source_target_pairs={{0,8},{4,12},{8,0},{12,4},{1,9},{5,13},{9,1},{13,5},{2,10},{6,14},... | collective-permute-start | bytes 178184 | tf_op jit(solution)/shard_map/ppermute | solution.py:41
  37.1 6.0 %collective-permute-start.9 = (bf16[8,3712]{1,0:T(8,128)(2,1)S(1)}, bf16[8,3712]{1,0:T(8,128)(2,1)S(1)}, u32[]{:S(2)}, u32[]{:S(2)}) collective-permute-start(bf16[8,3712]{1,0:T(8,128)(2,1)S(1)} %get-tuple-element.23.rest_0_), channel_id=1, source_target_pairs={{0,4},{4,0},{8,12},{12,8},{1,5},{5,1},{9,13},{13,9},{2,6},{6,2},{1... | collective-permute-start | bytes 178184 | tf_op jit(solution)/shard_map/ppermute | solution.py:41
  45.2 3.2 %collective-permute-start.14 = (bf16[4,2048]{1,0:T(4,128)(2,1)S(1)}, bf16[4,2048]{1,0:T(4,128)(2,1)S(1)}, u32[]{:S(2)}, u32[]{:S(2)}) collective-permute-start(bf16[4,2048]{1,0:T(4,128)(2,1)S(1)} %down.1), channel_id=1, source_target_pairs={{0,3},{1,2},{2,1},{3,0},{4,7},{5,6},{6,5},{7,4},{8,11},{9,10},{10,... | collective-permute-start | bytes 49160 | tf_op jit(solution)/shard_map/ppermute | solution.py:41
  45.8 3.8 %collective-permute-start.13 = (bf16[4,2048]{1,0:T(4,128)(2,1)S(1)}, bf16[4,2048]{1,0:T(4,128)(2,1)S(1)}, u32[]{:S(2)}, u32[]{:S(2)}) collective-permute-start(bf16[4,2048]{1,0:T(4,128)(2,1)S(1)} %down.1), channel_id=1, source_target_pairs={{0,2},{1,3},{2,0},{3,1},{4,6},{5,7},{6,4},{7,5},{8,10},{9,11},{10,... | collective-permute-start | bytes 49160 | tf_op jit(solution)/shard_map/ppermute | solution.py:41
  47.0 2.6 %collective-permute-start.12 = (bf16[4,2048]{1,0:T(4,128)(2,1)S(1)}, bf16[4,2048]{1,0:T(4,128)(2,1)S(1)}, u32[]{:S(2)}, u32[]{:S(2)}) collective-permute-start(bf16[4,2048]{1,0:T(4,128)(2,1)S(1)} %down.1), channel_id=1, source_target_pairs={{0,1},{1,0},{2,3},{3,2},{4,5},{5,4},{6,7},{7,6},{8,9},{9,8},{10,11... | collective-permute-start | bytes 49160 | tf_op jit(solution)/shard_map/ppermute | solution.py:41

commit v14 on v13

--- a/solution.py
+++ b/solution.py
@@ -68,6 +68,11 @@
     for c in range(chunks):
         piece = doubled[c * 4 * docs : (c + 1) * 4 * docs]
         out_ref[:, 2 * c * LANES : 2 * (c + 1) * LANES] = jnp.where(keep, piece, 0.0).astype(BF16)
+
+
+def start_all(copies):
+    for i, copy in enumerate(copies):
+        copy.start(priority=i % 2)
 
 
 def matrix_of(w):
@@ -164,8 +169,9 @@
         for c in range(parts)
     ]
     kv_copy = pltpu.make_async_copy(wkv, wkv_buf, sems.at[parts])
-    for copy in small + [kv_copy] + copies:
+    for copy in small:
         copy.start()
+    start_all([kv_copy] + copies)
     for copy in small:
         copy.wait()
     me = lax.axis_index("tp")
@@ -205,8 +211,7 @@
     parts = rest[:tp]
     heads_out, new_kv_out, w_ready, scores, new_kv, w_sems, out_sem = rest[-7:]
     w_copies = block_copies(matrix_of(w), first, w_ready, w_sems)
-    for copy in w_copies:
-        copy.start()
+    start_all(w_copies)
     blocks = cache.shape[0] // rows
     sums = tree_sum([part[...] for part in parts])
     sums = sums * lax.rsqrt(sums[heads + 2 : heads + 3, :] / D + EPS)
@@ -276,8 +281,7 @@
 def fetch_kernel(first, token, w, *rest):
     out, sems = rest[-2:]
     copies = block_copies(matrix_of(w), first, out, sems)
-    for copy in copies:
-        copy.start()
+    start_all(copies)
     for copy in copies:
         copy.wait()
 
@@ -292,8 +296,7 @@
     for i, block in enumerate(blocks):
         copies.append(block_copies(w_matrix, first, block, w_sems.at[i]))
         first += block.shape[1] // LANES
-        for copy in copies[-1]:
-            copy.start()
+        start_all(copies[-1])
     attn = tree_sum([part[...].astype(F32) for part in parts]).astype(BF16)
     attn_buf[...] = attn
     out_copy = pltpu.make_async_copy(attn_buf, attn_out, out_sem.at[0])
@@ -303,6 +306,12 @@
     high, low = two_parts(resid * gains[1:2, :])
     spread(jnp.concatenate([high, high, low, low], axis=0).astype(BF16), spread_buf, docs)
 
+    lane = lax.broadcasted_iota(jnp.int32, (docs, LANES), 1)
+    first = squares.astype(BF16).astype(F32)
+    second = (squares - first).astype(BF16).astype(F32)
+    third = squares - first - second
+    terms = jnp.where(lane == 0, first, jnp.where(lane == 1, second, jnp.where(lane == 2, third, 0.0)))
+    partial_out[:, hidden:] = jnp.concatenate([terms, terms], axis=0).astype(BF16)
     at = 0
     for i, block in enumerate([*ready, *blocks]):
         if i >= groups:
@@ -312,12 +321,6 @@
         columns = slice(at, at + block.shape[1])
         partial_out[:, columns] = (product[: 2 * docs] + product[2 * docs :]).astype(BF16)
         at += block.shape[1]
-    lane = lax.broadcasted_iota(jnp.int32, (docs, LANES), 1)
-    first = squares.astype(BF16).astype(F32)
-    second = (squares - first).astype(BF16).astype(F32)
-    third = squares - first - second
-    terms = jnp.where(lane == 0, first, jnp.where(lane == 1, second, jnp.where(lane == 2, third, 0.0)))
-    partial_out[:, hidden:] = jnp.concatenate([terms, terms], axis=0).astype(BF16)
     out_copy.wait()
 
 

time: 50.4 us -> 50.1 us (level)
  no operation moved by 1% of the time
where the time goes in v14:
time: 50.1 us; the launch traced here: 50 us
  Pallas kernels  21.3 us (43%)
  starting transfers between devices  18.5 us (37%)
  waiting for transfers between devices  8.75 us (17%)
  between operations  0.83 us (2%)
  other arithmetic  0.63 us (1%)
    ppermute x15, starting transfers between devices, exchange(): lax.ppermute(arrays[s], axis, [(i, i ^ s) for i in range(size)])  18.5 us
    ppermute x15, waiting for transfers between devices, exchange(): lax.ppermute(arrays[s], axis, [(i, i ^ s) for i in range(size)])  8.75 us
    pallas_call x3, Pallas kernels, fetch(): pl.pallas_call(functools.partial(fetch_kernel, share[0]), out_shape=block...  6.18 us
    pallas_call x1, Pallas kernels, per_device(): pl.pallas_call(functools.partial(gate_up_kernel, kv, len(fetched), shares...  5.77 us
    pallas_call x1, Pallas kernels, per_device(): pl.pallas_call(functools.partial(qkv_kernel, tp), out_shape=[jax.ShapeDty...  3.7 us
    pallas_call x1, Pallas kernels, per_device(): pl.pallas_call(functools.partial(attend_kernel, tp, heads, 512, shares[1]...  2.92 us
    pallas_call x1, Pallas kernels, per_device(): pl.pallas_call(functools.partial(down_kernel, tp), out_shape=jax.ShapeDty...  2.07 us
  transfers between devices with their start and end apart: 15, of which 6 were waited for; matrix products, arithmetic and copies ran while one was open for 0% of the time, Pallas kernels for 12%

profile of v14, /device:TPU:0, one launch (start us, length us, event | category | flops | bytes accessed | tf_op | source)
XLA Modules:
  0.0 50.0 jit_solution(14776490713788334526)
XLA Ops:
  0.6 3.7 %qkv.1 = (f32[16,128]{1,0:T(8,128)S(1)}, f32[16,128]{1,0:T(8,128)S(1)}, f32[16,128]{1,0:T(8,128)S(1)}, f32[16,128]{1,0:T(8,128)S(1)}, f32[8,128]{1,0:T(8,128)S(1)}, /*index=5*/s32[8,128]{1,0:T(8,128)S(1)}) custom-call(s32[4]{0:T(128)} %owner_hbm.1, s32[4]{0:T(128)} %lengths_hbm.1, f32[1,128]{1,0:T(1,128)} %constant.2.clone.frequency_hbm, ...), custom_call_target="tpu_custom_call" | custom-call | bytes 29520000 | tf_op jit(solution)/shard_map/qkv/pallas_call | solution.py:375
  4.3 5.1 %collective-permute-start = (f32[16,128]{1,0:T(8,128)S(1)}, f32[16,128]{1,0:T(8,128)S(1)}, u32[]{:S(2)}, u32[]{:S(2)}) collective-permute-start(f32[16,128]{1,0:T(8,128)S(1)} %get-tuple-element.15), channel_id=1, source_target_pairs={{0,12},{4,8},{8,4},{12,0},{1,13},{5,9},{9,5},{13,1},{2,14},{6,10},... | collective-permute-start | bytes 24584 | tf_op jit(solution)/shard_map/ppermute | solution.py:41
  9.5 0.0 collective-permute-start.1
  9.5 0.6 %collective-permute-start.2 = (f32[16,128]{1,0:T(8,128)S(1)}, f32[16,128]{1,0:T(8,128)S(1)}, u32[]{:S(2)}, u32[]{:S(2)}) collective-permute-start(f32[16,128]{1,0:T(8,128)S(1)} %get-tuple-element.17), channel_id=1, source_target_pairs={{0,4},{4,0},{8,12},{12,8},{1,5},{5,1},{9,13},{13,9},{2,6},{6,2},{1... | collective-permute-start | bytes 24584 | tf_op jit(solution)/shard_map/ppermute | solution.py:41
  10.1 2.3 %fetch.3.rest_4_.rest_0_ = bf16[4096,512]{1,0:T(8,128)(2,1)S(1)} custom-call(f32[8,128]{1,0:T(8,128)S(1)} %get-tuple-element.14.token.table, bf16[2048,2,3584]{2,1,0:T(2,128)(2,1)} %w.9, bf16[8192,256]{1,0:T(8,128)(2,1)S(1)} %bitcast.4), custom_call_target="tpu_custom_call" | custom-call | bytes 4428000 | tf_op jit(solution)/shard_map/fetch/pallas_call | solution.py:411
  12.4 1.6 %collective-permute-done.1.rest_1_ = f32[16,128]{1,0:T(8,128)S(1)} collective-permute-done((f32[16,128]{1,0:T(8,128)S(1)}, f32[16,128]{1,0:T(8,128)S(1)}, u32[]{:S(2)}, u32[]{:S(2)}) %collective-permute-start.1) | collective-permute-done | bytes 8224 | tf_op jit(solution)/shard_map/ppermute | solution.py:41
  14.0 0.0 collective-permute-done.2.rest_2_
  14.0 2.9 %attend.1 = (bf16[8,128]{1,0:T(8,128)(2,1)S(1)}, bf16[1,256]{1,0:T(2,128)(2,1)}, bf16[4096,768]{1,0:T(8,128)(2,1)S(1)}) custom-call(f32[8,128]{1,0:T(8,128)S(1)} %get-tuple-element.14.token.table, bf16[8192,256]{1,0:T(8,128)(2,1)S(1)} %bitcast.5, bf16[2048,2,3584]{2,1,0:T(2,128)(2,1)} %w.9, f32[16,128]{1,0:T(8,128)S(1)} %collective-permute-done.rest_0_, ...), custom_call_target="tpu_custom_call" | custom-call | bytes 29520000 | tf_op jit(solution)/shard_map/attend/pallas_call | solution.py:424
  16.9 0.0 copy-start.1
  17.0 2.2 %collective-permute-start.5 = (bf16[8,128]{1,0:T(8,128)(2,1)S(1)}, bf16[8,128]{1,0:T(8,128)(2,1)S(1)}, u32[]{:S(2)}, u32[]{:S(2)}) collective-permute-start(bf16[8,128]{1,0:T(8,128)(2,1)S(1)} %get-tuple-element.20.token.rest_0_), channel_id=1, source_target_pairs={{0,12},{4,8},{8,4},{12,0},{1,13},{5,9},{9,5},{13,1},{2,14},{6,10},... | collective-permute-start | bytes 6152 | tf_op jit(solution)/shard_map/ppermute | solution.py:41
  19.2 0.0 collective-permute-start.4
  19.2 2.2 %collective-permute-start.3 = (bf16[8,128]{1,0:T(8,128)(2,1)S(1)}, bf16[8,128]{1,0:T(8,128)(2,1)S(1)}, u32[]{:S(2)}, u32[]{:S(2)}) collective-permute-start(bf16[8,128]{1,0:T(8,128)(2,1)S(1)} %get-tuple-element.20.token.rest_0_), channel_id=1, source_target_pairs={{0,4},{4,0},{8,12},{12,8},{1,5},{5,1},{9,13},{13,9},{2,6},{6,2},{1... | collective-permute-start | bytes 6152 | tf_op jit(solution)/shard_map/ppermute | solution.py:41
  21.4 2.3 %fetch.4.rest_4_.rest_2_ = bf16[4096,512]{1,0:T(8,128)(2,1)S(1)} custom-call(bf16[8,128]{1,0:T(8,128)(2,1)S(1)} %get-tuple-element.20.token.rest_0_, bf16[2048,2,3584]{2,1,0:T(2,128)(2,1)} %w.9), custom_call_target="tpu_custom_call" | custom-call | bytes 4428000 | tf_op jit(solution)/shard_map/fetch/pallas_call | solution.py:411
  23.7 0.7 %attn_project.1.token.rest_4_ = bf16[4,2048]{1,0:T(4,128)(2,1)S(1)} custom-call(s32[8,128]{1,0:T(8,128)S(1)} %get-tuple-element.21.places, bf16[1024,2048]{1,0:T(8,128)(2,1)S(1)} %copy-done.1, bf16[8,128]{1,0:T(8,128)(2,1)S(1)} %get-tuple-element.20.token.rest_0_, bf16[8,128]{1,0:T(8,128)(2,1)S(1)} %collective-permute-done.3.rest_1_, ...), custom_call_target="tpu_custom_call" | custom-call | bytes 22140000 | tf_op jit(solution)/shard_map/attn_project/pallas_call | solution.py:447
  24.4 0.0 collective-permute-start.8
  24.4 1.6 %collective-permute-start.7 = (bf16[4,2048]{1,0:T(4,128)(2,1)S(1)}, bf16[4,2048]{1,0:T(4,128)(2,1)S(1)}, u32[]{:S(2)}, u32[]{:S(2)}) collective-permute-start(bf16[4,2048]{1,0:T(4,128)(2,1)S(1)} %attn_project.1.token.rest_4_), channel_id=1, source_target_pairs={{0,2},{1,3},{2,0},{3,1},{4,6},{5,7},{6,4},{7,5},{8,10},{9,11},{10,... | collective-permute-start | bytes 49160 | tf_op jit(solution)/shard_map/ppermute | solution.py:41
  26.0 0.3 collective-permute-start.6
  26.3 1.6 %fetch.5.rest_3_ = bf16[4096,256]{1,0:T(8,128)(2,1)S(1)} custom-call(bf16[4,2048]{1,0:T(4,128)(2,1)S(1)} %attn_project.1.token.rest_4_, bf16[2048,2,3584]{2,1,0:T(2,128)(2,1)} %w.9), custom_call_target="tpu_custom_call" | custom-call | bytes 2214000 | tf_op jit(solution)/shard_map/fetch/pallas_call | solution.py:411
  27.9 0.3 collective-permute-done.7.rest_6_
  28.3 5.8 %gate_up.1 = (bf16[4,2048]{1,0:T(4,128)(2,1)}, bf16[8,3712]{1,0:T(8,128)(2,1)S(1)}) custom-call(bf16[4,2048]{1,0:T(4,128)(2,1)S(1)} %copy-done.2, f32[2,2048]{1,0:T(2,128)S(1)} %copy-done.3, bf16[2048,2,3584]{2,1,0:T(2,128)(2,1)} %w.9, bf16[4096,512]{1,0:T(8,128)(2,1)S(1)} %fetch.3.rest_4_.rest_0_, bf16[4096,768]{1,0:T(8,128)(2,1)S(1)} %get-tuple-element.19.rest_1_, ...), custom_call_target="tpu_custom_call" | custom-call | bytes 36900000 | tf_op jit(solution)/shard_map/gate_up/pallas_call | solution.py:460
  34.1 2.3 %collective-permute-start.11 = (bf16[8,3712]{1,0:T(8,128)(2,1)S(1)}, bf16[8,3712]{1,0:T(8,128)(2,1)S(1)}, u32[]{:S(2)}, u32[]{:S(2)}) collective-permute-start(bf16[8,3712]{1,0:T(8,128)(2,1)S(1)} %get-tuple-element.23.rest_0_), channel_id=1, source_target_pairs={{0,12},{4,8},{8,4},{12,0},{1,13},{5,9},{9,5},{13,1},{2,14},{6,10},... | collective-permute-start | bytes 178184 | tf_op jit(solution)/shard_map/ppermute | solution.py:41
  36.3 0.5 %collective-permute-start.10 = (bf16[8,3712]{1,0:T(8,128)(2,1)S(1)}, bf16[8,3712]{1,0:T(8,128)(2,1)S(1)}, u32[]{:S(2)}, u32[]{:S(2)}) collective-permute-start(bf16[8,3712]{1,0:T(8,128)(2,1)S(1)} %get-tuple-element.23.rest_0_), channel_id=1, source_target_pairs={{0,8},{4,12},{8,0},{12,4},{1,9},{5,13},{9,1},{13,5},{2,10},{6,14},... | collective-permute-start | bytes 178184 | tf_op jit(solution)/shard_map/ppermute | solution.py:41
  36.9 1.7 %collective-permute-start.9 = (bf16[8,3712]{1,0:T(8,128)(2,1)S(1)}, bf16[8,3712]{1,0:T(8,128)(2,1)S(1)}, u32[]{:S(2)}, u32[]{:S(2)}) collective-permute-start(bf16[8,3712]{1,0:T(8,128)(2,1)S(1)} %get-tuple-element.23.rest_0_), channel_id=1, source_target_pairs={{0,4},{4,0},{8,12},{12,8},{1,5},{5,1},{9,13},{13,9},{2,6},{6,2},{1... | collective-permute-start | bytes 178184 | tf_op jit(solution)/shard_map/ppermute | solution.py:41
  38.5 2.2 %collective-permute-done.11.rest_3_ = bf16[8,3712]{1,0:T(8,128)(2,1)S(1)} collective-permute-done((bf16[8,3712]{1,0:T(8,128)(2,1)S(1)}, bf16[8,3712]{1,0:T(8,128)(2,1)S(1)}, u32[]{:S(2)}, u32[]{:S(2)}) %collective-permute-start.11) | collective-permute-done | bytes 59424 | tf_op jit(solution)/shard_map/ppermute | solution.py:41
  40.8 2.1 %collective-permute-done.10.rest_2_ = bf16[8,3712]{1,0:T(8,128)(2,1)S(1)} collective-permute-done((bf16[8,3712]{1,0:T(8,128)(2,1)S(1)}, bf16[8,3712]{1,0:T(8,128)(2,1)S(1)}, u32[]{:S(2)}, u32[]{:S(2)}) %collective-permute-start.10) | collective-permute-done | bytes 59424 | tf_op jit(solution)/shard_map/ppermute | solution.py:41
  42.9 2.1 %down.1 = bf16[4,2048]{1,0:T(4,128)(2,1)S(1)} custom-call(bf16[3584,2048]{1,0:T(8,128)(2,1)S(1)} %bitcast.7, bf16[8,3712]{1,0:T(8,128)(2,1)S(1)} %get-tuple-element.23.rest_0_, bf16[8,3712]{1,0:T(8,128)(2,1)S(1)} %collective-permute-done.9.rest_1_, bf16[8,3712]{1,0:T(8,128)(2,1)S(1)} %collective-permute-done.10.rest_2_, ...), custom_call_target="tpu_custom_call" | custom-call | bytes 18450000 | tf_op jit(solution)/shard_map/down/pallas_call | solution.py:481
  45.0 0.6 %collective-permute-start.14 = (bf16[4,2048]{1,0:T(4,128)(2,1)S(1)}, bf16[4,2048]{1,0:T(4,128)(2,1)S(1)}, u32[]{:S(2)}, u32[]{:S(2)}) collective-permute-start(bf16[4,2048]{1,0:T(4,128)(2,1)S(1)} %down.1), channel_id=1, source_target_pairs={{0,3},{1,2},{2,1},{3,0},{4,7},{5,6},{6,5},{7,4},{8,11},{9,10},{10,... | collective-permute-start | bytes 49160 | tf_op jit(solution)/shard_map/ppermute | solution.py:41
  45.5 1.2 %collective-permute-start.13 = (bf16[4,2048]{1,0:T(4,128)(2,1)S(1)}, bf16[4,2048]{1,0:T(4,128)(2,1)S(1)}, u32[]{:S(2)}, u32[]{:S(2)}) collective-permute-start(bf16[4,2048]{1,0:T(4,128)(2,1)S(1)} %down.1), channel_id=1, source_target_pairs={{0,2},{1,3},{2,0},{3,1},{4,6},{5,7},{6,4},{7,5},{8,10},{9,11},{10,... | collective-permute-start | bytes 49160 | tf_op jit(solution)/shard_map/ppermute | solution.py:41
  46.7 0.1 collective-permute-start.12
  46.9 1.3 %collective-permute-done.14 = bf16[4,2048]{1,0:T(4,128)(2,1)S(1)} collective-permute-done((bf16[4,2048]{1,0:T(4,128)(2,1)S(1)}, bf16[4,2048]{1,0:T(4,128)(2,1)S(1)}, u32[]{:S(2)}, u32[]{:S(2)}) %collective-permute-start.14) | collective-permute-done | bytes 16416 | tf_op jit(solution)/shard_map/ppermute | solution.py:41
  48.2 1.2 %collective-permute-done.13 = bf16[4,2048]{1,0:T(4,128)(2,1)S(1)} collective-permute-done((bf16[4,2048]{1,0:T(4,128)(2,1)S(1)}, bf16[4,2048]{1,0:T(4,128)(2,1)S(1)}, u32[]{:S(2)}, u32[]{:S(2)}) %collective-permute-start.13) | collective-permute-done | bytes 16416 | tf_op jit(solution)/shard_map/ppermute | solution.py:41
  49.4 0.6 %add_convert_fusion = bf16[4,2048]{1,0:T(4,128)(2,1)} fusion(bf16[4,2048]{1,0:T(4,128)(2,1)S(1)} %collective-permute-done.14, bf16[4,2048]{1,0:T(4,128)(2,1)S(1)} %collective-permute-done.13, bf16[4,2048]{1,0:T(4,128)(2,1)S(1)} %collective-permute-done.12, bf16[4,2048]{1,0:T(4,128)(2,1)S(1)} %down.1), kind=kLoop, calls=%fused_computation | loop fusion | flops 65536 | bytes 81920 | tf_op jit(solution)/shard_map/convert_element_type | solution.py:491
  (24 shorter events, 0.1 us)
Async XLA Ops:
  0.6 9.5 %copy-start = (bf16[1,8192,1,256]{3,1,2,0:T(8,128)(2,1)S(1)}, bf16[1,8192,1,256]{3,1,2,0:T(8,128)(2,1)}, u32[]{:S(2)}) copy-start(bf16[1,8192,1,256]{3,1,2,0:T(8,128)(2,1)} %param.18) | copy-start | bytes 12582916
  4.3 8.1 %collective-permute-start = (f32[16,128]{1,0:T(8,128)S(1)}, f32[16,128]{1,0:T(8,128)S(1)}, u32[]{:S(2)}, u32[]{:S(2)}) collective-permute-start(f32[16,128]{1,0:T(8,128)S(1)} %get-tuple-element.15), channel_id=1, source_target_pairs={{0,12},{4,8},{8,4},{12,0},{1,13},{5,9},{9,5},{13,1},{2,14},{6,10},... | collective-permute-start | bytes 24584 | tf_op jit(solution)/shard_map/ppermute | solution.py:41
  9.5 4.5 %collective-permute-start.1 = (f32[16,128]{1,0:T(8,128)S(1)}, f32[16,128]{1,0:T(8,128)S(1)}, u32[]{:S(2)}, u32[]{:S(2)}) collective-permute-start(f32[16,128]{1,0:T(8,128)S(1)} %get-tuple-element.16), channel_id=1, source_target_pairs={{0,8},{4,12},{8,0},{12,4},{1,9},{5,13},{9,1},{13,5},{2,10},{6,14},... | collective-permute-start | bytes 24584 | tf_op jit(solution)/shard_map/ppermute | solution.py:41
  9.5 4.5 %collective-permute-start.2 = (f32[16,128]{1,0:T(8,128)S(1)}, f32[16,128]{1,0:T(8,128)S(1)}, u32[]{:S(2)}, u32[]{:S(2)}) collective-permute-start(f32[16,128]{1,0:T(8,128)S(1)} %get-tuple-element.17), channel_id=1, source_target_pairs={{0,4},{4,0},{8,12},{12,8},{1,5},{5,1},{9,13},{13,9},{2,6},{6,2},{1... | collective-permute-start | bytes 24584 | tf_op jit(solution)/shard_map/ppermute | solution.py:41
  16.9 6.8 %copy-start.1 = (bf16[1024,2048]{1,0:T(8,128)(2,1)S(1)}, bf16[1024,2048]{1,0:T(8,128)(2,1)}, u32[]{:S(2)}) copy-start(bf16[1024,2048]{1,0:T(8,128)(2,1)} %w_out.1) | copy-start | bytes 12582916
  17.0 6.8 %collective-permute-start.5 = (bf16[8,128]{1,0:T(8,128)(2,1)S(1)}, bf16[8,128]{1,0:T(8,128)(2,1)S(1)}, u32[]{:S(2)}, u32[]{:S(2)}) collective-permute-start(bf16[8,128]{1,0:T(8,128)(2,1)S(1)} %get-tuple-element.20.token.rest_0_), channel_id=1, source_target_pairs={{0,12},{4,8},{8,4},{12,0},{1,13},{5,9},{9,5},{13,1},{2,14},{6,10},... | collective-permute-start | bytes 6152 | tf_op jit(solution)/shard_map/ppermute | solution.py:41
  19.2 4.5 %collective-permute-start.4 = (bf16[8,128]{1,0:T(8,128)(2,1)S(1)}, bf16[8,128]{1,0:T(8,128)(2,1)S(1)}, u32[]{:S(2)}, u32[]{:S(2)}) collective-permute-start(bf16[8,128]{1,0:T(8,128)(2,1)S(1)} %get-tuple-element.20.token.rest_0_), channel_id=1, source_target_pairs={{0,8},{4,12},{8,0},{12,4},{1,9},{5,13},{9,1},{13,5},{2,10},{6,14},... | collective-permute-start | bytes 6152 | tf_op jit(solution)/shard_map/ppermute | solution.py:41
  19.2 4.5 %collective-permute-start.3 = (bf16[8,128]{1,0:T(8,128)(2,1)S(1)}, bf16[8,128]{1,0:T(8,128)(2,1)S(1)}, u32[]{:S(2)}, u32[]{:S(2)}) collective-permute-start(bf16[8,128]{1,0:T(8,128)(2,1)S(1)} %get-tuple-element.20.token.rest_0_), channel_id=1, source_target_pairs={{0,4},{4,0},{8,12},{12,8},{1,5},{5,1},{9,13},{13,9},{2,6},{6,2},{1... | collective-permute-start | bytes 6152 | tf_op jit(solution)/shard_map/ppermute | solution.py:41
  24.4 3.8 %copy-start.2 = (bf16[4,2048]{1,0:T(4,128)(2,1)S(1)}, bf16[4,2048]{1,0:T(4,128)(2,1)}, u32[]{:S(2)}) copy-start(bf16[4,2048]{1,0:T(4,128)(2,1)} %states.1) | copy-start | bytes 49156
  24.4 3.8 %copy-start.3 = (f32[2,2048]{1,0:T(2,128)S(1)}, f32[2,2048]{1,0:T(2,128)}, u32[]{:S(2)}) copy-start(f32[2,2048]{1,0:T(2,128)} %gains.1) | copy-start | bytes 49156
  24.4 3.5 %collective-permute-start.8 = (bf16[4,2048]{1,0:T(4,128)(2,1)S(1)}, bf16[4,2048]{1,0:T(4,128)(2,1)S(1)}, u32[]{:S(2)}, u32[]{:S(2)}) collective-permute-start(bf16[4,2048]{1,0:T(4,128)(2,1)S(1)} %attn_project.1.token.rest_4_), channel_id=1, source_target_pairs={{0,3},{1,2},{2,1},{3,0},{4,7},{5,6},{6,5},{7,4},{8,11},{9,10},{10,... | collective-permute-start | bytes 49160 | tf_op jit(solution)/shard_map/ppermute | solution.py:41
  24.4 3.8 %collective-permute-start.7 = (bf16[4,2048]{1,0:T(4,128)(2,1)S(1)}, bf16[4,2048]{1,0:T(4,128)(2,1)S(1)}, u32[]{:S(2)}, u32[]{:S(2)}) collective-permute-start(bf16[4,2048]{1,0:T(4,128)(2,1)S(1)} %attn_project.1.token.rest_4_), channel_id=1, source_target_pairs={{0,2},{1,3},{2,0},{3,1},{4,6},{5,7},{6,4},{7,5},{8,10},{9,11},{10,... | collective-permute-start | bytes 49160 | tf_op jit(solution)/shard_map/ppermute | solution.py:41
  26.0 2.3 %collective-permute-start.6 = (bf16[4,2048]{1,0:T(4,128)(2,1)S(1)}, bf16[4,2048]{1,0:T(4,128)(2,1)S(1)}, u32[]{:S(2)}, u32[]{:S(2)}) collective-permute-start(bf16[4,2048]{1,0:T(4,128)(2,1)S(1)} %attn_project.1.token.rest_4_), channel_id=1, source_target_pairs={{0,1},{1,0},{2,3},{3,2},{4,5},{5,4},{6,7},{7,6},{8,9},{9,8},{10,11... | collective-permute-start | bytes 49160 | tf_op jit(solution)/shard_map/ppermute | solution.py:41
  28.2 14.6 %slice-start = ((s8[14680064]{0:T(1024)(128)(4,1)}), s8[4194304]{0:T(1024)(128)(4,1)S(1)}, s32[]{:S(2)}) async-start(s8[14680064]{0:T(1024)(128)(4,1)} %bitcast.6), calls=%async_computation | async-start | bytes 8388608
  28.2 14.6 %slice-start.1 = ((s8[14680064]{0:T(1024)(128)(4,1)}), s8[4194304]{0:T(1024)(128)(4,1)S(1)}, s32[]{:S(2)}) async-start(s8[14680064]{0:T(1024)(128)(4,1)} %bitcast.6), calls=%async_computation.1 | async-start | bytes 8388608
  28.3 14.6 %slice-start.2 = ((s8[14680064]{0:T(1024)(128)(4,1)}), s8[4194304]{0:T(1024)(128)(4,1)S(1)}, s32[]{:S(2)}) async-start(s8[14680064]{0:T(1024)(128)(4,1)} %bitcast.6), calls=%async_computation.2 | async-start | bytes 8388608
  28.3 14.6 %slice-start.3 = ((s8[14680064]{0:T(1024)(128)(4,1)}), s8[2097152]{0:T(1024)(128)(4,1)S(1)}, s32[]{:S(2)}) async-start(s8[14680064]{0:T(1024)(128)(4,1)} %bitcast.6), calls=%async_computation.3 | async-start | bytes 4194304
  34.1 6.7 %collective-permute-start.11 = (bf16[8,3712]{1,0:T(8,128)(2,1)S(1)}, bf16[8,3712]{1,0:T(8,128)(2,1)S(1)}, u32[]{:S(2)}, u32[]{:S(2)}) collective-permute-start(bf16[8,3712]{1,0:T(8,128)(2,1)S(1)} %get-tuple-element.23.rest_0_), channel_id=1, source_target_pairs={{0,12},{4,8},{8,4},{12,0},{1,13},{5,9},{9,5},{13,1},{2,14},{6,10},... | collective-permute-start | bytes 178184 | tf_op jit(solution)/shard_map/ppermute | solution.py:41
  36.3 6.5 %collective-permute-start.10 = (bf16[8,3712]{1,0:T(8,128)(2,1)S(1)}, bf16[8,3712]{1,0:T(8,128)(2,1)S(1)}, u32[]{:S(2)}, u32[]{:S(2)}) collective-permute-start(bf16[8,3712]{1,0:T(8,128)(2,1)S(1)} %get-tuple-element.23.rest_0_), channel_id=1, source_target_pairs={{0,8},{4,12},{8,0},{12,4},{1,9},{5,13},{9,1},{13,5},{2,10},{6,14},... | collective-permute-start | bytes 178184 | tf_op jit(solution)/shard_map/ppermute | solution.py:41
  36.9 6.0 %collective-permute-start.9 = (bf16[8,3712]{1,0:T(8,128)(2,1)S(1)}, bf16[8,3712]{1,0:T(8,128)(2,1)S(1)}, u32[]{:S(2)}, u32[]{:S(2)}) collective-permute-start(bf16[8,3712]{1,0:T(8,128)(2,1)S(1)} %get-tuple-element.23.rest_0_), channel_id=1, source_target_pairs={{0,4},{4,0},{8,12},{12,8},{1,5},{5,1},{9,13},{13,9},{2,6},{6,2},{1... | collective-permute-start | bytes 178184 | tf_op jit(solution)/shard_map/ppermute | solution.py:41
  45.0 3.2 %collective-permute-start.14 = (bf16[4,2048]{1,0:T(4,128)(2,1)S(1)}, bf16[4,2048]{1,0:T(4,128)(2,1)S(1)}, u32[]{:S(2)}, u32[]{:S(2)}) collective-permute-start(bf16[4,2048]{1,0:T(4,128)(2,1)S(1)} %down.1), channel_id=1, source_target_pairs={{0,3},{1,2},{2,1},{3,0},{4,7},{5,6},{6,5},{7,4},{8,11},{9,10},{10,... | collective-permute-start | bytes 49160 | tf_op jit(solution)/shard_map/ppermute | solution.py:41
  45.5 3.8 %collective-permute-start.13 = (bf16[4,2048]{1,0:T(4,128)(2,1)S(1)}, bf16[4,2048]{1,0:T(4,128)(2,1)S(1)}, u32[]{:S(2)}, u32[]{:S(2)}) collective-permute-start(bf16[4,2048]{1,0:T(4,128)(2,1)S(1)} %down.1), channel_id=1, source_target_pairs={{0,2},{1,3},{2,0},{3,1},{4,6},{5,7},{6,4},{7,5},{8,10},{9,11},{10,... | collective-permute-start | bytes 49160 | tf_op jit(solution)/shard_map/ppermute | solution.py:41
  46.7 2.6 %collective-permute-start.12 = (bf16[4,2048]{1,0:T(4,128)(2,1)S(1)}, bf16[4,2048]{1,0:T(4,128)(2,1)S(1)}, u32[]{:S(2)}, u32[]{:S(2)}) collective-permute-start(bf16[4,2048]{1,0:T(4,128)(2,1)S(1)} %down.1), channel_id=1, source_target_pairs={{0,1},{1,0},{2,3},{3,2},{4,5},{5,4},{6,7},{7,6},{8,9},{9,8},{10,11... | collective-permute-start | bytes 49160 | tf_op jit(solution)/shard_map/ppermute | solution.py:41

commit v15 on v14

--- a/solution.py
+++ b/solution.py
@@ -16,7 +16,7 @@
 MIB = 1 << 20
 COPY_ROWS = 2048
 DOWN_ROWS = 1024
-GU_SHARES = (4, 6, 4, 2, 4, 4, 2, 2)
+GU_SHARES = (4, 6, 4, 3, 4, 4, 3)
 F32 = jnp.float32
 BF16 = jnp.bfloat16
 QUARTER = (1.5703125, 4.837512969970703125e-4, 7.549789948768648e-8)
@@ -71,8 +71,8 @@
 
 
 def start_all(copies):
-    for i, copy in enumerate(copies):
-        copy.start(priority=i % 2)
+    for copy in copies:
+        copy.start(priority=1)
 
 
 def matrix_of(w):

time: 50.1 us -> 49.5 us (0.988)
  Pallas kernels: 21.3 us -> 20.7 us
  transfers between devices with their start and end apart: 15 -> 15, of which waited for: 6 -> 5; matrix products, arithmetic and copies ran while one was open for 0% -> 0% of each run, Pallas kernels for 12% -> 13%
where the time goes in v15:
time: 49.5 us; the launch traced here: 49.4 us
  Pallas kernels  20.7 us (42%)
  starting transfers between devices  18.4 us (37%)
  waiting for transfers between devices  8.66 us (17%)
  between operations  0.86 us (2%)
  other arithmetic  0.63 us (1%)
    ppermute x15, starting transfers between devices, exchange(): lax.ppermute(arrays[s], axis, [(i, i ^ s) for i in range(size)])  18.4 us
    ppermute x15, waiting for transfers between devices, exchange(): lax.ppermute(arrays[s], axis, [(i, i ^ s) for i in range(size)])  8.66 us
    pallas_call x3, Pallas kernels, fetch(): pl.pallas_call(functools.partial(fetch_kernel, share[0]), out_shape=block...  6.52 us
    pallas_call x1, Pallas kernels, per_device(): pl.pallas_call(functools.partial(gate_up_kernel, kv, len(fetched), shares...  5.33 us
    pallas_call x1, Pallas kernels, per_device(): pl.pallas_call(functools.partial(qkv_kernel, tp), out_shape=[jax.ShapeDty...  3.24 us
    pallas_call x1, Pallas kernels, per_device(): pl.pallas_call(functools.partial(attend_kernel, tp, heads, 512, shares[1]...  2.92 us
    pallas_call x1, Pallas kernels, per_device(): pl.pallas_call(functools.partial(down_kernel, tp), out_shape=jax.ShapeDty...  2.07 us
  transfers between devices with their start and end apart: 15, of which 5 were waited for; matrix products, arithmetic and copies ran while one was open for 0% of the time, Pallas kernels for 13%

profile of v15, /device:TPU:0, one launch (start us, length us, event | category | flops | bytes accessed | tf_op | source)
XLA Modules:
  0.0 49.4 jit_solution(6938784382553704836)
XLA Ops:
  0.6 3.2 %qkv.1 = (f32[16,128]{1,0:T(8,128)S(1)}, f32[16,128]{1,0:T(8,128)S(1)}, f32[16,128]{1,0:T(8,128)S(1)}, f32[16,128]{1,0:T(8,128)S(1)}, f32[8,128]{1,0:T(8,128)S(1)}, /*index=5*/s32[8,128]{1,0:T(8,128)S(1)}) custom-call(s32[4]{0:T(128)} %owner_hbm.1, s32[4]{0:T(128)} %lengths_hbm.1, f32[1,128]{1,0:T(1,128)} %constant.2.clone.frequency_hbm, ...), custom_call_target="tpu_custom_call" | custom-call | bytes 29520000 | tf_op jit(solution)/shard_map/qkv/pallas_call | solution.py:375
  3.9 5.1 %collective-permute-start = (f32[16,128]{1,0:T(8,128)S(1)}, f32[16,128]{1,0:T(8,128)S(1)}, u32[]{:S(2)}, u32[]{:S(2)}) collective-permute-start(f32[16,128]{1,0:T(8,128)S(1)} %get-tuple-element.15), channel_id=1, source_target_pairs={{0,12},{4,8},{8,4},{12,0},{1,13},{5,9},{9,5},{13,1},{2,14},{6,10},... | collective-permute-start | bytes 24584 | tf_op jit(solution)/shard_map/ppermute | solution.py:41
  9.0 0.0 collective-permute-start.1
  9.0 0.6 %collective-permute-start.2 = (f32[16,128]{1,0:T(8,128)S(1)}, f32[16,128]{1,0:T(8,128)S(1)}, u32[]{:S(2)}, u32[]{:S(2)}) collective-permute-start(f32[16,128]{1,0:T(8,128)S(1)} %get-tuple-element.17), channel_id=1, source_target_pairs={{0,4},{4,0},{8,12},{12,8},{1,5},{5,1},{9,13},{13,9},{2,6},{6,2},{1... | collective-permute-start | bytes 24584 | tf_op jit(solution)/shard_map/ppermute | solution.py:41
  9.7 2.3 %fetch.3.rest_4_.rest_0_ = bf16[4096,512]{1,0:T(8,128)(2,1)S(1)} custom-call(f32[8,128]{1,0:T(8,128)S(1)} %get-tuple-element.14.token.table, bf16[2048,2,3584]{2,1,0:T(2,128)(2,1)} %w.9, bf16[8192,256]{1,0:T(8,128)(2,1)S(1)} %bitcast.4), custom_call_target="tpu_custom_call" | custom-call | bytes 4428000 | tf_op jit(solution)/shard_map/fetch/pallas_call | solution.py:411
  11.9 0.0 collective-permute-done.rest_0_
  12.0 1.6 %collective-permute-done.1.rest_1_ = f32[16,128]{1,0:T(8,128)S(1)} collective-permute-done((f32[16,128]{1,0:T(8,128)S(1)}, f32[16,128]{1,0:T(8,128)S(1)}, u32[]{:S(2)}, u32[]{:S(2)}) %collective-permute-start.1) | collective-permute-done | bytes 8224 | tf_op jit(solution)/shard_map/ppermute | solution.py:41
  13.6 2.9 %attend.1 = (bf16[8,128]{1,0:T(8,128)(2,1)S(1)}, bf16[1,256]{1,0:T(2,128)(2,1)}, bf16[4096,768]{1,0:T(8,128)(2,1)S(1)}) custom-call(f32[8,128]{1,0:T(8,128)S(1)} %get-tuple-element.14.token.table, bf16[8192,256]{1,0:T(8,128)(2,1)S(1)} %bitcast.5, bf16[2048,2,3584]{2,1,0:T(2,128)(2,1)} %w.9, f32[16,128]{1,0:T(8,128)S(1)} %collective-permute-done.rest_0_, ...), custom_call_target="tpu_custom_call" | custom-call | bytes 29520000 | tf_op jit(solution)/shard_map/attend/pallas_call | solution.py:424
  16.5 0.0 copy-start.1
  16.5 2.2 %collective-permute-start.5 = (bf16[8,128]{1,0:T(8,128)(2,1)S(1)}, bf16[8,128]{1,0:T(8,128)(2,1)S(1)}, u32[]{:S(2)}, u32[]{:S(2)}) collective-permute-start(bf16[8,128]{1,0:T(8,128)(2,1)S(1)} %get-tuple-element.20.token.rest_0_), channel_id=1, source_target_pairs={{0,12},{4,8},{8,4},{12,0},{1,13},{5,9},{9,5},{13,1},{2,14},{6,10},... | collective-permute-start | bytes 6152 | tf_op jit(solution)/shard_map/ppermute | solution.py:41
  18.7 2.2 %collective-permute-start.3 = (bf16[8,128]{1,0:T(8,128)(2,1)S(1)}, bf16[8,128]{1,0:T(8,128)(2,1)S(1)}, u32[]{:S(2)}, u32[]{:S(2)}) collective-permute-start(bf16[8,128]{1,0:T(8,128)(2,1)S(1)} %get-tuple-element.20.token.rest_0_), channel_id=1, source_target_pairs={{0,4},{4,0},{8,12},{12,8},{1,5},{5,1},{9,13},{13,9},{2,6},{6,2},{1... | collective-permute-start | bytes 6152 | tf_op jit(solution)/shard_map/ppermute | solution.py:41
  21.0 2.3 %fetch.4.rest_4_.rest_2_ = bf16[4096,512]{1,0:T(8,128)(2,1)S(1)} custom-call(bf16[8,128]{1,0:T(8,128)(2,1)S(1)} %get-tuple-element.20.token.rest_0_, bf16[2048,2,3584]{2,1,0:T(2,128)(2,1)} %w.9), custom_call_target="tpu_custom_call" | custom-call | bytes 4428000 | tf_op jit(solution)/shard_map/fetch/pallas_call | solution.py:411
  23.3 0.0 collective-permute-done.4.rest_2_
  23.3 0.7 %attn_project.1.token.rest_4_ = bf16[4,2048]{1,0:T(4,128)(2,1)S(1)} custom-call(s32[8,128]{1,0:T(8,128)S(1)} %get-tuple-element.21.places, bf16[1024,2048]{1,0:T(8,128)(2,1)S(1)} %copy-done.1, bf16[8,128]{1,0:T(8,128)(2,1)S(1)} %get-tuple-element.20.token.rest_0_, bf16[8,128]{1,0:T(8,128)(2,1)S(1)} %collective-permute-done.3.rest_1_, ...), custom_call_target="tpu_custom_call" | custom-call | bytes 22140000 | tf_op jit(solution)/shard_map/attn_project/pallas_call | solution.py:447
  23.9 0.0 collective-permute-start.8
  24.0 1.6 %collective-permute-start.7 = (bf16[4,2048]{1,0:T(4,128)(2,1)S(1)}, bf16[4,2048]{1,0:T(4,128)(2,1)S(1)}, u32[]{:S(2)}, u32[]{:S(2)}) collective-permute-start(bf16[4,2048]{1,0:T(4,128)(2,1)S(1)} %attn_project.1.token.rest_4_), channel_id=1, source_target_pairs={{0,2},{1,3},{2,0},{3,1},{4,6},{5,7},{6,4},{7,5},{8,10},{9,11},{10,... | collective-permute-start | bytes 49160 | tf_op jit(solution)/shard_map/ppermute | solution.py:41
  25.5 0.3 collective-permute-start.6
  25.8 1.9 %fetch.5.rest_3_ = bf16[4096,384]{1,0:T(8,128)(2,1)S(1)} custom-call(bf16[4,2048]{1,0:T(4,128)(2,1)S(1)} %attn_project.1.token.rest_4_, bf16[2048,2,3584]{2,1,0:T(2,128)(2,1)} %w.9), custom_call_target="tpu_custom_call" | custom-call | bytes 3320999 | tf_op jit(solution)/shard_map/fetch/pallas_call | solution.py:411
  27.8 0.0 slice-start
  27.9 5.3 %gate_up.1 = (bf16[4,2048]{1,0:T(4,128)(2,1)}, bf16[8,3712]{1,0:T(8,128)(2,1)S(1)}) custom-call(bf16[4,2048]{1,0:T(4,128)(2,1)S(1)} %copy-done.2, f32[2,2048]{1,0:T(2,128)S(1)} %copy-done.3, bf16[2048,2,3584]{2,1,0:T(2,128)(2,1)} %w.9, bf16[4096,512]{1,0:T(8,128)(2,1)S(1)} %fetch.3.rest_4_.rest_0_, bf16[4096,768]{1,0:T(8,128)(2,1)S(1)} %get-tuple-element.19.rest_1_, ...), custom_call_target="tpu_custom_call" | custom-call | bytes 36900000 | tf_op jit(solution)/shard_map/gate_up/pallas_call | solution.py:460
  33.2 2.2 %collective-permute-start.11 = (bf16[8,3712]{1,0:T(8,128)(2,1)S(1)}, bf16[8,3712]{1,0:T(8,128)(2,1)S(1)}, u32[]{:S(2)}, u32[]{:S(2)}) collective-permute-start(bf16[8,3712]{1,0:T(8,128)(2,1)S(1)} %get-tuple-element.23.rest_0_), channel_id=1, source_target_pairs={{0,12},{4,8},{8,4},{12,0},{1,13},{5,9},{9,5},{13,1},{2,14},{6,10},... | collective-permute-start | bytes 178184 | tf_op jit(solution)/shard_map/ppermute | solution.py:41
  35.5 0.5 %collective-permute-start.10 = (bf16[8,3712]{1,0:T(8,128)(2,1)S(1)}, bf16[8,3712]{1,0:T(8,128)(2,1)S(1)}, u32[]{:S(2)}, u32[]{:S(2)}) collective-permute-start(bf16[8,3712]{1,0:T(8,128)(2,1)S(1)} %get-tuple-element.23.rest_0_), channel_id=1, source_target_pairs={{0,8},{4,12},{8,0},{12,4},{1,9},{5,13},{9,1},{13,5},{2,10},{6,14},... | collective-permute-start | bytes 178184 | tf_op jit(solution)/shard_map/ppermute | solution.py:41
  36.0 1.7 %collective-permute-start.9 = (bf16[8,3712]{1,0:T(8,128)(2,1)S(1)}, bf16[8,3712]{1,0:T(8,128)(2,1)S(1)}, u32[]{:S(2)}, u32[]{:S(2)}) collective-permute-start(bf16[8,3712]{1,0:T(8,128)(2,1)S(1)} %get-tuple-element.23.rest_0_), channel_id=1, source_target_pairs={{0,4},{4,0},{8,12},{12,8},{1,5},{5,1},{9,13},{13,9},{2,6},{6,2},{1... | collective-permute-start | bytes 178184 | tf_op jit(solution)/shard_map/ppermute | solution.py:41
  37.7 2.2 %collective-permute-done.11.rest_3_ = bf16[8,3712]{1,0:T(8,128)(2,1)S(1)} collective-permute-done((bf16[8,3712]{1,0:T(8,128)(2,1)S(1)}, bf16[8,3712]{1,0:T(8,128)(2,1)S(1)}, u32[]{:S(2)}, u32[]{:S(2)}) %collective-permute-start.11) | collective-permute-done | bytes 59424 | tf_op jit(solution)/shard_map/ppermute | solution.py:41
  39.9 2.1 %collective-permute-done.10.rest_2_ = bf16[8,3712]{1,0:T(8,128)(2,1)S(1)} collective-permute-done((bf16[8,3712]{1,0:T(8,128)(2,1)S(1)}, bf16[8,3712]{1,0:T(8,128)(2,1)S(1)}, u32[]{:S(2)}, u32[]{:S(2)}) %collective-permute-start.10) | collective-permute-done | bytes 59424 | tf_op jit(solution)/shard_map/ppermute | solution.py:41
  42.0 2.1 %down.1 = bf16[4,2048]{1,0:T(4,128)(2,1)S(1)} custom-call(bf16[3584,2048]{1,0:T(8,128)(2,1)S(1)} %bitcast.7, bf16[8,3712]{1,0:T(8,128)(2,1)S(1)} %get-tuple-element.23.rest_0_, bf16[8,3712]{1,0:T(8,128)(2,1)S(1)} %collective-permute-done.9.rest_1_, bf16[8,3712]{1,0:T(8,128)(2,1)S(1)} %collective-permute-done.10.rest_2_, ...), custom_call_target="tpu_custom_call" | custom-call | bytes 18450000 | tf_op jit(solution)/shard_map/down/pallas_call | solution.py:481
  44.1 0.9 %collective-permute-start.14 = (bf16[4,2048]{1,0:T(4,128)(2,1)S(1)}, bf16[4,2048]{1,0:T(4,128)(2,1)S(1)}, u32[]{:S(2)}, u32[]{:S(2)}) collective-permute-start(bf16[4,2048]{1,0:T(4,128)(2,1)S(1)} %down.1), channel_id=1, source_target_pairs={{0,3},{1,2},{2,1},{3,0},{4,7},{5,6},{6,5},{7,4},{8,11},{9,10},{10,... | collective-permute-start | bytes 49160 | tf_op jit(solution)/shard_map/ppermute | solution.py:41
  45.0 0.9 %collective-permute-start.13 = (bf16[4,2048]{1,0:T(4,128)(2,1)S(1)}, bf16[4,2048]{1,0:T(4,128)(2,1)S(1)}, u32[]{:S(2)}, u32[]{:S(2)}) collective-permute-start(bf16[4,2048]{1,0:T(4,128)(2,1)S(1)} %down.1), channel_id=1, source_target_pairs={{0,2},{1,3},{2,0},{3,1},{4,6},{5,7},{6,4},{7,5},{8,10},{9,11},{10,... | collective-permute-start | bytes 49160 | tf_op jit(solution)/shard_map/ppermute | solution.py:41
  45.9 0.1 collective-permute-start.12
  46.0 1.3 %collective-permute-done.14 = bf16[4,2048]{1,0:T(4,128)(2,1)S(1)} collective-permute-done((bf16[4,2048]{1,0:T(4,128)(2,1)S(1)}, bf16[4,2048]{1,0:T(4,128)(2,1)S(1)}, u32[]{:S(2)}, u32[]{:S(2)}) %collective-permute-start.14) | collective-permute-done | bytes 16416 | tf_op jit(solution)/shard_map/ppermute | solution.py:41
  47.3 1.5 %collective-permute-done.13 = bf16[4,2048]{1,0:T(4,128)(2,1)S(1)} collective-permute-done((bf16[4,2048]{1,0:T(4,128)(2,1)S(1)}, bf16[4,2048]{1,0:T(4,128)(2,1)S(1)}, u32[]{:S(2)}, u32[]{:S(2)}) %collective-permute-start.13) | collective-permute-done | bytes 16416 | tf_op jit(solution)/shard_map/ppermute | solution.py:41
  48.7 0.6 %add_convert_fusion = bf16[4,2048]{1,0:T(4,128)(2,1)} fusion(bf16[4,2048]{1,0:T(4,128)(2,1)S(1)} %collective-permute-done.14, bf16[4,2048]{1,0:T(4,128)(2,1)S(1)} %collective-permute-done.13, bf16[4,2048]{1,0:T(4,128)(2,1)S(1)} %collective-permute-done.12, bf16[4,2048]{1,0:T(4,128)(2,1)S(1)} %down.1), kind=kLoop, calls=%fused_computation | loop fusion | flops 65536 | bytes 81920 | tf_op jit(solution)/shard_map/convert_element_type | solution.py:491
  (24 shorter events, 0.1 us)
Async XLA Ops:
  0.6 9.0 %copy-start = (bf16[1,8192,1,256]{3,1,2,0:T(8,128)(2,1)S(1)}, bf16[1,8192,1,256]{3,1,2,0:T(8,128)(2,1)}, u32[]{:S(2)}) copy-start(bf16[1,8192,1,256]{3,1,2,0:T(8,128)(2,1)} %param.18) | copy-start | bytes 12582916
  3.9 8.1 %collective-permute-start = (f32[16,128]{1,0:T(8,128)S(1)}, f32[16,128]{1,0:T(8,128)S(1)}, u32[]{:S(2)}, u32[]{:S(2)}) collective-permute-start(f32[16,128]{1,0:T(8,128)S(1)} %get-tuple-element.15), channel_id=1, source_target_pairs={{0,12},{4,8},{8,4},{12,0},{1,13},{5,9},{9,5},{13,1},{2,14},{6,10},... | collective-permute-start | bytes 24584 | tf_op jit(solution)/shard_map/ppermute | solution.py:41
  9.0 4.5 %collective-permute-start.1 = (f32[16,128]{1,0:T(8,128)S(1)}, f32[16,128]{1,0:T(8,128)S(1)}, u32[]{:S(2)}, u32[]{:S(2)}) collective-permute-start(f32[16,128]{1,0:T(8,128)S(1)} %get-tuple-element.16), channel_id=1, source_target_pairs={{0,8},{4,12},{8,0},{12,4},{1,9},{5,13},{9,1},{13,5},{2,10},{6,14},... | collective-permute-start | bytes 24584 | tf_op jit(solution)/shard_map/ppermute | solution.py:41
  9.0 4.5 %collective-permute-start.2 = (f32[16,128]{1,0:T(8,128)S(1)}, f32[16,128]{1,0:T(8,128)S(1)}, u32[]{:S(2)}, u32[]{:S(2)}) collective-permute-start(f32[16,128]{1,0:T(8,128)S(1)} %get-tuple-element.17), channel_id=1, source_target_pairs={{0,4},{4,0},{8,12},{12,8},{1,5},{5,1},{9,13},{13,9},{2,6},{6,2},{1... | collective-permute-start | bytes 24584 | tf_op jit(solution)/shard_map/ppermute | solution.py:41
  16.5 6.8 %copy-start.1 = (bf16[1024,2048]{1,0:T(8,128)(2,1)S(1)}, bf16[1024,2048]{1,0:T(8,128)(2,1)}, u32[]{:S(2)}) copy-start(bf16[1024,2048]{1,0:T(8,128)(2,1)} %w_out.1) | copy-start | bytes 12582916
  16.5 6.8 %collective-permute-start.5 = (bf16[8,128]{1,0:T(8,128)(2,1)S(1)}, bf16[8,128]{1,0:T(8,128)(2,1)S(1)}, u32[]{:S(2)}, u32[]{:S(2)}) collective-permute-start(bf16[8,128]{1,0:T(8,128)(2,1)S(1)} %get-tuple-element.20.token.rest_0_), channel_id=1, source_target_pairs={{0,12},{4,8},{8,4},{12,0},{1,13},{5,9},{9,5},{13,1},{2,14},{6,10},... | collective-permute-start | bytes 6152 | tf_op jit(solution)/shard_map/ppermute | solution.py:41
  18.7 4.5 %collective-permute-start.4 = (bf16[8,128]{1,0:T(8,128)(2,1)S(1)}, bf16[8,128]{1,0:T(8,128)(2,1)S(1)}, u32[]{:S(2)}, u32[]{:S(2)}) collective-permute-start(bf16[8,128]{1,0:T(8,128)(2,1)S(1)} %get-tuple-element.20.token.rest_0_), channel_id=1, source_target_pairs={{0,8},{4,12},{8,0},{12,4},{1,9},{5,13},{9,1},{13,5},{2,10},{6,14},... | collective-permute-start | bytes 6152 | tf_op jit(solution)/shard_map/ppermute | solution.py:41
  18.7 4.5 %collective-permute-start.3 = (bf16[8,128]{1,0:T(8,128)(2,1)S(1)}, bf16[8,128]{1,0:T(8,128)(2,1)S(1)}, u32[]{:S(2)}, u32[]{:S(2)}) collective-permute-start(bf16[8,128]{1,0:T(8,128)(2,1)S(1)} %get-tuple-element.20.token.rest_0_), channel_id=1, source_target_pairs={{0,4},{4,0},{8,12},{12,8},{1,5},{5,1},{9,13},{13,9},{2,6},{6,2},{1... | collective-permute-start | bytes 6152 | tf_op jit(solution)/shard_map/ppermute | solution.py:41
  23.9 3.9 %copy-start.2 = (bf16[4,2048]{1,0:T(4,128)(2,1)S(1)}, bf16[4,2048]{1,0:T(4,128)(2,1)}, u32[]{:S(2)}) copy-start(bf16[4,2048]{1,0:T(4,128)(2,1)} %states.1) | copy-start | bytes 49156
  23.9 3.9 %copy-start.3 = (f32[2,2048]{1,0:T(2,128)S(1)}, f32[2,2048]{1,0:T(2,128)}, u32[]{:S(2)}) copy-start(f32[2,2048]{1,0:T(2,128)} %gains.1) | copy-start | bytes 49156
  23.9 3.8 %collective-permute-start.8 = (bf16[4,2048]{1,0:T(4,128)(2,1)S(1)}, bf16[4,2048]{1,0:T(4,128)(2,1)S(1)}, u32[]{:S(2)}, u32[]{:S(2)}) collective-permute-start(bf16[4,2048]{1,0:T(4,128)(2,1)S(1)} %attn_project.1.token.rest_4_), channel_id=1, source_target_pairs={{0,3},{1,2},{2,1},{3,0},{4,7},{5,6},{6,5},{7,4},{8,11},{9,10},{10,... | collective-permute-start | bytes 49160 | tf_op jit(solution)/shard_map/ppermute | solution.py:41
  24.0 3.8 %collective-permute-start.7 = (bf16[4,2048]{1,0:T(4,128)(2,1)S(1)}, bf16[4,2048]{1,0:T(4,128)(2,1)S(1)}, u32[]{:S(2)}, u32[]{:S(2)}) collective-permute-start(bf16[4,2048]{1,0:T(4,128)(2,1)S(1)} %attn_project.1.token.rest_4_), channel_id=1, source_target_pairs={{0,2},{1,3},{2,0},{3,1},{4,6},{5,7},{6,4},{7,5},{8,10},{9,11},{10,... | collective-permute-start | bytes 49160 | tf_op jit(solution)/shard_map/ppermute | solution.py:41
  25.5 2.3 %collective-permute-start.6 = (bf16[4,2048]{1,0:T(4,128)(2,1)S(1)}, bf16[4,2048]{1,0:T(4,128)(2,1)S(1)}, u32[]{:S(2)}, u32[]{:S(2)}) collective-permute-start(bf16[4,2048]{1,0:T(4,128)(2,1)S(1)} %attn_project.1.token.rest_4_), channel_id=1, source_target_pairs={{0,1},{1,0},{2,3},{3,2},{4,5},{5,4},{6,7},{7,6},{8,9},{9,8},{10,11... | collective-permute-start | bytes 49160 | tf_op jit(solution)/shard_map/ppermute | solution.py:41
  27.8 14.2 %slice-start = ((s8[14680064]{0:T(1024)(128)(4,1)}), s8[4194304]{0:T(1024)(128)(4,1)S(1)}, s32[]{:S(2)}) async-start(s8[14680064]{0:T(1024)(128)(4,1)} %bitcast.6), calls=%async_computation | async-start | bytes 8388608
  27.8 14.1 %slice-start.1 = ((s8[14680064]{0:T(1024)(128)(4,1)}), s8[4194304]{0:T(1024)(128)(4,1)S(1)}, s32[]{:S(2)}) async-start(s8[14680064]{0:T(1024)(128)(4,1)} %bitcast.6), calls=%async_computation.1 | async-start | bytes 8388608
  27.9 14.1 %slice-start.2 = ((s8[14680064]{0:T(1024)(128)(4,1)}), s8[4194304]{0:T(1024)(128)(4,1)S(1)}, s32[]{:S(2)}) async-start(s8[14680064]{0:T(1024)(128)(4,1)} %bitcast.6), calls=%async_computation.2 | async-start | bytes 8388608
  27.9 14.1 %slice-start.3 = ((s8[14680064]{0:T(1024)(128)(4,1)}), s8[2097152]{0:T(1024)(128)(4,1)S(1)}, s32[]{:S(2)}) async-start(s8[14680064]{0:T(1024)(128)(4,1)} %bitcast.6), calls=%async_computation.3 | async-start | bytes 4194304
  33.2 6.7 %collective-permute-start.11 = (bf16[8,3712]{1,0:T(8,128)(2,1)S(1)}, bf16[8,3712]{1,0:T(8,128)(2,1)S(1)}, u32[]{:S(2)}, u32[]{:S(2)}) collective-permute-start(bf16[8,3712]{1,0:T(8,128)(2,1)S(1)} %get-tuple-element.23.rest_0_), channel_id=1, source_target_pairs={{0,12},{4,8},{8,4},{12,0},{1,13},{5,9},{9,5},{13,1},{2,14},{6,10},... | collective-permute-start | bytes 178184 | tf_op jit(solution)/shard_map/ppermute | solution.py:41
  35.5 6.5 %collective-permute-start.10 = (bf16[8,3712]{1,0:T(8,128)(2,1)S(1)}, bf16[8,3712]{1,0:T(8,128)(2,1)S(1)}, u32[]{:S(2)}, u32[]{:S(2)}) collective-permute-start(bf16[8,3712]{1,0:T(8,128)(2,1)S(1)} %get-tuple-element.23.rest_0_), channel_id=1, source_target_pairs={{0,8},{4,12},{8,0},{12,4},{1,9},{5,13},{9,1},{13,5},{2,10},{6,14},... | collective-permute-start | bytes 178184 | tf_op jit(solution)/shard_map/ppermute | solution.py:41
  36.0 6.0 %collective-permute-start.9 = (bf16[8,3712]{1,0:T(8,128)(2,1)S(1)}, bf16[8,3712]{1,0:T(8,128)(2,1)S(1)}, u32[]{:S(2)}, u32[]{:S(2)}) collective-permute-start(bf16[8,3712]{1,0:T(8,128)(2,1)S(1)} %get-tuple-element.23.rest_0_), channel_id=1, source_target_pairs={{0,4},{4,0},{8,12},{12,8},{1,5},{5,1},{9,13},{13,9},{2,6},{6,2},{1... | collective-permute-start | bytes 178184 | tf_op jit(solution)/shard_map/ppermute | solution.py:41
  44.1 3.2 %collective-permute-start.14 = (bf16[4,2048]{1,0:T(4,128)(2,1)S(1)}, bf16[4,2048]{1,0:T(4,128)(2,1)S(1)}, u32[]{:S(2)}, u32[]{:S(2)}) collective-permute-start(bf16[4,2048]{1,0:T(4,128)(2,1)S(1)} %down.1), channel_id=1, source_target_pairs={{0,3},{1,2},{2,1},{3,0},{4,7},{5,6},{6,5},{7,4},{8,11},{9,10},{10,... | collective-permute-start | bytes 49160 | tf_op jit(solution)/shard_map/ppermute | solution.py:41
  45.0 3.7 %collective-permute-start.13 = (bf16[4,2048]{1,0:T(4,128)(2,1)S(1)}, bf16[4,2048]{1,0:T(4,128)(2,1)S(1)}, u32[]{:S(2)}, u32[]{:S(2)}) collective-permute-start(bf16[4,2048]{1,0:T(4,128)(2,1)S(1)} %down.1), channel_id=1, source_target_pairs={{0,2},{1,3},{2,0},{3,1},{4,6},{5,7},{6,4},{7,5},{8,10},{9,11},{10,... | collective-permute-start | bytes 49160 | tf_op jit(solution)/shard_map/ppermute | solution.py:41
  45.9 2.9 %collective-permute-start.12 = (bf16[4,2048]{1,0:T(4,128)(2,1)S(1)}, bf16[4,2048]{1,0:T(4,128)(2,1)S(1)}, u32[]{:S(2)}, u32[]{:S(2)}) collective-permute-start(bf16[4,2048]{1,0:T(4,128)(2,1)S(1)} %down.1), channel_id=1, source_target_pairs={{0,1},{1,0},{2,3},{3,2},{4,5},{5,4},{6,7},{7,6},{8,9},{9,8},{10,11... | collective-permute-start | bytes 49160 | tf_op jit(solution)/shard_map/ppermute | solution.py:41

commit v16 on v15

--- a/solution.py
+++ b/solution.py
@@ -169,9 +169,7 @@
         for c in range(parts)
     ]
     kv_copy = pltpu.make_async_copy(wkv, wkv_buf, sems.at[parts])
-    for copy in small:
-        copy.start()
-    start_all([kv_copy] + copies)
+    start_all(small + [kv_copy] + copies)
     for copy in small:
         copy.wait()
     me = lax.axis_index("tp")
@@ -455,7 +453,7 @@
         name="attn_project",
     )(places, w_out, *head_parts, fetched[-1])
 
-    fetched.append(fetch(shares[3], out_part))
+    fetched.append(fetch(shares[3], out_part, w_down))
     out_parts = exchange([out_part] * kv, "kv", kv)
     attn_out, gu_part = pl.pallas_call(
         functools.partial(gate_up_kernel, kv, len(fetched), shares[4][0]),

time: 49.5 us -> 50.2 us (1.014)
  Pallas kernels: 20.7 us -> 21.4 us
    pallas_call x1, Pallas kernels: 3.24 us -> 3.91 us  [per_device(): pl.pallas_call(functools.partial(qkv_kernel, tp), out_shape=[jax.ShapeDty...]
where the time goes in v16:
time: 50.2 us; the launch traced here: 50 us
  Pallas kernels  21.4 us (43%)
  starting transfers between devices  18.4 us (37%)
  waiting for transfers between devices  8.71 us (17%)
  between operations  0.83 us (2%)
  other arithmetic  0.63 us (1%)
    ppermute x15, starting transfers between devices, exchange(): lax.ppermute(arrays[s], axis, [(i, i ^ s) for i in range(size)])  18.4 us
    ppermute x15, waiting for transfers between devices, exchange(): lax.ppermute(arrays[s], axis, [(i, i ^ s) for i in range(size)])  8.71 us
    pallas_call x3, Pallas kernels, fetch(): pl.pallas_call(functools.partial(fetch_kernel, share[0]), out_shape=block...  6.54 us
    pallas_call x1, Pallas kernels, per_device(): pl.pallas_call(functools.partial(gate_up_kernel, kv, len(fetched), shares...  5.18 us
    pallas_call x1, Pallas kernels, per_device(): pl.pallas_call(functools.partial(qkv_kernel, tp), out_shape=[jax.ShapeDty...  3.91 us
    pallas_call x1, Pallas kernels, per_device(): pl.pallas_call(functools.partial(attend_kernel, tp, heads, 512, shares[1]...  3.07 us
    pallas_call x1, Pallas kernels, per_device(): pl.pallas_call(functools.partial(down_kernel, tp), out_shape=jax.ShapeDty...  2.08 us
  transfers between devices with their start and end apart: 15, of which 5 were waited for; matrix products, arithmetic and copies ran while one was open for 0% of the time, Pallas kernels for 13%

profile of v16, /device:TPU:0, one launch (start us, length us, event | category | flops | bytes accessed | tf_op | source)
XLA Modules:
  0.0 50.0 jit_solution(16235062575631773650)
XLA Ops:
  0.6 3.9 %qkv.1 = (f32[16,128]{1,0:T(8,128)S(1)}, f32[16,128]{1,0:T(8,128)S(1)}, f32[16,128]{1,0:T(8,128)S(1)}, f32[16,128]{1,0:T(8,128)S(1)}, f32[8,128]{1,0:T(8,128)S(1)}, /*index=5*/s32[8,128]{1,0:T(8,128)S(1)}) custom-call(s32[4]{0:T(128)} %owner_hbm.1, s32[4]{0:T(128)} %lengths_hbm.1, f32[1,128]{1,0:T(1,128)} %constant.2.clone.frequency_hbm, ...), custom_call_target="tpu_custom_call" | custom-call | bytes 29520000 | tf_op jit(solution)/shard_map/qkv/pallas_call | solution.py:373
  4.6 5.1 %collective-permute-start = (f32[16,128]{1,0:T(8,128)S(1)}, f32[16,128]{1,0:T(8,128)S(1)}, u32[]{:S(2)}, u32[]{:S(2)}) collective-permute-start(f32[16,128]{1,0:T(8,128)S(1)} %get-tuple-element.15), channel_id=1, source_target_pairs={{0,12},{4,8},{8,4},{12,0},{1,13},{5,9},{9,5},{13,1},{2,14},{6,10},... | collective-permute-start | bytes 24584 | tf_op jit(solution)/shard_map/ppermute | solution.py:41
  9.7 0.0 collective-permute-start.1
  9.7 0.6 %collective-permute-start.2 = (f32[16,128]{1,0:T(8,128)S(1)}, f32[16,128]{1,0:T(8,128)S(1)}, u32[]{:S(2)}, u32[]{:S(2)}) collective-permute-start(f32[16,128]{1,0:T(8,128)S(1)} %get-tuple-element.17), channel_id=1, source_target_pairs={{0,4},{4,0},{8,12},{12,8},{1,5},{5,1},{9,13},{13,9},{2,6},{6,2},{1... | collective-permute-start | bytes 24584 | tf_op jit(solution)/shard_map/ppermute | solution.py:41
  10.3 2.3 %fetch.3.rest_4_.rest_0_ = bf16[4096,512]{1,0:T(8,128)(2,1)S(1)} custom-call(f32[8,128]{1,0:T(8,128)S(1)} %get-tuple-element.14.token.table, bf16[2048,2,3584]{2,1,0:T(2,128)(2,1)} %w.9, bf16[8192,256]{1,0:T(8,128)(2,1)S(1)} %bitcast.6), custom_call_target="tpu_custom_call" | custom-call | bytes 4428000 | tf_op jit(solution)/shard_map/fetch/pallas_call | solution.py:409
  12.6 1.6 %collective-permute-done.1.rest_1_ = f32[16,128]{1,0:T(8,128)S(1)} collective-permute-done((f32[16,128]{1,0:T(8,128)S(1)}, f32[16,128]{1,0:T(8,128)S(1)}, u32[]{:S(2)}, u32[]{:S(2)}) %collective-permute-start.1) | collective-permute-done | bytes 8224 | tf_op jit(solution)/shard_map/ppermute | solution.py:41
  14.2 0.0 collective-permute-done.2.rest_2_
  14.2 3.1 %attend.1 = (bf16[8,128]{1,0:T(8,128)(2,1)S(1)}, bf16[1,256]{1,0:T(2,128)(2,1)}, bf16[4096,768]{1,0:T(8,128)(2,1)S(1)}) custom-call(f32[8,128]{1,0:T(8,128)S(1)} %get-tuple-element.14.token.table, bf16[8192,256]{1,0:T(8,128)(2,1)S(1)} %bitcast.7, bf16[2048,2,3584]{2,1,0:T(2,128)(2,1)} %w.9, f32[16,128]{1,0:T(8,128)S(1)} %collective-permute-done.rest_0_, ...), custom_call_target="tpu_custom_call" | custom-call | bytes 29520000 | tf_op jit(solution)/shard_map/attend/pallas_call | solution.py:422
  17.3 0.0 copy-start.1
  17.3 0.0 slice-start.2
  17.3 0.0 slice-start.3
  17.4 2.3 %collective-permute-start.5 = (bf16[8,128]{1,0:T(8,128)(2,1)S(1)}, bf16[8,128]{1,0:T(8,128)(2,1)S(1)}, u32[]{:S(2)}, u32[]{:S(2)}) collective-permute-start(bf16[8,128]{1,0:T(8,128)(2,1)S(1)} %get-tuple-element.20.token.rest_0_), channel_id=1, source_target_pairs={{0,12},{4,8},{8,4},{12,0},{1,13},{5,9},{9,5},{13,1},{2,14},{6,10},... | collective-permute-start | bytes 6152 | tf_op jit(solution)/shard_map/ppermute | solution.py:41
  19.6 2.2 %collective-permute-start.3 = (bf16[8,128]{1,0:T(8,128)(2,1)S(1)}, bf16[8,128]{1,0:T(8,128)(2,1)S(1)}, u32[]{:S(2)}, u32[]{:S(2)}) collective-permute-start(bf16[8,128]{1,0:T(8,128)(2,1)S(1)} %get-tuple-element.20.token.rest_0_), channel_id=1, source_target_pairs={{0,4},{4,0},{8,12},{12,8},{1,5},{5,1},{9,13},{13,9},{2,6},{6,2},{1... | collective-permute-start | bytes 6152 | tf_op jit(solution)/shard_map/ppermute | solution.py:41
  21.8 2.3 %fetch.4.rest_4_.rest_2_ = bf16[4096,512]{1,0:T(8,128)(2,1)S(1)} custom-call(bf16[8,128]{1,0:T(8,128)(2,1)S(1)} %get-tuple-element.20.token.rest_0_, bf16[2048,2,3584]{2,1,0:T(2,128)(2,1)} %w.9), custom_call_target="tpu_custom_call" | custom-call | bytes 4428000 | tf_op jit(solution)/shard_map/fetch/pallas_call | solution.py:409
  24.1 0.7 %attn_project.1.token.rest_4_ = bf16[4,2048]{1,0:T(4,128)(2,1)S(1)} custom-call(s32[8,128]{1,0:T(8,128)S(1)} %get-tuple-element.21.places, bf16[1024,2048]{1,0:T(8,128)(2,1)S(1)} %copy-done.1, bf16[8,128]{1,0:T(8,128)(2,1)S(1)} %get-tuple-element.20.token.rest_0_, bf16[8,128]{1,0:T(8,128)(2,1)S(1)} %collective-permute-done.3.rest_1_, ...), custom_call_target="tpu_custom_call" | custom-call | bytes 22140000 | tf_op jit(solution)/shard_map/attn_project/pallas_call | solution.py:445
  24.8 0.0 collective-permute-start.8
  24.8 1.6 %collective-permute-start.7 = (bf16[4,2048]{1,0:T(4,128)(2,1)S(1)}, bf16[4,2048]{1,0:T(4,128)(2,1)S(1)}, u32[]{:S(2)}, u32[]{:S(2)}) collective-permute-start(bf16[4,2048]{1,0:T(4,128)(2,1)S(1)} %attn_project.1.token.rest_4_), channel_id=1, source_target_pairs={{0,2},{1,3},{2,0},{3,1},{4,6},{5,7},{6,4},{7,5},{8,10},{9,11},{10,... | collective-permute-start | bytes 49160 | tf_op jit(solution)/shard_map/ppermute | solution.py:41
  26.4 0.3 collective-permute-start.6
  26.7 2.0 %fetch.5.rest_3_ = bf16[4096,384]{1,0:T(8,128)(2,1)S(1)} custom-call(bf16[4,2048]{1,0:T(4,128)(2,1)S(1)} %attn_project.1.token.rest_4_, bf16[2048,2,3584]{2,1,0:T(2,128)(2,1)} %w.9, bf16[3584,2048]{1,0:T(8,128)(2,1)S(1)} %bitcast.5), custom_call_target="tpu_custom_call" | custom-call | bytes 3320999 | tf_op jit(solution)/shard_map/fetch/pallas_call | solution.py:409
  28.7 5.2 %gate_up.1 = (bf16[4,2048]{1,0:T(4,128)(2,1)}, bf16[8,3712]{1,0:T(8,128)(2,1)S(1)}) custom-call(bf16[4,2048]{1,0:T(4,128)(2,1)S(1)} %copy-done.2, f32[2,2048]{1,0:T(2,128)S(1)} %copy-done.3, bf16[2048,2,3584]{2,1,0:T(2,128)(2,1)} %w.9, bf16[4096,512]{1,0:T(8,128)(2,1)S(1)} %fetch.3.rest_4_.rest_0_, bf16[4096,768]{1,0:T(8,128)(2,1)S(1)} %get-tuple-element.19.rest_1_, ...), custom_call_target="tpu_custom_call" | custom-call | bytes 36900000 | tf_op jit(solution)/shard_map/gate_up/pallas_call | solution.py:458
  33.9 2.3 %collective-permute-start.11 = (bf16[8,3712]{1,0:T(8,128)(2,1)S(1)}, bf16[8,3712]{1,0:T(8,128)(2,1)S(1)}, u32[]{:S(2)}, u32[]{:S(2)}) collective-permute-start(bf16[8,3712]{1,0:T(8,128)(2,1)S(1)} %get-tuple-element.23.rest_0_), channel_id=1, source_target_pairs={{0,12},{4,8},{8,4},{12,0},{1,13},{5,9},{9,5},{13,1},{2,14},{6,10},... | collective-permute-start | bytes 178184 | tf_op jit(solution)/shard_map/ppermute | solution.py:41
  36.2 0.5 %collective-permute-start.10 = (bf16[8,3712]{1,0:T(8,128)(2,1)S(1)}, bf16[8,3712]{1,0:T(8,128)(2,1)S(1)}, u32[]{:S(2)}, u32[]{:S(2)}) collective-permute-start(bf16[8,3712]{1,0:T(8,128)(2,1)S(1)} %get-tuple-element.23.rest_0_), channel_id=1, source_target_pairs={{0,8},{4,12},{8,0},{12,4},{1,9},{5,13},{9,1},{13,5},{2,10},{6,14},... | collective-permute-start | bytes 178184 | tf_op jit(solution)/shard_map/ppermute | solution.py:41
  36.7 1.7 %collective-permute-start.9 = (bf16[8,3712]{1,0:T(8,128)(2,1)S(1)}, bf16[8,3712]{1,0:T(8,128)(2,1)S(1)}, u32[]{:S(2)}, u32[]{:S(2)}) collective-permute-start(bf16[8,3712]{1,0:T(8,128)(2,1)S(1)} %get-tuple-element.23.rest_0_), channel_id=1, source_target_pairs={{0,4},{4,0},{8,12},{12,8},{1,5},{5,1},{9,13},{13,9},{2,6},{6,2},{1... | collective-permute-start | bytes 178184 | tf_op jit(solution)/shard_map/ppermute | solution.py:41
  38.4 2.2 %collective-permute-done.11.rest_3_ = bf16[8,3712]{1,0:T(8,128)(2,1)S(1)} collective-permute-done((bf16[8,3712]{1,0:T(8,128)(2,1)S(1)}, bf16[8,3712]{1,0:T(8,128)(2,1)S(1)}, u32[]{:S(2)}, u32[]{:S(2)}) %collective-permute-start.11) | collective-permute-done | bytes 59424 | tf_op jit(solution)/shard_map/ppermute | solution.py:41
  40.5 2.1 %collective-permute-done.10.rest_2_ = bf16[8,3712]{1,0:T(8,128)(2,1)S(1)} collective-permute-done((bf16[8,3712]{1,0:T(8,128)(2,1)S(1)}, bf16[8,3712]{1,0:T(8,128)(2,1)S(1)}, u32[]{:S(2)}, u32[]{:S(2)}) %collective-permute-start.10) | collective-permute-done | bytes 59424 | tf_op jit(solution)/shard_map/ppermute | solution.py:41
  42.7 2.1 %down.1 = bf16[4,2048]{1,0:T(4,128)(2,1)S(1)} custom-call(bf16[3584,2048]{1,0:T(8,128)(2,1)S(1)} %bitcast.5, bf16[8,3712]{1,0:T(8,128)(2,1)S(1)} %get-tuple-element.23.rest_0_, bf16[8,3712]{1,0:T(8,128)(2,1)S(1)} %collective-permute-done.9.rest_1_, bf16[8,3712]{1,0:T(8,128)(2,1)S(1)} %collective-permute-done.10.rest_2_, ...), custom_call_target="tpu_custom_call" | custom-call | bytes 18450000 | tf_op jit(solution)/shard_map/down/pallas_call | solution.py:479
  44.8 0.9 %collective-permute-start.14 = (bf16[4,2048]{1,0:T(4,128)(2,1)S(1)}, bf16[4,2048]{1,0:T(4,128)(2,1)S(1)}, u32[]{:S(2)}, u32[]{:S(2)}) collective-permute-start(bf16[4,2048]{1,0:T(4,128)(2,1)S(1)} %down.1), channel_id=1, source_target_pairs={{0,3},{1,2},{2,1},{3,0},{4,7},{5,6},{6,5},{7,4},{8,11},{9,10},{10,... | collective-permute-start | bytes 49160 | tf_op jit(solution)/shard_map/ppermute | solution.py:41
  45.7 0.8 %collective-permute-start.13 = (bf16[4,2048]{1,0:T(4,128)(2,1)S(1)}, bf16[4,2048]{1,0:T(4,128)(2,1)S(1)}, u32[]{:S(2)}, u32[]{:S(2)}) collective-permute-start(bf16[4,2048]{1,0:T(4,128)(2,1)S(1)} %down.1), channel_id=1, source_target_pairs={{0,2},{1,3},{2,0},{3,1},{4,6},{5,7},{6,4},{7,5},{8,10},{9,11},{10,... | collective-permute-start | bytes 49160 | tf_op jit(solution)/shard_map/ppermute | solution.py:41
  46.5 0.2 collective-permute-start.12
  46.6 1.3 %collective-permute-done.14 = bf16[4,2048]{1,0:T(4,128)(2,1)S(1)} collective-permute-done((bf16[4,2048]{1,0:T(4,128)(2,1)S(1)}, bf16[4,2048]{1,0:T(4,128)(2,1)S(1)}, u32[]{:S(2)}, u32[]{:S(2)}) %collective-permute-start.14) | collective-permute-done | bytes 16416 | tf_op jit(solution)/shard_map/ppermute | solution.py:41
  47.9 1.5 %collective-permute-done.13 = bf16[4,2048]{1,0:T(4,128)(2,1)S(1)} collective-permute-done((bf16[4,2048]{1,0:T(4,128)(2,1)S(1)}, bf16[4,2048]{1,0:T(4,128)(2,1)S(1)}, u32[]{:S(2)}, u32[]{:S(2)}) %collective-permute-start.13) | collective-permute-done | bytes 16416 | tf_op jit(solution)/shard_map/ppermute | solution.py:41
  49.4 0.6 %add_convert_fusion = bf16[4,2048]{1,0:T(4,128)(2,1)} fusion(bf16[4,2048]{1,0:T(4,128)(2,1)S(1)} %collective-permute-done.14, bf16[4,2048]{1,0:T(4,128)(2,1)S(1)} %collective-permute-done.13, bf16[4,2048]{1,0:T(4,128)(2,1)S(1)} %collective-permute-done.12, bf16[4,2048]{1,0:T(4,128)(2,1)S(1)} %down.1), kind=kLoop, calls=%fused_computation | loop fusion | flops 65536 | bytes 81920 | tf_op jit(solution)/shard_map/convert_element_type | solution.py:489
  (24 shorter events, 0.1 us)
Async XLA Ops:
  0.6 9.7 %copy-start = (bf16[1,8192,1,256]{3,1,2,0:T(8,128)(2,1)S(1)}, bf16[1,8192,1,256]{3,1,2,0:T(8,128)(2,1)}, u32[]{:S(2)}) copy-start(bf16[1,8192,1,256]{3,1,2,0:T(8,128)(2,1)} %param.18) | copy-start | bytes 12582916
  4.6 8.1 %collective-permute-start = (f32[16,128]{1,0:T(8,128)S(1)}, f32[16,128]{1,0:T(8,128)S(1)}, u32[]{:S(2)}, u32[]{:S(2)}) collective-permute-start(f32[16,128]{1,0:T(8,128)S(1)} %get-tuple-element.15), channel_id=1, source_target_pairs={{0,12},{4,8},{8,4},{12,0},{1,13},{5,9},{9,5},{13,1},{2,14},{6,10},... | collective-permute-start | bytes 24584 | tf_op jit(solution)/shard_map/ppermute | solution.py:41
  9.7 4.5 %collective-permute-start.1 = (f32[16,128]{1,0:T(8,128)S(1)}, f32[16,128]{1,0:T(8,128)S(1)}, u32[]{:S(2)}, u32[]{:S(2)}) collective-permute-start(f32[16,128]{1,0:T(8,128)S(1)} %get-tuple-element.16), channel_id=1, source_target_pairs={{0,8},{4,12},{8,0},{12,4},{1,9},{5,13},{9,1},{13,5},{2,10},{6,14},... | collective-permute-start | bytes 24584 | tf_op jit(solution)/shard_map/ppermute | solution.py:41
  9.7 4.5 %collective-permute-start.2 = (f32[16,128]{1,0:T(8,128)S(1)}, f32[16,128]{1,0:T(8,128)S(1)}, u32[]{:S(2)}, u32[]{:S(2)}) collective-permute-start(f32[16,128]{1,0:T(8,128)S(1)} %get-tuple-element.17), channel_id=1, source_target_pairs={{0,4},{4,0},{8,12},{12,8},{1,5},{5,1},{9,13},{13,9},{2,6},{6,2},{1... | collective-permute-start | bytes 24584 | tf_op jit(solution)/shard_map/ppermute | solution.py:41
  14.2 12.4 %slice-start = ((s8[14680064]{0:T(1024)(128)(4,1)}), s8[4194304]{0:T(1024)(128)(4,1)S(1)}, s32[]{:S(2)}) async-start(s8[14680064]{0:T(1024)(128)(4,1)} %bitcast.4), calls=%async_computation | async-start | bytes 8388608
  14.2 12.4 %slice-start.1 = ((s8[14680064]{0:T(1024)(128)(4,1)}), s8[4194304]{0:T(1024)(128)(4,1)S(1)}, s32[]{:S(2)}) async-start(s8[14680064]{0:T(1024)(128)(4,1)} %bitcast.4), calls=%async_computation.1 | async-start | bytes 8388608
  17.3 6.8 %copy-start.1 = (bf16[1024,2048]{1,0:T(8,128)(2,1)S(1)}, bf16[1024,2048]{1,0:T(8,128)(2,1)}, u32[]{:S(2)}) copy-start(bf16[1024,2048]{1,0:T(8,128)(2,1)} %w_out.1) | copy-start | bytes 12582916
  17.3 9.4 %slice-start.2 = ((s8[14680064]{0:T(1024)(128)(4,1)}), s8[4194304]{0:T(1024)(128)(4,1)S(1)}, s32[]{:S(2)}) async-start(s8[14680064]{0:T(1024)(128)(4,1)} %bitcast.4), calls=%async_computation.2 | async-start | bytes 8388608
  17.3 9.3 %slice-start.3 = ((s8[14680064]{0:T(1024)(128)(4,1)}), s8[2097152]{0:T(1024)(128)(4,1)S(1)}, s32[]{:S(2)}) async-start(s8[14680064]{0:T(1024)(128)(4,1)} %bitcast.4), calls=%async_computation.3 | async-start | bytes 4194304
  17.4 6.8 %collective-permute-start.5 = (bf16[8,128]{1,0:T(8,128)(2,1)S(1)}, bf16[8,128]{1,0:T(8,128)(2,1)S(1)}, u32[]{:S(2)}, u32[]{:S(2)}) collective-permute-start(bf16[8,128]{1,0:T(8,128)(2,1)S(1)} %get-tuple-element.20.token.rest_0_), channel_id=1, source_target_pairs={{0,12},{4,8},{8,4},{12,0},{1,13},{5,9},{9,5},{13,1},{2,14},{6,10},... | collective-permute-start | bytes 6152 | tf_op jit(solution)/shard_map/ppermute | solution.py:41
  19.6 4.5 %collective-permute-start.4 = (bf16[8,128]{1,0:T(8,128)(2,1)S(1)}, bf16[8,128]{1,0:T(8,128)(2,1)S(1)}, u32[]{:S(2)}, u32[]{:S(2)}) collective-permute-start(bf16[8,128]{1,0:T(8,128)(2,1)S(1)} %get-tuple-element.20.token.rest_0_), channel_id=1, source_target_pairs={{0,8},{4,12},{8,0},{12,4},{1,9},{5,13},{9,1},{13,5},{2,10},{6,14},... | collective-permute-start | bytes 6152 | tf_op jit(solution)/shard_map/ppermute | solution.py:41
  19.6 4.5 %collective-permute-start.3 = (bf16[8,128]{1,0:T(8,128)(2,1)S(1)}, bf16[8,128]{1,0:T(8,128)(2,1)S(1)}, u32[]{:S(2)}, u32[]{:S(2)}) collective-permute-start(bf16[8,128]{1,0:T(8,128)(2,1)S(1)} %get-tuple-element.20.token.rest_0_), channel_id=1, source_target_pairs={{0,4},{4,0},{8,12},{12,8},{1,5},{5,1},{9,13},{13,9},{2,6},{6,2},{1... | collective-permute-start | bytes 6152 | tf_op jit(solution)/shard_map/ppermute | solution.py:41
  24.8 3.9 %copy-start.2 = (bf16[4,2048]{1,0:T(4,128)(2,1)S(1)}, bf16[4,2048]{1,0:T(4,128)(2,1)}, u32[]{:S(2)}) copy-start(bf16[4,2048]{1,0:T(4,128)(2,1)} %states.1) | copy-start | bytes 49156
  24.8 3.9 %copy-start.3 = (f32[2,2048]{1,0:T(2,128)S(1)}, f32[2,2048]{1,0:T(2,128)}, u32[]{:S(2)}) copy-start(f32[2,2048]{1,0:T(2,128)} %gains.1) | copy-start | bytes 49156
  24.8 3.9 %collective-permute-start.8 = (bf16[4,2048]{1,0:T(4,128)(2,1)S(1)}, bf16[4,2048]{1,0:T(4,128)(2,1)S(1)}, u32[]{:S(2)}, u32[]{:S(2)}) collective-permute-start(bf16[4,2048]{1,0:T(4,128)(2,1)S(1)} %attn_project.1.token.rest_4_), channel_id=1, source_target_pairs={{0,3},{1,2},{2,1},{3,0},{4,7},{5,6},{6,5},{7,4},{8,11},{9,10},{10,... | collective-permute-start | bytes 49160 | tf_op jit(solution)/shard_map/ppermute | solution.py:41
  24.8 3.9 %collective-permute-start.7 = (bf16[4,2048]{1,0:T(4,128)(2,1)S(1)}, bf16[4,2048]{1,0:T(4,128)(2,1)S(1)}, u32[]{:S(2)}, u32[]{:S(2)}) collective-permute-start(bf16[4,2048]{1,0:T(4,128)(2,1)S(1)} %attn_project.1.token.rest_4_), channel_id=1, source_target_pairs={{0,2},{1,3},{2,0},{3,1},{4,6},{5,7},{6,4},{7,5},{8,10},{9,11},{10,... | collective-permute-start | bytes 49160 | tf_op jit(solution)/shard_map/ppermute | solution.py:41
  26.4 2.3 %collective-permute-start.6 = (bf16[4,2048]{1,0:T(4,128)(2,1)S(1)}, bf16[4,2048]{1,0:T(4,128)(2,1)S(1)}, u32[]{:S(2)}, u32[]{:S(2)}) collective-permute-start(bf16[4,2048]{1,0:T(4,128)(2,1)S(1)} %attn_project.1.token.rest_4_), channel_id=1, source_target_pairs={{0,1},{1,0},{2,3},{3,2},{4,5},{5,4},{6,7},{7,6},{8,9},{9,8},{10,11... | collective-permute-start | bytes 49160 | tf_op jit(solution)/shard_map/ppermute | solution.py:41
  33.9 6.6 %collective-permute-start.11 = (bf16[8,3712]{1,0:T(8,128)(2,1)S(1)}, bf16[8,3712]{1,0:T(8,128)(2,1)S(1)}, u32[]{:S(2)}, u32[]{:S(2)}) collective-permute-start(bf16[8,3712]{1,0:T(8,128)(2,1)S(1)} %get-tuple-element.23.rest_0_), channel_id=1, source_target_pairs={{0,12},{4,8},{8,4},{12,0},{1,13},{5,9},{9,5},{13,1},{2,14},{6,10},... | collective-permute-start | bytes 178184 | tf_op jit(solution)/shard_map/ppermute | solution.py:41
  36.2 6.5 %collective-permute-start.10 = (bf16[8,3712]{1,0:T(8,128)(2,1)S(1)}, bf16[8,3712]{1,0:T(8,128)(2,1)S(1)}, u32[]{:S(2)}, u32[]{:S(2)}) collective-permute-start(bf16[8,3712]{1,0:T(8,128)(2,1)S(1)} %get-tuple-element.23.rest_0_), channel_id=1, source_target_pairs={{0,8},{4,12},{8,0},{12,4},{1,9},{5,13},{9,1},{13,5},{2,10},{6,14},... | collective-permute-start | bytes 178184 | tf_op jit(solution)/shard_map/ppermute | solution.py:41
  36.7 6.0 %collective-permute-start.9 = (bf16[8,3712]{1,0:T(8,128)(2,1)S(1)}, bf16[8,3712]{1,0:T(8,128)(2,1)S(1)}, u32[]{:S(2)}, u32[]{:S(2)}) collective-permute-start(bf16[8,3712]{1,0:T(8,128)(2,1)S(1)} %get-tuple-element.23.rest_0_), channel_id=1, source_target_pairs={{0,4},{4,0},{8,12},{12,8},{1,5},{5,1},{9,13},{13,9},{2,6},{6,2},{1... | collective-permute-start | bytes 178184 | tf_op jit(solution)/shard_map/ppermute | solution.py:41
  44.8 3.2 %collective-permute-start.14 = (bf16[4,2048]{1,0:T(4,128)(2,1)S(1)}, bf16[4,2048]{1,0:T(4,128)(2,1)S(1)}, u32[]{:S(2)}, u32[]{:S(2)}) collective-permute-start(bf16[4,2048]{1,0:T(4,128)(2,1)S(1)} %down.1), channel_id=1, source_target_pairs={{0,3},{1,2},{2,1},{3,0},{4,7},{5,6},{6,5},{7,4},{8,11},{9,10},{10,... | collective-permute-start | bytes 49160 | tf_op jit(solution)/shard_map/ppermute | solution.py:41
  45.7 3.7 %collective-permute-start.13 = (bf16[4,2048]{1,0:T(4,128)(2,1)S(1)}, bf16[4,2048]{1,0:T(4,128)(2,1)S(1)}, u32[]{:S(2)}, u32[]{:S(2)}) collective-permute-start(bf16[4,2048]{1,0:T(4,128)(2,1)S(1)} %down.1), channel_id=1, source_target_pairs={{0,2},{1,3},{2,0},{3,1},{4,6},{5,7},{6,4},{7,5},{8,10},{9,11},{10,... | collective-permute-start | bytes 49160 | tf_op jit(solution)/shard_map/ppermute | solution.py:41
  46.5 2.9 %collective-permute-start.12 = (bf16[4,2048]{1,0:T(4,128)(2,1)S(1)}, bf16[4,2048]{1,0:T(4,128)(2,1)S(1)}, u32[]{:S(2)}, u32[]{:S(2)}) collective-permute-start(bf16[4,2048]{1,0:T(4,128)(2,1)S(1)} %down.1), channel_id=1, source_target_pairs={{0,1},{1,0},{2,3},{3,2},{4,5},{5,4},{6,7},{7,6},{8,9},{9,8},{10,11... | collective-permute-start | bytes 49160 | tf_op jit(solution)/shard_map/ppermute | solution.py:41

commit v17 on v15

--- a/solution.py
+++ b/solution.py
@@ -16,7 +16,7 @@
 MIB = 1 << 20
 COPY_ROWS = 2048
 DOWN_ROWS = 1024
-GU_SHARES = (4, 6, 4, 3, 4, 4, 3)
+GU_SHARES = (4, 6, 2, 3, 4, 4, 3, 2)
 F32 = jnp.float32
 BF16 = jnp.bfloat16
 QUARTER = (1.5703125, 4.837512969970703125e-4, 7.549789948768648e-8)
@@ -455,7 +455,7 @@
         name="attn_project",
     )(places, w_out, *head_parts, fetched[-1])
 
-    fetched.append(fetch(shares[3], out_part))
+    fetched.append(fetch(shares[3], out_part, w_down))
     out_parts = exchange([out_part] * kv, "kv", kv)
     attn_out, gu_part = pl.pallas_call(
         functools.partial(gate_up_kernel, kv, len(fetched), shares[4][0]),

time: 49.5 us -> 50.1 us (1.012)
  Pallas kernels: 20.7 us -> 21.4 us
    pallas_call x1, Pallas kernels: 5.33 us -> 5.86 us  [per_device(): pl.pallas_call(functools.partial(gate_up_kernel, kv, len(fetched), shares...]
where the time goes in v17:
time: 50.1 us; the launch traced here: 50 us
  Pallas kernels  21.4 us (43%)
  starting transfers between devices  18.4 us (37%)
  waiting for transfers between devices  8.67 us (17%)
  between operations  0.84 us (2%)
  other arithmetic  0.63 us (1%)
    ppermute x15, starting transfers between devices, exchange(): lax.ppermute(arrays[s], axis, [(i, i ^ s) for i in range(size)])  18.4 us
    ppermute x15, waiting for transfers between devices, exchange(): lax.ppermute(arrays[s], axis, [(i, i ^ s) for i in range(size)])  8.67 us
    pallas_call x3, Pallas kernels, fetch(): pl.pallas_call(functools.partial(fetch_kernel, share[0]), out_shape=block...  6.65 us
    pallas_call x1, Pallas kernels, per_device(): pl.pallas_call(functools.partial(gate_up_kernel, kv, len(fetched), shares...  5.86 us
    pallas_call x1, Pallas kernels, per_device(): pl.pallas_call(functools.partial(qkv_kernel, tp), out_shape=[jax.ShapeDty...  3.24 us
    pallas_call x1, Pallas kernels, per_device(): pl.pallas_call(functools.partial(attend_kernel, tp, heads, 512, shares[1]...  2.92 us
    pallas_call x1, Pallas kernels, per_device(): pl.pallas_call(functools.partial(down_kernel, tp), out_shape=jax.ShapeDty...  2.08 us
  transfers between devices with their start and end apart: 15, of which 5 were waited for; matrix products, arithmetic and copies ran while one was open for 0% of the time, Pallas kernels for 13%

profile of v17, /device:TPU:0, one launch (start us, length us, event | category | flops | bytes accessed | tf_op | source)
XLA Modules:
  0.0 50.0 jit_solution(10792111090306498614)
XLA Ops:
  0.6 3.2 %qkv.1 = (f32[16,128]{1,0:T(8,128)S(1)}, f32[16,128]{1,0:T(8,128)S(1)}, f32[16,128]{1,0:T(8,128)S(1)}, f32[16,128]{1,0:T(8,128)S(1)}, f32[8,128]{1,0:T(8,128)S(1)}, /*index=5*/s32[8,128]{1,0:T(8,128)S(1)}) custom-call(s32[4]{0:T(128)} %owner_hbm.1, s32[4]{0:T(128)} %lengths_hbm.1, f32[1,128]{1,0:T(1,128)} %constant.2.clone.frequency_hbm, ...), custom_call_target="tpu_custom_call" | custom-call | bytes 29520000 | tf_op jit(solution)/shard_map/qkv/pallas_call | solution.py:375
  3.9 5.1 %collective-permute-start = (f32[16,128]{1,0:T(8,128)S(1)}, f32[16,128]{1,0:T(8,128)S(1)}, u32[]{:S(2)}, u32[]{:S(2)}) collective-permute-start(f32[16,128]{1,0:T(8,128)S(1)} %get-tuple-element.15), channel_id=1, source_target_pairs={{0,12},{4,8},{8,4},{12,0},{1,13},{5,9},{9,5},{13,1},{2,14},{6,10},... | collective-permute-start | bytes 24584 | tf_op jit(solution)/shard_map/ppermute | solution.py:41
  9.0 0.6 %collective-permute-start.2 = (f32[16,128]{1,0:T(8,128)S(1)}, f32[16,128]{1,0:T(8,128)S(1)}, u32[]{:S(2)}, u32[]{:S(2)}) collective-permute-start(f32[16,128]{1,0:T(8,128)S(1)} %get-tuple-element.17), channel_id=1, source_target_pairs={{0,4},{4,0},{8,12},{12,8},{1,5},{5,1},{9,13},{13,9},{2,6},{6,2},{1... | collective-permute-start | bytes 24584 | tf_op jit(solution)/shard_map/ppermute | solution.py:41
  9.7 2.3 %fetch.3.rest_4_.rest_0_ = bf16[4096,512]{1,0:T(8,128)(2,1)S(1)} custom-call(f32[8,128]{1,0:T(8,128)S(1)} %get-tuple-element.14.token.table, bf16[2048,2,3584]{2,1,0:T(2,128)(2,1)} %w.9, bf16[8192,256]{1,0:T(8,128)(2,1)S(1)} %bitcast.6), custom_call_target="tpu_custom_call" | custom-call | bytes 4428000 | tf_op jit(solution)/shard_map/fetch/pallas_call | solution.py:411
  11.9 0.0 collective-permute-done.rest_0_
  12.0 1.6 %collective-permute-done.1.rest_1_ = f32[16,128]{1,0:T(8,128)S(1)} collective-permute-done((f32[16,128]{1,0:T(8,128)S(1)}, f32[16,128]{1,0:T(8,128)S(1)}, u32[]{:S(2)}, u32[]{:S(2)}) %collective-permute-start.1) | collective-permute-done | bytes 8224 | tf_op jit(solution)/shard_map/ppermute | solution.py:41
  13.6 0.0 collective-permute-done.2.rest_2_
  13.6 2.9 %attend.1 = (bf16[8,128]{1,0:T(8,128)(2,1)S(1)}, bf16[1,256]{1,0:T(2,128)(2,1)}, bf16[4096,768]{1,0:T(8,128)(2,1)S(1)}) custom-call(f32[8,128]{1,0:T(8,128)S(1)} %get-tuple-element.14.token.table, bf16[8192,256]{1,0:T(8,128)(2,1)S(1)} %bitcast.7, bf16[2048,2,3584]{2,1,0:T(2,128)(2,1)} %w.9, f32[16,128]{1,0:T(8,128)S(1)} %collective-permute-done.rest_0_, ...), custom_call_target="tpu_custom_call" | custom-call | bytes 29520000 | tf_op jit(solution)/shard_map/attend/pallas_call | solution.py:424
  16.5 0.0 slice-start
  16.5 0.0 copy-start.1
  16.5 0.0 slice-start.3
  16.5 2.2 %collective-permute-start.5 = (bf16[8,128]{1,0:T(8,128)(2,1)S(1)}, bf16[8,128]{1,0:T(8,128)(2,1)S(1)}, u32[]{:S(2)}, u32[]{:S(2)}) collective-permute-start(bf16[8,128]{1,0:T(8,128)(2,1)S(1)} %get-tuple-element.20.token.rest_0_), channel_id=1, source_target_pairs={{0,12},{4,8},{8,4},{12,0},{1,13},{5,9},{9,5},{13,1},{2,14},{6,10},... | collective-permute-start | bytes 6152 | tf_op jit(solution)/shard_map/ppermute | solution.py:41
  18.8 2.2 %collective-permute-start.3 = (bf16[8,128]{1,0:T(8,128)(2,1)S(1)}, bf16[8,128]{1,0:T(8,128)(2,1)S(1)}, u32[]{:S(2)}, u32[]{:S(2)}) collective-permute-start(bf16[8,128]{1,0:T(8,128)(2,1)S(1)} %get-tuple-element.20.token.rest_0_), channel_id=1, source_target_pairs={{0,4},{4,0},{8,12},{12,8},{1,5},{5,1},{9,13},{13,9},{2,6},{6,2},{1... | collective-permute-start | bytes 6152 | tf_op jit(solution)/shard_map/ppermute | solution.py:41
  21.0 2.4 %fetch.4.rest_4_.rest_2_ = bf16[4096,256]{1,0:T(8,128)(2,1)S(1)} custom-call(bf16[8,128]{1,0:T(8,128)(2,1)S(1)} %get-tuple-element.20.token.rest_0_, bf16[2048,2,3584]{2,1,0:T(2,128)(2,1)} %w.9), custom_call_target="tpu_custom_call" | custom-call | bytes 2214000 | tf_op jit(solution)/shard_map/fetch/pallas_call | solution.py:411
  23.5 0.7 %attn_project.1.token.rest_4_ = bf16[4,2048]{1,0:T(4,128)(2,1)S(1)} custom-call(s32[8,128]{1,0:T(8,128)S(1)} %get-tuple-element.21.places, bf16[1024,2048]{1,0:T(8,128)(2,1)S(1)} %copy-done.1, bf16[8,128]{1,0:T(8,128)(2,1)S(1)} %get-tuple-element.20.token.rest_0_, bf16[8,128]{1,0:T(8,128)(2,1)S(1)} %collective-permute-done.3.rest_1_, ...), custom_call_target="tpu_custom_call" | custom-call | bytes 22140000 | tf_op jit(solution)/shard_map/attn_project/pallas_call | solution.py:447
  24.1 0.0 collective-permute-start.8
  24.1 1.6 %collective-permute-start.7 = (bf16[4,2048]{1,0:T(4,128)(2,1)S(1)}, bf16[4,2048]{1,0:T(4,128)(2,1)S(1)}, u32[]{:S(2)}, u32[]{:S(2)}) collective-permute-start(bf16[4,2048]{1,0:T(4,128)(2,1)S(1)} %attn_project.1.token.rest_4_), channel_id=1, source_target_pairs={{0,2},{1,3},{2,0},{3,1},{4,6},{5,7},{6,4},{7,5},{8,10},{9,11},{10,... | collective-permute-start | bytes 49160 | tf_op jit(solution)/shard_map/ppermute | solution.py:41
  25.7 0.3 collective-permute-start.6
  26.0 2.0 %fetch.5.rest_3_ = bf16[4096,384]{1,0:T(8,128)(2,1)S(1)} custom-call(bf16[4,2048]{1,0:T(4,128)(2,1)S(1)} %attn_project.1.token.rest_4_, bf16[2048,2,3584]{2,1,0:T(2,128)(2,1)} %w.9, bf16[3584,2048]{1,0:T(8,128)(2,1)S(1)} %bitcast.5), custom_call_target="tpu_custom_call" | custom-call | bytes 3320999 | tf_op jit(solution)/shard_map/fetch/pallas_call | solution.py:411
  28.0 5.9 %gate_up.1 = (bf16[4,2048]{1,0:T(4,128)(2,1)}, bf16[8,3712]{1,0:T(8,128)(2,1)S(1)}) custom-call(bf16[4,2048]{1,0:T(4,128)(2,1)S(1)} %copy-done.2, f32[2,2048]{1,0:T(2,128)S(1)} %copy-done.3, bf16[2048,2,3584]{2,1,0:T(2,128)(2,1)} %w.9, bf16[4096,512]{1,0:T(8,128)(2,1)S(1)} %fetch.3.rest_4_.rest_0_, bf16[4096,768]{1,0:T(8,128)(2,1)S(1)} %get-tuple-element.19.rest_1_, ...), custom_call_target="tpu_custom_call" | custom-call | bytes 36900000 | tf_op jit(solution)/shard_map/gate_up/pallas_call | solution.py:460
  33.9 2.2 %collective-permute-start.11 = (bf16[8,3712]{1,0:T(8,128)(2,1)S(1)}, bf16[8,3712]{1,0:T(8,128)(2,1)S(1)}, u32[]{:S(2)}, u32[]{:S(2)}) collective-permute-start(bf16[8,3712]{1,0:T(8,128)(2,1)S(1)} %get-tuple-element.23.rest_0_), channel_id=1, source_target_pairs={{0,12},{4,8},{8,4},{12,0},{1,13},{5,9},{9,5},{13,1},{2,14},{6,10},... | collective-permute-start | bytes 178184 | tf_op jit(solution)/shard_map/ppermute | solution.py:41
  36.1 0.4 collective-permute-start.10
  36.6 1.8 %collective-permute-start.9 = (bf16[8,3712]{1,0:T(8,128)(2,1)S(1)}, bf16[8,3712]{1,0:T(8,128)(2,1)S(1)}, u32[]{:S(2)}, u32[]{:S(2)}) collective-permute-start(bf16[8,3712]{1,0:T(8,128)(2,1)S(1)} %get-tuple-element.23.rest_0_), channel_id=1, source_target_pairs={{0,4},{4,0},{8,12},{12,8},{1,5},{5,1},{9,13},{13,9},{2,6},{6,2},{1... | collective-permute-start | bytes 178184 | tf_op jit(solution)/shard_map/ppermute | solution.py:41
  38.3 2.3 %collective-permute-done.11.rest_3_ = bf16[8,3712]{1,0:T(8,128)(2,1)S(1)} collective-permute-done((bf16[8,3712]{1,0:T(8,128)(2,1)S(1)}, bf16[8,3712]{1,0:T(8,128)(2,1)S(1)}, u32[]{:S(2)}, u32[]{:S(2)}) %collective-permute-start.11) | collective-permute-done | bytes 59424 | tf_op jit(solution)/shard_map/ppermute | solution.py:41
  40.7 1.9 %collective-permute-done.10.rest_2_ = bf16[8,3712]{1,0:T(8,128)(2,1)S(1)} collective-permute-done((bf16[8,3712]{1,0:T(8,128)(2,1)S(1)}, bf16[8,3712]{1,0:T(8,128)(2,1)S(1)}, u32[]{:S(2)}, u32[]{:S(2)}) %collective-permute-start.10) | collective-permute-done | bytes 59424 | tf_op jit(solution)/shard_map/ppermute | solution.py:41
  42.5 2.1 %down.1 = bf16[4,2048]{1,0:T(4,128)(2,1)S(1)} custom-call(bf16[3584,2048]{1,0:T(8,128)(2,1)S(1)} %bitcast.5, bf16[8,3712]{1,0:T(8,128)(2,1)S(1)} %get-tuple-element.23.rest_0_, bf16[8,3712]{1,0:T(8,128)(2,1)S(1)} %collective-permute-done.9.rest_1_, bf16[8,3712]{1,0:T(8,128)(2,1)S(1)} %collective-permute-done.10.rest_2_, ...), custom_call_target="tpu_custom_call" | custom-call | bytes 18450000 | tf_op jit(solution)/shard_map/down/pallas_call | solution.py:481
  44.6 1.0 %collective-permute-start.14 = (bf16[4,2048]{1,0:T(4,128)(2,1)S(1)}, bf16[4,2048]{1,0:T(4,128)(2,1)S(1)}, u32[]{:S(2)}, u32[]{:S(2)}) collective-permute-start(bf16[4,2048]{1,0:T(4,128)(2,1)S(1)} %down.1), channel_id=1, source_target_pairs={{0,3},{1,2},{2,1},{3,0},{4,7},{5,6},{6,5},{7,4},{8,11},{9,10},{10,... | collective-permute-start | bytes 49160 | tf_op jit(solution)/shard_map/ppermute | solution.py:41
  45.6 0.7 %collective-permute-start.13 = (bf16[4,2048]{1,0:T(4,128)(2,1)S(1)}, bf16[4,2048]{1,0:T(4,128)(2,1)S(1)}, u32[]{:S(2)}, u32[]{:S(2)}) collective-permute-start(bf16[4,2048]{1,0:T(4,128)(2,1)S(1)} %down.1), channel_id=1, source_target_pairs={{0,2},{1,3},{2,0},{3,1},{4,6},{5,7},{6,4},{7,5},{8,10},{9,11},{10,... | collective-permute-start | bytes 49160 | tf_op jit(solution)/shard_map/ppermute | solution.py:41
  46.3 0.2 collective-permute-start.12
  46.5 1.3 %collective-permute-done.14 = bf16[4,2048]{1,0:T(4,128)(2,1)S(1)} collective-permute-done((bf16[4,2048]{1,0:T(4,128)(2,1)S(1)}, bf16[4,2048]{1,0:T(4,128)(2,1)S(1)}, u32[]{:S(2)}, u32[]{:S(2)}) %collective-permute-start.14) | collective-permute-done | bytes 16416 | tf_op jit(solution)/shard_map/ppermute | solution.py:41
  47.8 1.6 %collective-permute-done.13 = bf16[4,2048]{1,0:T(4,128)(2,1)S(1)} collective-permute-done((bf16[4,2048]{1,0:T(4,128)(2,1)S(1)}, bf16[4,2048]{1,0:T(4,128)(2,1)S(1)}, u32[]{:S(2)}, u32[]{:S(2)}) %collective-permute-start.13) | collective-permute-done | bytes 16416 | tf_op jit(solution)/shard_map/ppermute | solution.py:41
  49.4 0.6 %add_convert_fusion = bf16[4,2048]{1,0:T(4,128)(2,1)} fusion(bf16[4,2048]{1,0:T(4,128)(2,1)S(1)} %collective-permute-done.14, bf16[4,2048]{1,0:T(4,128)(2,1)S(1)} %collective-permute-done.13, bf16[4,2048]{1,0:T(4,128)(2,1)S(1)} %collective-permute-done.12, bf16[4,2048]{1,0:T(4,128)(2,1)S(1)} %down.1), kind=kLoop, calls=%fused_computation | loop fusion | flops 65536 | bytes 81920 | tf_op jit(solution)/shard_map/convert_element_type | solution.py:491
  (24 shorter events, 0.1 us)
Async XLA Ops:
  0.6 9.0 %copy-start = (bf16[1,8192,1,256]{3,1,2,0:T(8,128)(2,1)S(1)}, bf16[1,8192,1,256]{3,1,2,0:T(8,128)(2,1)}, u32[]{:S(2)}) copy-start(bf16[1,8192,1,256]{3,1,2,0:T(8,128)(2,1)} %param.18) | copy-start | bytes 12582916
  3.9 8.1 %collective-permute-start = (f32[16,128]{1,0:T(8,128)S(1)}, f32[16,128]{1,0:T(8,128)S(1)}, u32[]{:S(2)}, u32[]{:S(2)}) collective-permute-start(f32[16,128]{1,0:T(8,128)S(1)} %get-tuple-element.15), channel_id=1, source_target_pairs={{0,12},{4,8},{8,4},{12,0},{1,13},{5,9},{9,5},{13,1},{2,14},{6,10},... | collective-permute-start | bytes 24584 | tf_op jit(solution)/shard_map/ppermute | solution.py:41
  9.0 4.5 %collective-permute-start.1 = (f32[16,128]{1,0:T(8,128)S(1)}, f32[16,128]{1,0:T(8,128)S(1)}, u32[]{:S(2)}, u32[]{:S(2)}) collective-permute-start(f32[16,128]{1,0:T(8,128)S(1)} %get-tuple-element.16), channel_id=1, source_target_pairs={{0,8},{4,12},{8,0},{12,4},{1,9},{5,13},{9,1},{13,5},{2,10},{6,14},... | collective-permute-start | bytes 24584 | tf_op jit(solution)/shard_map/ppermute | solution.py:41
  9.0 4.5 %collective-permute-start.2 = (f32[16,128]{1,0:T(8,128)S(1)}, f32[16,128]{1,0:T(8,128)S(1)}, u32[]{:S(2)}, u32[]{:S(2)}) collective-permute-start(f32[16,128]{1,0:T(8,128)S(1)} %get-tuple-element.17), channel_id=1, source_target_pairs={{0,4},{4,0},{8,12},{12,8},{1,5},{5,1},{9,13},{13,9},{2,6},{6,2},{1... | collective-permute-start | bytes 24584 | tf_op jit(solution)/shard_map/ppermute | solution.py:41
  16.5 9.5 %slice-start = ((s8[14680064]{0:T(1024)(128)(4,1)}), s8[4194304]{0:T(1024)(128)(4,1)S(1)}, s32[]{:S(2)}) async-start(s8[14680064]{0:T(1024)(128)(4,1)} %bitcast.4), calls=%async_computation | async-start | bytes 8388608
  16.5 6.9 %copy-start.1 = (bf16[1024,2048]{1,0:T(8,128)(2,1)S(1)}, bf16[1024,2048]{1,0:T(8,128)(2,1)}, u32[]{:S(2)}) copy-start(bf16[1024,2048]{1,0:T(8,128)(2,1)} %w_out.1) | copy-start | bytes 12582916
  16.5 9.5 %slice-start.1 = ((s8[14680064]{0:T(1024)(128)(4,1)}), s8[4194304]{0:T(1024)(128)(4,1)S(1)}, s32[]{:S(2)}) async-start(s8[14680064]{0:T(1024)(128)(4,1)} %bitcast.4), calls=%async_computation.1 | async-start | bytes 8388608
  16.5 9.5 %slice-start.2 = ((s8[14680064]{0:T(1024)(128)(4,1)}), s8[4194304]{0:T(1024)(128)(4,1)S(1)}, s32[]{:S(2)}) async-start(s8[14680064]{0:T(1024)(128)(4,1)} %bitcast.4), calls=%async_computation.2 | async-start | bytes 8388608
  16.5 9.5 %slice-start.3 = ((s8[14680064]{0:T(1024)(128)(4,1)}), s8[2097152]{0:T(1024)(128)(4,1)S(1)}, s32[]{:S(2)}) async-start(s8[14680064]{0:T(1024)(128)(4,1)} %bitcast.4), calls=%async_computation.3 | async-start | bytes 4194304
  16.5 6.9 %collective-permute-start.5 = (bf16[8,128]{1,0:T(8,128)(2,1)S(1)}, bf16[8,128]{1,0:T(8,128)(2,1)S(1)}, u32[]{:S(2)}, u32[]{:S(2)}) collective-permute-start(bf16[8,128]{1,0:T(8,128)(2,1)S(1)} %get-tuple-element.20.token.rest_0_), channel_id=1, source_target_pairs={{0,12},{4,8},{8,4},{12,0},{1,13},{5,9},{9,5},{13,1},{2,14},{6,10},... | collective-permute-start | bytes 6152 | tf_op jit(solution)/shard_map/ppermute | solution.py:41
  18.8 4.6 %collective-permute-start.4 = (bf16[8,128]{1,0:T(8,128)(2,1)S(1)}, bf16[8,128]{1,0:T(8,128)(2,1)S(1)}, u32[]{:S(2)}, u32[]{:S(2)}) collective-permute-start(bf16[8,128]{1,0:T(8,128)(2,1)S(1)} %get-tuple-element.20.token.rest_0_), channel_id=1, source_target_pairs={{0,8},{4,12},{8,0},{12,4},{1,9},{5,13},{9,1},{13,5},{2,10},{6,14},... | collective-permute-start | bytes 6152 | tf_op jit(solution)/shard_map/ppermute | solution.py:41
  18.8 4.6 %collective-permute-start.3 = (bf16[8,128]{1,0:T(8,128)(2,1)S(1)}, bf16[8,128]{1,0:T(8,128)(2,1)S(1)}, u32[]{:S(2)}, u32[]{:S(2)}) collective-permute-start(bf16[8,128]{1,0:T(8,128)(2,1)S(1)} %get-tuple-element.20.token.rest_0_), channel_id=1, source_target_pairs={{0,4},{4,0},{8,12},{12,8},{1,5},{5,1},{9,13},{13,9},{2,6},{6,2},{1... | collective-permute-start | bytes 6152 | tf_op jit(solution)/shard_map/ppermute | solution.py:41
  24.1 3.9 %copy-start.2 = (bf16[4,2048]{1,0:T(4,128)(2,1)S(1)}, bf16[4,2048]{1,0:T(4,128)(2,1)}, u32[]{:S(2)}) copy-start(bf16[4,2048]{1,0:T(4,128)(2,1)} %states.1) | copy-start | bytes 49156
  24.1 3.9 %copy-start.3 = (f32[2,2048]{1,0:T(2,128)S(1)}, f32[2,2048]{1,0:T(2,128)}, u32[]{:S(2)}) copy-start(f32[2,2048]{1,0:T(2,128)} %gains.1) | copy-start | bytes 49156
  24.1 3.9 %collective-permute-start.8 = (bf16[4,2048]{1,0:T(4,128)(2,1)S(1)}, bf16[4,2048]{1,0:T(4,128)(2,1)S(1)}, u32[]{:S(2)}, u32[]{:S(2)}) collective-permute-start(bf16[4,2048]{1,0:T(4,128)(2,1)S(1)} %attn_project.1.token.rest_4_), channel_id=1, source_target_pairs={{0,3},{1,2},{2,1},{3,0},{4,7},{5,6},{6,5},{7,4},{8,11},{9,10},{10,... | collective-permute-start | bytes 49160 | tf_op jit(solution)/shard_map/ppermute | solution.py:41
  24.1 3.9 %collective-permute-start.7 = (bf16[4,2048]{1,0:T(4,128)(2,1)S(1)}, bf16[4,2048]{1,0:T(4,128)(2,1)S(1)}, u32[]{:S(2)}, u32[]{:S(2)}) collective-permute-start(bf16[4,2048]{1,0:T(4,128)(2,1)S(1)} %attn_project.1.token.rest_4_), channel_id=1, source_target_pairs={{0,2},{1,3},{2,0},{3,1},{4,6},{5,7},{6,4},{7,5},{8,10},{9,11},{10,... | collective-permute-start | bytes 49160 | tf_op jit(solution)/shard_map/ppermute | solution.py:41
  25.7 2.3 %collective-permute-start.6 = (bf16[4,2048]{1,0:T(4,128)(2,1)S(1)}, bf16[4,2048]{1,0:T(4,128)(2,1)S(1)}, u32[]{:S(2)}, u32[]{:S(2)}) collective-permute-start(bf16[4,2048]{1,0:T(4,128)(2,1)S(1)} %attn_project.1.token.rest_4_), channel_id=1, source_target_pairs={{0,1},{1,0},{2,3},{3,2},{4,5},{5,4},{6,7},{7,6},{8,9},{9,8},{10,11... | collective-permute-start | bytes 49160 | tf_op jit(solution)/shard_map/ppermute | solution.py:41
  33.9 6.8 %collective-permute-start.11 = (bf16[8,3712]{1,0:T(8,128)(2,1)S(1)}, bf16[8,3712]{1,0:T(8,128)(2,1)S(1)}, u32[]{:S(2)}, u32[]{:S(2)}) collective-permute-start(bf16[8,3712]{1,0:T(8,128)(2,1)S(1)} %get-tuple-element.23.rest_0_), channel_id=1, source_target_pairs={{0,12},{4,8},{8,4},{12,0},{1,13},{5,9},{9,5},{13,1},{2,14},{6,10},... | collective-permute-start | bytes 178184 | tf_op jit(solution)/shard_map/ppermute | solution.py:41
  36.1 6.4 %collective-permute-start.10 = (bf16[8,3712]{1,0:T(8,128)(2,1)S(1)}, bf16[8,3712]{1,0:T(8,128)(2,1)S(1)}, u32[]{:S(2)}, u32[]{:S(2)}) collective-permute-start(bf16[8,3712]{1,0:T(8,128)(2,1)S(1)} %get-tuple-element.23.rest_0_), channel_id=1, source_target_pairs={{0,8},{4,12},{8,0},{12,4},{1,9},{5,13},{9,1},{13,5},{2,10},{6,14},... | collective-permute-start | bytes 178184 | tf_op jit(solution)/shard_map/ppermute | solution.py:41
  36.6 6.0 %collective-permute-start.9 = (bf16[8,3712]{1,0:T(8,128)(2,1)S(1)}, bf16[8,3712]{1,0:T(8,128)(2,1)S(1)}, u32[]{:S(2)}, u32[]{:S(2)}) collective-permute-start(bf16[8,3712]{1,0:T(8,128)(2,1)S(1)} %get-tuple-element.23.rest_0_), channel_id=1, source_target_pairs={{0,4},{4,0},{8,12},{12,8},{1,5},{5,1},{9,13},{13,9},{2,6},{6,2},{1... | collective-permute-start | bytes 178184 | tf_op jit(solution)/shard_map/ppermute | solution.py:41
  44.6 3.2 %collective-permute-start.14 = (bf16[4,2048]{1,0:T(4,128)(2,1)S(1)}, bf16[4,2048]{1,0:T(4,128)(2,1)S(1)}, u32[]{:S(2)}, u32[]{:S(2)}) collective-permute-start(bf16[4,2048]{1,0:T(4,128)(2,1)S(1)} %down.1), channel_id=1, source_target_pairs={{0,3},{1,2},{2,1},{3,0},{4,7},{5,6},{6,5},{7,4},{8,11},{9,10},{10,... | collective-permute-start | bytes 49160 | tf_op jit(solution)/shard_map/ppermute | solution.py:41
  45.6 3.7 %collective-permute-start.13 = (bf16[4,2048]{1,0:T(4,128)(2,1)S(1)}, bf16[4,2048]{1,0:T(4,128)(2,1)S(1)}, u32[]{:S(2)}, u32[]{:S(2)}) collective-permute-start(bf16[4,2048]{1,0:T(4,128)(2,1)S(1)} %down.1), channel_id=1, source_target_pairs={{0,2},{1,3},{2,0},{3,1},{4,6},{5,7},{6,4},{7,5},{8,10},{9,11},{10,... | collective-permute-start | bytes 49160 | tf_op jit(solution)/shard_map/ppermute | solution.py:41
  46.3 3.0 %collective-permute-start.12 = (bf16[4,2048]{1,0:T(4,128)(2,1)S(1)}, bf16[4,2048]{1,0:T(4,128)(2,1)S(1)}, u32[]{:S(2)}, u32[]{:S(2)}) collective-permute-start(bf16[4,2048]{1,0:T(4,128)(2,1)S(1)} %down.1), channel_id=1, source_target_pairs={{0,1},{1,0},{2,3},{3,2},{4,5},{5,4},{6,7},{7,6},{8,9},{9,8},{10,11... | collective-permute-start | bytes 49160 | tf_op jit(solution)/shard_map/ppermute | solution.py:41

commit v18 on v17

--- a/solution.py
+++ b/solution.py
@@ -14,9 +14,9 @@
 ROPE_BASE = 500000.0
 LANES = 128
 MIB = 1 << 20
-COPY_ROWS = 2048
+COPY_ROWS = 4096
 DOWN_ROWS = 1024
-GU_SHARES = (4, 6, 2, 3, 4, 4, 3, 2)
+GU_SHARES = (4, 6, 4, 3, 4, 4, 3)
 F32 = jnp.float32
 BF16 = jnp.bfloat16
 QUARTER = (1.5703125, 4.837512969970703125e-4, 7.549789948768648e-8)
@@ -367,7 +367,7 @@
     wkv = w_keyval.reshape(width, 2 * LANES)
     cache = kv_cache.reshape(cache_len, 2 * LANES)
     packed = 2 * heads
-    wq_parts = 4
+    wq_parts = 8
 
     half = LANES // 2
     freq = ROPE_BASE ** (-(np.arange(half, dtype=np.float64) * 2.0 / LANES))

time: 50.1 us -> 49.9 us (level)
    pallas_call x1, Pallas kernels: 5.86 us -> 5.14 us  [per_device(): pl.pallas_call(functools.partial(gate_up_kernel, kv, len(fetched), shares...]
where the time goes in v18:
time: 49.9 us; the launch traced here: 49.6 us
  Pallas kernels  21 us (42%)
  starting transfers between devices  18.4 us (37%)
  waiting for transfers between devices  8.78 us (18%)
  between operations  0.83 us (2%)
  other arithmetic  0.63 us (1%)
    ppermute x15, starting transfers between devices, exchange(): lax.ppermute(arrays[s], axis, [(i, i ^ s) for i in range(size)])  18.4 us
    ppermute x15, waiting for transfers between devices, exchange(): lax.ppermute(arrays[s], axis, [(i, i ^ s) for i in range(size)])  8.78 us
    pallas_call x3, Pallas kernels, fetch(): pl.pallas_call(functools.partial(fetch_kernel, share[0]), out_shape=block...  6.41 us
    pallas_call x1, Pallas kernels, per_device(): pl.pallas_call(functools.partial(gate_up_kernel, kv, len(fetched), shares...  5.14 us
    pallas_call x1, Pallas kernels, per_device(): pl.pallas_call(functools.partial(qkv_kernel, tp), out_shape=[jax.ShapeDty...  3.71 us
    pallas_call x1, Pallas kernels, per_device(): pl.pallas_call(functools.partial(attend_kernel, tp, heads, 512, shares[1]...  3 us
    pallas_call x1, Pallas kernels, per_device(): pl.pallas_call(functools.partial(down_kernel, tp), out_shape=jax.ShapeDty...  2.08 us
  transfers between devices with their start and end apart: 15, of which 5 were waited for; matrix products, arithmetic and copies ran while one was open for 0% of the time, Pallas kernels for 13%

profile of v18, /device:TPU:0, one launch (start us, length us, event | category | flops | bytes accessed | tf_op | source)
XLA Modules:
  0.0 49.6 jit_solution(8553640472434584963)
XLA Ops:
  0.6 3.7 %qkv.1 = (f32[16,128]{1,0:T(8,128)S(1)}, f32[16,128]{1,0:T(8,128)S(1)}, f32[16,128]{1,0:T(8,128)S(1)}, f32[16,128]{1,0:T(8,128)S(1)}, f32[8,128]{1,0:T(8,128)S(1)}, /*index=5*/s32[8,128]{1,0:T(8,128)S(1)}) custom-call(s32[4]{0:T(128)} %owner_hbm.1, s32[4]{0:T(128)} %lengths_hbm.1, f32[1,128]{1,0:T(1,128)} %constant.2.clone.frequency_hbm, ...), custom_call_target="tpu_custom_call" | custom-call | bytes 29520000 | tf_op jit(solution)/shard_map/qkv/pallas_call | solution.py:375
  4.4 5.1 %collective-permute-start = (f32[16,128]{1,0:T(8,128)S(1)}, f32[16,128]{1,0:T(8,128)S(1)}, u32[]{:S(2)}, u32[]{:S(2)}) collective-permute-start(f32[16,128]{1,0:T(8,128)S(1)} %get-tuple-element.15), channel_id=1, source_target_pairs={{0,12},{4,8},{8,4},{12,0},{1,13},{5,9},{9,5},{13,1},{2,14},{6,10},... | collective-permute-start | bytes 24584 | tf_op jit(solution)/shard_map/ppermute | solution.py:41
  9.5 0.6 %collective-permute-start.2 = (f32[16,128]{1,0:T(8,128)S(1)}, f32[16,128]{1,0:T(8,128)S(1)}, u32[]{:S(2)}, u32[]{:S(2)}) collective-permute-start(f32[16,128]{1,0:T(8,128)S(1)} %get-tuple-element.17), channel_id=1, source_target_pairs={{0,4},{4,0},{8,12},{12,8},{1,5},{5,1},{9,13},{13,9},{2,6},{6,2},{1... | collective-permute-start | bytes 24584 | tf_op jit(solution)/shard_map/ppermute | solution.py:41
  10.1 2.2 %fetch.3.rest_4_.rest_0_ = bf16[4096,512]{1,0:T(8,128)(2,1)S(1)} custom-call(f32[8,128]{1,0:T(8,128)S(1)} %get-tuple-element.14.token.table, bf16[2048,2,3584]{2,1,0:T(2,128)(2,1)} %w.9, bf16[8192,256]{1,0:T(8,128)(2,1)S(1)} %bitcast.6), custom_call_target="tpu_custom_call" | custom-call | bytes 4428000 | tf_op jit(solution)/shard_map/fetch/pallas_call | solution.py:411
  12.4 0.0 collective-permute-done.rest_0_
  12.4 1.6 %collective-permute-done.1.rest_1_ = f32[16,128]{1,0:T(8,128)S(1)} collective-permute-done((f32[16,128]{1,0:T(8,128)S(1)}, f32[16,128]{1,0:T(8,128)S(1)}, u32[]{:S(2)}, u32[]{:S(2)}) %collective-permute-start.1) | collective-permute-done | bytes 8224 | tf_op jit(solution)/shard_map/ppermute | solution.py:41
  14.0 0.0 collective-permute-done.2.rest_2_
  14.0 3.0 %attend.1 = (bf16[8,128]{1,0:T(8,128)(2,1)S(1)}, bf16[1,256]{1,0:T(2,128)(2,1)}, bf16[4096,768]{1,0:T(8,128)(2,1)S(1)}) custom-call(f32[8,128]{1,0:T(8,128)S(1)} %get-tuple-element.14.token.table, bf16[8192,256]{1,0:T(8,128)(2,1)S(1)} %bitcast.7, bf16[2048,2,3584]{2,1,0:T(2,128)(2,1)} %w.9, f32[16,128]{1,0:T(8,128)S(1)} %collective-permute-done.rest_0_, ...), custom_call_target="tpu_custom_call" | custom-call | bytes 29520000 | tf_op jit(solution)/shard_map/attend/pallas_call | solution.py:424
  17.0 0.0 copy-start.1
  17.0 0.0 slice-start.2
  17.1 0.0 slice-start.3
  17.1 2.2 %collective-permute-start.5 = (bf16[8,128]{1,0:T(8,128)(2,1)S(1)}, bf16[8,128]{1,0:T(8,128)(2,1)S(1)}, u32[]{:S(2)}, u32[]{:S(2)}) collective-permute-start(bf16[8,128]{1,0:T(8,128)(2,1)S(1)} %get-tuple-element.20.token.rest_0_), channel_id=1, source_target_pairs={{0,12},{4,8},{8,4},{12,0},{1,13},{5,9},{9,5},{13,1},{2,14},{6,10},... | collective-permute-start | bytes 6152 | tf_op jit(solution)/shard_map/ppermute | solution.py:41
  19.3 2.2 %collective-permute-start.3 = (bf16[8,128]{1,0:T(8,128)(2,1)S(1)}, bf16[8,128]{1,0:T(8,128)(2,1)S(1)}, u32[]{:S(2)}, u32[]{:S(2)}) collective-permute-start(bf16[8,128]{1,0:T(8,128)(2,1)S(1)} %get-tuple-element.20.token.rest_0_), channel_id=1, source_target_pairs={{0,4},{4,0},{8,12},{12,8},{1,5},{5,1},{9,13},{13,9},{2,6},{6,2},{1... | collective-permute-start | bytes 6152 | tf_op jit(solution)/shard_map/ppermute | solution.py:41
  21.5 2.2 %fetch.4.rest_4_.rest_2_ = bf16[4096,512]{1,0:T(8,128)(2,1)S(1)} custom-call(bf16[8,128]{1,0:T(8,128)(2,1)S(1)} %get-tuple-element.20.token.rest_0_, bf16[2048,2,3584]{2,1,0:T(2,128)(2,1)} %w.9), custom_call_target="tpu_custom_call" | custom-call | bytes 4428000 | tf_op jit(solution)/shard_map/fetch/pallas_call | solution.py:411
  23.8 0.7 %attn_project.1.token.rest_4_ = bf16[4,2048]{1,0:T(4,128)(2,1)S(1)} custom-call(s32[8,128]{1,0:T(8,128)S(1)} %get-tuple-element.21.places, bf16[1024,2048]{1,0:T(8,128)(2,1)S(1)} %copy-done.1, bf16[8,128]{1,0:T(8,128)(2,1)S(1)} %get-tuple-element.20.token.rest_0_, bf16[8,128]{1,0:T(8,128)(2,1)S(1)} %collective-permute-done.3.rest_1_, ...), custom_call_target="tpu_custom_call" | custom-call | bytes 22140000 | tf_op jit(solution)/shard_map/attn_project/pallas_call | solution.py:447
  24.5 0.0 collective-permute-start.8
  24.5 1.6 %collective-permute-start.7 = (bf16[4,2048]{1,0:T(4,128)(2,1)S(1)}, bf16[4,2048]{1,0:T(4,128)(2,1)S(1)}, u32[]{:S(2)}, u32[]{:S(2)}) collective-permute-start(bf16[4,2048]{1,0:T(4,128)(2,1)S(1)} %attn_project.1.token.rest_4_), channel_id=1, source_target_pairs={{0,2},{1,3},{2,0},{3,1},{4,6},{5,7},{6,4},{7,5},{8,10},{9,11},{10,... | collective-permute-start | bytes 49160 | tf_op jit(solution)/shard_map/ppermute | solution.py:41
  26.0 0.3 collective-permute-start.6
  26.4 1.9 %fetch.5.rest_3_ = bf16[4096,384]{1,0:T(8,128)(2,1)S(1)} custom-call(bf16[4,2048]{1,0:T(4,128)(2,1)S(1)} %attn_project.1.token.rest_4_, bf16[2048,2,3584]{2,1,0:T(2,128)(2,1)} %w.9, bf16[3584,2048]{1,0:T(8,128)(2,1)S(1)} %bitcast.5), custom_call_target="tpu_custom_call" | custom-call | bytes 3320999 | tf_op jit(solution)/shard_map/fetch/pallas_call | solution.py:411
  28.4 5.1 %gate_up.1 = (bf16[4,2048]{1,0:T(4,128)(2,1)}, bf16[8,3712]{1,0:T(8,128)(2,1)S(1)}) custom-call(bf16[4,2048]{1,0:T(4,128)(2,1)S(1)} %copy-done.2, f32[2,2048]{1,0:T(2,128)S(1)} %copy-done.3, bf16[2048,2,3584]{2,1,0:T(2,128)(2,1)} %w.9, bf16[4096,512]{1,0:T(8,128)(2,1)S(1)} %fetch.3.rest_4_.rest_0_, bf16[4096,768]{1,0:T(8,128)(2,1)S(1)} %get-tuple-element.19.rest_1_, ...), custom_call_target="tpu_custom_call" | custom-call | bytes 36900000 | tf_op jit(solution)/shard_map/gate_up/pallas_call | solution.py:460
  33.5 2.2 %collective-permute-start.11 = (bf16[8,3712]{1,0:T(8,128)(2,1)S(1)}, bf16[8,3712]{1,0:T(8,128)(2,1)S(1)}, u32[]{:S(2)}, u32[]{:S(2)}) collective-permute-start(bf16[8,3712]{1,0:T(8,128)(2,1)S(1)} %get-tuple-element.23.rest_0_), channel_id=1, source_target_pairs={{0,12},{4,8},{8,4},{12,0},{1,13},{5,9},{9,5},{13,1},{2,14},{6,10},... | collective-permute-start | bytes 178184 | tf_op jit(solution)/shard_map/ppermute | solution.py:41
  35.7 0.6 %collective-permute-start.10 = (bf16[8,3712]{1,0:T(8,128)(2,1)S(1)}, bf16[8,3712]{1,0:T(8,128)(2,1)S(1)}, u32[]{:S(2)}, u32[]{:S(2)}) collective-permute-start(bf16[8,3712]{1,0:T(8,128)(2,1)S(1)} %get-tuple-element.23.rest_0_), channel_id=1, source_target_pairs={{0,8},{4,12},{8,0},{12,4},{1,9},{5,13},{9,1},{13,5},{2,10},{6,14},... | collective-permute-start | bytes 178184 | tf_op jit(solution)/shard_map/ppermute | solution.py:41
  36.3 1.6 %collective-permute-start.9 = (bf16[8,3712]{1,0:T(8,128)(2,1)S(1)}, bf16[8,3712]{1,0:T(8,128)(2,1)S(1)}, u32[]{:S(2)}, u32[]{:S(2)}) collective-permute-start(bf16[8,3712]{1,0:T(8,128)(2,1)S(1)} %get-tuple-element.23.rest_0_), channel_id=1, source_target_pairs={{0,4},{4,0},{8,12},{12,8},{1,5},{5,1},{9,13},{13,9},{2,6},{6,2},{1... | collective-permute-start | bytes 178184 | tf_op jit(solution)/shard_map/ppermute | solution.py:41
  38.0 2.2 %collective-permute-done.11.rest_3_ = bf16[8,3712]{1,0:T(8,128)(2,1)S(1)} collective-permute-done((bf16[8,3712]{1,0:T(8,128)(2,1)S(1)}, bf16[8,3712]{1,0:T(8,128)(2,1)S(1)}, u32[]{:S(2)}, u32[]{:S(2)}) %collective-permute-start.11) | collective-permute-done | bytes 59424 | tf_op jit(solution)/shard_map/ppermute | solution.py:41
  40.1 2.2 %collective-permute-done.10.rest_2_ = bf16[8,3712]{1,0:T(8,128)(2,1)S(1)} collective-permute-done((bf16[8,3712]{1,0:T(8,128)(2,1)S(1)}, bf16[8,3712]{1,0:T(8,128)(2,1)S(1)}, u32[]{:S(2)}, u32[]{:S(2)}) %collective-permute-start.10) | collective-permute-done | bytes 59424 | tf_op jit(solution)/shard_map/ppermute | solution.py:41
  42.3 2.1 %down.1 = bf16[4,2048]{1,0:T(4,128)(2,1)S(1)} custom-call(bf16[3584,2048]{1,0:T(8,128)(2,1)S(1)} %bitcast.5, bf16[8,3712]{1,0:T(8,128)(2,1)S(1)} %get-tuple-element.23.rest_0_, bf16[8,3712]{1,0:T(8,128)(2,1)S(1)} %collective-permute-done.9.rest_1_, bf16[8,3712]{1,0:T(8,128)(2,1)S(1)} %collective-permute-done.10.rest_2_, ...), custom_call_target="tpu_custom_call" | custom-call | bytes 18450000 | tf_op jit(solution)/shard_map/down/pallas_call | solution.py:481
  44.4 0.9 %collective-permute-start.14 = (bf16[4,2048]{1,0:T(4,128)(2,1)S(1)}, bf16[4,2048]{1,0:T(4,128)(2,1)S(1)}, u32[]{:S(2)}, u32[]{:S(2)}) collective-permute-start(bf16[4,2048]{1,0:T(4,128)(2,1)S(1)} %down.1), channel_id=1, source_target_pairs={{0,3},{1,2},{2,1},{3,0},{4,7},{5,6},{6,5},{7,4},{8,11},{9,10},{10,... | collective-permute-start | bytes 49160 | tf_op jit(solution)/shard_map/ppermute | solution.py:41
  45.3 0.8 %collective-permute-start.13 = (bf16[4,2048]{1,0:T(4,128)(2,1)S(1)}, bf16[4,2048]{1,0:T(4,128)(2,1)S(1)}, u32[]{:S(2)}, u32[]{:S(2)}) collective-permute-start(bf16[4,2048]{1,0:T(4,128)(2,1)S(1)} %down.1), channel_id=1, source_target_pairs={{0,2},{1,3},{2,0},{3,1},{4,6},{5,7},{6,4},{7,5},{8,10},{9,11},{10,... | collective-permute-start | bytes 49160 | tf_op jit(solution)/shard_map/ppermute | solution.py:41
  46.1 0.2 collective-permute-start.12
  46.3 1.3 %collective-permute-done.14 = bf16[4,2048]{1,0:T(4,128)(2,1)S(1)} collective-permute-done((bf16[4,2048]{1,0:T(4,128)(2,1)S(1)}, bf16[4,2048]{1,0:T(4,128)(2,1)S(1)}, u32[]{:S(2)}, u32[]{:S(2)}) %collective-permute-start.14) | collective-permute-done | bytes 16416 | tf_op jit(solution)/shard_map/ppermute | solution.py:41
  47.6 1.4 %collective-permute-done.13 = bf16[4,2048]{1,0:T(4,128)(2,1)S(1)} collective-permute-done((bf16[4,2048]{1,0:T(4,128)(2,1)S(1)}, bf16[4,2048]{1,0:T(4,128)(2,1)S(1)}, u32[]{:S(2)}, u32[]{:S(2)}) %collective-permute-start.13) | collective-permute-done | bytes 16416 | tf_op jit(solution)/shard_map/ppermute | solution.py:41
  49.0 0.6 %add_convert_fusion = bf16[4,2048]{1,0:T(4,128)(2,1)} fusion(bf16[4,2048]{1,0:T(4,128)(2,1)S(1)} %collective-permute-done.14, bf16[4,2048]{1,0:T(4,128)(2,1)S(1)} %collective-permute-done.13, bf16[4,2048]{1,0:T(4,128)(2,1)S(1)} %collective-permute-done.12, bf16[4,2048]{1,0:T(4,128)(2,1)S(1)} %down.1), kind=kLoop, calls=%fused_computation | loop fusion | flops 65536 | bytes 81920 | tf_op jit(solution)/shard_map/convert_element_type | solution.py:491
  (24 shorter events, 0.1 us)
Async XLA Ops:
  0.6 9.5 %copy-start = (bf16[1,8192,1,256]{3,1,2,0:T(8,128)(2,1)S(1)}, bf16[1,8192,1,256]{3,1,2,0:T(8,128)(2,1)}, u32[]{:S(2)}) copy-start(bf16[1,8192,1,256]{3,1,2,0:T(8,128)(2,1)} %param.18) | copy-start | bytes 12582916
  4.4 8.0 %collective-permute-start = (f32[16,128]{1,0:T(8,128)S(1)}, f32[16,128]{1,0:T(8,128)S(1)}, u32[]{:S(2)}, u32[]{:S(2)}) collective-permute-start(f32[16,128]{1,0:T(8,128)S(1)} %get-tuple-element.15), channel_id=1, source_target_pairs={{0,12},{4,8},{8,4},{12,0},{1,13},{5,9},{9,5},{13,1},{2,14},{6,10},... | collective-permute-start | bytes 24584 | tf_op jit(solution)/shard_map/ppermute | solution.py:41
  9.5 4.5 %collective-permute-start.1 = (f32[16,128]{1,0:T(8,128)S(1)}, f32[16,128]{1,0:T(8,128)S(1)}, u32[]{:S(2)}, u32[]{:S(2)}) collective-permute-start(f32[16,128]{1,0:T(8,128)S(1)} %get-tuple-element.16), channel_id=1, source_target_pairs={{0,8},{4,12},{8,0},{12,4},{1,9},{5,13},{9,1},{13,5},{2,10},{6,14},... | collective-permute-start | bytes 24584 | tf_op jit(solution)/shard_map/ppermute | solution.py:41
  9.5 4.5 %collective-permute-start.2 = (f32[16,128]{1,0:T(8,128)S(1)}, f32[16,128]{1,0:T(8,128)S(1)}, u32[]{:S(2)}, u32[]{:S(2)}) collective-permute-start(f32[16,128]{1,0:T(8,128)S(1)} %get-tuple-element.17), channel_id=1, source_target_pairs={{0,4},{4,0},{8,12},{12,8},{1,5},{5,1},{9,13},{13,9},{2,6},{6,2},{1... | collective-permute-start | bytes 24584 | tf_op jit(solution)/shard_map/ppermute | solution.py:41
  14.0 12.3 %slice-start = ((s8[14680064]{0:T(1024)(128)(4,1)}), s8[4194304]{0:T(1024)(128)(4,1)S(1)}, s32[]{:S(2)}) async-start(s8[14680064]{0:T(1024)(128)(4,1)} %bitcast.4), calls=%async_computation | async-start | bytes 8388608
  14.0 12.3 %slice-start.1 = ((s8[14680064]{0:T(1024)(128)(4,1)}), s8[4194304]{0:T(1024)(128)(4,1)S(1)}, s32[]{:S(2)}) async-start(s8[14680064]{0:T(1024)(128)(4,1)} %bitcast.4), calls=%async_computation.1 | async-start | bytes 8388608
  17.0 6.8 %copy-start.1 = (bf16[1024,2048]{1,0:T(8,128)(2,1)S(1)}, bf16[1024,2048]{1,0:T(8,128)(2,1)}, u32[]{:S(2)}) copy-start(bf16[1024,2048]{1,0:T(8,128)(2,1)} %w_out.1) | copy-start | bytes 12582916
  17.0 9.3 %slice-start.2 = ((s8[14680064]{0:T(1024)(128)(4,1)}), s8[4194304]{0:T(1024)(128)(4,1)S(1)}, s32[]{:S(2)}) async-start(s8[14680064]{0:T(1024)(128)(4,1)} %bitcast.4), calls=%async_computation.2 | async-start | bytes 8388608
  17.1 9.3 %slice-start.3 = ((s8[14680064]{0:T(1024)(128)(4,1)}), s8[2097152]{0:T(1024)(128)(4,1)S(1)}, s32[]{:S(2)}) async-start(s8[14680064]{0:T(1024)(128)(4,1)} %bitcast.4), calls=%async_computation.3 | async-start | bytes 4194304
  17.1 6.7 %collective-permute-start.5 = (bf16[8,128]{1,0:T(8,128)(2,1)S(1)}, bf16[8,128]{1,0:T(8,128)(2,1)S(1)}, u32[]{:S(2)}, u32[]{:S(2)}) collective-permute-start(bf16[8,128]{1,0:T(8,128)(2,1)S(1)} %get-tuple-element.20.token.rest_0_), channel_id=1, source_target_pairs={{0,12},{4,8},{8,4},{12,0},{1,13},{5,9},{9,5},{13,1},{2,14},{6,10},... | collective-permute-start | bytes 6152 | tf_op jit(solution)/shard_map/ppermute | solution.py:41
  19.3 4.5 %collective-permute-start.4 = (bf16[8,128]{1,0:T(8,128)(2,1)S(1)}, bf16[8,128]{1,0:T(8,128)(2,1)S(1)}, u32[]{:S(2)}, u32[]{:S(2)}) collective-permute-start(bf16[8,128]{1,0:T(8,128)(2,1)S(1)} %get-tuple-element.20.token.rest_0_), channel_id=1, source_target_pairs={{0,8},{4,12},{8,0},{12,4},{1,9},{5,13},{9,1},{13,5},{2,10},{6,14},... | collective-permute-start | bytes 6152 | tf_op jit(solution)/shard_map/ppermute | solution.py:41
  19.3 4.5 %collective-permute-start.3 = (bf16[8,128]{1,0:T(8,128)(2,1)S(1)}, bf16[8,128]{1,0:T(8,128)(2,1)S(1)}, u32[]{:S(2)}, u32[]{:S(2)}) collective-permute-start(bf16[8,128]{1,0:T(8,128)(2,1)S(1)} %get-tuple-element.20.token.rest_0_), channel_id=1, source_target_pairs={{0,4},{4,0},{8,12},{12,8},{1,5},{5,1},{9,13},{13,9},{2,6},{6,2},{1... | collective-permute-start | bytes 6152 | tf_op jit(solution)/shard_map/ppermute | solution.py:41
  24.5 3.9 %copy-start.2 = (bf16[4,2048]{1,0:T(4,128)(2,1)S(1)}, bf16[4,2048]{1,0:T(4,128)(2,1)}, u32[]{:S(2)}) copy-start(bf16[4,2048]{1,0:T(4,128)(2,1)} %states.1) | copy-start | bytes 49156
  24.5 3.9 %copy-start.3 = (f32[2,2048]{1,0:T(2,128)S(1)}, f32[2,2048]{1,0:T(2,128)}, u32[]{:S(2)}) copy-start(f32[2,2048]{1,0:T(2,128)} %gains.1) | copy-start | bytes 49156
  24.5 3.9 %collective-permute-start.8 = (bf16[4,2048]{1,0:T(4,128)(2,1)S(1)}, bf16[4,2048]{1,0:T(4,128)(2,1)S(1)}, u32[]{:S(2)}, u32[]{:S(2)}) collective-permute-start(bf16[4,2048]{1,0:T(4,128)(2,1)S(1)} %attn_project.1.token.rest_4_), channel_id=1, source_target_pairs={{0,3},{1,2},{2,1},{3,0},{4,7},{5,6},{6,5},{7,4},{8,11},{9,10},{10,... | collective-permute-start | bytes 49160 | tf_op jit(solution)/shard_map/ppermute | solution.py:41
  24.5 3.8 %collective-permute-start.7 = (bf16[4,2048]{1,0:T(4,128)(2,1)S(1)}, bf16[4,2048]{1,0:T(4,128)(2,1)S(1)}, u32[]{:S(2)}, u32[]{:S(2)}) collective-permute-start(bf16[4,2048]{1,0:T(4,128)(2,1)S(1)} %attn_project.1.token.rest_4_), channel_id=1, source_target_pairs={{0,2},{1,3},{2,0},{3,1},{4,6},{5,7},{6,4},{7,5},{8,10},{9,11},{10,... | collective-permute-start | bytes 49160 | tf_op jit(solution)/shard_map/ppermute | solution.py:41
  26.0 2.3 %collective-permute-start.6 = (bf16[4,2048]{1,0:T(4,128)(2,1)S(1)}, bf16[4,2048]{1,0:T(4,128)(2,1)S(1)}, u32[]{:S(2)}, u32[]{:S(2)}) collective-permute-start(bf16[4,2048]{1,0:T(4,128)(2,1)S(1)} %attn_project.1.token.rest_4_), channel_id=1, source_target_pairs={{0,1},{1,0},{2,3},{3,2},{4,5},{5,4},{6,7},{7,6},{8,9},{9,8},{10,11... | collective-permute-start | bytes 49160 | tf_op jit(solution)/shard_map/ppermute | solution.py:41
  33.5 6.6 %collective-permute-start.11 = (bf16[8,3712]{1,0:T(8,128)(2,1)S(1)}, bf16[8,3712]{1,0:T(8,128)(2,1)S(1)}, u32[]{:S(2)}, u32[]{:S(2)}) collective-permute-start(bf16[8,3712]{1,0:T(8,128)(2,1)S(1)} %get-tuple-element.23.rest_0_), channel_id=1, source_target_pairs={{0,12},{4,8},{8,4},{12,0},{1,13},{5,9},{9,5},{13,1},{2,14},{6,10},... | collective-permute-start | bytes 178184 | tf_op jit(solution)/shard_map/ppermute | solution.py:41
  35.7 6.6 %collective-permute-start.10 = (bf16[8,3712]{1,0:T(8,128)(2,1)S(1)}, bf16[8,3712]{1,0:T(8,128)(2,1)S(1)}, u32[]{:S(2)}, u32[]{:S(2)}) collective-permute-start(bf16[8,3712]{1,0:T(8,128)(2,1)S(1)} %get-tuple-element.23.rest_0_), channel_id=1, source_target_pairs={{0,8},{4,12},{8,0},{12,4},{1,9},{5,13},{9,1},{13,5},{2,10},{6,14},... | collective-permute-start | bytes 178184 | tf_op jit(solution)/shard_map/ppermute | solution.py:41
  36.3 6.0 %collective-permute-start.9 = (bf16[8,3712]{1,0:T(8,128)(2,1)S(1)}, bf16[8,3712]{1,0:T(8,128)(2,1)S(1)}, u32[]{:S(2)}, u32[]{:S(2)}) collective-permute-start(bf16[8,3712]{1,0:T(8,128)(2,1)S(1)} %get-tuple-element.23.rest_0_), channel_id=1, source_target_pairs={{0,4},{4,0},{8,12},{12,8},{1,5},{5,1},{9,13},{13,9},{2,6},{6,2},{1... | collective-permute-start | bytes 178184 | tf_op jit(solution)/shard_map/ppermute | solution.py:41
  44.4 3.2 %collective-permute-start.14 = (bf16[4,2048]{1,0:T(4,128)(2,1)S(1)}, bf16[4,2048]{1,0:T(4,128)(2,1)S(1)}, u32[]{:S(2)}, u32[]{:S(2)}) collective-permute-start(bf16[4,2048]{1,0:T(4,128)(2,1)S(1)} %down.1), channel_id=1, source_target_pairs={{0,3},{1,2},{2,1},{3,0},{4,7},{5,6},{6,5},{7,4},{8,11},{9,10},{10,... | collective-permute-start | bytes 49160 | tf_op jit(solution)/shard_map/ppermute | solution.py:41
  45.3 3.7 %collective-permute-start.13 = (bf16[4,2048]{1,0:T(4,128)(2,1)S(1)}, bf16[4,2048]{1,0:T(4,128)(2,1)S(1)}, u32[]{:S(2)}, u32[]{:S(2)}) collective-permute-start(bf16[4,2048]{1,0:T(4,128)(2,1)S(1)} %down.1), channel_id=1, source_target_pairs={{0,2},{1,3},{2,0},{3,1},{4,6},{5,7},{6,4},{7,5},{8,10},{9,11},{10,... | collective-permute-start | bytes 49160 | tf_op jit(solution)/shard_map/ppermute | solution.py:41
  46.1 2.9 %collective-permute-start.12 = (bf16[4,2048]{1,0:T(4,128)(2,1)S(1)}, bf16[4,2048]{1,0:T(4,128)(2,1)S(1)}, u32[]{:S(2)}, u32[]{:S(2)}) collective-permute-start(bf16[4,2048]{1,0:T(4,128)(2,1)S(1)} %down.1), channel_id=1, source_target_pairs={{0,1},{1,0},{2,3},{3,2},{4,5},{5,4},{6,7},{7,6},{8,9},{9,8},{10,11... | collective-permute-start | bytes 49160 | tf_op jit(solution)/shard_map/ppermute | solution.py:41
